TPU v7x, 32 devices: a whole 2x2x4 slice. The times are simulated.
32 devices in a mesh: groups: 2 (over y), blk: 8 (over z, x), heads: 2 (over core).
Axes of the slice: x: 2, y: 2, z: 4, core: 2. Of those that a mesh axis runs over, the one named last changes fastest.
Arguments:
- queries: bfloat16 [16, 64, 128], P(('groups', 'blk'), 'heads'), parts along dimension 0, may hold values from -256 to 256
- prefix_keys: bfloat16 [4096, 8, 128], P(('groups', 'blk'), 'heads'), parts along dimension 0, may hold values from -12 to 12
- prefix_values: bfloat16 [4096, 8, 128], P(('groups', 'blk'), 'heads'), parts along dimension 0, may hold values from -12 to 12
- suffix_pool: bfloat16 [48, 2, 16, 8, 128], P(('groups', 'blk'), None, None, 'heads'), parts along dimension 0, may hold values from -8.375 to 8.375
- page_owner: int32 [6, 8], P('groups'), parts along dimension 0, may hold values from 0 to 7, as said below
- page_slot: int32 [6, 8], P('groups'), parts along dimension 0, may hold values from 0 to 2, as said below
- suffix_len: int32 [6], P('groups'), parts along dimension 0, may hold values from 1 to 128, as said below
- row_request: int32 [16], P('groups'), parts along dimension 0, may hold values from 0 to 2, as said below
Outputs:
- attn_out: bfloat16 [16, 64, 128], P(('groups', 'blk'), 'heads'), parts along dimension 0
There are 2 independent parts, one for each index of `groups`. A program takes and returns all parts, laid end to end along the dimension named above; each array names one. Nothing has to cross between parts.
Inputs may be any that keep to these rules, and one draw needn't show every extreme that they name: `row_request`: rows 0 to 5 belong to one request, whose last 6 suffix tokens they are, in order; each later row is the only row of its request; every request has rows. `suffix_len`: counts the rows' own tokens; the prefill span's request has 6 or more, and some other request has exactly 128. Each request has one page on every blk index: page j lies on (page_owner[r, 0] + j) modulo the number of blk indices. `page_slot`: A local slot of the owner's pool; two requests never share a slot on one owner.
All inputs are finite; a program needn't handle non-finite values.
Results may differ from a plain program's by a relative error of at most 0.005.
Values may be sent and summed in bfloat16 or wider, within the bound.
No kernel may reach another device: no remote copies, remote signals or barrier semaphores. Data moves between devices by JAX's collectives and lax.ppermute only.
A program may use at most 64 MiB of HBM per device.

v0:
```python
import math

import jax
import jax.numpy as jnp
from jax import lax
from jax.sharding import PartitionSpec as P


def merge_parts(first, second):
    first_max, first_sum, first_acc = first
    second_max, second_sum, second_acc = second
    highest = jnp.maximum(first_max, second_max)
    first_weight = jnp.exp(first_max - highest)
    second_weight = jnp.exp(second_max - highest)
    return (
        highest,
        first_sum * first_weight + second_sum * second_weight,
        first_acc * first_weight[..., None] + second_acc * second_weight[..., None],
    )


def prefix_part(query_rows, prefix_keys, prefix_values, kblock):
    row_count, qheads, head_dim = query_rows.shape
    kv_heads = prefix_keys.shape[1]
    group = qheads // kv_heads
    score_scale = 1.0 / math.sqrt(head_dim)
    grouped = query_rows.reshape(row_count, kv_heads, group, head_dim)
    block_total = prefix_keys.shape[0] // kblock
    key_blocks = prefix_keys.reshape(block_total, kblock, kv_heads, head_dim)
    value_blocks = prefix_values.reshape(block_total, kblock, kv_heads, head_dim)

    def key_step(running, blocks):
        run_max, run_sum, run_acc = running
        key_blk, value_blk = blocks
        scores = (
            jnp.einsum("rgqd,kgd->rgqk", grouped, key_blk, preferred_element_type=jnp.float32)
            * score_scale
        )
        new_max = jnp.maximum(run_max, jnp.max(scores, axis=-1))
        rescale = jnp.exp(run_max - new_max)
        probs = jnp.exp(scores - new_max[..., None])
        run_sum = run_sum * rescale + jnp.sum(probs, axis=-1)
        run_acc = run_acc * rescale[..., None] + jnp.einsum(
            "rgqk,kgd->rgqd",
            probs.astype(jnp.bfloat16),
            value_blk,
            preferred_element_type=jnp.float32,
        )
        return ((new_max, run_sum, run_acc), None)

    initial = (
        jnp.full((row_count, kv_heads, group), -1e30, jnp.float32),
        jnp.zeros((row_count, kv_heads, group), jnp.float32),
        jnp.zeros((row_count, kv_heads, group, head_dim), jnp.float32),
    )
    (run_max, run_sum, run_acc), _ = lax.scan(key_step, initial, (key_blocks, value_blocks))
    return (
        run_max.reshape(row_count, qheads),
        run_sum.reshape(row_count, qheads),
        run_acc.reshape(row_count, qheads, head_dim),
    )


def paged_part(query_rows, page_keys, page_values, visible):
    row_count, qheads, head_dim = query_rows.shape
    kv_heads = page_keys.shape[2]
    group = qheads // kv_heads
    score_scale = 1.0 / math.sqrt(head_dim)
    grouped = query_rows.reshape(row_count, kv_heads, group, head_dim)
    scores = (
        jnp.einsum("rgqd,rkgd->rgqk", grouped, page_keys, preferred_element_type=jnp.float32)
        * score_scale
    )
    shown = visible[:, None, None, :]
    scores = jnp.where(shown, scores, -1e30)
    highest = jnp.max(scores, axis=-1)
    probs = jnp.where(shown, jnp.exp(scores - highest[..., None]), 0.0)
    totals = jnp.sum(probs, axis=-1)
    mixed = jnp.einsum(
        "rgqk,rkgd->rgqd",
        probs.astype(jnp.bfloat16),
        page_values,
        preferred_element_type=jnp.float32,
    )
    return (
        highest.reshape(row_count, qheads),
        totals.reshape(row_count, qheads),
        mixed.reshape(row_count, qheads, head_dim),
    )


def on_device(
    queries, prefix_keys, prefix_values, suffix_pool, page_owner, page_slot, suffix_len, row_request
):
    block_count = lax.axis_size("blk")
    self_index = lax.axis_index("blk")
    rows_dev, qheads, head_dim = queries.shape
    page_len = suffix_pool.shape[2]
    row_count = row_request.shape[0]
    req_count = suffix_len.shape[0]
    kblock = min(prefix_keys.shape[0], 256)
    row_order = jnp.arange(row_count, dtype=jnp.int32)
    same_req = row_request[:, None] == row_request[None, :]
    later_rows = jnp.sum(
        (same_req & (row_order[None, :] > row_order[:, None])).astype(jnp.int32), axis=1
    )
    one_hot = (row_request[:, None] == jnp.arange(req_count, dtype=jnp.int32)[None, :]).astype(
        jnp.int32
    )
    limits = jnp.sum(one_hot * suffix_len[None, :], axis=1) - later_rows
    home_owner = jnp.sum(one_hot * page_owner[None, :, 0], axis=1)
    own_slot = jnp.sum(jnp.where(page_owner == self_index, page_slot, 0), axis=1)
    row_slot = jnp.sum(one_hot * own_slot[None, :], axis=1)
    page_index = (self_index - home_owner) % block_count
    all_rows = lax.all_gather(queries, "blk", axis=0, tiled=True)
    partial_value = prefix_part(all_rows, prefix_keys, prefix_values, kblock)
    first_token = page_index * page_len
    page_data = suffix_pool[row_slot]
    visible = (
        first_token[:, None] + jnp.arange(page_len, dtype=jnp.int32)[None, :] < limits[:, None]
    )
    partial_value = merge_parts(
        partial_value, paged_part(all_rows, page_data[:, 0], page_data[:, 1], visible)
    )
    sectioned = (
        partial_value[0].reshape(block_count, rows_dev, qheads),
        partial_value[1].reshape(block_count, rows_dev, qheads),
        partial_value[2].reshape(block_count, rows_dev, qheads, head_dim),
    )
    part_max = lax.all_to_all(sectioned[0], "blk", split_axis=0, concat_axis=0, tiled=True)
    part_sum = lax.all_to_all(sectioned[1], "blk", split_axis=0, concat_axis=0, tiled=True)
    part_acc = lax.all_to_all(sectioned[2], "blk", split_axis=0, concat_axis=0, tiled=True)
    highest = jnp.max(part_max, axis=0)
    weight = jnp.exp(part_max - highest[None])
    return (
        jnp.sum(part_acc * weight[..., None], axis=0)
        / jnp.sum(part_sum * weight, axis=0)[..., None]
    ).astype(jnp.bfloat16)


def solution(mesh):
    placed = (
        P(("groups", "blk"), "heads", None),
        P(("groups", "blk"), "heads", None),
        P(("groups", "blk"), "heads", None),
        P(("groups", "blk"), None, None, "heads", None),
        P("groups", None),
        P("groups", None),
        P("groups"),
        P("groups"),
    )
    return jax.shard_map(
        on_device,
        mesh=mesh,
        in_specs=placed,
        out_specs=P(("groups", "blk"), "heads", None),
        check_vma=False,
    )
```

profile of v0, /device:TPU:0, one launch (start us, length us, event | category | flops | bytes accessed | tf_op | source)
XLA Modules:
  0.0 72.4 jit_solution(9709522602568486579)
XLA Ops:
  0.0 0.0 copy-start
  0.0 0.0 copy-start.3
  0.0 0.7 copy-done.3
  0.7 0.0 copy-start.5
  0.7 0.0 copy-start.4
  0.7 0.1 slice_reduce_fusion
  0.8 0.5 copy-done.5
  1.4 0.2 convert_reduce_fusion
  1.6 0.0 copy-done.4
  1.6 0.0 copy-start.6
  1.6 0.1 select_reduce_fusion.1
  1.7 0.5 copy-done.6
  2.2 0.1 select_reduce_fusion.3
  2.4 1.7 %gather_fusion = bf16[8,2,16,4,128]{4,3,2,1,0:T(4,128)(2,1)S(1)} fusion(bf16[3,2,16,4,128]{4,3,2,1,0:T(4,128)(2,1)} %param.11, s32[1024]{0:T(1024)S(1)} %pad_clamp_fusion), kind=kCustom, calls=%fused_computation | custom fusion | bytes 524320 | tf_op jit(solution)/shard_map/gather | solution.py:118
  4.0 0.0 copy-start.2
  4.0 0.1 fusion.29
  4.1 0.6 copy-done.2
  4.7 32.3 %all_gather.3 = bf16[8,32,128]{2,1,0:T(8,128)(2,1)S(1)} all-gather(bf16[1,32,128]{2,1,0:T(8,128)(2,1)S(1)} %copy-done.2), channel_id=1, replica_groups=mesh['groups'=2,'blk'=8,'heads'=2] {'blk'}, dimensions={0}, use_global_device_ids=true | all-gather | bytes 73728 | tf_op jit(solution)/shard_map/all_gather | solution.py:115
  37.0 0.1 add_compare_fusion
  37.1 0.0 copy-start.1
  37.1 0.3 fusion.31
  37.3 0.1 reshape.286
  37.4 0.2 fusion.13
  37.7 0.1 reshape.287
  37.7 0.3 copy-done.1
  38.0 0.3 fusion.30
  38.4 0.2 fusion.9
  38.6 0.1 reduce_sum.97
  38.7 0.1 max.64
  38.7 0.6 multiply_add_fusion
  39.4 5.5 %all-to-all-start.1 = ((f32[8,1,32]{2,1,0:T(1,128)}), f32[8,1,32]{2,1,0:T(1,128)S(1)}, u32[]{:S(2)}, u32[]{:S(2)}) async-start(f32[8,1,32]{2,1,0:T(1,128)} %bitcast.13), calls=%async_computation.1 | async-start | bytes 8192 | tf_op jit(solution)/shard_map/all_to_all | solution.py:130
  44.8 0.1 reshape.284
  44.9 0.1 max.62
  45.0 0.0 copy-done
  45.0 0.2 fusion.1
  45.2 6.0 %all-to-all-done.1 = f32[8,1,32]{2,1,0:T(1,128)S(1)} async-done(((f32[8,1,32]{2,1,0:T(1,128)}), f32[8,1,32]{2,1,0:T(1,128)S(1)}, u32[]{:S(2)}, u32[]{:S(2)}) %all-to-all-start.1) | async-done | bytes 1056 | tf_op jit(solution)/shard_map/all_to_all | solution.py:130
  51.3 3.3 %all-to-all-start.2 = ((f32[8,1,32]{2,1,0:T(1,128)}), f32[8,1,32]{2,1,0:T(1,128)S(1)}, u32[]{:S(2)}, u32[]{:S(2)}) async-start(f32[8,1,32]{2,1,0:T(1,128)} %bitcast.16), calls=%async_computation.2 | async-start | bytes 8192 | tf_op jit(solution)/shard_map/all_to_all | solution.py:131
  54.6 0.9 %fusion.6 = f32[8,1,32,128]{3,2,1,0:T(8,128)} fusion(bf16[8,1,16,4,128]{4,3,2,1,0:T(4,128)(2,1)S(1)} %get-tuple-element.34, f32[8,4,8,128]{3,2,0,1:T(8,128)S(1)} %fusion.1, f32[8,4,8,16]{3,2,1,0:T(8,128)S(1)} %get-tuple-element.42, f32[8,32]{1,0:T(8,128)S(1)} %get-tuple-element.38, f32[8,4,8]{2,1,0:T(4,128)S(1)} %get-tuple-element.41, ...), kind=kOutput, calls=%fused_computation.11 | convolution fusion | flops 1159168 | bytes 412800 | tf_op jit(solution)/shard_map/rgqk,rkgd->rgqd/dot_general | solution.py:79
  55.5 5.5 %all-to-all-done.2 = f32[8,1,32]{2,1,0:T(1,128)S(1)} async-done(((f32[8,1,32]{2,1,0:T(1,128)}), f32[8,1,32]{2,1,0:T(1,128)S(1)}, u32[]{:S(2)}, u32[]{:S(2)}) %all-to-all-start.2) | async-done | bytes 1056 | tf_op jit(solution)/shard_map/all_to_all | solution.py:131
  61.0 3.4 %all-to-all-start = ((f32[8,1,32,128]{3,2,1,0:T(8,128)}), f32[8,1,32,128]{3,2,1,0:T(8,128)S(1)}, u32[]{:S(2)}, u32[]{:S(2)}) async-start(f32[8,1,32,128]{3,2,1,0:T(8,128)} %fusion.6), calls=%async_computation | async-start | bytes 262144 | tf_op jit(solution)/shard_map/all_to_all | solution.py:132
  64.4 7.2 %all-to-all-done = f32[8,1,32,128]{3,2,1,0:T(8,128)S(1)} async-done(((f32[8,1,32,128]{3,2,1,0:T(8,128)}), f32[8,1,32,128]{3,2,1,0:T(8,128)S(1)}, u32[]{:S(2)}, u32[]{:S(2)}) %all-to-all-start) | async-done | bytes 131104 | tf_op jit(solution)/shard_map/all_to_all | solution.py:132
  71.6 0.1 multiply_reduce_fusion
  71.7 0.7 fusion.20
  (10 shorter events, 0.1 us)
Async XLA Ops:
  0.0 45.0 %copy-start = (bf16[256,4,128]{2,1,0:T(4,128)(2,1)S(1)}, bf16[256,4,128]{2,1,0:T(4,128)(2,1)}, u32[]{:S(2)}) copy-start(bf16[256,4,128]{2,1,0:T(4,128)(2,1)} %param.10) | copy-start | bytes 786436
  0.0 0.7 %copy-start.3 = (s32[3,8]{1,0:T(4,128)S(1)}, s32[3,8]{1,0:T(4,128)}, u32[]{:S(2)}) copy-start(s32[3,8]{1,0:T(4,128)} %param.12) | copy-start | bytes 292
  0.7 0.7 copy-start.5
  0.7 0.8 %copy-start.4 = (s32[3,8]{1,0:T(4,128)S(1)}, s32[3,8]{1,0:T(4,128)}, u32[]{:S(2)}) copy-start(s32[3,8]{1,0:T(4,128)} %param.13) | copy-start | bytes 292
  1.6 0.7 copy-start.6
  4.0 0.7 copy-start.2
  37.1 1.0 %copy-start.1 = (bf16[256,4,128]{2,1,0:T(4,128)(2,1)S(1)}, bf16[256,4,128]{2,1,0:T(4,128)(2,1)}, u32[]{:S(2)}) copy-start(bf16[256,4,128]{2,1,0:T(4,128)(2,1)} %param.9) | copy-start | bytes 786436
  39.4 11.9 %all-to-all-start.1 = ((f32[8,1,32]{2,1,0:T(1,128)}), f32[8,1,32]{2,1,0:T(1,128)S(1)}, u32[]{:S(2)}, u32[]{:S(2)}) async-start(f32[8,1,32]{2,1,0:T(1,128)} %bitcast.13), calls=%async_computation.1 | async-start | bytes 8192 | tf_op jit(solution)/shard_map/all_to_all | solution.py:130
  51.3 9.7 %all-to-all-start.2 = ((f32[8,1,32]{2,1,0:T(1,128)}), f32[8,1,32]{2,1,0:T(1,128)S(1)}, u32[]{:S(2)}, u32[]{:S(2)}) async-start(f32[8,1,32]{2,1,0:T(1,128)} %bitcast.16), calls=%async_computation.2 | async-start | bytes 8192 | tf_op jit(solution)/shard_map/all_to_all | solution.py:131
  61.0 10.7 %all-to-all-start = ((f32[8,1,32,128]{3,2,1,0:T(8,128)}), f32[8,1,32,128]{3,2,1,0:T(8,128)S(1)}, u32[]{:S(2)}, u32[]{:S(2)}) async-start(f32[8,1,32,128]{3,2,1,0:T(8,128)} %fusion.6), calls=%async_computation | async-start | bytes 262144 | tf_op jit(solution)/shard_map/all_to_all | solution.py:132
where the time goes:
time: 72.8 us; the launch traced here: 72.4 us
  blocking collectives  32.3 us (44%)
  waiting for transfers between devices  18.7 us (26%)
  starting transfers between devices  12.1 us (17%)
  local copies, waits for them, and re-layouts  5.05 us (7%)
  other arithmetic  2.39 us (3%)
  matrix products  1.66 us (2%)
    all_gather x1, blocking collectives, on_device(): all_rows = lax.all_gather(queries, 'blk', axis=0, tiled=True)  32.3 us
    all_to_all x1, waiting for transfers between devices, on_device(): lax.all_to_all(sectioned[2], 'blk', split_axis=0, concat_axis=0, tiled=True)  7.22 us
    all_to_all x1, waiting for transfers between devices, on_device(): lax.all_to_all(sectioned[0], 'blk', split_axis=0, concat_axis=0, tiled=True)  6.05 us
    all_to_all x1, waiting for transfers between devices, on_device(): lax.all_to_all(sectioned[1], 'blk', split_axis=0, concat_axis=0, tiled=True)  5.47 us
    all_to_all x1, starting transfers between devices, on_device(): lax.all_to_all(sectioned[0], 'blk', split_axis=0, concat_axis=0, tiled=True)  5.46 us
    all_to_all x1, starting transfers between devices, on_device(): lax.all_to_all(sectioned[2], 'blk', split_axis=0, concat_axis=0, tiled=True)  3.37 us
    all_to_all x1, starting transfers between devices, on_device(): lax.all_to_all(sectioned[1], 'blk', split_axis=0, concat_axis=0, tiled=True)  3.31 us
    unnamed x14, local copies, waits for them, and re-layouts  2.68 us
  transfers between devices with their start and end apart: 3, of which 3 were waited for; matrix products, arithmetic and copies ran while one was open for 2% of the time, Pallas kernels for 0%

commit v1 on v0

v1 whole, which is shorter than its diff:
```python
import math

import jax
import jax.numpy as jnp
from jax import lax
from jax.sharding import PartitionSpec as P


def on_device(
    queries, prefix_keys, prefix_values, suffix_pool, page_owner, page_slot, suffix_len, row_request
):
    block_count = lax.axis_size("blk")
    self_index = lax.axis_index("blk")
    rows_dev, qheads, head_dim = queries.shape
    slots, _, page_len, kv_heads, _ = suffix_pool.shape
    row_count = row_request.shape[0]
    req_count = suffix_len.shape[0]
    prefix_len = prefix_keys.shape[0]
    group = qheads // kv_heads
    score_scale = 1.0 / math.sqrt(head_dim)

    spread = jnp.broadcast_to(queries[None], (block_count,) + queries.shape)
    all_rows = lax.all_to_all(spread, "blk", split_axis=0, concat_axis=0, tiled=True)
    grouped = all_rows.reshape(row_count, kv_heads, group, head_dim)

    row_order = jnp.arange(row_count, dtype=jnp.int32)
    same_req = row_request[:, None] == row_request[None, :]
    later_rows = jnp.sum(
        (same_req & (row_order[None, :] > row_order[:, None])).astype(jnp.int32), axis=1
    )
    one_hot = (row_request[:, None] == jnp.arange(req_count, dtype=jnp.int32)[None, :]).astype(
        jnp.int32
    )
    limits = jnp.sum(one_hot * suffix_len[None, :], axis=1) - later_rows
    home_owner = jnp.sum(one_hot * page_owner[None, :, 0], axis=1)
    own_slot = jnp.sum(jnp.where(page_owner == self_index, page_slot, 0), axis=1)
    row_slot = jnp.sum(one_hot * own_slot[None, :], axis=1)
    page_index = (self_index - home_owner) % block_count
    token = page_index[:, None] * page_len + jnp.arange(page_len, dtype=jnp.int32)[None, :]
    in_slot = row_slot[:, None] == jnp.arange(slots, dtype=jnp.int32)[None, :]
    visible = (in_slot[:, :, None] & (token < limits[:, None])[:, None, :]).reshape(
        row_count, slots * page_len
    )
    shown = jnp.concatenate([jnp.ones((row_count, prefix_len), bool), visible], axis=1)
    keys = jnp.concatenate(
        [prefix_keys, suffix_pool[:, 0].reshape(slots * page_len, kv_heads, head_dim)], axis=0
    )
    values = jnp.concatenate(
        [prefix_values, suffix_pool[:, 1].reshape(slots * page_len, kv_heads, head_dim)], axis=0
    )
    scores = (
        jnp.einsum("rgqd,kgd->rgqk", grouped, keys, preferred_element_type=jnp.float32)
        * score_scale
    )
    scores = jnp.where(shown[:, None, None, :], scores, -jnp.inf)
    top = jnp.max(scores, axis=-1)
    probs = jnp.exp(scores - top[..., None])
    total = jnp.sum(probs, axis=-1)
    mixed = jnp.einsum(
        "rgqk,kgd->rgqd",
        probs.astype(jnp.bfloat16),
        values,
        preferred_element_type=jnp.float32,
    )
    stats = jnp.stack(
        [top.reshape(row_count, qheads), total.reshape(row_count, qheads)], axis=1
    ).reshape(row_count, 2 * qheads)
    stat_rows = -(-2 * qheads // head_dim)
    stats = jnp.pad(stats, ((0, 0), (0, stat_rows * head_dim - 2 * qheads)))
    parcel = jnp.concatenate(
        [mixed.reshape(row_count, qheads, head_dim), stats.reshape(row_count, stat_rows, head_dim)],
        axis=1,
    ).reshape(block_count, rows_dev, qheads + stat_rows, head_dim)
    parcel = lax.all_to_all(parcel, "blk", split_axis=0, concat_axis=0, tiled=True)
    stats = parcel[:, :, qheads:].reshape(block_count, rows_dev, -1)
    part_max = stats[:, :, :qheads]
    part_sum = stats[:, :, qheads : 2 * qheads]
    weight = jnp.exp(part_max - jnp.max(part_max, axis=0)[None])
    return (
        jnp.sum(parcel[:, :, :qheads] * weight[..., None], axis=0)
        / jnp.sum(part_sum * weight, axis=0)[..., None]
    ).astype(jnp.bfloat16)


def solution(mesh):
    placed = (
        P(("groups", "blk"), "heads", None),
        P(("groups", "blk"), "heads", None),
        P(("groups", "blk"), "heads", None),
        P(("groups", "blk"), None, None, "heads", None),
        P("groups", None),
        P("groups", None),
        P("groups"),
        P("groups"),
    )
    return jax.shard_map(
        on_device,
        mesh=mesh,
        in_specs=placed,
        out_specs=P(("groups", "blk"), "heads", None),
        check_vma=False,
    )
```

time: 72.8 us -> 28.3 us (0.39)
  blocking collectives: 32.3 us -> 9.77 us
  waiting for transfers between devices: 18.7 us -> 4.94 us
  starting transfers between devices: 12.1 us -> 7.39 us
  local copies, waits for them, and re-layouts: 5.05 us -> 3.08 us
  matrix products: 1.66 us -> 0.58 us
    all_gather x1 -> x0, blocking collectives: 32.3 us -> none  [on_device(): all_rows = lax.all_gather(queries, 'blk', axis=0, tiled=True)]
    all_to_all x3 -> x1, waiting for transfers between devices: 18.7 us -> 4.94 us  [on_device(): lax.all_to_all(spread, 'blk', split_axis=0, concat_axis=0, tiled=True)]
    all_to_all x0 -> x1, blocking collectives: none -> 9.77 us  [on_device(): lax.all_to_all(parcel, 'blk', split_axis=0, concat_axis=0, tiled=True)]
    all_to_all x3 -> x1, starting transfers between devices: 12.1 us -> 7.39 us  [on_device(): lax.all_to_all(spread, 'blk', split_axis=0, concat_axis=0, tiled=True)]
    unnamed x14 -> x16, local copies, waits for them, and re-layouts: 2.68 us -> 1 us
    gather x1 -> x0, local copies, waits for them, and re-layouts: 1.66 us -> none  [on_device(): page_data = suffix_pool[row_slot]]
    broadcast_in_dim x0 -> x1, local copies, waits for them, and re-layouts: none -> 1.39 us  [on_device(): spread = jnp.broadcast_to(queries[None], (block_count,) + queries.shape)]
    dot_general x4 -> x2, matrix products: 1.66 us -> 0.58 us  [the longest x1 0.31 us: on_device(): jnp.einsum('rgqd,kgd->rgqk', grouped, keys, preferred_element_type=jnp.fl...]
  transfers between devices with their start and end apart: 3 -> 1, of which waited for: 3 -> 1; matrix products, arithmetic and copies ran while one was open for 2% -> 4% of each run, Pallas kernels for 0% -> 0%
where the time goes in v1:
time: 28.3 us; the launch traced here: 27.9 us
  blocking collectives  9.77 us (35%)
  starting transfers between devices  7.39 us (26%)
  waiting for transfers between devices  4.94 us (17%)
  local copies, waits for them, and re-layouts  3.08 us (11%)
  other arithmetic  2.01 us (7%)
  matrix products  0.58 us (2%)
    all_to_all x1, blocking collectives, on_device(): lax.all_to_all(parcel, 'blk', split_axis=0, concat_axis=0, tiled=True)  9.77 us
    all_to_all x1, starting transfers between devices, on_device(): lax.all_to_all(spread, 'blk', split_axis=0, concat_axis=0, tiled=True)  7.39 us
    all_to_all x1, waiting for transfers between devices, on_device(): lax.all_to_all(spread, 'blk', split_axis=0, concat_axis=0, tiled=True)  4.94 us
    broadcast_in_dim x1, local copies, waits for them, and re-layouts, on_device(): spread = jnp.broadcast_to(queries[None], (block_count,) + queries.shape)  1.39 us
    unnamed x16, local copies, waits for them, and re-layouts  1 us
    convert_element_type x1, other arithmetic, on_device(): return (jnp.sum(parcel[:, :, :qheads] * weight[..., None], axis=0) / jnp....  0.68 us
  transfers between devices with their start and end apart: 1, of which 1 were waited for; matrix products, arithmetic and copies ran while one was open for 4% of the time, Pallas kernels for 0%

profile of v1, /device:TPU:0, one launch (start us, length us, event | category | flops | bytes accessed | tf_op | source)
XLA Modules:
  0.0 27.9 jit_solution(3556581340940261297)
XLA Ops:
  0.0 0.0 copy-start.3
  0.0 0.0 copy-start.5
  0.0 0.0 copy-start.4
  0.0 0.0 copy-start.6
  0.0 0.0 copy-start.2
  0.0 1.4 %broadcast_in_dim.19 = bf16[8,1,32,128]{3,2,1,0:T(8,128)(2,1)} broadcast(bf16[32,128]{1,0:T(8,128)(2,1)} %bitcast.44), dimensions={2,3} | broadcast | bytes 73728 | tf_op jit(solution)/shard_map/broadcast_in_dim | solution.py:22
  1.4 0.0 copy-start
  1.4 7.4 %all-to-all-start = ((bf16[8,1,32,128]{3,2,1,0:T(8,128)(2,1)}), bf16[8,1,32,128]{3,2,1,0:T(8,128)(2,1)S(1)}, u32[]{:S(2)}, u32[]{:S(2)}) async-start(bf16[8,1,32,128]{3,2,1,0:T(8,128)(2,1)} %broadcast_in_dim.19), calls=%async_computation | async-start | bytes 131072 | tf_op jit(solution)/shard_map/all_to_all | solution.py:23
  8.8 0.0 copy-done.3
  8.8 0.1 slice_reduce_fusion.1
  8.9 0.0 copy-done.5
  8.9 0.2 convert_reduce_fusion
  9.1 0.0 copy-done.4
  9.1 0.1 select_reduce_fusion.3
  9.2 0.0 copy-done.6
  9.2 0.1 select_reduce_fusion.2
  9.3 0.1 iota_compare_fusion.1
  9.4 0.1 add_compare_fusion
  9.5 0.1 broadcast_and_fusion
  9.6 0.1 and.38
  9.7 0.0 copy-done.2
  9.7 0.0 copy-done
  9.8 0.0 copy-start.1
  9.8 0.9 %copy-done.1 = bf16[256,4,128]{2,1,0:T(4,128)(2,1)S(1)} copy-done((bf16[256,4,128]{2,1,0:T(4,128)(2,1)S(1)}, bf16[256,4,128]{2,1,0:T(4,128)(2,1)}, u32[]{:S(2)}) %copy-start.1) | copy-done | bytes 262168
  10.8 4.9 %all-to-all-done = bf16[8,1,32,128]{3,2,1,0:T(8,128)(2,1)S(1)} async-done(((bf16[8,1,32,128]{3,2,1,0:T(8,128)(2,1)}), bf16[8,1,32,128]{3,2,1,0:T(8,128)(2,1)S(1)}, u32[]{:S(2)}, u32[]{:S(2)}) %all-to-all-start) | async-done | bytes 65568 | tf_op jit(solution)/shard_map/all_to_all | solution.py:23
  15.7 0.3 %fusion.20 = (f32[8,4,8]{2,0,1:T(8,128)S(1)}, f32[8,4,8,304]{3,2,0,1:T(8,128)S(1)}) fusion(bf16[48,4,128]{2,0,1:T(8,128)(2,1)S(1)} %bitcast.42, bf16[256,4,128]{2,0,1:T(8,128)(2,1)S(1)} %copy.43, pred[8,304]{1,0:T(8,128)(4,1)S(1)} %concatenate.13, bf16[8,1,32,128]{3,2,1,0:T(8,128)(2,1)S(1)} %all-to-all-done), kind=kOutput, calls=%fused_computation.46 | convolution fusion | flops 20778752 | bytes 691584 | tf_op jit(solution)/shard_map/rgqd,kgd->rgqk/dot_general | solution.py:52
  16.0 0.2 fusion.2
  16.3 0.1 stack_reshape.7
  16.4 0.1 stack_reshape.6
  16.5 0.1 reshape.148
  16.5 0.3 convolution_bitcast_fusion
  16.9 0.1 copy.49
  17.0 9.8 %all_to_all.10 = f32[8,1,33,128]{3,1,2,0:T(1,128)S(1)} all-to-all(f32[8,1,33,128]{3,1,2,0:T(1,128)S(1)} %copy.49), channel_id=1, replica_groups=mesh['groups'=2,'blk'=8,'heads'=2] {'blk'}, dimensions={0} | all-to-all | bytes 270336 | tf_op jit(solution)/shard_map/all_to_all | solution.py:74
  26.8 0.1 multiply_reduce_fusion
  26.9 0.3 %fusion.10 = f32[32,128]{1,0:T(8,128)S(1)} fusion(f32[8,1,33,128]{3,1,2,0:T(1,128)S(1)} %all_to_all.10, f32[8,32]{1,0:T(8,128)S(1)} %get-tuple-element.11), kind=kLoop, calls=%fused_computation.17 | loop fusion | flops 61440 | bytes 148480 | tf_op jit(solution)/shard_map/reduce_sum | solution.py:80
  27.2 0.7 %fusion.12 = bf16[1,32,128]{2,1,0:T(8,128)(2,1)} fusion(f32[32,128]{1,0:T(8,128)S(1)} %fusion.10, f32[32]{0:T(128)S(1)} %get-tuple-element.10), kind=kLoop, calls=%fused_computation.20 | loop fusion | flops 8192 | bytes 24704 | tf_op jit(solution)/shard_map/convert_element_type | solution.py:82
  (17 shorter events, 0.2 us)
Async XLA Ops:
  0.0 8.8 %copy-start.3 = (s32[3,8]{1,0:T(4,128)S(1)}, s32[3,8]{1,0:T(4,128)}, u32[]{:S(2)}) copy-start(s32[3,8]{1,0:T(4,128)} %param.12) | copy-start | bytes 292
  0.0 8.9 %copy-start.5 = (s32[8]{0:T(128)S(1)}, s32[8]{0:T(128)}, u32[]{:S(2)}) copy-start(s32[8]{0:T(128)} %param.15) | copy-start | bytes 100
  0.0 9.1 %copy-start.4 = (s32[3,8]{1,0:T(4,128)S(1)}, s32[3,8]{1,0:T(4,128)}, u32[]{:S(2)}) copy-start(s32[3,8]{1,0:T(4,128)} %param.13) | copy-start | bytes 292
  0.0 9.2 %copy-start.6 = (s32[3]{0:T(128)S(1)}, s32[3]{0:T(128)}, u32[]{:S(2)}) copy-start(s32[3]{0:T(128)} %param.14) | copy-start | bytes 40
  0.0 9.7 %copy-start.2 = (bf16[3,2,16,4,128]{4,3,2,1,0:T(4,128)(2,1)S(1)}, bf16[3,2,16,4,128]{4,3,2,1,0:T(4,128)(2,1)}, u32[]{:S(2)}) copy-start(bf16[3,2,16,4,128]{4,3,2,1,0:T(4,128)(2,1)} %param.11) | copy-start | bytes 294916
  1.4 8.3 %copy-start = (bf16[256,4,128]{2,1,0:T(4,128)(2,1)S(1)}, bf16[256,4,128]{2,1,0:T(4,128)(2,1)}, u32[]{:S(2)}) copy-start(bf16[256,4,128]{2,1,0:T(4,128)(2,1)} %param.9) | copy-start | bytes 786436
  1.4 14.3 %all-to-all-start = ((bf16[8,1,32,128]{3,2,1,0:T(8,128)(2,1)}), bf16[8,1,32,128]{3,2,1,0:T(8,128)(2,1)S(1)}, u32[]{:S(2)}, u32[]{:S(2)}) async-start(bf16[8,1,32,128]{3,2,1,0:T(8,128)(2,1)} %broadcast_in_dim.19), calls=%async_computation | async-start | bytes 131072 | tf_op jit(solution)/shard_map/all_to_all | solution.py:23
  9.8 1.0 %copy-start.1 = (bf16[256,4,128]{2,1,0:T(4,128)(2,1)S(1)}, bf16[256,4,128]{2,1,0:T(4,128)(2,1)}, u32[]{:S(2)}) copy-start(bf16[256,4,128]{2,1,0:T(4,128)(2,1)} %param.10) | copy-start | bytes 786436

commit v2 on v1

v2 whole, which is shorter than its diff:
```python
import math

import jax
import jax.numpy as jnp
from jax import lax
from jax.sharding import PartitionSpec as P


def exchange(value, bit):
    size = lax.axis_size("blk")
    return lax.ppermute(value, "blk", [(i, i ^ bit) for i in range(size)])


def row_tables(rows, page_owner, page_slot, suffix_len, row_request):
    row_count = row_request.shape[0]
    req_count = suffix_len.shape[0]
    row_order = jnp.arange(row_count, dtype=jnp.int32)
    same_req = row_request[rows][:, None] == row_request[None, :]
    later = jnp.sum((same_req & (row_order[None, :] > rows[:, None])).astype(jnp.int32), axis=1)
    one_hot = row_request[rows][:, None] == jnp.arange(req_count, dtype=jnp.int32)[None, :]
    limits = jnp.sum(jnp.where(one_hot, suffix_len[None, :], 0), axis=1) - later
    home = jnp.sum(jnp.where(one_hot, page_owner[None, :, 0], 0), axis=1)
    return one_hot, limits, home


def visible_pages(device, one_hot, limits, home, page_owner, page_slot, slots, page_len):
    block_count = lax.axis_size("blk")
    own_slot = jnp.sum(jnp.where(page_owner == device, page_slot, 0), axis=1)
    row_slot = jnp.sum(jnp.where(one_hot, own_slot[None, :], 0), axis=1)
    page_index = (device - home) % block_count
    token = page_index[:, None] * page_len + jnp.arange(page_len, dtype=jnp.int32)[None, :]
    in_slot = row_slot[:, None] == jnp.arange(slots, dtype=jnp.int32)[None, :]
    shown = in_slot[:, :, None] & (token < limits[:, None])[:, None, :]
    return shown.reshape(limits.shape[0], slots * page_len)


def attend(grouped, parts):
    score_scale = 1.0 / math.sqrt(grouped.shape[-1])
    scored = []
    for keys, _, shown in parts:
        scores = (
            jnp.einsum("rgqd,kgd->rgqk", grouped, keys, preferred_element_type=jnp.float32)
            * score_scale
        )
        if shown is not None:
            scores = jnp.where(shown[:, None, None, :], scores, -jnp.inf)
        scored.append(scores)
    top = jnp.max(scored[0], axis=-1)
    for scores in scored[1:]:
        top = jnp.maximum(top, jnp.max(scores, axis=-1))
    total = 0.0
    mixed = 0.0
    for scores, (_, values, _) in zip(scored, parts):
        probs = jnp.exp(scores - top[..., None])
        total = total + jnp.sum(probs, axis=-1)
        mixed = mixed + jnp.einsum(
            "rgqk,kgd->rgqd",
            probs.astype(jnp.bfloat16),
            values,
            preferred_element_type=jnp.float32,
        )
    return top, total, mixed


def pack(top, total, mixed):
    rows, qheads, head_dim = mixed.shape
    stat_rows = -(-2 * qheads // head_dim)
    stats = jnp.concatenate([top, total], axis=1)
    stats = jnp.pad(stats, ((0, 0), (0, stat_rows * head_dim - 2 * qheads)))
    return jnp.concatenate([mixed, stats.reshape(rows, stat_rows, head_dim)], axis=1)


def unpack(parcel, qheads):
    stats = parcel[:, qheads:].reshape(parcel.shape[0], -1)
    return stats[:, :qheads], stats[:, qheads : 2 * qheads], parcel[:, :qheads]


def merge(first, second):
    top = jnp.maximum(first[0], second[0])
    first_weight = jnp.exp(first[0] - top)
    second_weight = jnp.exp(second[0] - top)
    return (
        top,
        first[1] * first_weight + second[1] * second_weight,
        first[2] * first_weight[..., None] + second[2] * second_weight[..., None],
    )


def on_device(
    queries, prefix_keys, prefix_values, suffix_pool, page_owner, page_slot, suffix_len, row_request
):
    block_count = lax.axis_size("blk")
    me = lax.axis_index("blk")
    rows_dev, qheads, head_dim = queries.shape
    slots, _, page_len, kv_heads, _ = suffix_pool.shape
    bits = [1 << b for b in range(1, block_count.bit_length() - 1)]

    far_keys = exchange(prefix_keys, 1)
    held = queries
    for bit in bits:
        held = jnp.concatenate([held, exchange(held, bit)], axis=0)
    far_values = exchange(prefix_values, 1)
    far_pool = exchange(suffix_pool, 1)
    held_count = held.shape[0]

    order = jnp.arange(held_count, dtype=jnp.int32)
    rows = (me ^ ((order // rows_dev) * 2)) * rows_dev + order % rows_dev
    one_hot, limits, home = row_tables(rows, page_owner, page_slot, suffix_len, row_request)
    parts = [(prefix_keys, prefix_values, None), (far_keys, far_values, None)]
    for device, pool in ((me, suffix_pool), (me ^ 1, far_pool)):
        shown = visible_pages(device, one_hot, limits, home, page_owner, page_slot, slots, page_len)
        pages = pool.reshape(slots, 2, page_len, kv_heads, head_dim)
        parts.append(
            (
                pages[:, 0].reshape(slots * page_len, kv_heads, head_dim),
                pages[:, 1].reshape(slots * page_len, kv_heads, head_dim),
                shown,
            )
        )
    grouped = held.reshape(held_count, kv_heads, qheads // kv_heads, head_dim)
    top, total, mixed = attend(grouped, parts)
    part = (
        top.reshape(held_count, qheads),
        total.reshape(held_count, qheads),
        mixed.reshape(held_count, qheads, head_dim),
    )
    for bit in reversed(bits):
        half = part[0].shape[0] // 2
        sent = pack(*(value[half:] for value in part))
        part = merge(tuple(value[:half] for value in part), unpack(exchange(sent, bit), qheads))
    return (part[2] / part[1][..., None]).astype(jnp.bfloat16)


def solution(mesh):
    placed = (
        P(("groups", "blk"), "heads", None),
        P(("groups", "blk"), "heads", None),
        P(("groups", "blk"), "heads", None),
        P(("groups", "blk"), None, None, "heads", None),
        P("groups", None),
        P("groups", None),
        P("groups"),
        P("groups"),
    )
    return jax.shard_map(
        on_device,
        mesh=mesh,
        in_specs=placed,
        out_specs=P(("groups", "blk"), "heads", None),
        check_vma=False,
    )
```

time: 28.3 us -> 29.8 us (1.053)
  blocking collectives: 9.77 us -> 0 us
  starting transfers between devices: 7.39 us -> 12.1 us
  waiting for transfers between devices: 4.94 us -> 9.28 us
  matrix products: 0.58 us -> 1.86 us
  local copies, waits for them, and re-layouts: 3.08 us -> 3.69 us
  other arithmetic: 2.01 us -> 2.41 us
    ppermute x0 -> x7, starting transfers between devices: none -> 12.1 us  [exchange(): return lax.ppermute(value, 'blk', [(i, i ^ bit) for i in range(size)])]
    all_to_all x1 -> x0, blocking collectives: 9.77 us -> none  [on_device(): lax.all_to_all(parcel, 'blk', split_axis=0, concat_axis=0, tiled=True)]
    ppermute x0 -> x7, waiting for transfers between devices: none -> 9.28 us  [exchange(): return lax.ppermute(value, 'blk', [(i, i ^ bit) for i in range(size)])]
    all_to_all x1 -> x0, starting transfers between devices: 7.39 us -> none  [on_device(): lax.all_to_all(spread, 'blk', split_axis=0, concat_axis=0, tiled=True)]
    all_to_all x1 -> x0, waiting for transfers between devices: 4.94 us -> none  [on_device(): lax.all_to_all(spread, 'blk', split_axis=0, concat_axis=0, tiled=True)]
    broadcast_in_dim x1 -> x0, local copies, waits for them, and re-layouts: 1.39 us -> none  [on_device(): spread = jnp.broadcast_to(queries[None], (block_count,) + queries.shape)]
    dot_general x2 -> x8, matrix products: 0.58 us -> 1.86 us  [the longest x4 1.01 us: attend(): jnp.einsum('rgqd,kgd->rgqk', grouped, keys, preferred_element_type=jnp.fl...]
    unnamed x16 -> x18, local copies, waits for them, and re-layouts: 1 us -> 2.27 us
  transfers between devices with their start and end apart: 1 -> 7, of which waited for: 1 -> 4; matrix products, arithmetic and copies ran while one was open for 4% -> 17% of each run, Pallas kernels for 0% -> 0%
where the time goes in v2:
time: 29.8 us; the launch traced here: 29.6 us
  starting transfers between devices  12.1 us (41%)
  waiting for transfers between devices  9.28 us (31%)
  local copies, waits for them, and re-layouts  3.69 us (12%)
  other arithmetic  2.41 us (8%)
  matrix products  1.86 us (6%)
    ppermute x7, starting transfers between devices, exchange(): return lax.ppermute(value, 'blk', [(i, i ^ bit) for i in range(size)])  12.1 us
    ppermute x7, waiting for transfers between devices, exchange(): return lax.ppermute(value, 'blk', [(i, i ^ bit) for i in range(size)])  9.28 us
    unnamed x18, local copies, waits for them, and re-layouts  2.27 us
    dot_general x4, matrix products, attend(): jnp.einsum('rgqd,kgd->rgqk', grouped, keys, preferred_element_type=jnp.fl...  1.01 us
    dot_general x4, matrix products, attend(): jnp.einsum('rgqk,kgd->rgqd', probs.astype(jnp.bfloat16), values, preferre...  0.85 us
    convert_element_type x1, other arithmetic, on_device(): return (part[2] / part[1][..., None]).astype(jnp.bfloat16)  0.69 us
    gather x1, local copies, waits for them, and re-layouts, row_tables(): row_request[rows][:, None]  0.64 us
  transfers between devices with their start and end apart: 7, of which 4 were waited for; matrix products, arithmetic and copies ran while one was open for 17% of the time, Pallas kernels for 0%

profile of v2, /device:TPU:0, one launch (start us, length us, event | category | flops | bytes accessed | tf_op | source)
XLA Modules:
  0.0 29.6 jit_solution(10061661578644954255)
XLA Ops:
  0.0 3.0 %collective-permute-start = (bf16[1,32,128]{2,1,0:T(8,128)(2,1)}, bf16[1,32,128]{2,1,0:T(8,128)(2,1)S(1)}, u32[]{:S(2)}, u32[]{:S(2)}) collective-permute-start(bf16[1,32,128]{2,1,0:T(8,128)(2,1)} %param.8), channel_id=1, source_target_pairs={{0,4},{2,6},{4,0},{6,2},{8,12},{10,14},{12,8},{14,10},{1,5},{3,7},... | collective-permute-start | bytes 24584 | tf_op jit(solution)/shard_map/ppermute | solution.py:11
  3.0 1.5 %collective-permute-start.3 = (bf16[3,2,16,4,128]{4,3,2,1,0:T(4,128)(2,1)}, bf16[3,2,16,4,128]{4,3,2,1,0:T(4,128)(2,1)S(1)}, u32[]{:S(2)}, u32[]{:S(2)}) collective-permute-start(bf16[3,2,16,4,128]{4,3,2,1,0:T(4,128)(2,1)} %param.11), channel_id=1, source_target_pairs={{0,2},{2,0},{4,6},{6,4},{8,10},{10,8},{12,14},{14,12},{1,3},{3,1},... | collective-permute-start | bytes 294920 | tf_op jit(solution)/shard_map/ppermute | solution.py:11
  4.5 1.0 %copy.59 = bf16[256,4,128]{2,0,1:T(8,128)(2,1)S(1)} copy(bf16[256,4,128]{2,1,0:T(4,128)(2,1)} %param.9) | data formatting | bytes 524288 | tf_op args[1]
  5.5 0.0 copy-start.3
  5.5 0.6 %collective-permute-start.2 = (bf16[256,4,128]{2,0,1:T(8,128)(2,1)S(1)}, bf16[256,4,128]{2,0,1:T(8,128)(2,1)S(1)}, u32[]{:S(2)}, u32[]{:S(2)}) collective-permute-start(bf16[256,4,128]{2,0,1:T(8,128)(2,1)S(1)} %copy.59), channel_id=1, source_target_pairs={{0,2},{2,0},{4,6},{6,4},{8,10},{10,8},{12,14},{14,12},{1,3},{3,1},... | collective-permute-start | bytes 786440 | tf_op jit(solution)/shard_map/ppermute | solution.py:11
  6.2 1.6 %collective-permute-start.4 = (bf16[256,4,128]{2,0,1:T(8,128)(2,1)S(1)}, bf16[256,4,128]{2,0,1:T(8,128)(2,1)S(1)}, u32[]{:S(2)}, u32[]{:S(2)}) collective-permute-start(bf16[256,4,128]{2,0,1:T(8,128)(2,1)S(1)} %copy.66), channel_id=1, source_target_pairs={{0,2},{2,0},{4,6},{6,4},{8,10},{10,8},{12,14},{14,12},{1,3},{3,1},... | collective-permute-start | bytes 786440 | tf_op jit(solution)/shard_map/ppermute | solution.py:11
  7.8 0.0 copy-start.5
  7.8 0.6 %copy-done.5 = s32[3,8]{1,0:T(4,128)S(1)} copy-done((s32[3,8]{1,0:T(4,128)S(1)}, s32[3,8]{1,0:T(4,128)}, u32[]{:S(2)}) %copy-start.5) | copy-done | bytes 120
  8.5 0.1 slice_reduce_fusion
  8.6 0.6 %copy-done.6 = s32[3,8]{1,0:T(4,128)S(1)} copy-done((s32[3,8]{1,0:T(4,128)S(1)}, s32[3,8]{1,0:T(4,128)}, u32[]{:S(2)}) %copy-start.6) | copy-done | bytes 120
  9.1 0.1 select_reduce_fusion.5
  9.3 0.0 copy-start.7
  9.3 0.6 %gather_fusion = s32[4]{0:T(128)S(1)} fusion(s32[8]{0:T(128)S(1)} %copy-done, s32[1024]{0:T(1024)S(1)} %pad_clamp_fusion), kind=kCustom, calls=%fused_computation | custom fusion | bytes 48 | tf_op jit(solution)/shard_map/gather | solution.py:20
  10.0 0.2 select_reduce_fusion.4
  10.2 0.2 convert_reduce_fusion
  10.4 0.1 iota_compare_fusion
  10.5 0.1 add_compare_fusion
  10.5 0.1 broadcast_and_fusion.1
  10.6 2.7 %collective-permute-start.1 = (bf16[2,32,128]{2,1,0:T(8,128)(2,1)S(1)}, bf16[2,32,128]{2,1,0:T(8,128)(2,1)S(1)}, u32[]{:S(2)}, u32[]{:S(2)}) collective-permute-start(bf16[2,32,128]{2,1,0:T(8,128)(2,1)S(1)} %pad_maximum_fusion.2), channel_id=1, source_target_pairs={{0,8},{2,10},{4,12},{6,14},{8,0},{10,2},{12,4},{14,6},{1,9},{3,11}... | collective-permute-start | bytes 49160 | tf_op jit(solution)/shard_map/ppermute | solution.py:11
  13.3 0.1 broadcast_and_fusion
  13.4 0.1 and.85
  13.5 0.1 and.90
  13.6 1.8 %collective-permute-done.1 = bf16[2,32,128]{2,1,0:T(8,128)(2,1)S(1)} collective-permute-done((bf16[2,32,128]{2,1,0:T(8,128)(2,1)S(1)}, bf16[2,32,128]{2,1,0:T(8,128)(2,1)S(1)}, u32[]{:S(2)}, u32[]{:S(2)}) %collective-permute-start.1) | collective-permute-done | bytes 16416 | tf_op jit(solution)/shard_map/ppermute | solution.py:11
  15.4 0.3 fusion.55
  15.7 0.2 fusion.54
  16.0 0.2 fusion.53
  16.3 0.3 fusion.56
  16.6 0.2 fusion.20
  16.8 0.2 fusion.14
  17.1 0.1 slice.107
  17.1 0.1 slice.105
  17.2 0.2 fusion.9
  17.4 1.6 %collective-permute-done.4 = bf16[256,4,128]{2,0,1:T(8,128)(2,1)S(1)} collective-permute-done((bf16[256,4,128]{2,0,1:T(8,128)(2,1)S(1)}, bf16[256,4,128]{2,0,1:T(8,128)(2,1)S(1)}, u32[]{:S(2)}, u32[]{:S(2)}) %collective-permute-start.4) | collective-permute-done | bytes 262176 | tf_op jit(solution)/shard_map/ppermute | solution.py:11
  19.1 0.2 convolution_add_fusion.2
  19.3 0.2 convolution_add_fusion.1
  19.5 0.2 fusion.2
  19.8 0.1 select_maximum_fusion
  19.8 2.6 %collective-permute-start.5 = (f32[2,33,128]{2,1,0:T(8,128)S(1)}, f32[2,33,128]{2,1,0:T(8,128)S(1)}, u32[]{:S(2)}, u32[]{:S(2)}) collective-permute-start(f32[2,33,128]{2,1,0:T(8,128)S(1)} %pad_maximum_fusion), channel_id=1, source_target_pairs={{0,8},{2,10},{4,12},{6,14},{8,0},{10,2},{12,4},{14,6},{1,9},{3,11}... | collective-permute-start | bytes 101384 | tf_op jit(solution)/shard_map/ppermute | solution.py:11
  22.5 0.1 slice.116
  22.6 0.1 slice.101
  22.6 2.1 %collective-permute-done.5 = f32[2,33,128]{2,1,0:T(8,128)S(1)} collective-permute-done((f32[2,33,128]{2,1,0:T(8,128)S(1)}, f32[2,33,128]{2,1,0:T(8,128)S(1)}, u32[]{:S(2)}, u32[]{:S(2)}) %collective-permute-start.5) | collective-permute-done | bytes 33824 | tf_op jit(solution)/shard_map/ppermute | solution.py:11
  24.8 0.1 multiply_add_fusion
  24.9 0.1 fusion.26
  25.0 0.1 fusion.45
  25.1 0.1 collective-permute-start.6
  25.2 3.7 %collective-permute-done.6 = f32[1,33,128]{2,1,0:T(8,128)S(1)} collective-permute-done((f32[1,33,128]{2,1,0:T(8,128)S(1)}, f32[1,33,128]{2,1,0:T(8,128)S(1)}, u32[]{:S(2)}, u32[]{:S(2)}) %collective-permute-start.6) | collective-permute-done | bytes 16928 | tf_op jit(solution)/shard_map/ppermute | solution.py:11
  28.8 0.1 fusion.47
  28.9 0.7 %fusion.35 = bf16[1,32,128]{2,1,0:T(8,128)(2,1)} fusion(f32[1,33,128]{2,1,0:T(8,128)S(1)} %collective-permute-done.6, f32[2,32,128]{2,1,0:T(8,128)S(1)} %fusion.26, f32[32]{0:T(128)S(1)} %get-tuple-element.31, f32[32]{0:T(128)S(1)} %get-tuple-element.30, f32[32]{0:T(128)S(1)} %get-tuple-element.29), kind=kLoop, calls=%fused_computation.52 | loop fusion | flops 20480 | bytes 41344 | tf_op jit(solution)/shard_map/convert_element_type | solution.py:131
  (43 shorter events, 0.3 us)
Async XLA Ops:
  0.0 6.1 %copy-start.1 = (bf16[256,4,128]{2,1,0:T(4,128)(2,1)S(1)}, bf16[256,4,128]{2,1,0:T(4,128)(2,1)}, u32[]{:S(2)}) copy-start(bf16[256,4,128]{2,1,0:T(4,128)(2,1)} %param.10) | copy-start | bytes 786436
  0.0 10.6 %collective-permute-start = (bf16[1,32,128]{2,1,0:T(8,128)(2,1)}, bf16[1,32,128]{2,1,0:T(8,128)(2,1)S(1)}, u32[]{:S(2)}, u32[]{:S(2)}) collective-permute-start(bf16[1,32,128]{2,1,0:T(8,128)(2,1)} %param.8), channel_id=1, source_target_pairs={{0,4},{2,6},{4,0},{6,2},{8,12},{10,14},{12,8},{14,10},{1,5},{3,7},... | collective-permute-start | bytes 24584 | tf_op jit(solution)/shard_map/ppermute | solution.py:11
  3.0 12.9 %collective-permute-start.3 = (bf16[3,2,16,4,128]{4,3,2,1,0:T(4,128)(2,1)}, bf16[3,2,16,4,128]{4,3,2,1,0:T(4,128)(2,1)S(1)}, u32[]{:S(2)}, u32[]{:S(2)}) collective-permute-start(bf16[3,2,16,4,128]{4,3,2,1,0:T(4,128)(2,1)} %param.11), channel_id=1, source_target_pairs={{0,2},{2,0},{4,6},{6,4},{8,10},{10,8},{12,14},{14,12},{1,3},{3,1},... | collective-permute-start | bytes 294920 | tf_op jit(solution)/shard_map/ppermute | solution.py:11
  5.5 2.2 %copy-start.3 = (bf16[3,2,16,4,128]{4,3,2,1,0:T(4,128)(2,1)S(1)}, bf16[3,2,16,4,128]{4,3,2,1,0:T(4,128)(2,1)}, u32[]{:S(2)}) copy-start(bf16[3,2,16,4,128]{4,3,2,1,0:T(4,128)(2,1)} %param.11) | copy-start | bytes 294916
  5.5 10.7 %collective-permute-start.2 = (bf16[256,4,128]{2,0,1:T(8,128)(2,1)S(1)}, bf16[256,4,128]{2,0,1:T(8,128)(2,1)S(1)}, u32[]{:S(2)}, u32[]{:S(2)}) collective-permute-start(bf16[256,4,128]{2,0,1:T(8,128)(2,1)S(1)} %copy.59), channel_id=1, source_target_pairs={{0,2},{2,0},{4,6},{6,4},{8,10},{10,8},{12,14},{14,12},{1,3},{3,1},... | collective-permute-start | bytes 786440 | tf_op jit(solution)/shard_map/ppermute | solution.py:11
  6.2 12.9 %collective-permute-start.4 = (bf16[256,4,128]{2,0,1:T(8,128)(2,1)S(1)}, bf16[256,4,128]{2,0,1:T(8,128)(2,1)S(1)}, u32[]{:S(2)}, u32[]{:S(2)}) collective-permute-start(bf16[256,4,128]{2,0,1:T(8,128)(2,1)S(1)} %copy.66), channel_id=1, source_target_pairs={{0,2},{2,0},{4,6},{6,4},{8,10},{10,8},{12,14},{14,12},{1,3},{3,1},... | collective-permute-start | bytes 786440 | tf_op jit(solution)/shard_map/ppermute | solution.py:11
  7.8 0.7 %copy-start.5 = (s32[3,8]{1,0:T(4,128)S(1)}, s32[3,8]{1,0:T(4,128)}, u32[]{:S(2)}) copy-start(s32[3,8]{1,0:T(4,128)} %param.12) | copy-start | bytes 292
  7.8 1.5 %copy-start = (s32[8]{0:T(128)S(1)}, s32[8]{0:T(128)}, u32[]{:S(2)}) copy-start(s32[8]{0:T(128)} %param.15) | copy-start | bytes 100
  8.5 0.7 %copy-start.6 = (s32[3,8]{1,0:T(4,128)S(1)}, s32[3,8]{1,0:T(4,128)}, u32[]{:S(2)}) copy-start(s32[3,8]{1,0:T(4,128)} %param.13) | copy-start | bytes 292
  9.3 0.7 %copy-start.7 = (s32[3]{0:T(128)S(1)}, s32[3]{0:T(128)}, u32[]{:S(2)}) copy-start(s32[3]{0:T(128)} %param.14) | copy-start | bytes 40
  9.3 1.3 %copy-start.4 = (bf16[1,32,128]{2,1,0:T(8,128)(2,1)S(1)}, bf16[1,32,128]{2,1,0:T(8,128)(2,1)}, u32[]{:S(2)}) copy-start(bf16[1,32,128]{2,1,0:T(8,128)(2,1)} %param.8) | copy-start | bytes 24580
  10.0 5.5 %copy-start.2 = (bf16[256,4,128]{2,1,0:T(4,128)(2,1)S(1)}, bf16[256,4,128]{2,1,0:T(4,128)(2,1)}, u32[]{:S(2)}) copy-start(bf16[256,4,128]{2,1,0:T(4,128)(2,1)} %param.9) | copy-start | bytes 786436
  10.6 4.8 %collective-permute-start.1 = (bf16[2,32,128]{2,1,0:T(8,128)(2,1)S(1)}, bf16[2,32,128]{2,1,0:T(8,128)(2,1)S(1)}, u32[]{:S(2)}, u32[]{:S(2)}) collective-permute-start(bf16[2,32,128]{2,1,0:T(8,128)(2,1)S(1)} %pad_maximum_fusion.2), channel_id=1, source_target_pairs={{0,8},{2,10},{4,12},{6,14},{8,0},{10,2},{12,4},{14,6},{1,9},{3,11}... | collective-permute-start | bytes 49160 | tf_op jit(solution)/shard_map/ppermute | solution.py:11
  19.8 4.9 %collective-permute-start.5 = (f32[2,33,128]{2,1,0:T(8,128)S(1)}, f32[2,33,128]{2,1,0:T(8,128)S(1)}, u32[]{:S(2)}, u32[]{:S(2)}) collective-permute-start(f32[2,33,128]{2,1,0:T(8,128)S(1)} %pad_maximum_fusion), channel_id=1, source_target_pairs={{0,8},{2,10},{4,12},{6,14},{8,0},{10,2},{12,4},{14,6},{1,9},{3,11}... | collective-permute-start | bytes 101384 | tf_op jit(solution)/shard_map/ppermute | solution.py:11
  25.1 3.8 %collective-permute-start.6 = (f32[1,33,128]{2,1,0:T(8,128)S(1)}, f32[1,33,128]{2,1,0:T(8,128)S(1)}, u32[]{:S(2)}, u32[]{:S(2)}) collective-permute-start(f32[1,33,128]{2,1,0:T(8,128)S(1)} %pad_maximum_fusion.1), channel_id=1, source_target_pairs={{0,4},{2,6},{4,0},{6,2},{8,12},{10,14},{12,8},{14,10},{1,5},{3,7},... | collective-permute-start | bytes 50696 | tf_op jit(solution)/shard_map/ppermute | solution.py:11

commit v3 on v1

v3 whole, which is shorter than its diff:
```python
import functools
import math

import jax
import jax.numpy as jnp
from jax import lax
from jax.experimental import pallas as pl
from jax.experimental.pallas import tpu as pltpu
from jax.sharding import PartitionSpec as P

VMEM_BYTES = 40 * 1024 * 1024
STAT_ROWS = 16
CHUNK = 4


def exchange(value, even_bit, odd_bit):
    blocks = lax.axis_size("blk")
    cores = lax.axis_size("heads")
    pairs = [
        (b * cores + c, (b ^ (odd_bit if c % 2 else even_bit)) * cores + c)
        for b in range(blocks)
        for c in range(cores)
    ]
    return lax.ppermute(value, ("blk", "heads"), pairs)


def loop(count, body):
    if count <= 4:
        for i in range(count):
            body(i)
    else:
        lax.fori_loop(0, count, lambda i, carry: (body(i), carry)[1], 0)


def spread_rows(qheads, lanes):
    sub = lax.broadcasted_iota(jnp.int32, (qheads, lanes), 0)
    lane = lax.broadcasted_iota(jnp.int32, (qheads, lanes), 1)
    return sub == lane


def to_row(column, diagonal):
    return jnp.sum(jnp.where(diagonal, column, 0.0), axis=0, keepdims=True)


def to_column(row, diagonal):
    return jnp.sum(jnp.where(diagonal, row, 0.0), axis=1, keepdims=True)


def split(value):
    high = value.astype(jnp.bfloat16).astype(jnp.float32)
    return high, (value - high).astype(jnp.bfloat16).astype(jnp.float32)


def stat_block(top_row, total_row):
    top_high, top_low = split(top_row)
    total_high, total_low = split(total_row)
    blank = jnp.zeros((STAT_ROWS - 4, top_row.shape[1]), jnp.float32)
    return jnp.concatenate([top_high, top_low, total_high, total_low, blank], axis=0)


def suffix_rows(bulk_ref, start, slots, page_rows):
    return jnp.concatenate(
        [bulk_ref[start + s * 2 * page_rows : start + s * 2 * page_rows + page_rows] for s in range(slots)],
        axis=0,
    )


def attend(query, bulk_ref, bias, sizes):
    kv_heads, group, prefix_rows, slots, page_rows, scale = sizes
    rows = query.shape[0]
    qheads = kv_heads * group
    suffix_count = slots * page_rows
    key = bulk_ref[0:prefix_rows]
    value = bulk_ref[prefix_rows : 2 * prefix_rows]
    page_key = suffix_rows(bulk_ref, 2 * prefix_rows, slots, page_rows)
    page_value = suffix_rows(bulk_ref, 2 * prefix_rows + page_rows, slots, page_rows)
    contract = (((1,), (1,)), ((), ()))
    near = lax.dot_general(query, key, contract, preferred_element_type=jnp.float32)
    page = lax.dot_general(query, page_key, contract, preferred_element_type=jnp.float32)

    def own_head(width):
        row = lax.broadcasted_iota(jnp.int32, (rows, width), 0)
        column = lax.broadcasted_iota(jnp.int32, (rows, width), 1)
        return (row % qheads) // group == column % kv_heads

    near = jnp.where(own_head(prefix_rows), near, -jnp.inf)
    page = jnp.where(own_head(suffix_count), page, -jnp.inf) + bias
    top = jnp.maximum(
        jnp.max(near, axis=1, keepdims=True), jnp.max(page, axis=1, keepdims=True)
    )
    near = jnp.exp2((near - top) * scale)
    page = jnp.exp2((page - top) * scale)
    total = jnp.sum(near, axis=1, keepdims=True) + jnp.sum(page, axis=1, keepdims=True)
    mixed = jnp.dot(near.astype(jnp.bfloat16), value, preferred_element_type=jnp.float32)
    mixed = mixed + jnp.dot(
        page.astype(jnp.bfloat16), page_value, preferred_element_type=jnp.float32
    )
    return top, total, mixed


def chunk_bias(bias_ref, first, count, qheads):
    return jnp.concatenate(
        [
            jnp.broadcast_to(bias_ref[pl.ds(first + j, 1), :], (qheads, bias_ref.shape[1]))
            for j in range(count)
        ],
        axis=0,
    )


def bias_kernel(
    place_ref, owner_ref, slot_ref, len_ref, request_ref, near_ref, far_ref, *, rows_dev, page_len, kv_heads, blocks
):
    row_total = near_ref.shape[0]
    width = near_ref.shape[1]
    me, query_bit, key_bit = place_ref[0], place_ref[1], place_ref[2]
    all_rows = request_ref.shape[0]
    column = lax.broadcasted_iota(jnp.int32, (1, width), 1)

    def one(i):
        place = i // rows_dev
        device = me ^ jnp.where(place % 2 == 1, query_bit, 0) ^ ((place // 2) * 4)
        row = device * rows_dev + i % rows_dev
        request = request_ref[row]

        def count(j, later):
            return later + jnp.where((request_ref[j] == request) & (j > row), 1, 0)

        if all_rows <= 16:
            later = jnp.int32(0)
            for j in range(all_rows):
                later = count(j, later)
        else:
            later = lax.fori_loop(0, all_rows, count, jnp.int32(0))
        limit = len_ref[request] - later
        for holder, out_ref in ((me, near_ref), (me ^ key_bit, far_ref)):
            page = lax.rem(holder - owner_ref[request, 0] + blocks, blocks)
            shown = jnp.clip(limit - page * page_len, 0, page_len) * kv_heads
            first = slot_ref[request, page] * (page_len * kv_heads)
            out_ref[pl.ds(i, 1), :] = jnp.where(
                (column >= first) & (column < first + shown), 0.0, -jnp.inf
            )

    loop(row_total, one)


def near_kernel(first_ref, second_ref, bulk_ref, bias_ref, mixed_ref, top_ref, total_ref, *, sizes):
    half, qheads, head_dim = first_ref.shape
    chunk = min(CHUNK, half * 2)
    part = chunk // 2

    def one(i):
        base = i * part
        query = jnp.concatenate(
            [
                first_ref[pl.ds(base, part)].reshape(part * qheads, head_dim),
                second_ref[pl.ds(base, part)].reshape(part * qheads, head_dim),
            ],
            axis=0,
        )
        bias = jnp.concatenate(
            [
                chunk_bias(bias_ref, base, part, qheads),
                chunk_bias(bias_ref, half + base, part, qheads),
            ],
            axis=0,
        )
        top, total, mixed = attend(query, bulk_ref, bias, sizes)
        mixed_ref[i] = mixed
        top_ref[i] = jnp.broadcast_to(top, mixed.shape)
        total_ref[i] = jnp.broadcast_to(total, mixed.shape)

    loop(half // part, one)


def far_kernel(
    first_ref, second_ref, bulk_ref, bias_ref, mixed_ref, top_ref, total_ref,
    send_ref, keep_ref, stat_ref, *, sizes,
):
    half, qheads, head_dim = first_ref.shape
    scale = sizes[-1]
    chunk = min(CHUNK, half * 2)
    part = chunk // 2
    diagonal = spread_rows(qheads, head_dim)

    def one(i):
        base = i * part
        query = jnp.concatenate(
            [
                first_ref[pl.ds(base, part)].reshape(part * qheads, head_dim),
                second_ref[pl.ds(base, part)].reshape(part * qheads, head_dim),
            ],
            axis=0,
        )
        bias = jnp.concatenate(
            [
                chunk_bias(bias_ref, base, part, qheads),
                chunk_bias(bias_ref, half + base, part, qheads),
            ],
            axis=0,
        )
        top, total, mixed = attend(query, bulk_ref, bias, sizes)
        near_top = top_ref[i][:, :1]
        high, low = split(jnp.maximum(near_top, top))
        point = high + low
        near_scale = jnp.exp2((near_top - point) * scale)
        far_scale = jnp.exp2((top - point) * scale)
        total = total_ref[i][:, :1] * near_scale + total * far_scale
        mixed = (mixed_ref[i] * near_scale + mixed * far_scale) / total
        for j in range(part):
            rows = slice(j * qheads, (j + 1) * qheads)
            keep_ref[base + j] = mixed[rows]
            stat_ref[base + j, 0:1] = to_row(point[rows], diagonal)
            stat_ref[base + j, 1:2] = to_row(total[rows], diagonal)
            rows = slice((part + j) * qheads, (part + j + 1) * qheads)
            stats = stat_block(to_row(point[rows], diagonal), to_row(total[rows], diagonal))
            send_ref[base + j] = jnp.concatenate([mixed[rows], stats], axis=0).astype(jnp.bfloat16)

    loop(half // part, one)


def merge_rows(keep, top, total, parcel, qheads, diagonal, scale):
    stats = parcel[qheads:]
    other_top = stats[0:1] + stats[1:2]
    other_total = stats[2:3] + stats[3:4]
    point = jnp.maximum(top, other_top)
    own = total * jnp.exp2((top - point) * scale)
    other = other_total * jnp.exp2((other_top - point) * scale)
    total = own + other
    weight = to_column(other / total, diagonal)
    return keep + (parcel[:qheads] - keep) * weight, point, total


def merge_kernel(keep_in, stat_in, parcel_ref, send_ref, keep_ref, stat_ref, *, scale):
    count, qheads, head_dim = keep_in.shape
    diagonal = spread_rows(qheads, head_dim)
    half = count // 2

    def merged(i):
        return merge_rows(
            keep_in[i], stat_in[i, 0:1], stat_in[i, 1:2], parcel_ref[i].astype(jnp.float32),
            qheads, diagonal, scale,
        )

    def one(i):
        mixed, top, total = merged(half + i)
        send_ref[i] = jnp.concatenate([mixed, stat_block(top, total)], axis=0).astype(jnp.bfloat16)
        keep_ref[i], stat_ref[i, 0:1], stat_ref[i, 1:2] = merged(i)

    loop(half, one)


def last_kernel(keep_in, stat_in, parcel_ref, out_ref, *, scale):
    count, qheads, head_dim = keep_in.shape
    diagonal = spread_rows(qheads, head_dim)

    def one(i):
        mixed, _, _ = merge_rows(
            keep_in[i], stat_in[i, 0:1], stat_in[i, 1:2], parcel_ref[i].astype(jnp.float32),
            qheads, diagonal, scale,
        )
        out_ref[i] = mixed.astype(out_ref.dtype)

    loop(count, one)


def call(kernel, outs, operands, scalars=0, **static):
    return pl.pallas_call(
        functools.partial(kernel, **static),
        out_shape=outs,
        in_specs=[pl.BlockSpec(memory_space=pltpu.SMEM)] * scalars
        + [pl.BlockSpec(memory_space=pltpu.VMEM)] * (len(operands) - scalars),
        compiler_params=pltpu.CompilerParams(vmem_limit_bytes=VMEM_BYTES),
    )(*operands)


def on_device(
    queries, prefix_keys, prefix_values, suffix_pool, page_owner, page_slot, suffix_len, row_request
):
    blocks = lax.axis_size("blk")
    me = lax.axis_index("blk")
    odd_core = lax.axis_index("heads") % 2
    rows_dev, qheads, head_dim = queries.shape
    slots, _, page_len, kv_heads, _ = suffix_pool.shape
    prefix_rows = prefix_keys.shape[0] * kv_heads
    page_rows = page_len * kv_heads
    scale = math.log2(math.e) / math.sqrt(head_dim)
    sizes = (kv_heads, qheads // kv_heads, prefix_rows, slots, page_rows, scale)
    shared_bits = [1 << b for b in range(2, blocks.bit_length() - 1)]

    bulk = jnp.concatenate(
        [
            prefix_keys.reshape(prefix_rows, head_dim),
            prefix_values.reshape(prefix_rows, head_dim),
            suffix_pool.reshape(slots * 2 * page_rows, head_dim),
        ],
        axis=0,
    )
    far_bulk = exchange(bulk, 2, 1)
    first = queries
    second = exchange(first, 1, 2)
    for bit in shared_bits:
        first = jnp.concatenate([first, second], axis=0)
        second = exchange(first, bit, bit)
    half = first.shape[0]
    rows = 2 * half

    place = jnp.stack([me, 1 + odd_core, 2 - odd_core]).astype(jnp.int32)
    table = jax.ShapeDtypeStruct((rows, slots * page_rows), jnp.float32)
    near_bias, far_bias = call(
        bias_kernel, (table, table), (place, page_owner, page_slot, suffix_len, row_request), 5,
        rows_dev=rows_dev, page_len=page_len, kv_heads=kv_heads, blocks=blocks,
    )
    chunk = min(CHUNK, rows)
    block = jax.ShapeDtypeStruct((rows // chunk, chunk * qheads, head_dim), jnp.float32)
    near = call(
        near_kernel, (block, block, block), (first, second, bulk, near_bias), sizes=sizes
    )

    def parcel(count):
        return (
            jax.ShapeDtypeStruct((count, qheads + STAT_ROWS, head_dim), jnp.bfloat16),
            jax.ShapeDtypeStruct((count, qheads, head_dim), jnp.float32),
            jax.ShapeDtypeStruct((count, 8, head_dim), jnp.float32),
        )

    send, keep, stats = call(
        far_kernel, parcel(half), (first, second, far_bulk, far_bias, *near), sizes=sizes
    )
    for bit in reversed(shared_bits):
        arrived = exchange(send, bit, bit)
        half //= 2
        send, keep, stats = call(merge_kernel, parcel(half), (keep, stats, arrived), scale=scale)
    arrived = exchange(send, 1, 2)
    return call(
        last_kernel, jax.ShapeDtypeStruct(queries.shape, queries.dtype), (keep, stats, arrived),
        scale=scale,
    )


def solution(mesh):
    placed = (
        P(("groups", "blk"), "heads", None),
        P(("groups", "blk"), "heads", None),
        P(("groups", "blk"), "heads", None),
        P(("groups", "blk"), None, None, "heads", None),
        P("groups", None),
        P("groups", None),
        P("groups"),
        P("groups"),
    )
    return jax.shard_map(
        on_device,
        mesh=mesh,
        in_specs=placed,
        out_specs=P(("groups", "blk"), "heads", None),
        check_vma=False,
    )
```

time: 28.3 us -> 23.8 us (0.84)
  blocking collectives: 9.77 us -> 0 us
  starting transfers between devices: 7.39 us -> 11.6 us
  local copies, waits for them, and re-layouts: 3.08 us -> 0.03 us
  Pallas kernels: 0 us -> 2.97 us
  waiting for transfers between devices: 4.94 us -> 7.74 us
  other arithmetic: 2.01 us -> 1.26 us
  matrix products: 0.58 us -> 0 us
    ppermute x0 -> x5, starting transfers between devices: none -> 11.6 us  [exchange(): return lax.ppermute(value, ('blk', 'heads'), pairs)]
    all_to_all x1 -> x0, blocking collectives: 9.77 us -> none  [on_device(): lax.all_to_all(parcel, 'blk', split_axis=0, concat_axis=0, tiled=True)]
    ppermute x0 -> x5, waiting for transfers between devices: none -> 7.74 us  [exchange(): return lax.ppermute(value, ('blk', 'heads'), pairs)]
    all_to_all x1 -> x0, starting transfers between devices: 7.39 us -> none  [on_device(): lax.all_to_all(spread, 'blk', split_axis=0, concat_axis=0, tiled=True)]
    all_to_all x1 -> x0, waiting for transfers between devices: 4.94 us -> none  [on_device(): lax.all_to_all(spread, 'blk', split_axis=0, concat_axis=0, tiled=True)]
    pallas_call x0 -> x5, Pallas kernels: none -> 2.97 us  [call(): pl.pallas_call(functools.partial(kernel, **static), out_shape=outs, in_sp...]
    broadcast_in_dim x1 -> x0, local copies, waits for them, and re-layouts: 1.39 us -> none  [on_device(): spread = jnp.broadcast_to(queries[None], (block_count,) + queries.shape)]
    concatenate x0 -> x1, other arithmetic: none -> 1.18 us  [on_device(): jnp.concatenate([prefix_keys.reshape(prefix_rows, head_dim), prefix_value...]
  transfers between devices with their start and end apart: 1 -> 5, of which waited for: 1 -> 4; matrix products, arithmetic and copies ran while one was open for 4% -> 0% of each run, Pallas kernels for 0% -> 6%
where the time goes in v3:
time: 23.8 us; the launch traced here: 23.7 us
  starting transfers between devices  11.6 us (49%)
  waiting for transfers between devices  7.74 us (33%)
  Pallas kernels  2.97 us (12%)
  other arithmetic  1.26 us (5%)
    ppermute x5, starting transfers between devices, exchange(): return lax.ppermute(value, ('blk', 'heads'), pairs)  11.6 us
    ppermute x5, waiting for transfers between devices, exchange(): return lax.ppermute(value, ('blk', 'heads'), pairs)  7.74 us
    pallas_call x5, Pallas kernels, call(): pl.pallas_call(functools.partial(kernel, **static), out_shape=outs, in_sp...  2.97 us
    concatenate x1, other arithmetic, on_device(): jnp.concatenate([prefix_keys.reshape(prefix_rows, head_dim), prefix_value...  1.18 us
  transfers between devices with their start and end apart: 5, of which 4 were waited for; matrix products, arithmetic and copies ran while one was open for 0% of the time, Pallas kernels for 6%

profile of v3, /device:TPU:0, one launch (start us, length us, event | category | flops | bytes accessed | tf_op | source)
XLA Modules:
  0.0 23.7 jit_solution(12532327384133950514)
XLA Ops:
  0.0 0.0 copy-start.4
  0.0 0.0 copy-start
  0.0 0.0 copy-start.1
  0.0 0.0 copy-start.2
  0.0 0.0 copy-start.3
  0.0 1.2 %pad_maximum_fusion.bulk_ref = bf16[2432,128]{1,0:T(8,128)(2,1)S(1)} fusion(bf16[384,128]{1,0:T(8,128)(2,1)} %bitcast.8, bf16[1024,128]{1,0:T(8,128)(2,1)} %bitcast.6, bf16[1024,128]{1,0:T(8,128)(2,1)} %bitcast.7), kind=kLoop, calls=%fused_computation | loop fusion | flops 1867776 | bytes 1245184 | tf_op jit(solution)/shard_map/concatenate | solution.py:291
  1.2 3.1 %collective-permute-start.2 = (bf16[2432,128]{1,0:T(8,128)(2,1)S(1)}, bf16[2432,128]{1,0:T(8,128)(2,1)S(1)}, u32[]{:S(2)}, u32[]{:S(2)}) collective-permute-start(bf16[2432,128]{1,0:T(8,128)(2,1)S(1)} %pad_maximum_fusion.bulk_ref), channel_id=1, source_target_pairs={{0,4},{1,3},{2,6},{3,1},{4,0},{5,7},{6,2},{7,5},{8,12},{9,11},{10,... | collective-permute-start | bytes 1867784 | tf_op jit(solution)/shard_map/ppermute | solution.py:24
  4.3 0.0 copy-done.4
  4.3 1.5 %collective-permute-start = (bf16[1,32,128]{2,1,0:T(8,128)(2,1)S(1)}, bf16[1,32,128]{2,1,0:T(8,128)(2,1)S(1)}, u32[]{:S(2)}, u32[]{:S(2)}) collective-permute-start(bf16[1,32,128]{2,1,0:T(8,128)(2,1)S(1)} %copy-done.4), channel_id=1, source_target_pairs={{0,2},{1,5},{2,0},{3,7},{4,6},{5,1},{6,4},{7,3},{8,10},{9,13},{10,... | collective-permute-start | bytes 24584 | tf_op jit(solution)/shard_map/ppermute | solution.py:24
  5.8 2.3 %collective-permute-done = bf16[1,32,128]{2,1,0:T(8,128)(2,1)S(1)} collective-permute-done((bf16[1,32,128]{2,1,0:T(8,128)(2,1)S(1)}, bf16[1,32,128]{2,1,0:T(8,128)(2,1)S(1)}, u32[]{:S(2)}, u32[]{:S(2)}) %collective-permute-start) | collective-permute-done | bytes 8224 | tf_op jit(solution)/shard_map/ppermute | solution.py:24
  8.1 2.6 %collective-permute-start.1 = (bf16[2,32,128]{2,1,0:T(8,128)(2,1)S(1)}, bf16[2,32,128]{2,1,0:T(8,128)(2,1)S(1)}, u32[]{:S(2)}, u32[]{:S(2)}) collective-permute-start(bf16[2,32,128]{2,1,0:T(8,128)(2,1)S(1)} %constant_dynamic-update-slice_fusion.first_ref), channel_id=1, source_target_pairs={{0,8},{1,9},{2,10},{3,11},{4,12},{5,13},{6,14},{7,15},{8,0},{9,1},... | collective-permute-start | bytes 49160 | tf_op jit(solution)/shard_map/ppermute | solution.py:24
  10.7 0.1 pad_add_fusion.place_ref
  10.8 0.0 copy-done
  10.8 0.0 copy-done.1
  10.8 0.0 copy-done.2
  10.8 0.0 copy-done.3
  10.8 0.7 %shard_map.82 = (f32[4,192]{1,0:T(4,128)S(1)}, f32[4,192]{1,0:T(4,128)S(1)}) custom-call(s32[3]{0:T(128)S(1)} %pad_add_fusion.place_ref, s32[3,8]{1,0:T(4,128)S(1)} %copy-done, s32[3,8]{1,0:T(4,128)S(1)} %copy-done.1, s32[3]{0:T(128)S(1)} %copy-done.2, s32[8]{0:T(128)S(1)} %copy-done.3), custom_call_target="tpu_custom_call" | custom-call | tf_op jit(solution)/shard_map/pallas_call | solution.py:268
  11.5 1.3 %collective-permute-done.1.second_ref = bf16[2,32,128]{2,1,0:T(8,128)(2,1)S(1)} collective-permute-done((bf16[2,32,128]{2,1,0:T(8,128)(2,1)S(1)}, bf16[2,32,128]{2,1,0:T(8,128)(2,1)S(1)}, u32[]{:S(2)}, u32[]{:S(2)}) %collective-permute-start.1) | collective-permute-done | bytes 16416 | tf_op jit(solution)/shard_map/ppermute | solution.py:24
  12.8 0.6 %shard_map.83 = (f32[1,128,128]{2,1,0:T(8,128)S(1)}, f32[1,128,128]{2,1,0:T(8,128)S(1)}, f32[1,128,128]{2,1,0:T(8,128)S(1)}) custom-call(bf16[2,32,128]{2,1,0:T(8,128)(2,1)S(1)} %constant_dynamic-update-slice_fusion.first_ref, bf16[2,32,128]{2,1,0:T(8,128)(2,1)S(1)} %collective-permute-done.1.second_ref, bf16[2432,128]{1,0:T(8,128)(2,1)S(1)} %pad_maximum_fusion.bulk_ref, ...), custom_call_target="tpu_custom_call" | custom-call | tf_op jit(solution)/shard_map/pallas_call | solution.py:268
  13.5 0.0 collective-permute-done.2.bulk_ref
  13.5 0.8 %shard_map.84 = (bf16[2,48,128]{2,1,0:T(8,128)(2,1)S(1)}, f32[2,32,128]{2,1,0:T(8,128)S(1)}, f32[2,8,128]{2,1,0:T(8,128)S(1)}) custom-call(bf16[2,32,128]{2,1,0:T(8,128)(2,1)S(1)} %constant_dynamic-update-slice_fusion.first_ref, bf16[2,32,128]{2,1,0:T(8,128)(2,1)S(1)} %collective-permute-done.1.second_ref, ...), custom_call_target="tpu_custom_call" | custom-call | tf_op jit(solution)/shard_map/pallas_call | solution.py:268
  14.3 3.1 %collective-permute-start.3 = (bf16[2,48,128]{2,1,0:T(8,128)(2,1)S(1)}, bf16[2,48,128]{2,1,0:T(8,128)(2,1)S(1)}, u32[]{:S(2)}, u32[]{:S(2)}) collective-permute-start(bf16[2,48,128]{2,1,0:T(8,128)(2,1)S(1)} %get-tuple-element.23), channel_id=1, source_target_pairs={{0,8},{1,9},{2,10},{3,11},{4,12},{5,13},{6,14},{7,15},{8,0},{9,1},... | collective-permute-start | bytes 73736 | tf_op jit(solution)/shard_map/ppermute | solution.py:24
  17.4 1.8 %collective-permute-done.3.parcel_ref = bf16[2,48,128]{2,1,0:T(8,128)(2,1)S(1)} collective-permute-done((bf16[2,48,128]{2,1,0:T(8,128)(2,1)S(1)}, bf16[2,48,128]{2,1,0:T(8,128)(2,1)S(1)}, u32[]{:S(2)}, u32[]{:S(2)}) %collective-permute-start.3) | collective-permute-done | bytes 24608 | tf_op jit(solution)/shard_map/ppermute | solution.py:24
  19.2 0.1 shard_map.85
  19.3 1.4 %collective-permute-start.4 = (bf16[1,48,128]{2,1,0:T(8,128)(2,1)S(1)}, bf16[1,48,128]{2,1,0:T(8,128)(2,1)S(1)}, u32[]{:S(2)}, u32[]{:S(2)}) collective-permute-start(bf16[1,48,128]{2,1,0:T(8,128)(2,1)S(1)} %get-tuple-element.26), channel_id=1, source_target_pairs={{0,2},{1,5},{2,0},{3,7},{4,6},{5,1},{6,4},{7,3},{8,10},{9,13},{10,... | collective-permute-start | bytes 36872 | tf_op jit(solution)/shard_map/ppermute | solution.py:24
  20.7 2.3 %collective-permute-done.4.parcel_ref = bf16[1,48,128]{2,1,0:T(8,128)(2,1)S(1)} collective-permute-done((bf16[1,48,128]{2,1,0:T(8,128)(2,1)S(1)}, bf16[1,48,128]{2,1,0:T(8,128)(2,1)S(1)}, u32[]{:S(2)}, u32[]{:S(2)}) %collective-permute-start.4) | collective-permute-done | bytes 12320 | tf_op jit(solution)/shard_map/ppermute | solution.py:24
  23.0 0.7 %shard_map.86 = bf16[1,32,128]{2,1,0:T(8,128)(2,1)} custom-call(f32[1,32,128]{2,1,0:T(8,128)S(1)} %get-tuple-element.24.keep_in, f32[1,8,128]{2,1,0:T(8,128)S(1)} %get-tuple-element.25.stat_in, bf16[1,48,128]{2,1,0:T(8,128)(2,1)S(1)} %collective-permute-done.4.parcel_ref), custom_call_target="tpu_custom_call" | custom-call | tf_op jit(solution)/shard_map/pallas_call | solution.py:268
  (2 shorter events, 0.0 us)
Async XLA Ops:
  0.0 4.3 %copy-start.4 = (bf16[1,32,128]{2,1,0:T(8,128)(2,1)S(1)}, bf16[1,32,128]{2,1,0:T(8,128)(2,1)}, u32[]{:S(2)}) copy-start(bf16[1,32,128]{2,1,0:T(8,128)(2,1)} %param.8) | copy-start | bytes 24580
  0.0 10.8 %copy-start = (s32[3,8]{1,0:T(4,128)S(1)}, s32[3,8]{1,0:T(4,128)}, u32[]{:S(2)}) copy-start(s32[3,8]{1,0:T(4,128)} %owner_ref.1) | copy-start | bytes 292
  0.0 10.8 %copy-start.1 = (s32[3,8]{1,0:T(4,128)S(1)}, s32[3,8]{1,0:T(4,128)}, u32[]{:S(2)}) copy-start(s32[3,8]{1,0:T(4,128)} %slot_ref.1) | copy-start | bytes 292
  0.0 10.8 %copy-start.2 = (s32[3]{0:T(128)S(1)}, s32[3]{0:T(128)}, u32[]{:S(2)}) copy-start(s32[3]{0:T(128)} %len_ref.1) | copy-start | bytes 40
  0.0 10.8 %copy-start.3 = (s32[8]{0:T(128)S(1)}, s32[8]{0:T(128)}, u32[]{:S(2)}) copy-start(s32[8]{0:T(128)} %request_ref.1) | copy-start | bytes 100
  1.2 12.3 %collective-permute-start.2 = (bf16[2432,128]{1,0:T(8,128)(2,1)S(1)}, bf16[2432,128]{1,0:T(8,128)(2,1)S(1)}, u32[]{:S(2)}, u32[]{:S(2)}) collective-permute-start(bf16[2432,128]{1,0:T(8,128)(2,1)S(1)} %pad_maximum_fusion.bulk_ref), channel_id=1, source_target_pairs={{0,4},{1,3},{2,6},{3,1},{4,0},{5,7},{6,2},{7,5},{8,12},{9,11},{10,... | collective-permute-start | bytes 1867784 | tf_op jit(solution)/shard_map/ppermute | solution.py:24
  4.3 3.8 %collective-permute-start = (bf16[1,32,128]{2,1,0:T(8,128)(2,1)S(1)}, bf16[1,32,128]{2,1,0:T(8,128)(2,1)S(1)}, u32[]{:S(2)}, u32[]{:S(2)}) collective-permute-start(bf16[1,32,128]{2,1,0:T(8,128)(2,1)S(1)} %copy-done.4), channel_id=1, source_target_pairs={{0,2},{1,5},{2,0},{3,7},{4,6},{5,1},{6,4},{7,3},{8,10},{9,13},{10,... | collective-permute-start | bytes 24584 | tf_op jit(solution)/shard_map/ppermute | solution.py:24
  8.1 4.7 %collective-permute-start.1 = (bf16[2,32,128]{2,1,0:T(8,128)(2,1)S(1)}, bf16[2,32,128]{2,1,0:T(8,128)(2,1)S(1)}, u32[]{:S(2)}, u32[]{:S(2)}) collective-permute-start(bf16[2,32,128]{2,1,0:T(8,128)(2,1)S(1)} %constant_dynamic-update-slice_fusion.first_ref), channel_id=1, source_target_pairs={{0,8},{1,9},{2,10},{3,11},{4,12},{5,13},{6,14},{7,15},{8,0},{9,1},... | collective-permute-start | bytes 49160 | tf_op jit(solution)/shard_map/ppermute | solution.py:24
  14.3 4.9 %collective-permute-start.3 = (bf16[2,48,128]{2,1,0:T(8,128)(2,1)S(1)}, bf16[2,48,128]{2,1,0:T(8,128)(2,1)S(1)}, u32[]{:S(2)}, u32[]{:S(2)}) collective-permute-start(bf16[2,48,128]{2,1,0:T(8,128)(2,1)S(1)} %get-tuple-element.23), channel_id=1, source_target_pairs={{0,8},{1,9},{2,10},{3,11},{4,12},{5,13},{6,14},{7,15},{8,0},{9,1},... | collective-permute-start | bytes 73736 | tf_op jit(solution)/shard_map/ppermute | solution.py:24
  19.3 3.7 %collective-permute-start.4 = (bf16[1,48,128]{2,1,0:T(8,128)(2,1)S(1)}, bf16[1,48,128]{2,1,0:T(8,128)(2,1)S(1)}, u32[]{:S(2)}, u32[]{:S(2)}) collective-permute-start(bf16[1,48,128]{2,1,0:T(8,128)(2,1)S(1)} %get-tuple-element.26), channel_id=1, source_target_pairs={{0,2},{1,5},{2,0},{3,7},{4,6},{5,1},{6,4},{7,3},{8,10},{9,13},{10,... | collective-permute-start | bytes 36872 | tf_op jit(solution)/shard_map/ppermute | solution.py:24

commit v4 on v3

--- a/solution.py
+++ b/solution.py
@@ -296,16 +296,16 @@
         ],
         axis=0,
     )
-    far_bulk = exchange(bulk, 2, 1)
+    far_bulk = exchange(bulk, 1, 2)
     first = queries
-    second = exchange(first, 1, 2)
+    second = exchange(first, 2, 1)
     for bit in shared_bits:
         first = jnp.concatenate([first, second], axis=0)
         second = exchange(first, bit, bit)
     half = first.shape[0]
     rows = 2 * half
 
-    place = jnp.stack([me, 1 + odd_core, 2 - odd_core]).astype(jnp.int32)
+    place = jnp.stack([me, 2 - odd_core, 1 + odd_core]).astype(jnp.int32)
     table = jax.ShapeDtypeStruct((rows, slots * page_rows), jnp.float32)
     near_bias, far_bias = call(
         bias_kernel, (table, table), (place, page_owner, page_slot, suffix_len, row_request), 5,
@@ -331,7 +331,7 @@
         arrived = exchange(send, bit, bit)
         half //= 2
         send, keep, stats = call(merge_kernel, parcel(half), (keep, stats, arrived), scale=scale)
-    arrived = exchange(send, 1, 2)
+    arrived = exchange(send, 2, 1)
     return call(
         last_kernel, jax.ShapeDtypeStruct(queries.shape, queries.dtype), (keep, stats, arrived),
         scale=scale,

time: 23.8 us -> 23.5 us (0.987)
  waiting for transfers between devices: 7.74 us -> 7.44 us
    ppermute x5, waiting for transfers between devices: 7.74 us -> 7.44 us  [exchange(): return lax.ppermute(value, ('blk', 'heads'), pairs)]
where the time goes in v4:
time: 23.5 us; the launch traced here: 23.4 us
  starting transfers between devices  11.6 us (49%)
  waiting for transfers between devices  7.44 us (32%)
  Pallas kernels  2.97 us (13%)
  other arithmetic  1.26 us (5%)
    ppermute x5, starting transfers between devices, exchange(): return lax.ppermute(value, ('blk', 'heads'), pairs)  11.6 us
    ppermute x5, waiting for transfers between devices, exchange(): return lax.ppermute(value, ('blk', 'heads'), pairs)  7.44 us
    pallas_call x5, Pallas kernels, call(): pl.pallas_call(functools.partial(kernel, **static), out_shape=outs, in_sp...  2.97 us
    concatenate x1, other arithmetic, on_device(): jnp.concatenate([prefix_keys.reshape(prefix_rows, head_dim), prefix_value...  1.18 us
  transfers between devices with their start and end apart: 5, of which 4 were waited for; matrix products, arithmetic and copies ran while one was open for 0% of the time, Pallas kernels for 6%

profile of v4, /device:TPU:0, one launch (start us, length us, event | category | flops | bytes accessed | tf_op | source)
XLA Modules:
  0.0 23.4 jit_solution(1624736534092824264)
XLA Ops:
  0.0 0.0 copy-start.4
  0.0 0.0 copy-start
  0.0 0.0 copy-start.1
  0.0 0.0 copy-start.2
  0.0 0.0 copy-start.3
  0.0 1.2 %pad_maximum_fusion.bulk_ref = bf16[2432,128]{1,0:T(8,128)(2,1)S(1)} fusion(bf16[384,128]{1,0:T(8,128)(2,1)} %bitcast.8, bf16[1024,128]{1,0:T(8,128)(2,1)} %bitcast.6, bf16[1024,128]{1,0:T(8,128)(2,1)} %bitcast.7), kind=kLoop, calls=%fused_computation | loop fusion | flops 1867776 | bytes 1245184 | tf_op jit(solution)/shard_map/concatenate | solution.py:291
  1.2 3.0 %collective-permute-start.2 = (bf16[2432,128]{1,0:T(8,128)(2,1)S(1)}, bf16[2432,128]{1,0:T(8,128)(2,1)S(1)}, u32[]{:S(2)}, u32[]{:S(2)}) collective-permute-start(bf16[2432,128]{1,0:T(8,128)(2,1)S(1)} %pad_maximum_fusion.bulk_ref), channel_id=1, source_target_pairs={{0,2},{1,5},{2,0},{3,7},{4,6},{5,1},{6,4},{7,3},{8,10},{9,13},{10,... | collective-permute-start | bytes 1867784 | tf_op jit(solution)/shard_map/ppermute | solution.py:24
  4.2 0.0 copy-done.4
  4.2 1.6 %collective-permute-start = (bf16[1,32,128]{2,1,0:T(8,128)(2,1)S(1)}, bf16[1,32,128]{2,1,0:T(8,128)(2,1)S(1)}, u32[]{:S(2)}, u32[]{:S(2)}) collective-permute-start(bf16[1,32,128]{2,1,0:T(8,128)(2,1)S(1)} %copy-done.4), channel_id=1, source_target_pairs={{0,4},{1,3},{2,6},{3,1},{4,0},{5,7},{6,2},{7,5},{8,12},{9,11},{10,... | collective-permute-start | bytes 24584 | tf_op jit(solution)/shard_map/ppermute | solution.py:24
  5.8 2.2 %collective-permute-done = bf16[1,32,128]{2,1,0:T(8,128)(2,1)S(1)} collective-permute-done((bf16[1,32,128]{2,1,0:T(8,128)(2,1)S(1)}, bf16[1,32,128]{2,1,0:T(8,128)(2,1)S(1)}, u32[]{:S(2)}, u32[]{:S(2)}) %collective-permute-start) | collective-permute-done | bytes 8224 | tf_op jit(solution)/shard_map/ppermute | solution.py:24
  8.0 2.6 %collective-permute-start.1 = (bf16[2,32,128]{2,1,0:T(8,128)(2,1)S(1)}, bf16[2,32,128]{2,1,0:T(8,128)(2,1)S(1)}, u32[]{:S(2)}, u32[]{:S(2)}) collective-permute-start(bf16[2,32,128]{2,1,0:T(8,128)(2,1)S(1)} %constant_dynamic-update-slice_fusion.first_ref), channel_id=1, source_target_pairs={{0,8},{1,9},{2,10},{3,11},{4,12},{5,13},{6,14},{7,15},{8,0},{9,1},... | collective-permute-start | bytes 49160 | tf_op jit(solution)/shard_map/ppermute | solution.py:24
  10.6 0.1 pad_add_fusion.place_ref
  10.7 0.0 copy-done
  10.7 0.0 copy-done.1
  10.7 0.0 copy-done.2
  10.7 0.0 copy-done.3
  10.7 0.7 %shard_map.82 = (f32[4,192]{1,0:T(4,128)S(1)}, f32[4,192]{1,0:T(4,128)S(1)}) custom-call(s32[3]{0:T(128)S(1)} %pad_add_fusion.place_ref, s32[3,8]{1,0:T(4,128)S(1)} %copy-done, s32[3,8]{1,0:T(4,128)S(1)} %copy-done.1, s32[3]{0:T(128)S(1)} %copy-done.2, s32[8]{0:T(128)S(1)} %copy-done.3), custom_call_target="tpu_custom_call" | custom-call | tf_op jit(solution)/shard_map/pallas_call | solution.py:268
  11.5 1.2 %collective-permute-done.1.second_ref = bf16[2,32,128]{2,1,0:T(8,128)(2,1)S(1)} collective-permute-done((bf16[2,32,128]{2,1,0:T(8,128)(2,1)S(1)}, bf16[2,32,128]{2,1,0:T(8,128)(2,1)S(1)}, u32[]{:S(2)}, u32[]{:S(2)}) %collective-permute-start.1) | collective-permute-done | bytes 16416 | tf_op jit(solution)/shard_map/ppermute | solution.py:24
  12.7 0.6 %shard_map.83 = (f32[1,128,128]{2,1,0:T(8,128)S(1)}, f32[1,128,128]{2,1,0:T(8,128)S(1)}, f32[1,128,128]{2,1,0:T(8,128)S(1)}) custom-call(bf16[2,32,128]{2,1,0:T(8,128)(2,1)S(1)} %constant_dynamic-update-slice_fusion.first_ref, bf16[2,32,128]{2,1,0:T(8,128)(2,1)S(1)} %collective-permute-done.1.second_ref, bf16[2432,128]{1,0:T(8,128)(2,1)S(1)} %pad_maximum_fusion.bulk_ref, ...), custom_call_target="tpu_custom_call" | custom-call | tf_op jit(solution)/shard_map/pallas_call | solution.py:268
  13.3 0.0 collective-permute-done.2.bulk_ref
  13.3 0.8 %shard_map.84 = (bf16[2,48,128]{2,1,0:T(8,128)(2,1)S(1)}, f32[2,32,128]{2,1,0:T(8,128)S(1)}, f32[2,8,128]{2,1,0:T(8,128)S(1)}) custom-call(bf16[2,32,128]{2,1,0:T(8,128)(2,1)S(1)} %constant_dynamic-update-slice_fusion.first_ref, bf16[2,32,128]{2,1,0:T(8,128)(2,1)S(1)} %collective-permute-done.1.second_ref, ...), custom_call_target="tpu_custom_call" | custom-call | tf_op jit(solution)/shard_map/pallas_call | solution.py:268
  14.1 2.7 %collective-permute-start.3 = (bf16[2,48,128]{2,1,0:T(8,128)(2,1)S(1)}, bf16[2,48,128]{2,1,0:T(8,128)(2,1)S(1)}, u32[]{:S(2)}, u32[]{:S(2)}) collective-permute-start(bf16[2,48,128]{2,1,0:T(8,128)(2,1)S(1)} %get-tuple-element.23), channel_id=1, source_target_pairs={{0,8},{1,9},{2,10},{3,11},{4,12},{5,13},{6,14},{7,15},{8,0},{9,1},... | collective-permute-start | bytes 73736 | tf_op jit(solution)/shard_map/ppermute | solution.py:24
  16.8 2.1 %collective-permute-done.3.parcel_ref = bf16[2,48,128]{2,1,0:T(8,128)(2,1)S(1)} collective-permute-done((bf16[2,48,128]{2,1,0:T(8,128)(2,1)S(1)}, bf16[2,48,128]{2,1,0:T(8,128)(2,1)S(1)}, u32[]{:S(2)}, u32[]{:S(2)}) %collective-permute-start.3) | collective-permute-done | bytes 24608 | tf_op jit(solution)/shard_map/ppermute | solution.py:24
  18.9 0.1 shard_map.85
  19.0 1.8 %collective-permute-start.4 = (bf16[1,48,128]{2,1,0:T(8,128)(2,1)S(1)}, bf16[1,48,128]{2,1,0:T(8,128)(2,1)S(1)}, u32[]{:S(2)}, u32[]{:S(2)}) collective-permute-start(bf16[1,48,128]{2,1,0:T(8,128)(2,1)S(1)} %get-tuple-element.26), channel_id=1, source_target_pairs={{0,4},{1,3},{2,6},{3,1},{4,0},{5,7},{6,2},{7,5},{8,12},{9,11},{10,... | collective-permute-start | bytes 36872 | tf_op jit(solution)/shard_map/ppermute | solution.py:24
  20.8 1.9 %collective-permute-done.4.parcel_ref = bf16[1,48,128]{2,1,0:T(8,128)(2,1)S(1)} collective-permute-done((bf16[1,48,128]{2,1,0:T(8,128)(2,1)S(1)}, bf16[1,48,128]{2,1,0:T(8,128)(2,1)S(1)}, u32[]{:S(2)}, u32[]{:S(2)}) %collective-permute-start.4) | collective-permute-done | bytes 12320 | tf_op jit(solution)/shard_map/ppermute | solution.py:24
  22.7 0.7 %shard_map.86 = bf16[1,32,128]{2,1,0:T(8,128)(2,1)} custom-call(f32[1,32,128]{2,1,0:T(8,128)S(1)} %get-tuple-element.24.keep_in, f32[1,8,128]{2,1,0:T(8,128)S(1)} %get-tuple-element.25.stat_in, bf16[1,48,128]{2,1,0:T(8,128)(2,1)S(1)} %collective-permute-done.4.parcel_ref), custom_call_target="tpu_custom_call" | custom-call | tf_op jit(solution)/shard_map/pallas_call | solution.py:268
  (2 shorter events, 0.0 us)
Async XLA Ops:
  0.0 4.2 %copy-start.4 = (bf16[1,32,128]{2,1,0:T(8,128)(2,1)S(1)}, bf16[1,32,128]{2,1,0:T(8,128)(2,1)}, u32[]{:S(2)}) copy-start(bf16[1,32,128]{2,1,0:T(8,128)(2,1)} %param.8) | copy-start | bytes 24580
  0.0 10.7 %copy-start = (s32[3,8]{1,0:T(4,128)S(1)}, s32[3,8]{1,0:T(4,128)}, u32[]{:S(2)}) copy-start(s32[3,8]{1,0:T(4,128)} %owner_ref.1) | copy-start | bytes 292
  0.0 10.7 %copy-start.1 = (s32[3,8]{1,0:T(4,128)S(1)}, s32[3,8]{1,0:T(4,128)}, u32[]{:S(2)}) copy-start(s32[3,8]{1,0:T(4,128)} %slot_ref.1) | copy-start | bytes 292
  0.0 10.7 %copy-start.2 = (s32[3]{0:T(128)S(1)}, s32[3]{0:T(128)}, u32[]{:S(2)}) copy-start(s32[3]{0:T(128)} %len_ref.1) | copy-start | bytes 40
  0.0 10.7 %copy-start.3 = (s32[8]{0:T(128)S(1)}, s32[8]{0:T(128)}, u32[]{:S(2)}) copy-start(s32[8]{0:T(128)} %request_ref.1) | copy-start | bytes 100
  1.2 12.1 %collective-permute-start.2 = (bf16[2432,128]{1,0:T(8,128)(2,1)S(1)}, bf16[2432,128]{1,0:T(8,128)(2,1)S(1)}, u32[]{:S(2)}, u32[]{:S(2)}) collective-permute-start(bf16[2432,128]{1,0:T(8,128)(2,1)S(1)} %pad_maximum_fusion.bulk_ref), channel_id=1, source_target_pairs={{0,2},{1,5},{2,0},{3,7},{4,6},{5,1},{6,4},{7,3},{8,10},{9,13},{10,... | collective-permute-start | bytes 1867784 | tf_op jit(solution)/shard_map/ppermute | solution.py:24
  4.2 3.8 %collective-permute-start = (bf16[1,32,128]{2,1,0:T(8,128)(2,1)S(1)}, bf16[1,32,128]{2,1,0:T(8,128)(2,1)S(1)}, u32[]{:S(2)}, u32[]{:S(2)}) collective-permute-start(bf16[1,32,128]{2,1,0:T(8,128)(2,1)S(1)} %copy-done.4), channel_id=1, source_target_pairs={{0,4},{1,3},{2,6},{3,1},{4,0},{5,7},{6,2},{7,5},{8,12},{9,11},{10,... | collective-permute-start | bytes 24584 | tf_op jit(solution)/shard_map/ppermute | solution.py:24
  8.0 4.6 %collective-permute-start.1 = (bf16[2,32,128]{2,1,0:T(8,128)(2,1)S(1)}, bf16[2,32,128]{2,1,0:T(8,128)(2,1)S(1)}, u32[]{:S(2)}, u32[]{:S(2)}) collective-permute-start(bf16[2,32,128]{2,1,0:T(8,128)(2,1)S(1)} %constant_dynamic-update-slice_fusion.first_ref), channel_id=1, source_target_pairs={{0,8},{1,9},{2,10},{3,11},{4,12},{5,13},{6,14},{7,15},{8,0},{9,1},... | collective-permute-start | bytes 49160 | tf_op jit(solution)/shard_map/ppermute | solution.py:24
  14.1 4.8 %collective-permute-start.3 = (bf16[2,48,128]{2,1,0:T(8,128)(2,1)S(1)}, bf16[2,48,128]{2,1,0:T(8,128)(2,1)S(1)}, u32[]{:S(2)}, u32[]{:S(2)}) collective-permute-start(bf16[2,48,128]{2,1,0:T(8,128)(2,1)S(1)} %get-tuple-element.23), channel_id=1, source_target_pairs={{0,8},{1,9},{2,10},{3,11},{4,12},{5,13},{6,14},{7,15},{8,0},{9,1},... | collective-permute-start | bytes 73736 | tf_op jit(solution)/shard_map/ppermute | solution.py:24
  19.0 3.7 %collective-permute-start.4 = (bf16[1,48,128]{2,1,0:T(8,128)(2,1)S(1)}, bf16[1,48,128]{2,1,0:T(8,128)(2,1)S(1)}, u32[]{:S(2)}, u32[]{:S(2)}) collective-permute-start(bf16[1,48,128]{2,1,0:T(8,128)(2,1)S(1)} %get-tuple-element.26), channel_id=1, source_target_pairs={{0,4},{1,3},{2,6},{3,1},{4,0},{5,7},{6,2},{7,5},{8,12},{9,11},{10,... | collective-permute-start | bytes 36872 | tf_op jit(solution)/shard_map/ppermute | solution.py:24

commit v5 on v4

--- a/solution.py
+++ b/solution.py
@@ -106,6 +106,31 @@
         ],
         axis=0,
     )
+
+
+def pack_kernel(key_ref, value_ref, pool_ref, bulk_ref, sems):
+    start = 0
+    copies = []
+    for i, source in enumerate((key_ref, value_ref, pool_ref)):
+        rows = source.shape[0]
+        copies.append(pltpu.make_async_copy(source, bulk_ref.at[start : start + rows], sems.at[i]))
+        start += rows
+    for copy in copies:
+        copy.start()
+    for copy in copies:
+        copy.wait()
+
+
+def pack(*sources):
+    rows = sum(source.shape[0] for source in sources)
+    return pl.pallas_call(
+        pack_kernel,
+        out_shape=jax.ShapeDtypeStruct((rows, sources[0].shape[1]), sources[0].dtype),
+        in_specs=[pl.BlockSpec(memory_space=pltpu.HBM)] * len(sources),
+        out_specs=pl.BlockSpec(memory_space=pltpu.VMEM),
+        scratch_shapes=[pltpu.SemaphoreType.DMA((len(sources),))],
+        compiler_params=pltpu.CompilerParams(vmem_limit_bytes=VMEM_BYTES),
+    )(*(pltpu.with_memory_space_constraint(source, pltpu.HBM) for source in sources))
 
 
 def bias_kernel(
@@ -144,61 +169,40 @@
     loop(row_total, one)
 
 
-def near_kernel(first_ref, second_ref, bulk_ref, bias_ref, mixed_ref, top_ref, total_ref, *, sizes):
-    half, qheads, head_dim = first_ref.shape
-    chunk = min(CHUNK, half * 2)
-    part = chunk // 2
-
-    def one(i):
-        base = i * part
-        query = jnp.concatenate(
-            [
-                first_ref[pl.ds(base, part)].reshape(part * qheads, head_dim),
-                second_ref[pl.ds(base, part)].reshape(part * qheads, head_dim),
-            ],
-            axis=0,
-        )
-        bias = jnp.concatenate(
-            [
-                chunk_bias(bias_ref, base, part, qheads),
-                chunk_bias(bias_ref, half + base, part, qheads),
-            ],
-            axis=0,
-        )
+def chunks(query_ref):
+    count, qheads, head_dim = query_ref.shape
+    chunk = min(CHUNK, count)
+
+    def load(i, bias_ref, offset):
+        query = query_ref[pl.ds(i * chunk, chunk)].reshape(chunk * qheads, head_dim)
+        return query, chunk_bias(bias_ref, offset + i * chunk, chunk, qheads)
+
+    return chunk, count // chunk, load
+
+
+def near_kernel(query_ref, bulk_ref, bias_ref, mixed_ref, top_ref, total_ref, *, offset, sizes):
+    _, steps, load = chunks(query_ref)
+
+    def one(i):
+        query, bias = load(i, bias_ref, offset)
         top, total, mixed = attend(query, bulk_ref, bias, sizes)
         mixed_ref[i] = mixed
         top_ref[i] = jnp.broadcast_to(top, mixed.shape)
         total_ref[i] = jnp.broadcast_to(total, mixed.shape)
 
-    loop(half // part, one)
+    loop(steps, one)
 
 
 def far_kernel(
-    first_ref, second_ref, bulk_ref, bias_ref, mixed_ref, top_ref, total_ref,
-    send_ref, keep_ref, stat_ref, *, sizes,
+    query_ref, bulk_ref, bias_ref, mixed_ref, top_ref, total_ref, *out_refs, offset, sizes
 ):
-    half, qheads, head_dim = first_ref.shape
+    _, qheads, head_dim = query_ref.shape
     scale = sizes[-1]
-    chunk = min(CHUNK, half * 2)
-    part = chunk // 2
+    chunk, steps, load = chunks(query_ref)
     diagonal = spread_rows(qheads, head_dim)
 
     def one(i):
-        base = i * part
-        query = jnp.concatenate(
-            [
-                first_ref[pl.ds(base, part)].reshape(part * qheads, head_dim),
-                second_ref[pl.ds(base, part)].reshape(part * qheads, head_dim),
-            ],
-            axis=0,
-        )
-        bias = jnp.concatenate(
-            [
-                chunk_bias(bias_ref, base, part, qheads),
-                chunk_bias(bias_ref, half + base, part, qheads),
-            ],
-            axis=0,
-        )
+        query, bias = load(i, bias_ref, offset)
         top, total, mixed = attend(query, bulk_ref, bias, sizes)
         near_top = top_ref[i][:, :1]
         high, low = split(jnp.maximum(near_top, top))
@@ -207,16 +211,22 @@
         far_scale = jnp.exp2((top - point) * scale)
         total = total_ref[i][:, :1] * near_scale + total * far_scale
         mixed = (mixed_ref[i] * near_scale + mixed * far_scale) / total
-        for j in range(part):
+        for j in range(chunk):
             rows = slice(j * qheads, (j + 1) * qheads)
-            keep_ref[base + j] = mixed[rows]
-            stat_ref[base + j, 0:1] = to_row(point[rows], diagonal)
-            stat_ref[base + j, 1:2] = to_row(total[rows], diagonal)
-            rows = slice((part + j) * qheads, (part + j + 1) * qheads)
-            stats = stat_block(to_row(point[rows], diagonal), to_row(total[rows], diagonal))
-            send_ref[base + j] = jnp.concatenate([mixed[rows], stats], axis=0).astype(jnp.bfloat16)
-
-    loop(half // part, one)
+            place = i * chunk + j
+            point_row = to_row(point[rows], diagonal)
+            total_row = to_row(total[rows], diagonal)
+            if len(out_refs) == 1:
+                (send_ref,) = out_refs
+                stats = stat_block(point_row, total_row)
+                send_ref[place] = jnp.concatenate([mixed[rows], stats], axis=0).astype(jnp.bfloat16)
+            else:
+                keep_ref, stat_ref = out_refs
+                keep_ref[place] = mixed[rows]
+                stat_ref[place, 0:1] = point_row
+                stat_ref[place, 1:2] = total_row
+
+    loop(steps, one)
 
 
 def merge_rows(keep, top, total, parcel, qheads, diagonal, scale):
@@ -288,13 +298,10 @@
     sizes = (kv_heads, qheads // kv_heads, prefix_rows, slots, page_rows, scale)
     shared_bits = [1 << b for b in range(2, blocks.bit_length() - 1)]
 
-    bulk = jnp.concatenate(
-        [
-            prefix_keys.reshape(prefix_rows, head_dim),
-            prefix_values.reshape(prefix_rows, head_dim),
-            suffix_pool.reshape(slots * 2 * page_rows, head_dim),
-        ],
-        axis=0,
+    bulk = pack(
+        prefix_keys.reshape(prefix_rows, head_dim),
+        prefix_values.reshape(prefix_rows, head_dim),
+        suffix_pool.reshape(slots * 2 * page_rows, head_dim),
     )
     far_bulk = exchange(bulk, 1, 2)
     first = queries
@@ -311,11 +318,14 @@
         bias_kernel, (table, table), (place, page_owner, page_slot, suffix_len, row_request), 5,
         rows_dev=rows_dev, page_len=page_len, kv_heads=kv_heads, blocks=blocks,
     )
-    chunk = min(CHUNK, rows)
-    block = jax.ShapeDtypeStruct((rows // chunk, chunk * qheads, head_dim), jnp.float32)
-    near = call(
-        near_kernel, (block, block, block), (first, second, bulk, near_bias), sizes=sizes
-    )
+    chunk = min(CHUNK, half)
+    block = jax.ShapeDtypeStruct((half // chunk, chunk * qheads, head_dim), jnp.float32)
+    near = [
+        call(
+            near_kernel, (block, block, block), (query, bulk, near_bias), offset=offset, sizes=sizes
+        )
+        for query, offset in ((first, 0), (second, half))
+    ]
 
     def parcel(count):
         return (
@@ -324,8 +334,12 @@
             jax.ShapeDtypeStruct((count, 8, head_dim), jnp.float32),
         )
 
-    send, keep, stats = call(
-        far_kernel, parcel(half), (first, second, far_bulk, far_bias, *near), sizes=sizes
+    outs = parcel(half)
+    (send,) = call(
+        far_kernel, outs[:1], (second, far_bulk, far_bias, *near[1]), offset=half, sizes=sizes
+    )
+    keep, stats = call(
+        far_kernel, outs[1:], (first, far_bulk, far_bias, *near[0]), offset=0, sizes=sizes
     )
     for bit in reversed(shared_bits):
         arrived = exchange(send, bit, bit)

time: 23.5 us -> 23.2 us (0.987)
  Pallas kernels: 2.97 us -> 4.9 us
  waiting for transfers between devices: 7.44 us -> 5.69 us
  other arithmetic: 1.26 us -> 0.08 us
  local copies, waits for them, and re-layouts: 0.03 us -> 0.63 us
    ppermute x5, waiting for transfers between devices: 7.44 us -> 5.69 us  [exchange(): return lax.ppermute(value, ('blk', 'heads'), pairs)]
    concatenate x1 -> x0, other arithmetic: 1.18 us -> none  [on_device(): jnp.concatenate([prefix_keys.reshape(prefix_rows, head_dim), prefix_value...]
    pallas_call x0 -> x1, Pallas kernels: none -> 1.09 us  [pack(): pl.pallas_call(pack_kernel, out_shape=jax.ShapeDtypeStruct((rows, sources...]
    pallas_call x5 -> x7, Pallas kernels: 2.97 us -> 3.81 us  [call(): pl.pallas_call(functools.partial(kernel, **static), out_shape=outs, in_sp...]
    unnamed x11, local copies, waits for them, and re-layouts: 0.02 us -> 0.62 us
  transfers between devices with their start and end apart: 5 -> 5, of which waited for: 4 -> 4; matrix products, arithmetic and copies ran while one was open for 0% -> 0% of each run, Pallas kernels for 6% -> 10%
where the time goes in v5:
time: 23.2 us; the launch traced here: 23 us
  starting transfers between devices  11.7 us (50%)
  waiting for transfers between devices  5.69 us (25%)
  Pallas kernels  4.9 us (21%)
  local copies, waits for them, and re-layouts  0.63 us (3%)
    ppermute x5, starting transfers between devices, exchange(): return lax.ppermute(value, ('blk', 'heads'), pairs)  11.7 us
    ppermute x5, waiting for transfers between devices, exchange(): return lax.ppermute(value, ('blk', 'heads'), pairs)  5.69 us
    pallas_call x7, Pallas kernels, call(): pl.pallas_call(functools.partial(kernel, **static), out_shape=outs, in_sp...  3.81 us
    pallas_call x1, Pallas kernels, pack(): pl.pallas_call(pack_kernel, out_shape=jax.ShapeDtypeStruct((rows, sources...  1.09 us
    unnamed x11, local copies, waits for them, and re-layouts  0.62 us
  transfers between devices with their start and end apart: 5, of which 4 were waited for; matrix products, arithmetic and copies ran while one was open for 0% of the time, Pallas kernels for 10%

profile of v5, /device:TPU:0, one launch (start us, length us, event | category | flops | bytes accessed | tf_op | source)
XLA Modules:
  0.0 23.0 jit_solution(1652842627139855099)
XLA Ops:
  0.0 0.0 copy-start.4
  0.0 1.1 %shard_map.82.bulk_ref = bf16[2432,128]{1,0:T(8,128)(2,1)S(1)} custom-call(bf16[1024,128]{1,0:T(8,128)(2,1)} %bitcast.6, bf16[1024,128]{1,0:T(8,128)(2,1)} %bitcast.7, bf16[384,128]{1,0:T(8,128)(2,1)} %bitcast.8), custom_call_target="tpu_custom_call" | custom-call | tf_op jit(solution)/shard_map/pallas_call | solution.py:126
  1.1 3.0 %collective-permute-start.1 = (bf16[2432,128]{1,0:T(8,128)(2,1)S(1)}, bf16[2432,128]{1,0:T(8,128)(2,1)S(1)}, u32[]{:S(2)}, u32[]{:S(2)}) collective-permute-start(bf16[2432,128]{1,0:T(8,128)(2,1)S(1)} %shard_map.82.bulk_ref), channel_id=1, source_target_pairs={{0,2},{1,5},{2,0},{3,7},{4,6},{5,1},{6,4},{7,3},{8,10},{9,13},{10,... | collective-permute-start | bytes 1867784 | tf_op jit(solution)/shard_map/ppermute | solution.py:24
  4.1 0.0 copy-done.4
  4.1 1.6 %collective-permute-start = (bf16[1,32,128]{2,1,0:T(8,128)(2,1)S(1)}, bf16[1,32,128]{2,1,0:T(8,128)(2,1)S(1)}, u32[]{:S(2)}, u32[]{:S(2)}) collective-permute-start(bf16[1,32,128]{2,1,0:T(8,128)(2,1)S(1)} %copy-done.4), channel_id=1, source_target_pairs={{0,4},{1,3},{2,6},{3,1},{4,0},{5,7},{6,2},{7,5},{8,12},{9,11},{10,... | collective-permute-start | bytes 24584 | tf_op jit(solution)/shard_map/ppermute | solution.py:24
  5.7 2.2 %collective-permute-done = bf16[1,32,128]{2,1,0:T(8,128)(2,1)S(1)} collective-permute-done((bf16[1,32,128]{2,1,0:T(8,128)(2,1)S(1)}, bf16[1,32,128]{2,1,0:T(8,128)(2,1)S(1)}, u32[]{:S(2)}, u32[]{:S(2)}) %collective-permute-start) | collective-permute-done | bytes 8224 | tf_op jit(solution)/shard_map/ppermute | solution.py:24
  7.9 2.6 %collective-permute-start.2 = (bf16[2,32,128]{2,1,0:T(8,128)(2,1)S(1)}, bf16[2,32,128]{2,1,0:T(8,128)(2,1)S(1)}, u32[]{:S(2)}, u32[]{:S(2)}) collective-permute-start(bf16[2,32,128]{2,1,0:T(8,128)(2,1)S(1)} %constant_dynamic-update-slice_fusion.query_ref), channel_id=1, source_target_pairs={{0,8},{1,9},{2,10},{3,11},{4,12},{5,13},{6,14},{7,15},{8,0},{9,1},... | collective-permute-start | bytes 49160 | tf_op jit(solution)/shard_map/ppermute | solution.py:24
  10.5 0.0 copy-start.1
  10.5 0.0 copy-start
  10.5 0.0 copy-start.2
  10.5 0.0 copy-start.3
  10.5 0.1 pad_add_fusion.place_ref
  10.6 0.6 %copy-done.1 = s32[3,8]{1,0:T(4,128)S(1)} copy-done((s32[3,8]{1,0:T(4,128)S(1)}, s32[3,8]{1,0:T(4,128)}, u32[]{:S(2)}) %copy-start.1) | copy-done | bytes 120
  11.2 0.0 copy-done
  11.2 0.0 copy-done.2
  11.2 0.0 copy-done.3
  11.2 0.7 %shard_map.83 = (f32[4,192]{1,0:T(4,128)S(1)}, f32[4,192]{1,0:T(4,128)S(1)}) custom-call(s32[3]{0:T(128)S(1)} %pad_add_fusion.place_ref, s32[3,8]{1,0:T(4,128)S(1)} %copy-done, s32[3,8]{1,0:T(4,128)S(1)} %copy-done.1, s32[3]{0:T(128)S(1)} %copy-done.2, s32[8]{0:T(128)S(1)} %copy-done.3), custom_call_target="tpu_custom_call" | custom-call | tf_op jit(solution)/shard_map/pallas_call | solution.py:278
  12.0 0.6 %collective-permute-done.2.query_ref = bf16[2,32,128]{2,1,0:T(8,128)(2,1)S(1)} collective-permute-done((bf16[2,32,128]{2,1,0:T(8,128)(2,1)S(1)}, bf16[2,32,128]{2,1,0:T(8,128)(2,1)S(1)}, u32[]{:S(2)}, u32[]{:S(2)}) %collective-permute-start.2) | collective-permute-done | bytes 16416 | tf_op jit(solution)/shard_map/ppermute | solution.py:24
  12.6 0.5 %shard_map.86 = (f32[1,64,128]{2,1,0:T(8,128)S(1)}, f32[1,64,128]{2,1,0:T(8,128)S(1)}, f32[1,64,128]{2,1,0:T(8,128)S(1)}) custom-call(bf16[2,32,128]{2,1,0:T(8,128)(2,1)S(1)} %collective-permute-done.2.query_ref, bf16[2432,128]{1,0:T(8,128)(2,1)S(1)} %shard_map.82.bulk_ref, f32[4,192]{1,0:T(4,128)S(1)} %get-tuple-element.19.bias_ref), custom_call_target="tpu_custom_call" | custom-call | tf_op jit(solution)/shard_map/pallas_call | solution.py:278
  13.1 0.0 collective-permute-done.1.bulk_ref
  13.1 0.6 %shard_map.87 = bf16[2,48,128]{2,1,0:T(8,128)(2,1)S(1)} custom-call(bf16[2,32,128]{2,1,0:T(8,128)(2,1)S(1)} %collective-permute-done.2.query_ref, bf16[2432,128]{1,0:T(8,128)(2,1)S(1)} %collective-permute-done.1.bulk_ref, f32[4,192]{1,0:T(4,128)S(1)} %get-tuple-element.18.bias_ref, f32[1,64,128]{2,1,0:T(8,128)S(1)} %get-tuple-element.25.mixed_ref, ...), custom_call_target="tpu_custom_call" | custom-call | tf_op jit(solution)/shard_map/pallas_call | solution.py:278
  13.7 2.7 %collective-permute-start.3 = (bf16[2,48,128]{2,1,0:T(8,128)(2,1)S(1)}, bf16[2,48,128]{2,1,0:T(8,128)(2,1)S(1)}, u32[]{:S(2)}, u32[]{:S(2)}) collective-permute-start(bf16[2,48,128]{2,1,0:T(8,128)(2,1)S(1)} %shard_map.87), channel_id=1, source_target_pairs={{0,8},{1,9},{2,10},{3,11},{4,12},{5,13},{6,14},{7,15},{8,0},{9,1},... | collective-permute-start | bytes 73736 | tf_op jit(solution)/shard_map/ppermute | solution.py:24
  16.4 0.5 %shard_map.84 = (f32[1,64,128]{2,1,0:T(8,128)S(1)}, f32[1,64,128]{2,1,0:T(8,128)S(1)}, f32[1,64,128]{2,1,0:T(8,128)S(1)}) custom-call(bf16[2,32,128]{2,1,0:T(8,128)(2,1)S(1)} %constant_dynamic-update-slice_fusion.query_ref, bf16[2432,128]{1,0:T(8,128)(2,1)S(1)} %shard_map.82.bulk_ref, f32[4,192]{1,0:T(4,128)S(1)} %get-tuple-element.19.bias_ref), custom_call_target="tpu_custom_call" | custom-call | tf_op jit(solution)/shard_map/pallas_call | solution.py:278
  16.9 0.6 %shard_map.85 = (f32[2,32,128]{2,1,0:T(8,128)S(1)}, f32[2,8,128]{2,1,0:T(8,128)S(1)}) custom-call(bf16[2,32,128]{2,1,0:T(8,128)(2,1)S(1)} %constant_dynamic-update-slice_fusion.query_ref, bf16[2432,128]{1,0:T(8,128)(2,1)S(1)} %collective-permute-done.1.bulk_ref, f32[4,192]{1,0:T(4,128)S(1)} %get-tuple-element.18.bias_ref, ...), custom_call_target="tpu_custom_call" | custom-call | tf_op jit(solution)/shard_map/pallas_call | solution.py:278
  17.5 1.0 %collective-permute-done.3.parcel_ref = bf16[2,48,128]{2,1,0:T(8,128)(2,1)S(1)} collective-permute-done((bf16[2,48,128]{2,1,0:T(8,128)(2,1)S(1)}, bf16[2,48,128]{2,1,0:T(8,128)(2,1)S(1)}, u32[]{:S(2)}, u32[]{:S(2)}) %collective-permute-start.3) | collective-permute-done | bytes 24608 | tf_op jit(solution)/shard_map/ppermute | solution.py:24
  18.5 0.1 shard_map.88
  18.6 1.8 %collective-permute-start.4 = (bf16[1,48,128]{2,1,0:T(8,128)(2,1)S(1)}, bf16[1,48,128]{2,1,0:T(8,128)(2,1)S(1)}, u32[]{:S(2)}, u32[]{:S(2)}) collective-permute-start(bf16[1,48,128]{2,1,0:T(8,128)(2,1)S(1)} %get-tuple-element.30), channel_id=1, source_target_pairs={{0,4},{1,3},{2,6},{3,1},{4,0},{5,7},{6,2},{7,5},{8,12},{9,11},{10,... | collective-permute-start | bytes 36872 | tf_op jit(solution)/shard_map/ppermute | solution.py:24
  20.4 1.9 %collective-permute-done.4.parcel_ref = bf16[1,48,128]{2,1,0:T(8,128)(2,1)S(1)} collective-permute-done((bf16[1,48,128]{2,1,0:T(8,128)(2,1)S(1)}, bf16[1,48,128]{2,1,0:T(8,128)(2,1)S(1)}, u32[]{:S(2)}, u32[]{:S(2)}) %collective-permute-start.4) | collective-permute-done | bytes 12320 | tf_op jit(solution)/shard_map/ppermute | solution.py:24
  22.3 0.7 %shard_map.89 = bf16[1,32,128]{2,1,0:T(8,128)(2,1)} custom-call(f32[1,32,128]{2,1,0:T(8,128)S(1)} %get-tuple-element.28.keep_in, f32[1,8,128]{2,1,0:T(8,128)S(1)} %get-tuple-element.29.stat_in, bf16[1,48,128]{2,1,0:T(8,128)(2,1)S(1)} %collective-permute-done.4.parcel_ref), custom_call_target="tpu_custom_call" | custom-call | tf_op jit(solution)/shard_map/pallas_call | solution.py:278
  (2 shorter events, 0.0 us)
Async XLA Ops:
  0.0 4.1 %copy-start.4 = (bf16[1,32,128]{2,1,0:T(8,128)(2,1)S(1)}, bf16[1,32,128]{2,1,0:T(8,128)(2,1)}, u32[]{:S(2)}) copy-start(bf16[1,32,128]{2,1,0:T(8,128)(2,1)} %param.8) | copy-start | bytes 24580
  1.1 12.0 %collective-permute-start.1 = (bf16[2432,128]{1,0:T(8,128)(2,1)S(1)}, bf16[2432,128]{1,0:T(8,128)(2,1)S(1)}, u32[]{:S(2)}, u32[]{:S(2)}) collective-permute-start(bf16[2432,128]{1,0:T(8,128)(2,1)S(1)} %shard_map.82.bulk_ref), channel_id=1, source_target_pairs={{0,2},{1,5},{2,0},{3,7},{4,6},{5,1},{6,4},{7,3},{8,10},{9,13},{10,... | collective-permute-start | bytes 1867784 | tf_op jit(solution)/shard_map/ppermute | solution.py:24
  4.1 3.8 %collective-permute-start = (bf16[1,32,128]{2,1,0:T(8,128)(2,1)S(1)}, bf16[1,32,128]{2,1,0:T(8,128)(2,1)S(1)}, u32[]{:S(2)}, u32[]{:S(2)}) collective-permute-start(bf16[1,32,128]{2,1,0:T(8,128)(2,1)S(1)} %copy-done.4), channel_id=1, source_target_pairs={{0,4},{1,3},{2,6},{3,1},{4,0},{5,7},{6,2},{7,5},{8,12},{9,11},{10,... | collective-permute-start | bytes 24584 | tf_op jit(solution)/shard_map/ppermute | solution.py:24
  7.9 4.6 %collective-permute-start.2 = (bf16[2,32,128]{2,1,0:T(8,128)(2,1)S(1)}, bf16[2,32,128]{2,1,0:T(8,128)(2,1)S(1)}, u32[]{:S(2)}, u32[]{:S(2)}) collective-permute-start(bf16[2,32,128]{2,1,0:T(8,128)(2,1)S(1)} %constant_dynamic-update-slice_fusion.query_ref), channel_id=1, source_target_pairs={{0,8},{1,9},{2,10},{3,11},{4,12},{5,13},{6,14},{7,15},{8,0},{9,1},... | collective-permute-start | bytes 49160 | tf_op jit(solution)/shard_map/ppermute | solution.py:24
  10.5 0.7 %copy-start.1 = (s32[3,8]{1,0:T(4,128)S(1)}, s32[3,8]{1,0:T(4,128)}, u32[]{:S(2)}) copy-start(s32[3,8]{1,0:T(4,128)} %slot_ref.1) | copy-start | bytes 292
  10.5 0.7 %copy-start = (s32[3,8]{1,0:T(4,128)S(1)}, s32[3,8]{1,0:T(4,128)}, u32[]{:S(2)}) copy-start(s32[3,8]{1,0:T(4,128)} %owner_ref.1) | copy-start | bytes 292
  10.5 0.7 %copy-start.2 = (s32[3]{0:T(128)S(1)}, s32[3]{0:T(128)}, u32[]{:S(2)}) copy-start(s32[3]{0:T(128)} %len_ref.1) | copy-start | bytes 40
  10.5 0.7 %copy-start.3 = (s32[8]{0:T(128)S(1)}, s32[8]{0:T(128)}, u32[]{:S(2)}) copy-start(s32[8]{0:T(128)} %request_ref.1) | copy-start | bytes 100
  13.7 4.8 %collective-permute-start.3 = (bf16[2,48,128]{2,1,0:T(8,128)(2,1)S(1)}, bf16[2,48,128]{2,1,0:T(8,128)(2,1)S(1)}, u32[]{:S(2)}, u32[]{:S(2)}) collective-permute-start(bf16[2,48,128]{2,1,0:T(8,128)(2,1)S(1)} %shard_map.87), channel_id=1, source_target_pairs={{0,8},{1,9},{2,10},{3,11},{4,12},{5,13},{6,14},{7,15},{8,0},{9,1},... | collective-permute-start | bytes 73736 | tf_op jit(solution)/shard_map/ppermute | solution.py:24
  18.6 3.7 %collective-permute-start.4 = (bf16[1,48,128]{2,1,0:T(8,128)(2,1)S(1)}, bf16[1,48,128]{2,1,0:T(8,128)(2,1)S(1)}, u32[]{:S(2)}, u32[]{:S(2)}) collective-permute-start(bf16[1,48,128]{2,1,0:T(8,128)(2,1)S(1)} %get-tuple-element.30), channel_id=1, source_target_pairs={{0,4},{1,3},{2,6},{3,1},{4,0},{5,7},{6,2},{7,5},{8,12},{9,11},{10,... | collective-permute-start | bytes 36872 | tf_op jit(solution)/shard_map/ppermute | solution.py:24

commit v6 on v5

--- a/solution.py
+++ b/solution.py
@@ -11,6 +11,7 @@
 VMEM_BYTES = 40 * 1024 * 1024
 STAT_ROWS = 16
 CHUNK = 4
+PACK_BYTES = 4 * 1024 * 1024
 
 
 def exchange(value, even_bit, odd_bit):
@@ -58,22 +59,22 @@
     return jnp.concatenate([top_high, top_low, total_high, total_low, blank], axis=0)
 
 
-def suffix_rows(bulk_ref, start, slots, page_rows):
+def suffix_rows(rest_ref, start, slots, page_rows):
     return jnp.concatenate(
-        [bulk_ref[start + s * 2 * page_rows : start + s * 2 * page_rows + page_rows] for s in range(slots)],
+        [rest_ref[start + s * 2 * page_rows : start + s * 2 * page_rows + page_rows] for s in range(slots)],
         axis=0,
     )
 
 
-def attend(query, bulk_ref, bias, sizes):
+def attend(query, key_ref, rest_ref, bias, sizes):
     kv_heads, group, prefix_rows, slots, page_rows, scale = sizes
     rows = query.shape[0]
     qheads = kv_heads * group
     suffix_count = slots * page_rows
-    key = bulk_ref[0:prefix_rows]
-    value = bulk_ref[prefix_rows : 2 * prefix_rows]
-    page_key = suffix_rows(bulk_ref, 2 * prefix_rows, slots, page_rows)
-    page_value = suffix_rows(bulk_ref, 2 * prefix_rows + page_rows, slots, page_rows)
+    key = key_ref[...]
+    value = rest_ref[0:prefix_rows]
+    page_key = suffix_rows(rest_ref, prefix_rows, slots, page_rows)
+    page_value = suffix_rows(rest_ref, prefix_rows + page_rows, slots, page_rows)
     contract = (((1,), (1,)), ((), ()))
     near = lax.dot_general(query, key, contract, preferred_element_type=jnp.float32)
     page = lax.dot_general(query, page_key, contract, preferred_element_type=jnp.float32)
@@ -108,12 +109,13 @@
     )
 
 
-def pack_kernel(key_ref, value_ref, pool_ref, bulk_ref, sems):
+def pack_kernel(*refs):
+    *sources, rest_ref, sems = refs
     start = 0
     copies = []
-    for i, source in enumerate((key_ref, value_ref, pool_ref)):
+    for i, source in enumerate(sources):
         rows = source.shape[0]
-        copies.append(pltpu.make_async_copy(source, bulk_ref.at[start : start + rows], sems.at[i]))
+        copies.append(pltpu.make_async_copy(source, rest_ref.at[start : start + rows], sems.at[i]))
         start += rows
     for copy in copies:
         copy.start()
@@ -130,6 +132,7 @@
         out_specs=pl.BlockSpec(memory_space=pltpu.VMEM),
         scratch_shapes=[pltpu.SemaphoreType.DMA((len(sources),))],
         compiler_params=pltpu.CompilerParams(vmem_limit_bytes=VMEM_BYTES),
+        cost_estimate=pl.CostEstimate(flops=0, bytes_accessed=PACK_BYTES, transcendentals=0),
     )(*(pltpu.with_memory_space_constraint(source, pltpu.HBM) for source in sources))
 
 
@@ -180,12 +183,14 @@
     return chunk, count // chunk, load
 
 
-def near_kernel(query_ref, bulk_ref, bias_ref, mixed_ref, top_ref, total_ref, *, offset, sizes):
+def near_kernel(
+    query_ref, key_ref, rest_ref, bias_ref, mixed_ref, top_ref, total_ref, *, offset, sizes
+):
     _, steps, load = chunks(query_ref)
 
     def one(i):
         query, bias = load(i, bias_ref, offset)
-        top, total, mixed = attend(query, bulk_ref, bias, sizes)
+        top, total, mixed = attend(query, key_ref, rest_ref, bias, sizes)
         mixed_ref[i] = mixed
         top_ref[i] = jnp.broadcast_to(top, mixed.shape)
         total_ref[i] = jnp.broadcast_to(total, mixed.shape)
@@ -194,7 +199,7 @@
 
 
 def far_kernel(
-    query_ref, bulk_ref, bias_ref, mixed_ref, top_ref, total_ref, *out_refs, offset, sizes
+    query_ref, key_ref, rest_ref, bias_ref, mixed_ref, top_ref, total_ref, *out_refs, offset, sizes
 ):
     _, qheads, head_dim = query_ref.shape
     scale = sizes[-1]
@@ -203,7 +208,7 @@
 
     def one(i):
         query, bias = load(i, bias_ref, offset)
-        top, total, mixed = attend(query, bulk_ref, bias, sizes)
+        top, total, mixed = attend(query, key_ref, rest_ref, bias, sizes)
         near_top = top_ref[i][:, :1]
         high, low = split(jnp.maximum(near_top, top))
         point = high + low
@@ -298,14 +303,15 @@
     sizes = (kv_heads, qheads // kv_heads, prefix_rows, slots, page_rows, scale)
     shared_bits = [1 << b for b in range(2, blocks.bit_length() - 1)]
 
-    bulk = pack(
-        prefix_keys.reshape(prefix_rows, head_dim),
+    keys = prefix_keys.reshape(prefix_rows, head_dim)
+    rest = pack(
         prefix_values.reshape(prefix_rows, head_dim),
         suffix_pool.reshape(slots * 2 * page_rows, head_dim),
     )
-    far_bulk = exchange(bulk, 1, 2)
+    far_keys = exchange(keys, 1, 2)
     first = queries
     second = exchange(first, 2, 1)
+    far_rest = exchange(rest, 1, 2)
     for bit in shared_bits:
         first = jnp.concatenate([first, second], axis=0)
         second = exchange(first, bit, bit)
@@ -322,7 +328,7 @@
     block = jax.ShapeDtypeStruct((half // chunk, chunk * qheads, head_dim), jnp.float32)
     near = [
         call(
-            near_kernel, (block, block, block), (query, bulk, near_bias), offset=offset, sizes=sizes
+            near_kernel, (block, block, block), (query, pack(keys), rest, near_bias), offset=offset, sizes=sizes
         )
         for query, offset in ((first, 0), (second, half))
     ]
@@ -336,10 +342,10 @@
 
     outs = parcel(half)
     (send,) = call(
-        far_kernel, outs[:1], (second, far_bulk, far_bias, *near[1]), offset=half, sizes=sizes
+        far_kernel, outs[:1], (second, far_keys, far_rest, far_bias, *near[1]), offset=half, sizes=sizes
     )
     keep, stats = call(
-        far_kernel, outs[1:], (first, far_bulk, far_bias, *near[0]), offset=0, sizes=sizes
+        far_kernel, outs[1:], (first, far_keys, far_rest, far_bias, *near[0]), offset=0, sizes=sizes
     )
     for bit in reversed(shared_bits):
         arrived = exchange(send, bit, bit)

time: 23.2 us -> 23.1 us (level)
  waiting for transfers between devices: 5.69 us -> 4.72 us
  Pallas kernels: 4.9 us -> 5.85 us
  local copies, waits for them, and re-layouts: 0.63 us -> 0.03 us
  starting transfers between devices: 11.7 us -> 12.2 us
    ppermute x5 -> x6, waiting for transfers between devices: 5.69 us -> 4.72 us  [exchange(): return lax.ppermute(value, ('blk', 'heads'), pairs)]
    pallas_call x1 -> x2, Pallas kernels: 1.09 us -> 2.04 us  [pack(): pl.pallas_call(pack_kernel, out_shape=jax.ShapeDtypeStruct((rows, sources...]
    unnamed x11 -> x13, local copies, waits for them, and re-layouts: 0.62 us -> 0.02 us
    ppermute x5 -> x6, starting transfers between devices: 11.7 us -> 12.2 us  [exchange(): return lax.ppermute(value, ('blk', 'heads'), pairs)]
  transfers between devices with their start and end apart: 5 -> 6, of which waited for: 4 -> 4; matrix products, arithmetic and copies ran while one was open for 0% -> 0% of each run, Pallas kernels for 10% -> 15%
where the time goes in v6:
time: 23.1 us; the launch traced here: 23 us
  starting transfers between devices  12.2 us (53%)
  Pallas kernels  5.85 us (25%)
  waiting for transfers between devices  4.72 us (20%)
    ppermute x6, starting transfers between devices, exchange(): return lax.ppermute(value, ('blk', 'heads'), pairs)  12.2 us
    ppermute x6, waiting for transfers between devices, exchange(): return lax.ppermute(value, ('blk', 'heads'), pairs)  4.72 us
    pallas_call x7, Pallas kernels, call(): pl.pallas_call(functools.partial(kernel, **static), out_shape=outs, in_sp...  3.81 us
    pallas_call x2, Pallas kernels, pack(): pl.pallas_call(pack_kernel, out_shape=jax.ShapeDtypeStruct((rows, sources...  2.04 us
  transfers between devices with their start and end apart: 6, of which 4 were waited for; matrix products, arithmetic and copies ran while one was open for 0% of the time, Pallas kernels for 15%

profile of v6, /device:TPU:0, one launch (start us, length us, event | category | flops | bytes accessed | tf_op | source)
XLA Modules:
  0.0 23.0 jit_solution(2957078467227553945)
XLA Ops:
  0.0 0.0 copy-start.5
  0.0 0.0 copy-start.4
  0.0 1.0 %shard_map.82.rest_ref = bf16[1408,128]{1,0:T(8,128)(2,1)S(1)} custom-call(bf16[1024,128]{1,0:T(8,128)(2,1)} %bitcast.8, bf16[384,128]{1,0:T(8,128)(2,1)} %bitcast.9), custom_call_target="tpu_custom_call" | custom-call | bytes 4194304 | tf_op jit(solution)/shard_map/pallas_call | solution.py:128
  1.0 3.0 %collective-permute-start.2 = (bf16[1408,128]{1,0:T(8,128)(2,1)S(1)}, bf16[1408,128]{1,0:T(8,128)(2,1)S(1)}, u32[]{:S(2)}, u32[]{:S(2)}) collective-permute-start(bf16[1408,128]{1,0:T(8,128)(2,1)S(1)} %shard_map.82.rest_ref), channel_id=1, source_target_pairs={{0,2},{1,5},{2,0},{3,7},{4,6},{5,1},{6,4},{7,3},{8,10},{9,13},{10,... | collective-permute-start | bytes 1081352 | tf_op jit(solution)/shard_map/ppermute | solution.py:25
  4.0 0.0 copy-done.5
  4.1 1.6 %collective-permute-start = (bf16[1,32,128]{2,1,0:T(8,128)(2,1)S(1)}, bf16[1,32,128]{2,1,0:T(8,128)(2,1)S(1)}, u32[]{:S(2)}, u32[]{:S(2)}) collective-permute-start(bf16[1,32,128]{2,1,0:T(8,128)(2,1)S(1)} %copy-done.5), channel_id=1, source_target_pairs={{0,4},{1,3},{2,6},{3,1},{4,0},{5,7},{6,2},{7,5},{8,12},{9,11},{10,... | collective-permute-start | bytes 24584 | tf_op jit(solution)/shard_map/ppermute | solution.py:25
  5.6 0.0 copy-done.4
  5.6 0.5 %collective-permute-start.1 = (bf16[1024,128]{1,0:T(8,128)(2,1)S(1)}, bf16[1024,128]{1,0:T(8,128)(2,1)S(1)}, u32[]{:S(2)}, u32[]{:S(2)}) collective-permute-start(bf16[1024,128]{1,0:T(8,128)(2,1)S(1)} %bitcast.7), channel_id=1, source_target_pairs={{0,2},{1,5},{2,0},{3,7},{4,6},{5,1},{6,4},{7,3},{8,10},{9,13},{10,... | collective-permute-start | bytes 786440 | tf_op jit(solution)/shard_map/ppermute | solution.py:25
  6.2 1.7 %collective-permute-done = bf16[1,32,128]{2,1,0:T(8,128)(2,1)S(1)} collective-permute-done((bf16[1,32,128]{2,1,0:T(8,128)(2,1)S(1)}, bf16[1,32,128]{2,1,0:T(8,128)(2,1)S(1)}, u32[]{:S(2)}, u32[]{:S(2)}) %collective-permute-start) | collective-permute-done | bytes 8224 | tf_op jit(solution)/shard_map/ppermute | solution.py:25
  7.9 2.6 %collective-permute-start.3 = (bf16[2,32,128]{2,1,0:T(8,128)(2,1)S(1)}, bf16[2,32,128]{2,1,0:T(8,128)(2,1)S(1)}, u32[]{:S(2)}, u32[]{:S(2)}) collective-permute-start(bf16[2,32,128]{2,1,0:T(8,128)(2,1)S(1)} %constant_dynamic-update-slice_fusion.query_ref), channel_id=1, source_target_pairs={{0,8},{1,9},{2,10},{3,11},{4,12},{5,13},{6,14},{7,15},{8,0},{9,1},... | collective-permute-start | bytes 49160 | tf_op jit(solution)/shard_map/ppermute | solution.py:25
  10.5 0.1 pad_add_fusion.place_ref
  10.5 0.0 copy-start
  10.5 0.0 copy-start.1
  10.5 0.0 copy-start.2
  10.5 0.0 copy-start.3
  10.5 1.0 %shard_map.84.key_ref = bf16[1024,128]{1,0:T(8,128)(2,1)S(1)} custom-call(bf16[1024,128]{1,0:T(8,128)(2,1)} %bitcast.6), custom_call_target="tpu_custom_call" | custom-call | bytes 4194304 | tf_op jit(solution)/shard_map/pallas_call | solution.py:128
  11.6 0.0 copy-done
  11.6 0.0 copy-done.1
  11.6 0.0 copy-done.2
  11.6 0.0 copy-done.3
  11.6 0.7 %shard_map.83 = (f32[4,192]{1,0:T(4,128)S(1)}, f32[4,192]{1,0:T(4,128)S(1)}) custom-call(s32[3]{0:T(128)S(1)} %pad_add_fusion.place_ref, s32[3,8]{1,0:T(4,128)S(1)} %copy-done, s32[3,8]{1,0:T(4,128)S(1)} %copy-done.1, s32[3]{0:T(128)S(1)} %copy-done.2, s32[8]{0:T(128)S(1)} %copy-done.3), custom_call_target="tpu_custom_call" | custom-call | tf_op jit(solution)/shard_map/pallas_call | solution.py:283
  12.3 0.2 collective-permute-done.3.query_ref
  12.5 0.5 %shard_map.87 = (f32[1,64,128]{2,1,0:T(8,128)S(1)}, f32[1,64,128]{2,1,0:T(8,128)S(1)}, f32[1,64,128]{2,1,0:T(8,128)S(1)}) custom-call(bf16[2,32,128]{2,1,0:T(8,128)(2,1)S(1)} %collective-permute-done.3.query_ref, bf16[1024,128]{1,0:T(8,128)(2,1)S(1)} %shard_map.84.key_ref, bf16[1408,128]{1,0:T(8,128)(2,1)S(1)} %shard_map.82.rest_ref, ...), custom_call_target="tpu_custom_call" | custom-call | tf_op jit(solution)/shard_map/pallas_call | solution.py:283
  13.1 0.0 collective-permute-done.1.key_ref
  13.1 0.0 collective-permute-done.2.rest_ref
  13.1 0.6 %shard_map.88 = bf16[2,48,128]{2,1,0:T(8,128)(2,1)S(1)} custom-call(bf16[2,32,128]{2,1,0:T(8,128)(2,1)S(1)} %collective-permute-done.3.query_ref, bf16[1024,128]{1,0:T(8,128)(2,1)S(1)} %collective-permute-done.1.key_ref, bf16[1408,128]{1,0:T(8,128)(2,1)S(1)} %collective-permute-done.2.rest_ref, f32[4,192]{1,0:T(4,128)S(1)} %get-tuple-element.18.bias_ref, ...), custom_call_target="tpu_custom_call" | custom-call | tf_op jit(solution)/shard_map/pallas_call | solution.py:283
  13.7 2.7 %collective-permute-start.4 = (bf16[2,48,128]{2,1,0:T(8,128)(2,1)S(1)}, bf16[2,48,128]{2,1,0:T(8,128)(2,1)S(1)}, u32[]{:S(2)}, u32[]{:S(2)}) collective-permute-start(bf16[2,48,128]{2,1,0:T(8,128)(2,1)S(1)} %shard_map.88), channel_id=1, source_target_pairs={{0,8},{1,9},{2,10},{3,11},{4,12},{5,13},{6,14},{7,15},{8,0},{9,1},... | collective-permute-start | bytes 73736 | tf_op jit(solution)/shard_map/ppermute | solution.py:25
  16.3 0.5 %shard_map.85 = (f32[1,64,128]{2,1,0:T(8,128)S(1)}, f32[1,64,128]{2,1,0:T(8,128)S(1)}, f32[1,64,128]{2,1,0:T(8,128)S(1)}) custom-call(bf16[2,32,128]{2,1,0:T(8,128)(2,1)S(1)} %constant_dynamic-update-slice_fusion.query_ref, bf16[1024,128]{1,0:T(8,128)(2,1)S(1)} %shard_map.84.key_ref, bf16[1408,128]{1,0:T(8,128)(2,1)S(1)} %shard_map.82.rest_ref, ...), custom_call_target="tpu_custom_call" | custom-call | tf_op jit(solution)/shard_map/pallas_call | solution.py:283
  16.9 0.6 %shard_map.86 = (f32[2,32,128]{2,1,0:T(8,128)S(1)}, f32[2,8,128]{2,1,0:T(8,128)S(1)}) custom-call(bf16[2,32,128]{2,1,0:T(8,128)(2,1)S(1)} %constant_dynamic-update-slice_fusion.query_ref, bf16[1024,128]{1,0:T(8,128)(2,1)S(1)} %collective-permute-done.1.key_ref, bf16[1408,128]{1,0:T(8,128)(2,1)S(1)} %collective-permute-done.2.rest_ref, ...), custom_call_target="tpu_custom_call" | custom-call | tf_op jit(solution)/shard_map/pallas_call | solution.py:283
  17.5 1.0 %collective-permute-done.4.parcel_ref = bf16[2,48,128]{2,1,0:T(8,128)(2,1)S(1)} collective-permute-done((bf16[2,48,128]{2,1,0:T(8,128)(2,1)S(1)}, bf16[2,48,128]{2,1,0:T(8,128)(2,1)S(1)}, u32[]{:S(2)}, u32[]{:S(2)}) %collective-permute-start.4) | collective-permute-done | bytes 24608 | tf_op jit(solution)/shard_map/ppermute | solution.py:25
  18.5 0.1 shard_map.89
  18.6 1.8 %collective-permute-start.5 = (bf16[1,48,128]{2,1,0:T(8,128)(2,1)S(1)}, bf16[1,48,128]{2,1,0:T(8,128)(2,1)S(1)}, u32[]{:S(2)}, u32[]{:S(2)}) collective-permute-start(bf16[1,48,128]{2,1,0:T(8,128)(2,1)S(1)} %get-tuple-element.30), channel_id=1, source_target_pairs={{0,4},{1,3},{2,6},{3,1},{4,0},{5,7},{6,2},{7,5},{8,12},{9,11},{10,... | collective-permute-start | bytes 36872 | tf_op jit(solution)/shard_map/ppermute | solution.py:25
  20.4 1.9 %collective-permute-done.5.parcel_ref = bf16[1,48,128]{2,1,0:T(8,128)(2,1)S(1)} collective-permute-done((bf16[1,48,128]{2,1,0:T(8,128)(2,1)S(1)}, bf16[1,48,128]{2,1,0:T(8,128)(2,1)S(1)}, u32[]{:S(2)}, u32[]{:S(2)}) %collective-permute-start.5) | collective-permute-done | bytes 12320 | tf_op jit(solution)/shard_map/ppermute | solution.py:25
  22.3 0.7 %shard_map.90 = bf16[1,32,128]{2,1,0:T(8,128)(2,1)} custom-call(f32[1,32,128]{2,1,0:T(8,128)S(1)} %get-tuple-element.28.keep_in, f32[1,8,128]{2,1,0:T(8,128)S(1)} %get-tuple-element.29.stat_in, bf16[1,48,128]{2,1,0:T(8,128)(2,1)S(1)} %collective-permute-done.5.parcel_ref), custom_call_target="tpu_custom_call" | custom-call | tf_op jit(solution)/shard_map/pallas_call | solution.py:283
  (2 shorter events, 0.0 us)
Async XLA Ops:
  0.0 4.0 %copy-start.5 = (bf16[1,32,128]{2,1,0:T(8,128)(2,1)S(1)}, bf16[1,32,128]{2,1,0:T(8,128)(2,1)}, u32[]{:S(2)}) copy-start(bf16[1,32,128]{2,1,0:T(8,128)(2,1)} %param.8) | copy-start | bytes 24580
  0.0 5.6 %copy-start.4 = (bf16[256,4,128]{2,1,0:T(4,128)(2,1)S(1)}, bf16[256,4,128]{2,1,0:T(4,128)(2,1)}, u32[]{:S(2)}) copy-start(bf16[256,4,128]{2,1,0:T(4,128)(2,1)} %param.9) | copy-start | bytes 786436
  1.0 12.0 %collective-permute-start.2 = (bf16[1408,128]{1,0:T(8,128)(2,1)S(1)}, bf16[1408,128]{1,0:T(8,128)(2,1)S(1)}, u32[]{:S(2)}, u32[]{:S(2)}) collective-permute-start(bf16[1408,128]{1,0:T(8,128)(2,1)S(1)} %shard_map.82.rest_ref), channel_id=1, source_target_pairs={{0,2},{1,5},{2,0},{3,7},{4,6},{5,1},{6,4},{7,3},{8,10},{9,13},{10,... | collective-permute-start | bytes 1081352 | tf_op jit(solution)/shard_map/ppermute | solution.py:25
  4.1 3.8 %collective-permute-start = (bf16[1,32,128]{2,1,0:T(8,128)(2,1)S(1)}, bf16[1,32,128]{2,1,0:T(8,128)(2,1)S(1)}, u32[]{:S(2)}, u32[]{:S(2)}) collective-permute-start(bf16[1,32,128]{2,1,0:T(8,128)(2,1)S(1)} %copy-done.5), channel_id=1, source_target_pairs={{0,4},{1,3},{2,6},{3,1},{4,0},{5,7},{6,2},{7,5},{8,12},{9,11},{10,... | collective-permute-start | bytes 24584 | tf_op jit(solution)/shard_map/ppermute | solution.py:25
  5.6 7.4 %collective-permute-start.1 = (bf16[1024,128]{1,0:T(8,128)(2,1)S(1)}, bf16[1024,128]{1,0:T(8,128)(2,1)S(1)}, u32[]{:S(2)}, u32[]{:S(2)}) collective-permute-start(bf16[1024,128]{1,0:T(8,128)(2,1)S(1)} %bitcast.7), channel_id=1, source_target_pairs={{0,2},{1,5},{2,0},{3,7},{4,6},{5,1},{6,4},{7,3},{8,10},{9,13},{10,... | collective-permute-start | bytes 786440 | tf_op jit(solution)/shard_map/ppermute | solution.py:25
  7.9 4.6 %collective-permute-start.3 = (bf16[2,32,128]{2,1,0:T(8,128)(2,1)S(1)}, bf16[2,32,128]{2,1,0:T(8,128)(2,1)S(1)}, u32[]{:S(2)}, u32[]{:S(2)}) collective-permute-start(bf16[2,32,128]{2,1,0:T(8,128)(2,1)S(1)} %constant_dynamic-update-slice_fusion.query_ref), channel_id=1, source_target_pairs={{0,8},{1,9},{2,10},{3,11},{4,12},{5,13},{6,14},{7,15},{8,0},{9,1},... | collective-permute-start | bytes 49160 | tf_op jit(solution)/shard_map/ppermute | solution.py:25
  10.5 1.0 %copy-start = (s32[3,8]{1,0:T(4,128)S(1)}, s32[3,8]{1,0:T(4,128)}, u32[]{:S(2)}) copy-start(s32[3,8]{1,0:T(4,128)} %owner_ref.1) | copy-start | bytes 292
  10.5 1.0 %copy-start.1 = (s32[3,8]{1,0:T(4,128)S(1)}, s32[3,8]{1,0:T(4,128)}, u32[]{:S(2)}) copy-start(s32[3,8]{1,0:T(4,128)} %slot_ref.1) | copy-start | bytes 292
  10.5 1.0 %copy-start.2 = (s32[3]{0:T(128)S(1)}, s32[3]{0:T(128)}, u32[]{:S(2)}) copy-start(s32[3]{0:T(128)} %len_ref.1) | copy-start | bytes 40
  10.5 1.1 %copy-start.3 = (s32[8]{0:T(128)S(1)}, s32[8]{0:T(128)}, u32[]{:S(2)}) copy-start(s32[8]{0:T(128)} %request_ref.1) | copy-start | bytes 100
  13.7 4.8 %collective-permute-start.4 = (bf16[2,48,128]{2,1,0:T(8,128)(2,1)S(1)}, bf16[2,48,128]{2,1,0:T(8,128)(2,1)S(1)}, u32[]{:S(2)}, u32[]{:S(2)}) collective-permute-start(bf16[2,48,128]{2,1,0:T(8,128)(2,1)S(1)} %shard_map.88), channel_id=1, source_target_pairs={{0,8},{1,9},{2,10},{3,11},{4,12},{5,13},{6,14},{7,15},{8,0},{9,1},... | collective-permute-start | bytes 73736 | tf_op jit(solution)/shard_map/ppermute | solution.py:25
  18.6 3.7 %collective-permute-start.5 = (bf16[1,48,128]{2,1,0:T(8,128)(2,1)S(1)}, bf16[1,48,128]{2,1,0:T(8,128)(2,1)S(1)}, u32[]{:S(2)}, u32[]{:S(2)}) collective-permute-start(bf16[1,48,128]{2,1,0:T(8,128)(2,1)S(1)} %get-tuple-element.30), channel_id=1, source_target_pairs={{0,4},{1,3},{2,6},{3,1},{4,0},{5,7},{6,2},{7,5},{8,12},{9,11},{10,... | collective-permute-start | bytes 36872 | tf_op jit(solution)/shard_map/ppermute | solution.py:25

commit v7 on v6

--- a/solution.py
+++ b/solution.py
@@ -14,14 +14,14 @@
 PACK_BYTES = 4 * 1024 * 1024
 
 
-def exchange(value, even_bit, odd_bit):
+def exchange(value, even_bit, odd_bit, turn=0):
     blocks = lax.axis_size("blk")
     cores = lax.axis_size("heads")
-    pairs = [
-        (b * cores + c, (b ^ (odd_bit if c % 2 else even_bit)) * cores + c)
-        for b in range(blocks)
-        for c in range(cores)
-    ]
+    pairs = []
+    for b in range(blocks):
+        for c in range(cores):
+            goal = c ^ turn
+            pairs.append((b * cores + c, (b ^ (odd_bit if goal % 2 else even_bit)) * cores + goal))
     return lax.ppermute(value, ("blk", "heads"), pairs)
 
 
@@ -172,24 +172,37 @@
     loop(row_total, one)
 
 
-def chunks(query_ref):
-    count, qheads, head_dim = query_ref.shape
-    chunk = min(CHUNK, count)
-
-    def load(i, bias_ref, offset):
-        query = query_ref[pl.ds(i * chunk, chunk)].reshape(chunk * qheads, head_dim)
-        return query, chunk_bias(bias_ref, offset + i * chunk, chunk, qheads)
-
-    return chunk, count // chunk, load
+def chunks(first_ref, second_ref, bias_ref):
+    half, qheads, head_dim = first_ref.shape
+    part = min(CHUNK // 2, half)
+
+    def load(i):
+        query = jnp.concatenate(
+            [
+                ref[pl.ds(i * part, part)].reshape(part * qheads, head_dim)
+                for ref in (first_ref, second_ref)
+            ],
+            axis=0,
+        )
+        bias = jnp.concatenate(
+            [
+                chunk_bias(bias_ref, i * part, part, qheads),
+                chunk_bias(bias_ref, half + i * part, part, qheads),
+            ],
+            axis=0,
+        )
+        return query, bias
+
+    return part, half // part, load
 
 
 def near_kernel(
-    query_ref, key_ref, rest_ref, bias_ref, mixed_ref, top_ref, total_ref, *, offset, sizes
+    first_ref, second_ref, key_ref, rest_ref, bias_ref, mixed_ref, top_ref, total_ref, *, sizes
 ):
-    _, steps, load = chunks(query_ref)
-
-    def one(i):
-        query, bias = load(i, bias_ref, offset)
+    _, steps, load = chunks(first_ref, second_ref, bias_ref)
+
+    def one(i):
+        query, bias = load(i)
         top, total, mixed = attend(query, key_ref, rest_ref, bias, sizes)
         mixed_ref[i] = mixed
         top_ref[i] = jnp.broadcast_to(top, mixed.shape)
@@ -199,15 +212,16 @@
 
 
 def far_kernel(
-    query_ref, key_ref, rest_ref, bias_ref, mixed_ref, top_ref, total_ref, *out_refs, offset, sizes
+    first_ref, second_ref, key_ref, rest_ref, bias_ref, mixed_ref, top_ref, total_ref,
+    send_ref, keep_ref, *, sizes,
 ):
-    _, qheads, head_dim = query_ref.shape
+    _, qheads, head_dim = first_ref.shape
     scale = sizes[-1]
-    chunk, steps, load = chunks(query_ref)
+    part, steps, load = chunks(first_ref, second_ref, bias_ref)
     diagonal = spread_rows(qheads, head_dim)
 
     def one(i):
-        query, bias = load(i, bias_ref, offset)
+        query, bias = load(i)
         top, total, mixed = attend(query, key_ref, rest_ref, bias, sizes)
         near_top = top_ref[i][:, :1]
         high, low = split(jnp.maximum(near_top, top))
@@ -216,64 +230,57 @@
         far_scale = jnp.exp2((top - point) * scale)
         total = total_ref[i][:, :1] * near_scale + total * far_scale
         mixed = (mixed_ref[i] * near_scale + mixed * far_scale) / total
-        for j in range(chunk):
+        for j in range(2 * part):
             rows = slice(j * qheads, (j + 1) * qheads)
-            place = i * chunk + j
-            point_row = to_row(point[rows], diagonal)
-            total_row = to_row(total[rows], diagonal)
-            if len(out_refs) == 1:
-                (send_ref,) = out_refs
-                stats = stat_block(point_row, total_row)
-                send_ref[place] = jnp.concatenate([mixed[rows], stats], axis=0).astype(jnp.bfloat16)
-            else:
-                keep_ref, stat_ref = out_refs
-                keep_ref[place] = mixed[rows]
-                stat_ref[place, 0:1] = point_row
-                stat_ref[place, 1:2] = total_row
+            place = i * part + j % part
+            out_ref = keep_ref if j < part else send_ref
+            out_ref[place] = write(
+                mixed[rows], to_row(point[rows], diagonal), to_row(total[rows], diagonal),
+                out_ref.dtype,
+            )
 
     loop(steps, one)
 
 
-def merge_rows(keep, top, total, parcel, qheads, diagonal, scale):
+def read(parcel):
+    parcel = parcel.astype(jnp.float32)
+    qheads = parcel.shape[0] - STAT_ROWS
     stats = parcel[qheads:]
-    other_top = stats[0:1] + stats[1:2]
-    other_total = stats[2:3] + stats[3:4]
+    return parcel[:qheads], stats[0:1] + stats[1:2], stats[2:3] + stats[3:4]
+
+
+def write(mixed, top, total, dtype):
+    return jnp.concatenate([mixed, stat_block(top, total)], axis=0).astype(dtype)
+
+
+def merged(keep_ref, parcel_ref, i, diagonal, scale):
+    keep, top, total = read(keep_ref[i])
+    other, other_top, other_total = read(parcel_ref[i])
     point = jnp.maximum(top, other_top)
-    own = total * jnp.exp2((top - point) * scale)
-    other = other_total * jnp.exp2((other_top - point) * scale)
-    total = own + other
-    weight = to_column(other / total, diagonal)
-    return keep + (parcel[:qheads] - keep) * weight, point, total
-
-
-def merge_kernel(keep_in, stat_in, parcel_ref, send_ref, keep_ref, stat_ref, *, scale):
-    count, qheads, head_dim = keep_in.shape
-    diagonal = spread_rows(qheads, head_dim)
+    own_weight = total * jnp.exp2((top - point) * scale)
+    other_weight = other_total * jnp.exp2((other_top - point) * scale)
+    total = own_weight + other_weight
+    return keep + (other - keep) * to_column(other_weight / total, diagonal), point, total
+
+
+def merge_kernel(parcel_ref, keep_in, send_ref, keep_ref, *, scale):
+    count, rows, head_dim = keep_in.shape
+    diagonal = spread_rows(rows - STAT_ROWS, head_dim)
     half = count // 2
 
-    def merged(i):
-        return merge_rows(
-            keep_in[i], stat_in[i, 0:1], stat_in[i, 1:2], parcel_ref[i].astype(jnp.float32),
-            qheads, diagonal, scale,
-        )
-
-    def one(i):
-        mixed, top, total = merged(half + i)
-        send_ref[i] = jnp.concatenate([mixed, stat_block(top, total)], axis=0).astype(jnp.bfloat16)
-        keep_ref[i], stat_ref[i, 0:1], stat_ref[i, 1:2] = merged(i)
+    def one(i):
+        send_ref[i] = write(*merged(keep_in, parcel_ref, half + i, diagonal, scale), send_ref.dtype)
+        keep_ref[i] = write(*merged(keep_in, parcel_ref, i, diagonal, scale), keep_ref.dtype)
 
     loop(half, one)
 
 
-def last_kernel(keep_in, stat_in, parcel_ref, out_ref, *, scale):
-    count, qheads, head_dim = keep_in.shape
-    diagonal = spread_rows(qheads, head_dim)
-
-    def one(i):
-        mixed, _, _ = merge_rows(
-            keep_in[i], stat_in[i, 0:1], stat_in[i, 1:2], parcel_ref[i].astype(jnp.float32),
-            qheads, diagonal, scale,
-        )
+def last_kernel(parcel_ref, keep_in, out_ref, *, scale):
+    count, rows, head_dim = keep_in.shape
+    diagonal = spread_rows(rows - STAT_ROWS, head_dim)
+
+    def one(i):
+        mixed, _, _ = merged(keep_in, parcel_ref, i, diagonal, scale)
         out_ref[i] = mixed.astype(out_ref.dtype)
 
     loop(count, one)
@@ -324,37 +331,33 @@
         bias_kernel, (table, table), (place, page_owner, page_slot, suffix_len, row_request), 5,
         rows_dev=rows_dev, page_len=page_len, kv_heads=kv_heads, blocks=blocks,
     )
-    chunk = min(CHUNK, half)
-    block = jax.ShapeDtypeStruct((half // chunk, chunk * qheads, head_dim), jnp.float32)
-    near = [
-        call(
-            near_kernel, (block, block, block), (query, pack(keys), rest, near_bias), offset=offset, sizes=sizes
-        )
-        for query, offset in ((first, 0), (second, half))
-    ]
-
-    def parcel(count):
-        return (
-            jax.ShapeDtypeStruct((count, qheads + STAT_ROWS, head_dim), jnp.bfloat16),
-            jax.ShapeDtypeStruct((count, qheads, head_dim), jnp.float32),
-            jax.ShapeDtypeStruct((count, 8, head_dim), jnp.float32),
-        )
-
-    outs = parcel(half)
-    (send,) = call(
-        far_kernel, outs[:1], (second, far_keys, far_rest, far_bias, *near[1]), offset=half, sizes=sizes
-    )
-    keep, stats = call(
-        far_kernel, outs[1:], (first, far_keys, far_rest, far_bias, *near[0]), offset=0, sizes=sizes
-    )
+    part = min(CHUNK // 2, half)
+    block = jax.ShapeDtypeStruct((half // part, 2 * part * qheads, head_dim), jnp.float32)
+    near = call(
+        near_kernel, (block, block, block), (first, second, pack(keys), rest, near_bias), sizes=sizes
+    )
+
+    def parcels(count):
+        shape = (count, qheads + STAT_ROWS, head_dim)
+        return jax.ShapeDtypeStruct(shape, jnp.bfloat16), jax.ShapeDtypeStruct(shape, jnp.float32)
+
+    send, keep = call(
+        far_kernel, parcels(half), (first, second, far_keys, far_rest, far_bias, *near), sizes=sizes
+    )
+    cross = 1 if shared_bits and lax.axis_size("heads") % 2 == 0 else 0
+    turn = cross
     for bit in reversed(shared_bits):
-        arrived = exchange(send, bit, bit)
+        arrived = exchange(send, bit, bit, turn)
+        if turn:
+            keep = exchange(keep, 0, 0, turn)
         half //= 2
-        send, keep, stats = call(merge_kernel, parcel(half), (keep, stats, arrived), scale=scale)
-    arrived = exchange(send, 2, 1)
+        send, keep = call(merge_kernel, parcels(half), (arrived, keep), scale=scale)
+        turn = 0
+    arrived = exchange(send, 2, 1, cross)
+    if cross:
+        keep = exchange(keep, 0, 0, cross)
     return call(
-        last_kernel, jax.ShapeDtypeStruct(queries.shape, queries.dtype), (keep, stats, arrived),
-        scale=scale,
+        last_kernel, jax.ShapeDtypeStruct(queries.shape, queries.dtype), (arrived, keep), scale=scale
     )
 
 

time: 23.1 us -> 22.8 us (0.987)
  waiting for transfers between devices: 4.72 us -> 5.6 us
  Pallas kernels: 5.85 us -> 5.01 us
  starting transfers between devices: 12.2 us -> 11.8 us
    ppermute x6 -> x8, waiting for transfers between devices: 4.72 us -> 5.6 us  [exchange(): return lax.ppermute(value, ('blk', 'heads'), pairs)]
    pallas_call x7 -> x5, Pallas kernels: 3.81 us -> 2.97 us  [call(): pl.pallas_call(functools.partial(kernel, **static), out_shape=outs, in_sp...]
    ppermute x6 -> x8, starting transfers between devices: 12.2 us -> 11.8 us  [exchange(): return lax.ppermute(value, ('blk', 'heads'), pairs)]
  transfers between devices with their start and end apart: 6 -> 8, of which waited for: 4 -> 4; matrix products, arithmetic and copies ran while one was open for 0% -> 0% of each run, Pallas kernels for 15% -> 11%
where the time goes in v7:
time: 22.8 us; the launch traced here: 22.6 us
  starting transfers between devices  11.8 us (52%)
  waiting for transfers between devices  5.6 us (25%)
  Pallas kernels  5.01 us (22%)
    ppermute x8, starting transfers between devices, exchange(): return lax.ppermute(value, ('blk', 'heads'), pairs)  11.8 us
    ppermute x8, waiting for transfers between devices, exchange(): return lax.ppermute(value, ('blk', 'heads'), pairs)  5.6 us
    pallas_call x5, Pallas kernels, call(): pl.pallas_call(functools.partial(kernel, **static), out_shape=outs, in_sp...  2.97 us
    pallas_call x2, Pallas kernels, pack(): pl.pallas_call(pack_kernel, out_shape=jax.ShapeDtypeStruct((rows, sources...  2.04 us
  transfers between devices with their start and end apart: 8, of which 4 were waited for; matrix products, arithmetic and copies ran while one was open for 0% of the time, Pallas kernels for 11%

profile of v7, /device:TPU:0, one launch (start us, length us, event | category | flops | bytes accessed | tf_op | source)
XLA Modules:
  0.0 22.6 jit_solution(7019539161245187854)
XLA Ops:
  0.0 0.0 copy-start.5
  0.0 0.0 copy-start.4
  0.0 1.0 %shard_map.82.rest_ref = bf16[1408,128]{1,0:T(8,128)(2,1)S(1)} custom-call(bf16[1024,128]{1,0:T(8,128)(2,1)} %bitcast.8, bf16[384,128]{1,0:T(8,128)(2,1)} %bitcast.9), custom_call_target="tpu_custom_call" | custom-call | bytes 4194304 | tf_op jit(solution)/shard_map/pallas_call | solution.py:128
  1.0 3.0 %collective-permute-start.3 = (bf16[1408,128]{1,0:T(8,128)(2,1)S(1)}, bf16[1408,128]{1,0:T(8,128)(2,1)S(1)}, u32[]{:S(2)}, u32[]{:S(2)}) collective-permute-start(bf16[1408,128]{1,0:T(8,128)(2,1)S(1)} %shard_map.82.rest_ref), channel_id=1, source_target_pairs={{0,2},{1,5},{2,0},{3,7},{4,6},{5,1},{6,4},{7,3},{8,10},{9,13},{10,... | collective-permute-start | bytes 1081352 | tf_op jit(solution)/shard_map/ppermute | solution.py:25
  4.0 0.0 copy-done.5
  4.1 1.6 %collective-permute-start = (bf16[1,32,128]{2,1,0:T(8,128)(2,1)S(1)}, bf16[1,32,128]{2,1,0:T(8,128)(2,1)S(1)}, u32[]{:S(2)}, u32[]{:S(2)}) collective-permute-start(bf16[1,32,128]{2,1,0:T(8,128)(2,1)S(1)} %copy-done.5), channel_id=1, source_target_pairs={{0,4},{1,3},{2,6},{3,1},{4,0},{5,7},{6,2},{7,5},{8,12},{9,11},{10,... | collective-permute-start | bytes 24584 | tf_op jit(solution)/shard_map/ppermute | solution.py:25
  5.6 0.0 copy-done.4
  5.6 0.5 %collective-permute-start.2 = (bf16[1024,128]{1,0:T(8,128)(2,1)S(1)}, bf16[1024,128]{1,0:T(8,128)(2,1)S(1)}, u32[]{:S(2)}, u32[]{:S(2)}) collective-permute-start(bf16[1024,128]{1,0:T(8,128)(2,1)S(1)} %bitcast.7), channel_id=1, source_target_pairs={{0,2},{1,5},{2,0},{3,7},{4,6},{5,1},{6,4},{7,3},{8,10},{9,13},{10,... | collective-permute-start | bytes 786440 | tf_op jit(solution)/shard_map/ppermute | solution.py:25
  6.2 1.7 %collective-permute-done = bf16[1,32,128]{2,1,0:T(8,128)(2,1)S(1)} collective-permute-done((bf16[1,32,128]{2,1,0:T(8,128)(2,1)S(1)}, bf16[1,32,128]{2,1,0:T(8,128)(2,1)S(1)}, u32[]{:S(2)}, u32[]{:S(2)}) %collective-permute-start) | collective-permute-done | bytes 8224 | tf_op jit(solution)/shard_map/ppermute | solution.py:25
  7.9 2.6 %collective-permute-start.1 = (bf16[2,32,128]{2,1,0:T(8,128)(2,1)S(1)}, bf16[2,32,128]{2,1,0:T(8,128)(2,1)S(1)}, u32[]{:S(2)}, u32[]{:S(2)}) collective-permute-start(bf16[2,32,128]{2,1,0:T(8,128)(2,1)S(1)} %constant_dynamic-update-slice_fusion.first_ref), channel_id=1, source_target_pairs={{0,8},{1,9},{2,10},{3,11},{4,12},{5,13},{6,14},{7,15},{8,0},{9,1},... | collective-permute-start | bytes 49160 | tf_op jit(solution)/shard_map/ppermute | solution.py:25
  10.5 0.1 pad_add_fusion.place_ref
  10.5 0.0 copy-start
  10.5 0.0 copy-start.1
  10.5 0.0 copy-start.2
  10.5 0.0 copy-start.3
  10.5 1.0 %shard_map.84.key_ref = bf16[1024,128]{1,0:T(8,128)(2,1)S(1)} custom-call(bf16[1024,128]{1,0:T(8,128)(2,1)} %bitcast.6), custom_call_target="tpu_custom_call" | custom-call | bytes 4194304 | tf_op jit(solution)/shard_map/pallas_call | solution.py:128
  11.6 0.0 copy-done
  11.6 0.0 copy-done.1
  11.6 0.0 copy-done.2
  11.6 0.0 copy-done.3
  11.6 0.7 %shard_map.83 = (f32[4,192]{1,0:T(4,128)S(1)}, f32[4,192]{1,0:T(4,128)S(1)}) custom-call(s32[3]{0:T(128)S(1)} %pad_add_fusion.place_ref, s32[3,8]{1,0:T(4,128)S(1)} %copy-done, s32[3,8]{1,0:T(4,128)S(1)} %copy-done.1, s32[3]{0:T(128)S(1)} %copy-done.2, s32[8]{0:T(128)S(1)} %copy-done.3), custom_call_target="tpu_custom_call" | custom-call | tf_op jit(solution)/shard_map/pallas_call | solution.py:290
  12.3 0.2 collective-permute-done.1.second_ref
  12.5 0.6 %shard_map.85 = (f32[1,128,128]{2,1,0:T(8,128)S(1)}, f32[1,128,128]{2,1,0:T(8,128)S(1)}, f32[1,128,128]{2,1,0:T(8,128)S(1)}) custom-call(bf16[2,32,128]{2,1,0:T(8,128)(2,1)S(1)} %constant_dynamic-update-slice_fusion.first_ref, bf16[2,32,128]{2,1,0:T(8,128)(2,1)S(1)} %collective-permute-done.1.second_ref, bf16[1024,128]{1,0:T(8,128)(2,1)S(1)} %shard_map.84.key_ref, ...), custom_call_target="tpu_custom_call" | custom-call | tf_op jit(solution)/shard_map/pallas_call | solution.py:290
  13.1 0.0 collective-permute-done.2.key_ref
  13.2 0.0 collective-permute-done.3.rest_ref
  13.2 0.8 %shard_map.86 = (bf16[2,48,128]{2,1,0:T(8,128)(2,1)S(1)}, f32[2,48,128]{2,1,0:T(8,128)S(1)}) custom-call(bf16[2,32,128]{2,1,0:T(8,128)(2,1)S(1)} %constant_dynamic-update-slice_fusion.first_ref, bf16[2,32,128]{2,1,0:T(8,128)(2,1)S(1)} %collective-permute-done.1.second_ref, bf16[1024,128]{1,0:T(8,128)(2,1)S(1)} %collective-permute-done.2.key_ref, ...), custom_call_target="tpu_custom_call" | custom-call | tf_op jit(solution)/shard_map/pallas_call | solution.py:290
  14.0 0.1 collective-permute-start.5
  14.0 2.7 %collective-permute-start.4 = (bf16[2,48,128]{2,1,0:T(8,128)(2,1)S(1)}, bf16[2,48,128]{2,1,0:T(8,128)(2,1)S(1)}, u32[]{:S(2)}, u32[]{:S(2)}) collective-permute-start(bf16[2,48,128]{2,1,0:T(8,128)(2,1)S(1)} %get-tuple-element.19), channel_id=1, source_target_pairs={{0,9},{1,8},{2,11},{3,10},{4,13},{5,12},{6,15},{7,14},{8,1},{9,0},... | collective-permute-start | bytes 73736 | tf_op jit(solution)/shard_map/ppermute | solution.py:25
  16.7 1.5 %collective-permute-done.4.parcel_ref = bf16[2,48,128]{2,1,0:T(8,128)(2,1)S(1)} collective-permute-done((bf16[2,48,128]{2,1,0:T(8,128)(2,1)S(1)}, bf16[2,48,128]{2,1,0:T(8,128)(2,1)S(1)}, u32[]{:S(2)}, u32[]{:S(2)}) %collective-permute-start.4) | collective-permute-done | bytes 24608 | tf_op jit(solution)/shard_map/ppermute | solution.py:25
  18.2 0.0 collective-permute-done.5.keep_in
  18.3 0.1 shard_map.87
  18.4 0.4 %collective-permute-start.7 = (f32[1,48,128]{2,1,0:T(8,128)S(1)}, f32[1,48,128]{2,1,0:T(8,128)S(1)}, u32[]{:S(2)}, u32[]{:S(2)}) collective-permute-start(f32[1,48,128]{2,1,0:T(8,128)S(1)} %get-tuple-element.22), channel_id=1, source_target_pairs={{0,1},{1,0},{2,3},{3,2},{4,5},{5,4},{6,7},{7,6},{8,9},{9,8},{10,11... | collective-permute-start | bytes 73736 | tf_op jit(solution)/shard_map/ppermute | solution.py:25
  18.8 0.9 %collective-permute-start.6 = (bf16[1,48,128]{2,1,0:T(8,128)(2,1)S(1)}, bf16[1,48,128]{2,1,0:T(8,128)(2,1)S(1)}, u32[]{:S(2)}, u32[]{:S(2)}) collective-permute-start(bf16[1,48,128]{2,1,0:T(8,128)(2,1)S(1)} %get-tuple-element.21), channel_id=1, source_target_pairs={{0,3},{1,4},{2,1},{3,6},{4,7},{5,0},{6,5},{7,2},{8,11},{9,12},{10,... | collective-permute-start | bytes 36872 | tf_op jit(solution)/shard_map/ppermute | solution.py:25
  19.7 2.2 %collective-permute-done.6.parcel_ref = bf16[1,48,128]{2,1,0:T(8,128)(2,1)S(1)} collective-permute-done((bf16[1,48,128]{2,1,0:T(8,128)(2,1)S(1)}, bf16[1,48,128]{2,1,0:T(8,128)(2,1)S(1)}, u32[]{:S(2)}, u32[]{:S(2)}) %collective-permute-start.6) | collective-permute-done | bytes 12320 | tf_op jit(solution)/shard_map/ppermute | solution.py:25
  21.9 0.0 collective-permute-done.7.keep_in
  21.9 0.7 %shard_map.88 = bf16[1,32,128]{2,1,0:T(8,128)(2,1)} custom-call(bf16[1,48,128]{2,1,0:T(8,128)(2,1)S(1)} %collective-permute-done.6.parcel_ref, f32[1,48,128]{2,1,0:T(8,128)S(1)} %collective-permute-done.7.keep_in), custom_call_target="tpu_custom_call" | custom-call | tf_op jit(solution)/shard_map/pallas_call | solution.py:290
  (2 shorter events, 0.0 us)
Async XLA Ops:
  0.0 4.0 %copy-start.5 = (bf16[1,32,128]{2,1,0:T(8,128)(2,1)S(1)}, bf16[1,32,128]{2,1,0:T(8,128)(2,1)}, u32[]{:S(2)}) copy-start(bf16[1,32,128]{2,1,0:T(8,128)(2,1)} %param.8) | copy-start | bytes 24580
  0.0 5.6 %copy-start.4 = (bf16[256,4,128]{2,1,0:T(4,128)(2,1)S(1)}, bf16[256,4,128]{2,1,0:T(4,128)(2,1)}, u32[]{:S(2)}) copy-start(bf16[256,4,128]{2,1,0:T(4,128)(2,1)} %param.9) | copy-start | bytes 786436
  1.0 12.1 %collective-permute-start.3 = (bf16[1408,128]{1,0:T(8,128)(2,1)S(1)}, bf16[1408,128]{1,0:T(8,128)(2,1)S(1)}, u32[]{:S(2)}, u32[]{:S(2)}) collective-permute-start(bf16[1408,128]{1,0:T(8,128)(2,1)S(1)} %shard_map.82.rest_ref), channel_id=1, source_target_pairs={{0,2},{1,5},{2,0},{3,7},{4,6},{5,1},{6,4},{7,3},{8,10},{9,13},{10,... | collective-permute-start | bytes 1081352 | tf_op jit(solution)/shard_map/ppermute | solution.py:25
  4.1 3.8 %collective-permute-start = (bf16[1,32,128]{2,1,0:T(8,128)(2,1)S(1)}, bf16[1,32,128]{2,1,0:T(8,128)(2,1)S(1)}, u32[]{:S(2)}, u32[]{:S(2)}) collective-permute-start(bf16[1,32,128]{2,1,0:T(8,128)(2,1)S(1)} %copy-done.5), channel_id=1, source_target_pairs={{0,4},{1,3},{2,6},{3,1},{4,0},{5,7},{6,2},{7,5},{8,12},{9,11},{10,... | collective-permute-start | bytes 24584 | tf_op jit(solution)/shard_map/ppermute | solution.py:25
  5.6 7.5 %collective-permute-start.2 = (bf16[1024,128]{1,0:T(8,128)(2,1)S(1)}, bf16[1024,128]{1,0:T(8,128)(2,1)S(1)}, u32[]{:S(2)}, u32[]{:S(2)}) collective-permute-start(bf16[1024,128]{1,0:T(8,128)(2,1)S(1)} %bitcast.7), channel_id=1, source_target_pairs={{0,2},{1,5},{2,0},{3,7},{4,6},{5,1},{6,4},{7,3},{8,10},{9,13},{10,... | collective-permute-start | bytes 786440 | tf_op jit(solution)/shard_map/ppermute | solution.py:25
  7.9 4.6 %collective-permute-start.1 = (bf16[2,32,128]{2,1,0:T(8,128)(2,1)S(1)}, bf16[2,32,128]{2,1,0:T(8,128)(2,1)S(1)}, u32[]{:S(2)}, u32[]{:S(2)}) collective-permute-start(bf16[2,32,128]{2,1,0:T(8,128)(2,1)S(1)} %constant_dynamic-update-slice_fusion.first_ref), channel_id=1, source_target_pairs={{0,8},{1,9},{2,10},{3,11},{4,12},{5,13},{6,14},{7,15},{8,0},{9,1},... | collective-permute-start | bytes 49160 | tf_op jit(solution)/shard_map/ppermute | solution.py:25
  10.5 1.0 %copy-start = (s32[3,8]{1,0:T(4,128)S(1)}, s32[3,8]{1,0:T(4,128)}, u32[]{:S(2)}) copy-start(s32[3,8]{1,0:T(4,128)} %owner_ref.1) | copy-start | bytes 292
  10.5 1.0 %copy-start.1 = (s32[3,8]{1,0:T(4,128)S(1)}, s32[3,8]{1,0:T(4,128)}, u32[]{:S(2)}) copy-start(s32[3,8]{1,0:T(4,128)} %slot_ref.1) | copy-start | bytes 292
  10.5 1.0 %copy-start.2 = (s32[3]{0:T(128)S(1)}, s32[3]{0:T(128)}, u32[]{:S(2)}) copy-start(s32[3]{0:T(128)} %len_ref.1) | copy-start | bytes 40
  10.5 1.1 %copy-start.3 = (s32[8]{0:T(128)S(1)}, s32[8]{0:T(128)}, u32[]{:S(2)}) copy-start(s32[8]{0:T(128)} %request_ref.1) | copy-start | bytes 100
  14.0 4.3 %collective-permute-start.5 = (f32[2,48,128]{2,1,0:T(8,128)S(1)}, f32[2,48,128]{2,1,0:T(8,128)S(1)}, u32[]{:S(2)}, u32[]{:S(2)}) collective-permute-start(f32[2,48,128]{2,1,0:T(8,128)S(1)} %get-tuple-element.20), channel_id=1, source_target_pairs={{0,1},{1,0},{2,3},{3,2},{4,5},{5,4},{6,7},{7,6},{8,9},{9,8},{10,11... | collective-permute-start | bytes 147464 | tf_op jit(solution)/shard_map/ppermute | solution.py:25
  14.0 4.2 %collective-permute-start.4 = (bf16[2,48,128]{2,1,0:T(8,128)(2,1)S(1)}, bf16[2,48,128]{2,1,0:T(8,128)(2,1)S(1)}, u32[]{:S(2)}, u32[]{:S(2)}) collective-permute-start(bf16[2,48,128]{2,1,0:T(8,128)(2,1)S(1)} %get-tuple-element.19), channel_id=1, source_target_pairs={{0,9},{1,8},{2,11},{3,10},{4,13},{5,12},{6,15},{7,14},{8,1},{9,0},... | collective-permute-start | bytes 73736 | tf_op jit(solution)/shard_map/ppermute | solution.py:25
  18.4 3.6 %collective-permute-start.7 = (f32[1,48,128]{2,1,0:T(8,128)S(1)}, f32[1,48,128]{2,1,0:T(8,128)S(1)}, u32[]{:S(2)}, u32[]{:S(2)}) collective-permute-start(f32[1,48,128]{2,1,0:T(8,128)S(1)} %get-tuple-element.22), channel_id=1, source_target_pairs={{0,1},{1,0},{2,3},{3,2},{4,5},{5,4},{6,7},{7,6},{8,9},{9,8},{10,11... | collective-permute-start | bytes 73736 | tf_op jit(solution)/shard_map/ppermute | solution.py:25
  18.8 3.1 %collective-permute-start.6 = (bf16[1,48,128]{2,1,0:T(8,128)(2,1)S(1)}, bf16[1,48,128]{2,1,0:T(8,128)(2,1)S(1)}, u32[]{:S(2)}, u32[]{:S(2)}) collective-permute-start(bf16[1,48,128]{2,1,0:T(8,128)(2,1)S(1)} %get-tuple-element.21), channel_id=1, source_target_pairs={{0,3},{1,4},{2,1},{3,6},{4,7},{5,0},{6,5},{7,2},{8,11},{9,12},{10,... | collective-permute-start | bytes 36872 | tf_op jit(solution)/shard_map/ppermute | solution.py:25

commit v8 on v7

--- a/solution.py
+++ b/solution.py
@@ -339,7 +339,7 @@
 
     def parcels(count):
         shape = (count, qheads + STAT_ROWS, head_dim)
-        return jax.ShapeDtypeStruct(shape, jnp.bfloat16), jax.ShapeDtypeStruct(shape, jnp.float32)
+        return jax.ShapeDtypeStruct(shape, jnp.bfloat16), jax.ShapeDtypeStruct(shape, jnp.bfloat16)
 
     send, keep = call(
         far_kernel, parcels(half), (first, second, far_keys, far_rest, far_bias, *near), sizes=sizes

time: 22.8 us -> 22.3 us (0.978)
  waiting for transfers between devices: 5.6 us -> 4.52 us
  starting transfers between devices: 11.8 us -> 12.4 us
    ppermute x8, waiting for transfers between devices: 5.6 us -> 4.52 us  [exchange(): return lax.ppermute(value, ('blk', 'heads'), pairs)]
    ppermute x8, starting transfers between devices: 11.8 us -> 12.4 us  [exchange(): return lax.ppermute(value, ('blk', 'heads'), pairs)]
where the time goes in v8:
time: 22.3 us; the launch traced here: 22.1 us
  starting transfers between devices  12.4 us (56%)
  Pallas kernels  5.01 us (22%)
  waiting for transfers between devices  4.52 us (20%)
    ppermute x8, starting transfers between devices, exchange(): return lax.ppermute(value, ('blk', 'heads'), pairs)  12.4 us
    ppermute x8, waiting for transfers between devices, exchange(): return lax.ppermute(value, ('blk', 'heads'), pairs)  4.52 us
    pallas_call x5, Pallas kernels, call(): pl.pallas_call(functools.partial(kernel, **static), out_shape=outs, in_sp...  2.97 us
    pallas_call x2, Pallas kernels, pack(): pl.pallas_call(pack_kernel, out_shape=jax.ShapeDtypeStruct((rows, sources...  2.04 us
  transfers between devices with their start and end apart: 8, of which 4 were waited for; matrix products, arithmetic and copies ran while one was open for 0% of the time, Pallas kernels for 11%

profile of v8, /device:TPU:0, one launch (start us, length us, event | category | flops | bytes accessed | tf_op | source)
XLA Modules:
  0.0 22.1 jit_solution(15870397379576888695)
XLA Ops:
  0.0 0.0 copy-start.5
  0.0 0.0 copy-start.4
  0.0 1.0 %shard_map.82.rest_ref = bf16[1408,128]{1,0:T(8,128)(2,1)S(1)} custom-call(bf16[1024,128]{1,0:T(8,128)(2,1)} %bitcast.8, bf16[384,128]{1,0:T(8,128)(2,1)} %bitcast.9), custom_call_target="tpu_custom_call" | custom-call | bytes 4194304 | tf_op jit(solution)/shard_map/pallas_call | solution.py:128
  1.0 3.0 %collective-permute-start.3 = (bf16[1408,128]{1,0:T(8,128)(2,1)S(1)}, bf16[1408,128]{1,0:T(8,128)(2,1)S(1)}, u32[]{:S(2)}, u32[]{:S(2)}) collective-permute-start(bf16[1408,128]{1,0:T(8,128)(2,1)S(1)} %shard_map.82.rest_ref), channel_id=1, source_target_pairs={{0,2},{1,5},{2,0},{3,7},{4,6},{5,1},{6,4},{7,3},{8,10},{9,13},{10,... | collective-permute-start | bytes 1081352 | tf_op jit(solution)/shard_map/ppermute | solution.py:25
  4.0 0.0 copy-done.5
  4.1 1.6 %collective-permute-start = (bf16[1,32,128]{2,1,0:T(8,128)(2,1)S(1)}, bf16[1,32,128]{2,1,0:T(8,128)(2,1)S(1)}, u32[]{:S(2)}, u32[]{:S(2)}) collective-permute-start(bf16[1,32,128]{2,1,0:T(8,128)(2,1)S(1)} %copy-done.5), channel_id=1, source_target_pairs={{0,4},{1,3},{2,6},{3,1},{4,0},{5,7},{6,2},{7,5},{8,12},{9,11},{10,... | collective-permute-start | bytes 24584 | tf_op jit(solution)/shard_map/ppermute | solution.py:25
  5.6 0.0 copy-done.4
  5.6 0.5 %collective-permute-start.2 = (bf16[1024,128]{1,0:T(8,128)(2,1)S(1)}, bf16[1024,128]{1,0:T(8,128)(2,1)S(1)}, u32[]{:S(2)}, u32[]{:S(2)}) collective-permute-start(bf16[1024,128]{1,0:T(8,128)(2,1)S(1)} %bitcast.7), channel_id=1, source_target_pairs={{0,2},{1,5},{2,0},{3,7},{4,6},{5,1},{6,4},{7,3},{8,10},{9,13},{10,... | collective-permute-start | bytes 786440 | tf_op jit(solution)/shard_map/ppermute | solution.py:25
  6.2 1.7 %collective-permute-done = bf16[1,32,128]{2,1,0:T(8,128)(2,1)S(1)} collective-permute-done((bf16[1,32,128]{2,1,0:T(8,128)(2,1)S(1)}, bf16[1,32,128]{2,1,0:T(8,128)(2,1)S(1)}, u32[]{:S(2)}, u32[]{:S(2)}) %collective-permute-start) | collective-permute-done | bytes 8224 | tf_op jit(solution)/shard_map/ppermute | solution.py:25
  7.9 2.6 %collective-permute-start.1 = (bf16[2,32,128]{2,1,0:T(8,128)(2,1)S(1)}, bf16[2,32,128]{2,1,0:T(8,128)(2,1)S(1)}, u32[]{:S(2)}, u32[]{:S(2)}) collective-permute-start(bf16[2,32,128]{2,1,0:T(8,128)(2,1)S(1)} %constant_dynamic-update-slice_fusion.first_ref), channel_id=1, source_target_pairs={{0,8},{1,9},{2,10},{3,11},{4,12},{5,13},{6,14},{7,15},{8,0},{9,1},... | collective-permute-start | bytes 49160 | tf_op jit(solution)/shard_map/ppermute | solution.py:25
  10.5 0.1 pad_add_fusion.place_ref
  10.5 0.0 copy-start
  10.5 0.0 copy-start.1
  10.5 0.0 copy-start.2
  10.5 0.0 copy-start.3
  10.5 1.0 %shard_map.84.key_ref = bf16[1024,128]{1,0:T(8,128)(2,1)S(1)} custom-call(bf16[1024,128]{1,0:T(8,128)(2,1)} %bitcast.6), custom_call_target="tpu_custom_call" | custom-call | bytes 4194304 | tf_op jit(solution)/shard_map/pallas_call | solution.py:128
  11.6 0.0 copy-done
  11.6 0.0 copy-done.1
  11.6 0.0 copy-done.2
  11.6 0.0 copy-done.3
  11.6 0.7 %shard_map.83 = (f32[4,192]{1,0:T(4,128)S(1)}, f32[4,192]{1,0:T(4,128)S(1)}) custom-call(s32[3]{0:T(128)S(1)} %pad_add_fusion.place_ref, s32[3,8]{1,0:T(4,128)S(1)} %copy-done, s32[3,8]{1,0:T(4,128)S(1)} %copy-done.1, s32[3]{0:T(128)S(1)} %copy-done.2, s32[8]{0:T(128)S(1)} %copy-done.3), custom_call_target="tpu_custom_call" | custom-call | tf_op jit(solution)/shard_map/pallas_call | solution.py:290
  12.3 0.2 collective-permute-done.1.second_ref
  12.5 0.6 %shard_map.85 = (f32[1,128,128]{2,1,0:T(8,128)S(1)}, f32[1,128,128]{2,1,0:T(8,128)S(1)}, f32[1,128,128]{2,1,0:T(8,128)S(1)}) custom-call(bf16[2,32,128]{2,1,0:T(8,128)(2,1)S(1)} %constant_dynamic-update-slice_fusion.first_ref, bf16[2,32,128]{2,1,0:T(8,128)(2,1)S(1)} %collective-permute-done.1.second_ref, bf16[1024,128]{1,0:T(8,128)(2,1)S(1)} %shard_map.84.key_ref, ...), custom_call_target="tpu_custom_call" | custom-call | tf_op jit(solution)/shard_map/pallas_call | solution.py:290
  13.1 0.0 collective-permute-done.2.key_ref
  13.2 0.0 collective-permute-done.3.rest_ref
  13.2 0.8 %shard_map.86 = (bf16[2,48,128]{2,1,0:T(8,128)(2,1)S(1)}, bf16[2,48,128]{2,1,0:T(8,128)(2,1)S(1)}) custom-call(bf16[2,32,128]{2,1,0:T(8,128)(2,1)S(1)} %constant_dynamic-update-slice_fusion.first_ref, bf16[2,32,128]{2,1,0:T(8,128)(2,1)S(1)} %collective-permute-done.1.second_ref, bf16[1024,128]{1,0:T(8,128)(2,1)S(1)} %collective-permute-done.2.key_ref, ...), custom_call_target="tpu_custom_call" | custom-call | tf_op jit(solution)/shard_map/pallas_call | solution.py:290
  13.9 1.4 %collective-permute-start.4 = (bf16[2,48,128]{2,1,0:T(8,128)(2,1)S(1)}, bf16[2,48,128]{2,1,0:T(8,128)(2,1)S(1)}, u32[]{:S(2)}, u32[]{:S(2)}) collective-permute-start(bf16[2,48,128]{2,1,0:T(8,128)(2,1)S(1)} %get-tuple-element.19), channel_id=1, source_target_pairs={{0,9},{1,8},{2,11},{3,10},{4,13},{5,12},{6,15},{7,14},{8,1},{9,0},... | collective-permute-start | bytes 73736 | tf_op jit(solution)/shard_map/ppermute | solution.py:25
  15.3 1.4 %collective-permute-start.5 = (bf16[2,48,128]{2,1,0:T(8,128)(2,1)S(1)}, bf16[2,48,128]{2,1,0:T(8,128)(2,1)S(1)}, u32[]{:S(2)}, u32[]{:S(2)}) collective-permute-start(bf16[2,48,128]{2,1,0:T(8,128)(2,1)S(1)} %get-tuple-element.20), channel_id=1, source_target_pairs={{0,1},{1,0},{2,3},{3,2},{4,5},{5,4},{6,7},{7,6},{8,9},{9,8},{10,11... | collective-permute-start | bytes 73736 | tf_op jit(solution)/shard_map/ppermute | solution.py:25
  16.7 1.5 %collective-permute-done.4.parcel_ref = bf16[2,48,128]{2,1,0:T(8,128)(2,1)S(1)} collective-permute-done((bf16[2,48,128]{2,1,0:T(8,128)(2,1)S(1)}, bf16[2,48,128]{2,1,0:T(8,128)(2,1)S(1)}, u32[]{:S(2)}, u32[]{:S(2)}) %collective-permute-start.4) | collective-permute-done | bytes 24608 | tf_op jit(solution)/shard_map/ppermute | solution.py:25
  18.2 0.0 collective-permute-done.5.keep_in
  18.2 0.1 shard_map.87
  18.3 0.9 %collective-permute-start.6 = (bf16[1,48,128]{2,1,0:T(8,128)(2,1)S(1)}, bf16[1,48,128]{2,1,0:T(8,128)(2,1)S(1)}, u32[]{:S(2)}, u32[]{:S(2)}) collective-permute-start(bf16[1,48,128]{2,1,0:T(8,128)(2,1)S(1)} %get-tuple-element.21), channel_id=1, source_target_pairs={{0,3},{1,4},{2,1},{3,6},{4,7},{5,0},{6,5},{7,2},{8,11},{9,12},{10,... | collective-permute-start | bytes 36872 | tf_op jit(solution)/shard_map/ppermute | solution.py:25
  19.2 1.0 %collective-permute-start.7 = (bf16[1,48,128]{2,1,0:T(8,128)(2,1)S(1)}, bf16[1,48,128]{2,1,0:T(8,128)(2,1)S(1)}, u32[]{:S(2)}, u32[]{:S(2)}) collective-permute-start(bf16[1,48,128]{2,1,0:T(8,128)(2,1)S(1)} %get-tuple-element.22), channel_id=1, source_target_pairs={{0,1},{1,0},{2,3},{3,2},{4,5},{5,4},{6,7},{7,6},{8,9},{9,8},{10,11... | collective-permute-start | bytes 36872 | tf_op jit(solution)/shard_map/ppermute | solution.py:25
  20.2 1.2 %collective-permute-done.6.parcel_ref = bf16[1,48,128]{2,1,0:T(8,128)(2,1)S(1)} collective-permute-done((bf16[1,48,128]{2,1,0:T(8,128)(2,1)S(1)}, bf16[1,48,128]{2,1,0:T(8,128)(2,1)S(1)}, u32[]{:S(2)}, u32[]{:S(2)}) %collective-permute-start.6) | collective-permute-done | bytes 12320 | tf_op jit(solution)/shard_map/ppermute | solution.py:25
  21.4 0.0 collective-permute-done.7.keep_in
  21.4 0.7 %shard_map.88 = bf16[1,32,128]{2,1,0:T(8,128)(2,1)} custom-call(bf16[1,48,128]{2,1,0:T(8,128)(2,1)S(1)} %collective-permute-done.6.parcel_ref, bf16[1,48,128]{2,1,0:T(8,128)(2,1)S(1)} %collective-permute-done.7.keep_in), custom_call_target="tpu_custom_call" | custom-call | tf_op jit(solution)/shard_map/pallas_call | solution.py:290
  (2 shorter events, 0.0 us)
Async XLA Ops:
  0.0 4.0 %copy-start.5 = (bf16[1,32,128]{2,1,0:T(8,128)(2,1)S(1)}, bf16[1,32,128]{2,1,0:T(8,128)(2,1)}, u32[]{:S(2)}) copy-start(bf16[1,32,128]{2,1,0:T(8,128)(2,1)} %param.8) | copy-start | bytes 24580
  0.0 5.6 %copy-start.4 = (bf16[256,4,128]{2,1,0:T(4,128)(2,1)S(1)}, bf16[256,4,128]{2,1,0:T(4,128)(2,1)}, u32[]{:S(2)}) copy-start(bf16[256,4,128]{2,1,0:T(4,128)(2,1)} %param.9) | copy-start | bytes 786436
  1.0 12.1 %collective-permute-start.3 = (bf16[1408,128]{1,0:T(8,128)(2,1)S(1)}, bf16[1408,128]{1,0:T(8,128)(2,1)S(1)}, u32[]{:S(2)}, u32[]{:S(2)}) collective-permute-start(bf16[1408,128]{1,0:T(8,128)(2,1)S(1)} %shard_map.82.rest_ref), channel_id=1, source_target_pairs={{0,2},{1,5},{2,0},{3,7},{4,6},{5,1},{6,4},{7,3},{8,10},{9,13},{10,... | collective-permute-start | bytes 1081352 | tf_op jit(solution)/shard_map/ppermute | solution.py:25
  4.1 3.8 %collective-permute-start = (bf16[1,32,128]{2,1,0:T(8,128)(2,1)S(1)}, bf16[1,32,128]{2,1,0:T(8,128)(2,1)S(1)}, u32[]{:S(2)}, u32[]{:S(2)}) collective-permute-start(bf16[1,32,128]{2,1,0:T(8,128)(2,1)S(1)} %copy-done.5), channel_id=1, source_target_pairs={{0,4},{1,3},{2,6},{3,1},{4,0},{5,7},{6,2},{7,5},{8,12},{9,11},{10,... | collective-permute-start | bytes 24584 | tf_op jit(solution)/shard_map/ppermute | solution.py:25
  5.6 7.5 %collective-permute-start.2 = (bf16[1024,128]{1,0:T(8,128)(2,1)S(1)}, bf16[1024,128]{1,0:T(8,128)(2,1)S(1)}, u32[]{:S(2)}, u32[]{:S(2)}) collective-permute-start(bf16[1024,128]{1,0:T(8,128)(2,1)S(1)} %bitcast.7), channel_id=1, source_target_pairs={{0,2},{1,5},{2,0},{3,7},{4,6},{5,1},{6,4},{7,3},{8,10},{9,13},{10,... | collective-permute-start | bytes 786440 | tf_op jit(solution)/shard_map/ppermute | solution.py:25
  7.9 4.6 %collective-permute-start.1 = (bf16[2,32,128]{2,1,0:T(8,128)(2,1)S(1)}, bf16[2,32,128]{2,1,0:T(8,128)(2,1)S(1)}, u32[]{:S(2)}, u32[]{:S(2)}) collective-permute-start(bf16[2,32,128]{2,1,0:T(8,128)(2,1)S(1)} %constant_dynamic-update-slice_fusion.first_ref), channel_id=1, source_target_pairs={{0,8},{1,9},{2,10},{3,11},{4,12},{5,13},{6,14},{7,15},{8,0},{9,1},... | collective-permute-start | bytes 49160 | tf_op jit(solution)/shard_map/ppermute | solution.py:25
  10.5 1.0 %copy-start = (s32[3,8]{1,0:T(4,128)S(1)}, s32[3,8]{1,0:T(4,128)}, u32[]{:S(2)}) copy-start(s32[3,8]{1,0:T(4,128)} %owner_ref.1) | copy-start | bytes 292
  10.5 1.0 %copy-start.1 = (s32[3,8]{1,0:T(4,128)S(1)}, s32[3,8]{1,0:T(4,128)}, u32[]{:S(2)}) copy-start(s32[3,8]{1,0:T(4,128)} %slot_ref.1) | copy-start | bytes 292
  10.5 1.0 %copy-start.2 = (s32[3]{0:T(128)S(1)}, s32[3]{0:T(128)}, u32[]{:S(2)}) copy-start(s32[3]{0:T(128)} %len_ref.1) | copy-start | bytes 40
  10.5 1.1 %copy-start.3 = (s32[8]{0:T(128)S(1)}, s32[8]{0:T(128)}, u32[]{:S(2)}) copy-start(s32[8]{0:T(128)} %request_ref.1) | copy-start | bytes 100
  13.9 4.2 %collective-permute-start.4 = (bf16[2,48,128]{2,1,0:T(8,128)(2,1)S(1)}, bf16[2,48,128]{2,1,0:T(8,128)(2,1)S(1)}, u32[]{:S(2)}, u32[]{:S(2)}) collective-permute-start(bf16[2,48,128]{2,1,0:T(8,128)(2,1)S(1)} %get-tuple-element.19), channel_id=1, source_target_pairs={{0,9},{1,8},{2,11},{3,10},{4,13},{5,12},{6,15},{7,14},{8,1},{9,0},... | collective-permute-start | bytes 73736 | tf_op jit(solution)/shard_map/ppermute | solution.py:25
  15.3 2.9 %collective-permute-start.5 = (bf16[2,48,128]{2,1,0:T(8,128)(2,1)S(1)}, bf16[2,48,128]{2,1,0:T(8,128)(2,1)S(1)}, u32[]{:S(2)}, u32[]{:S(2)}) collective-permute-start(bf16[2,48,128]{2,1,0:T(8,128)(2,1)S(1)} %get-tuple-element.20), channel_id=1, source_target_pairs={{0,1},{1,0},{2,3},{3,2},{4,5},{5,4},{6,7},{7,6},{8,9},{9,8},{10,11... | collective-permute-start | bytes 73736 | tf_op jit(solution)/shard_map/ppermute | solution.py:25
  18.3 3.1 %collective-permute-start.6 = (bf16[1,48,128]{2,1,0:T(8,128)(2,1)S(1)}, bf16[1,48,128]{2,1,0:T(8,128)(2,1)S(1)}, u32[]{:S(2)}, u32[]{:S(2)}) collective-permute-start(bf16[1,48,128]{2,1,0:T(8,128)(2,1)S(1)} %get-tuple-element.21), channel_id=1, source_target_pairs={{0,3},{1,4},{2,1},{3,6},{4,7},{5,0},{6,5},{7,2},{8,11},{9,12},{10,... | collective-permute-start | bytes 36872 | tf_op jit(solution)/shard_map/ppermute | solution.py:25
  19.2 2.2 %collective-permute-start.7 = (bf16[1,48,128]{2,1,0:T(8,128)(2,1)S(1)}, bf16[1,48,128]{2,1,0:T(8,128)(2,1)S(1)}, u32[]{:S(2)}, u32[]{:S(2)}) collective-permute-start(bf16[1,48,128]{2,1,0:T(8,128)(2,1)S(1)} %get-tuple-element.22), channel_id=1, source_target_pairs={{0,1},{1,0},{2,3},{3,2},{4,5},{5,4},{6,7},{7,6},{8,9},{9,8},{10,11... | collective-permute-start | bytes 36872 | tf_op jit(solution)/shard_map/ppermute | solution.py:25

commit v9 on v8

--- a/solution.py
+++ b/solution.py
@@ -66,37 +66,40 @@
     )
 
 
-def attend(query, key_ref, rest_ref, bias, sizes):
-    kv_heads, group, prefix_rows, slots, page_rows, scale = sizes
+def attend(query, sides, sizes):
+    kv_heads, group, slots, page_rows, scale = sizes
     rows = query.shape[0]
     qheads = kv_heads * group
-    suffix_count = slots * page_rows
-    key = key_ref[...]
-    value = rest_ref[0:prefix_rows]
-    page_key = suffix_rows(rest_ref, prefix_rows, slots, page_rows)
-    page_value = suffix_rows(rest_ref, prefix_rows + page_rows, slots, page_rows)
-    contract = (((1,), (1,)), ((), ()))
-    near = lax.dot_general(query, key, contract, preferred_element_type=jnp.float32)
-    page = lax.dot_general(query, page_key, contract, preferred_element_type=jnp.float32)
 
     def own_head(width):
         row = lax.broadcasted_iota(jnp.int32, (rows, width), 0)
         column = lax.broadcasted_iota(jnp.int32, (rows, width), 1)
         return (row % qheads) // group == column % kv_heads
 
-    near = jnp.where(own_head(prefix_rows), near, -jnp.inf)
-    page = jnp.where(own_head(suffix_count), page, -jnp.inf) + bias
-    top = jnp.maximum(
-        jnp.max(near, axis=1, keepdims=True), jnp.max(page, axis=1, keepdims=True)
-    )
-    near = jnp.exp2((near - top) * scale)
-    page = jnp.exp2((page - top) * scale)
-    total = jnp.sum(near, axis=1, keepdims=True) + jnp.sum(page, axis=1, keepdims=True)
-    mixed = jnp.dot(near.astype(jnp.bfloat16), value, preferred_element_type=jnp.float32)
-    mixed = mixed + jnp.dot(
-        page.astype(jnp.bfloat16), page_value, preferred_element_type=jnp.float32
-    )
-    return top, total, mixed
+    def scores(key):
+        product = lax.dot_general(
+            query, key, (((1,), (1,)), ((), ())), preferred_element_type=jnp.float32
+        )
+        return jnp.where(own_head(key.shape[0]), product, -jnp.inf)
+
+    parts = []
+    for key_ref, rest_ref, bias in sides:
+        prefix_rows = key_ref.shape[0]
+        page_key = suffix_rows(rest_ref, prefix_rows, slots, page_rows)
+        page_value = suffix_rows(rest_ref, prefix_rows + page_rows, slots, page_rows)
+        parts.append((scores(key_ref[...]), rest_ref[0:prefix_rows]))
+        parts.append((scores(page_key) + bias, page_value))
+    top = functools.reduce(jnp.maximum, [jnp.max(score, axis=1, keepdims=True) for score, _ in parts])
+    high, low = split(top)
+    point = high + low
+    total = mixed = 0.0
+    for score, value in parts:
+        weight = jnp.exp2((score - point) * scale)
+        total = total + jnp.sum(weight, axis=1, keepdims=True)
+        mixed = mixed + jnp.dot(
+            weight.astype(jnp.bfloat16), value, preferred_element_type=jnp.float32
+        )
+    return point, total, mixed / total
 
 
 def chunk_bias(bias_ref, first, count, qheads):
@@ -143,11 +146,12 @@
     width = near_ref.shape[1]
     me, query_bit, key_bit = place_ref[0], place_ref[1], place_ref[2]
     all_rows = request_ref.shape[0]
+    half = row_total // rows_dev // 2
     column = lax.broadcasted_iota(jnp.int32, (1, width), 1)
 
     def one(i):
         place = i // rows_dev
-        device = me ^ jnp.where(place % 2 == 1, query_bit, 0) ^ ((place // 2) * 4)
+        device = me ^ jnp.where(place >= half, query_bit, 0) ^ ((place % half) * 4)
         row = device * rows_dev + i % rows_dev
         request = request_ref[row]
 
@@ -172,11 +176,15 @@
     loop(row_total, one)
 
 
-def chunks(first_ref, second_ref, bias_ref):
+def attend_kernel(
+    first_ref, second_ref, near_key_ref, near_rest_ref, near_bias_ref,
+    far_key_ref, far_rest_ref, far_bias_ref, send_ref, keep_ref, *, sizes,
+):
     half, qheads, head_dim = first_ref.shape
     part = min(CHUNK // 2, half)
-
-    def load(i):
+    diagonal = spread_rows(qheads, head_dim)
+
+    def one(i):
         query = jnp.concatenate(
             [
                 ref[pl.ds(i * part, part)].reshape(part * qheads, head_dim)
@@ -184,62 +192,30 @@
             ],
             axis=0,
         )
-        bias = jnp.concatenate(
-            [
-                chunk_bias(bias_ref, i * part, part, qheads),
-                chunk_bias(bias_ref, half + i * part, part, qheads),
-            ],
-            axis=0,
+
+        def bias(ref):
+            return jnp.concatenate(
+                [
+                    chunk_bias(ref, i * part, part, qheads),
+                    chunk_bias(ref, half + i * part, part, qheads),
+                ],
+                axis=0,
+            )
+
+        sides = (
+            (near_key_ref, near_rest_ref, bias(near_bias_ref)),
+            (far_key_ref, far_rest_ref, bias(far_bias_ref)),
         )
-        return query, bias
-
-    return part, half // part, load
-
-
-def near_kernel(
-    first_ref, second_ref, key_ref, rest_ref, bias_ref, mixed_ref, top_ref, total_ref, *, sizes
-):
-    _, steps, load = chunks(first_ref, second_ref, bias_ref)
-
-    def one(i):
-        query, bias = load(i)
-        top, total, mixed = attend(query, key_ref, rest_ref, bias, sizes)
-        mixed_ref[i] = mixed
-        top_ref[i] = jnp.broadcast_to(top, mixed.shape)
-        total_ref[i] = jnp.broadcast_to(total, mixed.shape)
-
-    loop(steps, one)
-
-
-def far_kernel(
-    first_ref, second_ref, key_ref, rest_ref, bias_ref, mixed_ref, top_ref, total_ref,
-    send_ref, keep_ref, *, sizes,
-):
-    _, qheads, head_dim = first_ref.shape
-    scale = sizes[-1]
-    part, steps, load = chunks(first_ref, second_ref, bias_ref)
-    diagonal = spread_rows(qheads, head_dim)
-
-    def one(i):
-        query, bias = load(i)
-        top, total, mixed = attend(query, key_ref, rest_ref, bias, sizes)
-        near_top = top_ref[i][:, :1]
-        high, low = split(jnp.maximum(near_top, top))
-        point = high + low
-        near_scale = jnp.exp2((near_top - point) * scale)
-        far_scale = jnp.exp2((top - point) * scale)
-        total = total_ref[i][:, :1] * near_scale + total * far_scale
-        mixed = (mixed_ref[i] * near_scale + mixed * far_scale) / total
+        point, total, mixed = attend(query, sides, sizes)
         for j in range(2 * part):
             rows = slice(j * qheads, (j + 1) * qheads)
-            place = i * part + j % part
             out_ref = keep_ref if j < part else send_ref
-            out_ref[place] = write(
+            out_ref[i * part + j % part] = write(
                 mixed[rows], to_row(point[rows], diagonal), to_row(total[rows], diagonal),
                 out_ref.dtype,
             )
 
-    loop(steps, one)
+    loop(half // part, one)
 
 
 def read(parcel):
@@ -307,7 +283,7 @@
     prefix_rows = prefix_keys.shape[0] * kv_heads
     page_rows = page_len * kv_heads
     scale = math.log2(math.e) / math.sqrt(head_dim)
-    sizes = (kv_heads, qheads // kv_heads, prefix_rows, slots, page_rows, scale)
+    sizes = (kv_heads, qheads // kv_heads, slots, page_rows, scale)
     shared_bits = [1 << b for b in range(2, blocks.bit_length() - 1)]
 
     keys = prefix_keys.reshape(prefix_rows, head_dim)
@@ -316,12 +292,11 @@
         suffix_pool.reshape(slots * 2 * page_rows, head_dim),
     )
     far_keys = exchange(keys, 1, 2)
+    far_rest = exchange(rest, 1, 2)
     first = queries
+    for bit in shared_bits:
+        first = jnp.concatenate([first, exchange(first, bit, bit)], axis=0)
     second = exchange(first, 2, 1)
-    far_rest = exchange(rest, 1, 2)
-    for bit in shared_bits:
-        first = jnp.concatenate([first, second], axis=0)
-        second = exchange(first, bit, bit)
     half = first.shape[0]
     rows = 2 * half
 
@@ -331,29 +306,24 @@
         bias_kernel, (table, table), (place, page_owner, page_slot, suffix_len, row_request), 5,
         rows_dev=rows_dev, page_len=page_len, kv_heads=kv_heads, blocks=blocks,
     )
-    part = min(CHUNK // 2, half)
-    block = jax.ShapeDtypeStruct((half // part, 2 * part * qheads, head_dim), jnp.float32)
-    near = call(
-        near_kernel, (block, block, block), (first, second, pack(keys), rest, near_bias), sizes=sizes
-    )
-
     def parcels(count):
         shape = (count, qheads + STAT_ROWS, head_dim)
         return jax.ShapeDtypeStruct(shape, jnp.bfloat16), jax.ShapeDtypeStruct(shape, jnp.bfloat16)
 
     send, keep = call(
-        far_kernel, parcels(half), (first, second, far_keys, far_rest, far_bias, *near), sizes=sizes
+        attend_kernel, parcels(half),
+        (first, second, keys, rest, near_bias, far_keys, far_rest, far_bias), sizes=sizes,
     )
     cross = 1 if shared_bits and lax.axis_size("heads") % 2 == 0 else 0
+    arrived = exchange(send, 1, 2, 1) if cross else exchange(send, 2, 1)
     turn = cross
     for bit in reversed(shared_bits):
-        arrived = exchange(send, bit, bit, turn)
         if turn:
             keep = exchange(keep, 0, 0, turn)
         half //= 2
         send, keep = call(merge_kernel, parcels(half), (arrived, keep), scale=scale)
-        turn = 0
-    arrived = exchange(send, 2, 1, cross)
+        turn = cross if bit == shared_bits[0] else 0
+        arrived = exchange(send, bit, bit, turn)
     if cross:
         keep = exchange(keep, 0, 0, cross)
     return call(

time: 22.3 us -> 22.4 us (level)
  waiting for transfers between devices: 4.52 us -> 6.34 us
  Pallas kernels: 5.01 us -> 3.44 us
  starting transfers between devices: 12.4 us -> 11.7 us
  local copies, waits for them, and re-layouts: 0.03 us -> 0.63 us
    ppermute x8, waiting for transfers between devices: 4.52 us -> 6.34 us  [exchange(): return lax.ppermute(value, ('blk', 'heads'), pairs)]
    pallas_call x2 -> x1, Pallas kernels: 2.04 us -> 1.03 us  [pack(): pl.pallas_call(pack_kernel, out_shape=jax.ShapeDtypeStruct((rows, sources...]
    ppermute x8, starting transfers between devices: 12.4 us -> 11.7 us  [exchange(): return lax.ppermute(value, ('blk', 'heads'), pairs)]
    unnamed x13, local copies, waits for them, and re-layouts: 0.02 us -> 0.62 us
    pallas_call x5 -> x4, Pallas kernels: 2.97 us -> 2.41 us  [call(): pl.pallas_call(functools.partial(kernel, **static), out_shape=outs, in_sp...]
  transfers between devices with their start and end apart: 8 -> 8, of which waited for: 4 -> 5; matrix products, arithmetic and copies ran while one was open for 0% -> 0% of each run, Pallas kernels for 11% -> 3%
where the time goes in v9:
time: 22.4 us; the launch traced here: 22.2 us
  starting transfers between devices  11.7 us (52%)
  waiting for transfers between devices  6.34 us (28%)
  Pallas kernels  3.44 us (15%)
  local copies, waits for them, and re-layouts  0.63 us (3%)
    ppermute x8, starting transfers between devices, exchange(): return lax.ppermute(value, ('blk', 'heads'), pairs)  11.7 us
    ppermute x8, waiting for transfers between devices, exchange(): return lax.ppermute(value, ('blk', 'heads'), pairs)  6.34 us
    pallas_call x4, Pallas kernels, call(): pl.pallas_call(functools.partial(kernel, **static), out_shape=outs, in_sp...  2.41 us
    pallas_call x1, Pallas kernels, pack(): pl.pallas_call(pack_kernel, out_shape=jax.ShapeDtypeStruct((rows, sources...  1.03 us
    unnamed x13, local copies, waits for them, and re-layouts  0.62 us
  transfers between devices with their start and end apart: 8, of which 5 were waited for; matrix products, arithmetic and copies ran while one was open for 0% of the time, Pallas kernels for 3%

profile of v9, /device:TPU:0, one launch (start us, length us, event | category | flops | bytes accessed | tf_op | source)
XLA Modules:
  0.0 22.2 jit_solution(11494181045192650589)
XLA Ops:
  0.0 0.0 copy-start.5
  0.0 0.0 copy-start
  0.0 1.0 %shard_map.82.near_rest_ref = bf16[1408,128]{1,0:T(8,128)(2,1)S(1)} custom-call(bf16[1024,128]{1,0:T(8,128)(2,1)} %bitcast.8, bf16[384,128]{1,0:T(8,128)(2,1)} %bitcast.9), custom_call_target="tpu_custom_call" | custom-call | bytes 4194304 | tf_op jit(solution)/shard_map/pallas_call | solution.py:131
  1.0 3.0 %collective-permute-start.3 = (bf16[1408,128]{1,0:T(8,128)(2,1)S(1)}, bf16[1408,128]{1,0:T(8,128)(2,1)S(1)}, u32[]{:S(2)}, u32[]{:S(2)}) collective-permute-start(bf16[1408,128]{1,0:T(8,128)(2,1)S(1)} %shard_map.82.near_rest_ref), channel_id=1, source_target_pairs={{0,2},{1,5},{2,0},{3,7},{4,6},{5,1},{6,4},{7,3},{8,10},{9,13},{10,... | collective-permute-start | bytes 1081352 | tf_op jit(solution)/shard_map/ppermute | solution.py:25
  4.0 0.0 copy-done.5
  4.1 2.6 %collective-permute-start = (bf16[1,32,128]{2,1,0:T(8,128)(2,1)S(1)}, bf16[1,32,128]{2,1,0:T(8,128)(2,1)S(1)}, u32[]{:S(2)}, u32[]{:S(2)}) collective-permute-start(bf16[1,32,128]{2,1,0:T(8,128)(2,1)S(1)} %copy-done.5), channel_id=1, source_target_pairs={{0,8},{1,9},{2,10},{3,11},{4,12},{5,13},{6,14},{7,15},{8,0},{9,1},... | collective-permute-start | bytes 24584 | tf_op jit(solution)/shard_map/ppermute | solution.py:25
  6.6 0.0 copy-done
  6.6 0.5 %collective-permute-start.2 = (bf16[1024,128]{1,0:T(8,128)(2,1)S(1)}, bf16[1024,128]{1,0:T(8,128)(2,1)S(1)}, u32[]{:S(2)}, u32[]{:S(2)}) collective-permute-start(bf16[1024,128]{1,0:T(8,128)(2,1)S(1)} %bitcast.6), channel_id=1, source_target_pairs={{0,2},{1,5},{2,0},{3,7},{4,6},{5,1},{6,4},{7,3},{8,10},{9,13},{10,... | collective-permute-start | bytes 786440 | tf_op jit(solution)/shard_map/ppermute | solution.py:25
  7.2 1.5 %collective-permute-done = bf16[1,32,128]{2,1,0:T(8,128)(2,1)S(1)} collective-permute-done((bf16[1,32,128]{2,1,0:T(8,128)(2,1)S(1)}, bf16[1,32,128]{2,1,0:T(8,128)(2,1)S(1)}, u32[]{:S(2)}, u32[]{:S(2)}) %collective-permute-start) | collective-permute-done | bytes 8224 | tf_op jit(solution)/shard_map/ppermute | solution.py:25
  8.7 1.6 %collective-permute-start.1 = (bf16[2,32,128]{2,1,0:T(8,128)(2,1)S(1)}, bf16[2,32,128]{2,1,0:T(8,128)(2,1)S(1)}, u32[]{:S(2)}, u32[]{:S(2)}) collective-permute-start(bf16[2,32,128]{2,1,0:T(8,128)(2,1)S(1)} %constant_dynamic-update-slice_fusion.first_ref), channel_id=1, source_target_pairs={{0,4},{1,3},{2,6},{3,1},{4,0},{5,7},{6,2},{7,5},{8,12},{9,11},{10,... | collective-permute-start | bytes 49160 | tf_op jit(solution)/shard_map/ppermute | solution.py:25
  10.3 0.0 copy-start.2
  10.3 0.0 copy-start.1
  10.3 0.0 copy-start.3
  10.3 0.0 copy-start.4
  10.3 0.1 pad_add_fusion.place_ref
  10.4 0.6 %copy-done.2 = s32[3,8]{1,0:T(4,128)S(1)} copy-done((s32[3,8]{1,0:T(4,128)S(1)}, s32[3,8]{1,0:T(4,128)}, u32[]{:S(2)}) %copy-start.2) | copy-done | bytes 120
  11.0 0.0 copy-done.1
  11.0 0.0 copy-done.3
  11.0 0.0 copy-done.4
  11.0 0.7 %shard_map.83 = (f32[4,192]{1,0:T(4,128)S(1)}, f32[4,192]{1,0:T(4,128)S(1)}) custom-call(s32[3]{0:T(128)S(1)} %pad_add_fusion.place_ref, s32[3,8]{1,0:T(4,128)S(1)} %copy-done.1, s32[3,8]{1,0:T(4,128)S(1)} %copy-done.2, s32[3]{0:T(128)S(1)} %copy-done.3, s32[8]{0:T(128)S(1)} %copy-done.4), custom_call_target="tpu_custom_call" | custom-call | tf_op jit(solution)/shard_map/pallas_call | solution.py:266
  11.8 0.7 %collective-permute-done.1.second_ref = bf16[2,32,128]{2,1,0:T(8,128)(2,1)S(1)} collective-permute-done((bf16[2,32,128]{2,1,0:T(8,128)(2,1)S(1)}, bf16[2,32,128]{2,1,0:T(8,128)(2,1)S(1)}, u32[]{:S(2)}, u32[]{:S(2)}) %collective-permute-start.1) | collective-permute-done | bytes 16416 | tf_op jit(solution)/shard_map/ppermute | solution.py:25
  12.5 0.7 %collective-permute-done.2.far_key_ref = bf16[1024,128]{1,0:T(8,128)(2,1)S(1)} collective-permute-done((bf16[1024,128]{1,0:T(8,128)(2,1)S(1)}, bf16[1024,128]{1,0:T(8,128)(2,1)S(1)}, u32[]{:S(2)}, u32[]{:S(2)}) %collective-permute-start.2) | collective-permute-done | bytes 262176 | tf_op jit(solution)/shard_map/ppermute | solution.py:25
  13.2 0.0 collective-permute-done.3.far_rest_ref
  13.2 0.9 %shard_map.84 = (bf16[2,48,128]{2,1,0:T(8,128)(2,1)S(1)}, bf16[2,48,128]{2,1,0:T(8,128)(2,1)S(1)}) custom-call(bf16[2,32,128]{2,1,0:T(8,128)(2,1)S(1)} %constant_dynamic-update-slice_fusion.first_ref, bf16[2,32,128]{2,1,0:T(8,128)(2,1)S(1)} %collective-permute-done.1.second_ref, bf16[1024,128]{1,0:T(8,128)(2,1)S(1)} %bitcast.7, ...), custom_call_target="tpu_custom_call" | custom-call | tf_op jit(solution)/shard_map/pallas_call | solution.py:266
  14.1 1.0 %collective-permute-start.4 = (bf16[2,48,128]{2,1,0:T(8,128)(2,1)S(1)}, bf16[2,48,128]{2,1,0:T(8,128)(2,1)S(1)}, u32[]{:S(2)}, u32[]{:S(2)}) collective-permute-start(bf16[2,48,128]{2,1,0:T(8,128)(2,1)S(1)} %get-tuple-element.13), channel_id=1, source_target_pairs={{0,5},{1,2},{2,7},{3,0},{4,1},{5,6},{6,3},{7,4},{8,13},{9,10},{10,... | collective-permute-start | bytes 73736 | tf_op jit(solution)/shard_map/ppermute | solution.py:25
  15.1 0.4 %collective-permute-start.5 = (bf16[2,48,128]{2,1,0:T(8,128)(2,1)S(1)}, bf16[2,48,128]{2,1,0:T(8,128)(2,1)S(1)}, u32[]{:S(2)}, u32[]{:S(2)}) collective-permute-start(bf16[2,48,128]{2,1,0:T(8,128)(2,1)S(1)} %get-tuple-element.14), channel_id=1, source_target_pairs={{0,1},{1,0},{2,3},{3,2},{4,5},{5,4},{6,7},{7,6},{8,9},{9,8},{10,11... | collective-permute-start | bytes 73736 | tf_op jit(solution)/shard_map/ppermute | solution.py:25
  15.5 1.9 %collective-permute-done.4.parcel_ref = bf16[2,48,128]{2,1,0:T(8,128)(2,1)S(1)} collective-permute-done((bf16[2,48,128]{2,1,0:T(8,128)(2,1)S(1)}, bf16[2,48,128]{2,1,0:T(8,128)(2,1)S(1)}, u32[]{:S(2)}, u32[]{:S(2)}) %collective-permute-start.4) | collective-permute-done | bytes 24608 | tf_op jit(solution)/shard_map/ppermute | solution.py:25
  17.4 0.0 collective-permute-done.5.keep_in
  17.4 0.1 shard_map.85
  17.5 2.1 %collective-permute-start.6 = (bf16[1,48,128]{2,1,0:T(8,128)(2,1)S(1)}, bf16[1,48,128]{2,1,0:T(8,128)(2,1)S(1)}, u32[]{:S(2)}, u32[]{:S(2)}) collective-permute-start(bf16[1,48,128]{2,1,0:T(8,128)(2,1)S(1)} %get-tuple-element.15), channel_id=1, source_target_pairs={{0,9},{1,8},{2,11},{3,10},{4,13},{5,12},{6,15},{7,14},{8,1},{9,0},... | collective-permute-start | bytes 36872 | tf_op jit(solution)/shard_map/ppermute | solution.py:25
  19.6 0.4 %collective-permute-start.7 = (bf16[1,48,128]{2,1,0:T(8,128)(2,1)S(1)}, bf16[1,48,128]{2,1,0:T(8,128)(2,1)S(1)}, u32[]{:S(2)}, u32[]{:S(2)}) collective-permute-start(bf16[1,48,128]{2,1,0:T(8,128)(2,1)S(1)} %get-tuple-element.16), channel_id=1, source_target_pairs={{0,1},{1,0},{2,3},{3,2},{4,5},{5,4},{6,7},{7,6},{8,9},{9,8},{10,11... | collective-permute-start | bytes 36872 | tf_op jit(solution)/shard_map/ppermute | solution.py:25
  20.0 1.5 %collective-permute-done.6.parcel_ref = bf16[1,48,128]{2,1,0:T(8,128)(2,1)S(1)} collective-permute-done((bf16[1,48,128]{2,1,0:T(8,128)(2,1)S(1)}, bf16[1,48,128]{2,1,0:T(8,128)(2,1)S(1)}, u32[]{:S(2)}, u32[]{:S(2)}) %collective-permute-start.6) | collective-permute-done | bytes 12320 | tf_op jit(solution)/shard_map/ppermute | solution.py:25
  21.5 0.0 collective-permute-done.7.keep_in
  21.5 0.7 %shard_map.86 = bf16[1,32,128]{2,1,0:T(8,128)(2,1)} custom-call(bf16[1,48,128]{2,1,0:T(8,128)(2,1)S(1)} %collective-permute-done.6.parcel_ref, bf16[1,48,128]{2,1,0:T(8,128)(2,1)S(1)} %collective-permute-done.7.keep_in), custom_call_target="tpu_custom_call" | custom-call | tf_op jit(solution)/shard_map/pallas_call | solution.py:266
  (2 shorter events, 0.0 us)
Async XLA Ops:
  0.0 4.0 %copy-start.5 = (bf16[1,32,128]{2,1,0:T(8,128)(2,1)S(1)}, bf16[1,32,128]{2,1,0:T(8,128)(2,1)}, u32[]{:S(2)}) copy-start(bf16[1,32,128]{2,1,0:T(8,128)(2,1)} %param.8) | copy-start | bytes 24580
  0.0 6.6 %copy-start = (bf16[256,4,128]{2,1,0:T(4,128)(2,1)S(1)}, bf16[256,4,128]{2,1,0:T(4,128)(2,1)}, u32[]{:S(2)}) copy-start(bf16[256,4,128]{2,1,0:T(4,128)(2,1)} %param.9) | copy-start | bytes 786436
  1.0 12.2 %collective-permute-start.3 = (bf16[1408,128]{1,0:T(8,128)(2,1)S(1)}, bf16[1408,128]{1,0:T(8,128)(2,1)S(1)}, u32[]{:S(2)}, u32[]{:S(2)}) collective-permute-start(bf16[1408,128]{1,0:T(8,128)(2,1)S(1)} %shard_map.82.near_rest_ref), channel_id=1, source_target_pairs={{0,2},{1,5},{2,0},{3,7},{4,6},{5,1},{6,4},{7,3},{8,10},{9,13},{10,... | collective-permute-start | bytes 1081352 | tf_op jit(solution)/shard_map/ppermute | solution.py:25
  4.1 4.7 %collective-permute-start = (bf16[1,32,128]{2,1,0:T(8,128)(2,1)S(1)}, bf16[1,32,128]{2,1,0:T(8,128)(2,1)S(1)}, u32[]{:S(2)}, u32[]{:S(2)}) collective-permute-start(bf16[1,32,128]{2,1,0:T(8,128)(2,1)S(1)} %copy-done.5), channel_id=1, source_target_pairs={{0,8},{1,9},{2,10},{3,11},{4,12},{5,13},{6,14},{7,15},{8,0},{9,1},... | collective-permute-start | bytes 24584 | tf_op jit(solution)/shard_map/ppermute | solution.py:25
  6.6 6.5 %collective-permute-start.2 = (bf16[1024,128]{1,0:T(8,128)(2,1)S(1)}, bf16[1024,128]{1,0:T(8,128)(2,1)S(1)}, u32[]{:S(2)}, u32[]{:S(2)}) collective-permute-start(bf16[1024,128]{1,0:T(8,128)(2,1)S(1)} %bitcast.6), channel_id=1, source_target_pairs={{0,2},{1,5},{2,0},{3,7},{4,6},{5,1},{6,4},{7,3},{8,10},{9,13},{10,... | collective-permute-start | bytes 786440 | tf_op jit(solution)/shard_map/ppermute | solution.py:25
  8.7 3.7 %collective-permute-start.1 = (bf16[2,32,128]{2,1,0:T(8,128)(2,1)S(1)}, bf16[2,32,128]{2,1,0:T(8,128)(2,1)S(1)}, u32[]{:S(2)}, u32[]{:S(2)}) collective-permute-start(bf16[2,32,128]{2,1,0:T(8,128)(2,1)S(1)} %constant_dynamic-update-slice_fusion.first_ref), channel_id=1, source_target_pairs={{0,4},{1,3},{2,6},{3,1},{4,0},{5,7},{6,2},{7,5},{8,12},{9,11},{10,... | collective-permute-start | bytes 49160 | tf_op jit(solution)/shard_map/ppermute | solution.py:25
  10.3 0.7 %copy-start.2 = (s32[3,8]{1,0:T(4,128)S(1)}, s32[3,8]{1,0:T(4,128)}, u32[]{:S(2)}) copy-start(s32[3,8]{1,0:T(4,128)} %slot_ref.1) | copy-start | bytes 292
  10.3 0.7 %copy-start.1 = (s32[3,8]{1,0:T(4,128)S(1)}, s32[3,8]{1,0:T(4,128)}, u32[]{:S(2)}) copy-start(s32[3,8]{1,0:T(4,128)} %owner_ref.1) | copy-start | bytes 292
  10.3 0.7 %copy-start.3 = (s32[3]{0:T(128)S(1)}, s32[3]{0:T(128)}, u32[]{:S(2)}) copy-start(s32[3]{0:T(128)} %len_ref.1) | copy-start | bytes 40
  10.3 0.7 %copy-start.4 = (s32[8]{0:T(128)S(1)}, s32[8]{0:T(128)}, u32[]{:S(2)}) copy-start(s32[8]{0:T(128)} %request_ref.1) | copy-start | bytes 100
  14.1 3.3 %collective-permute-start.4 = (bf16[2,48,128]{2,1,0:T(8,128)(2,1)S(1)}, bf16[2,48,128]{2,1,0:T(8,128)(2,1)S(1)}, u32[]{:S(2)}, u32[]{:S(2)}) collective-permute-start(bf16[2,48,128]{2,1,0:T(8,128)(2,1)S(1)} %get-tuple-element.13), channel_id=1, source_target_pairs={{0,5},{1,2},{2,7},{3,0},{4,1},{5,6},{6,3},{7,4},{8,13},{9,10},{10,... | collective-permute-start | bytes 73736 | tf_op jit(solution)/shard_map/ppermute | solution.py:25
  15.1 2.3 %collective-permute-start.5 = (bf16[2,48,128]{2,1,0:T(8,128)(2,1)S(1)}, bf16[2,48,128]{2,1,0:T(8,128)(2,1)S(1)}, u32[]{:S(2)}, u32[]{:S(2)}) collective-permute-start(bf16[2,48,128]{2,1,0:T(8,128)(2,1)S(1)} %get-tuple-element.14), channel_id=1, source_target_pairs={{0,1},{1,0},{2,3},{3,2},{4,5},{5,4},{6,7},{7,6},{8,9},{9,8},{10,11... | collective-permute-start | bytes 73736 | tf_op jit(solution)/shard_map/ppermute | solution.py:25
  17.5 4.0 %collective-permute-start.6 = (bf16[1,48,128]{2,1,0:T(8,128)(2,1)S(1)}, bf16[1,48,128]{2,1,0:T(8,128)(2,1)S(1)}, u32[]{:S(2)}, u32[]{:S(2)}) collective-permute-start(bf16[1,48,128]{2,1,0:T(8,128)(2,1)S(1)} %get-tuple-element.15), channel_id=1, source_target_pairs={{0,9},{1,8},{2,11},{3,10},{4,13},{5,12},{6,15},{7,14},{8,1},{9,0},... | collective-permute-start | bytes 36872 | tf_op jit(solution)/shard_map/ppermute | solution.py:25
  19.6 1.9 %collective-permute-start.7 = (bf16[1,48,128]{2,1,0:T(8,128)(2,1)S(1)}, bf16[1,48,128]{2,1,0:T(8,128)(2,1)S(1)}, u32[]{:S(2)}, u32[]{:S(2)}) collective-permute-start(bf16[1,48,128]{2,1,0:T(8,128)(2,1)S(1)} %get-tuple-element.16), channel_id=1, source_target_pairs={{0,1},{1,0},{2,3},{3,2},{4,5},{5,4},{6,7},{7,6},{8,9},{9,8},{10,11... | collective-permute-start | bytes 36872 | tf_op jit(solution)/shard_map/ppermute | solution.py:25

commit v10 on v9

--- a/solution.py
+++ b/solution.py
@@ -8,7 +8,7 @@
 from jax.experimental.pallas import tpu as pltpu
 from jax.sharding import PartitionSpec as P
 
-VMEM_BYTES = 40 * 1024 * 1024
+VMEM_BYTES = 32 * 1024 * 1024
 STAT_ROWS = 16
 CHUNK = 4
 PACK_BYTES = 4 * 1024 * 1024
@@ -83,23 +83,26 @@
         return jnp.where(own_head(key.shape[0]), product, -jnp.inf)
 
     parts = []
-    for key_ref, rest_ref, bias in sides:
-        prefix_rows = key_ref.shape[0]
-        page_key = suffix_rows(rest_ref, prefix_rows, slots, page_rows)
-        page_value = suffix_rows(rest_ref, prefix_rows + page_rows, slots, page_rows)
-        parts.append((scores(key_ref[...]), rest_ref[0:prefix_rows]))
+    for key_ref, bias, value_ref in sides:
+        prefix_rows = key_ref.shape[0] - 2 * slots * page_rows
+        page_key = suffix_rows(key_ref, prefix_rows, slots, page_rows)
+        page_value = suffix_rows(key_ref, prefix_rows + page_rows, slots, page_rows)
+        parts.append((scores(key_ref[0:prefix_rows]), value_ref))
         parts.append((scores(page_key) + bias, page_value))
     top = functools.reduce(jnp.maximum, [jnp.max(score, axis=1, keepdims=True) for score, _ in parts])
     high, low = split(top)
     point = high + low
     total = mixed = 0.0
+    late = None
     for score, value in parts:
         weight = jnp.exp2((score - point) * scale)
         total = total + jnp.sum(weight, axis=1, keepdims=True)
-        mixed = mixed + jnp.dot(
-            weight.astype(jnp.bfloat16), value, preferred_element_type=jnp.float32
-        )
-    return point, total, mixed / total
+        weight = weight.astype(jnp.bfloat16)
+        if value is None:
+            late = weight
+        else:
+            mixed = mixed + jnp.dot(weight, value[...], preferred_element_type=jnp.float32)
+    return point, total, mixed, late
 
 
 def chunk_bias(bias_ref, first, count, qheads):
@@ -176,13 +179,12 @@
     loop(row_total, one)
 
 
-def attend_kernel(
-    first_ref, second_ref, near_key_ref, near_rest_ref, near_bias_ref,
-    far_key_ref, far_rest_ref, far_bias_ref, send_ref, keep_ref, *, sizes,
+def weigh_kernel(
+    first_ref, second_ref, near_ref, near_value_ref, near_bias_ref, far_ref, far_bias_ref,
+    late_ref, mixed_ref, point_ref, total_ref, *, sizes,
 ):
     half, qheads, head_dim = first_ref.shape
     part = min(CHUNK // 2, half)
-    diagonal = spread_rows(qheads, head_dim)
 
     def one(i):
         query = jnp.concatenate(
@@ -203,19 +205,39 @@
             )
 
         sides = (
-            (near_key_ref, near_rest_ref, bias(near_bias_ref)),
-            (far_key_ref, far_rest_ref, bias(far_bias_ref)),
+            (near_ref, bias(near_bias_ref), near_value_ref),
+            (far_ref, bias(far_bias_ref), None),
         )
-        point, total, mixed = attend(query, sides, sizes)
+        point, total, mixed, late_ref[i] = attend(query, sides, sizes)
+        mixed_ref[i] = mixed
+        point_ref[i] = jnp.broadcast_to(point, mixed.shape)
+        total_ref[i] = jnp.broadcast_to(total, mixed.shape)
+
+    loop(half // part, one)
+
+
+def finish_kernel(late_ref, mixed_ref, point_ref, total_ref, far_value_ref, send_ref, keep_ref):
+    steps, rows, head_dim = mixed_ref.shape
+    qheads = send_ref.shape[1] - STAT_ROWS
+    part = rows // qheads // 2
+    diagonal = spread_rows(qheads, head_dim)
+
+    def one(i):
+        mixed = mixed_ref[i] + jnp.dot(
+            late_ref[i], far_value_ref[...], preferred_element_type=jnp.float32
+        )
+        mixed = mixed / total_ref[i]
         for j in range(2 * part):
             rows = slice(j * qheads, (j + 1) * qheads)
             out_ref = keep_ref if j < part else send_ref
             out_ref[i * part + j % part] = write(
-                mixed[rows], to_row(point[rows], diagonal), to_row(total[rows], diagonal),
+                mixed[rows],
+                to_row(point_ref[i, rows], diagonal),
+                to_row(total_ref[i, rows], diagonal),
                 out_ref.dtype,
             )
 
-    loop(half // part, one)
+    loop(steps, one)
 
 
 def read(parcel):
@@ -286,13 +308,13 @@
     sizes = (kv_heads, qheads // kv_heads, slots, page_rows, scale)
     shared_bits = [1 << b for b in range(2, blocks.bit_length() - 1)]
 
-    keys = prefix_keys.reshape(prefix_rows, head_dim)
-    rest = pack(
-        prefix_values.reshape(prefix_rows, head_dim),
+    values = prefix_values.reshape(prefix_rows, head_dim)
+    near = pack(
+        prefix_keys.reshape(prefix_rows, head_dim),
         suffix_pool.reshape(slots * 2 * page_rows, head_dim),
     )
-    far_keys = exchange(keys, 1, 2)
-    far_rest = exchange(rest, 1, 2)
+    far = exchange(near, 1, 2)
+    far_values = exchange(values, 1, 2)
     first = queries
     for bit in shared_bits:
         first = jnp.concatenate([first, exchange(first, bit, bit)], axis=0)
@@ -310,10 +332,15 @@
         shape = (count, qheads + STAT_ROWS, head_dim)
         return jax.ShapeDtypeStruct(shape, jnp.bfloat16), jax.ShapeDtypeStruct(shape, jnp.bfloat16)
 
-    send, keep = call(
-        attend_kernel, parcels(half),
-        (first, second, keys, rest, near_bias, far_keys, far_rest, far_bias), sizes=sizes,
-    )
+    part = min(CHUNK // 2, half)
+    shape = (half // part, 2 * part * qheads)
+    late = jax.ShapeDtypeStruct((*shape, prefix_rows), jnp.bfloat16)
+    block = jax.ShapeDtypeStruct((*shape, head_dim), jnp.float32)
+    weighed = call(
+        weigh_kernel, (late, block, block, block),
+        (first, second, near, values, near_bias, far, far_bias), sizes=sizes,
+    )
+    send, keep = call(finish_kernel, parcels(half), (*weighed, far_values))
     cross = 1 if shared_bits and lax.axis_size("heads") % 2 == 0 else 0
     arrived = exchange(send, 1, 2, 1) if cross else exchange(send, 2, 1)
     turn = cross

time: 22.4 us -> 21.8 us (0.973)
  waiting for transfers between devices: 6.34 us -> 5.02 us
  starting transfers between devices: 11.7 us -> 12.3 us
    ppermute x8, waiting for transfers between devices: 6.34 us -> 5.02 us  [exchange(): return lax.ppermute(value, ('blk', 'heads'), pairs)]
    ppermute x8, starting transfers between devices: 11.7 us -> 12.3 us  [exchange(): return lax.ppermute(value, ('blk', 'heads'), pairs)]
    pallas_call x4 -> x5, Pallas kernels: 2.41 us -> 2.56 us  [call(): pl.pallas_call(functools.partial(kernel, **static), out_shape=outs, in_sp...]
  transfers between devices with their start and end apart: 8 -> 8, of which waited for: 5 -> 4; matrix products, arithmetic and copies ran while one was open for 0% -> 0% of each run, Pallas kernels for 3% -> 7%
where the time goes in v10:
time: 21.8 us; the launch traced here: 21.6 us
  starting transfers between devices  12.3 us (56%)
  waiting for transfers between devices  5.02 us (23%)
  Pallas kernels  3.6 us (17%)
  local copies, waits for them, and re-layouts  0.63 us (3%)
    ppermute x8, starting transfers between devices, exchange(): return lax.ppermute(value, ('blk', 'heads'), pairs)  12.3 us
    ppermute x8, waiting for transfers between devices, exchange(): return lax.ppermute(value, ('blk', 'heads'), pairs)  5.02 us
    pallas_call x5, Pallas kernels, call(): pl.pallas_call(functools.partial(kernel, **static), out_shape=outs, in_sp...  2.56 us
    pallas_call x1, Pallas kernels, pack(): pl.pallas_call(pack_kernel, out_shape=jax.ShapeDtypeStruct((rows, sources...  1.03 us
    unnamed x13, local copies, waits for them, and re-layouts  0.62 us
  transfers between devices with their start and end apart: 8, of which 4 were waited for; matrix products, arithmetic and copies ran while one was open for 0% of the time, Pallas kernels for 7%

profile of v10, /device:TPU:0, one launch (start us, length us, event | category | flops | bytes accessed | tf_op | source)
XLA Modules:
  0.0 21.6 jit_solution(1892668998309085238)
XLA Ops:
  0.0 0.0 copy-start.5
  0.0 0.0 copy-start
  0.0 1.0 %shard_map.82.near_ref = bf16[1408,128]{1,0:T(8,128)(2,1)S(1)} custom-call(bf16[1024,128]{1,0:T(8,128)(2,1)} %bitcast.8, bf16[384,128]{1,0:T(8,128)(2,1)} %bitcast.9), custom_call_target="tpu_custom_call" | custom-call | bytes 4194304 | tf_op jit(solution)/shard_map/pallas_call | solution.py:134
  1.0 3.0 %collective-permute-start.2 = (bf16[1408,128]{1,0:T(8,128)(2,1)S(1)}, bf16[1408,128]{1,0:T(8,128)(2,1)S(1)}, u32[]{:S(2)}, u32[]{:S(2)}) collective-permute-start(bf16[1408,128]{1,0:T(8,128)(2,1)S(1)} %shard_map.82.near_ref), channel_id=1, source_target_pairs={{0,2},{1,5},{2,0},{3,7},{4,6},{5,1},{6,4},{7,3},{8,10},{9,13},{10,... | collective-permute-start | bytes 1081352 | tf_op jit(solution)/shard_map/ppermute | solution.py:25
  4.0 0.0 copy-done.5
  4.1 2.6 %collective-permute-start = (bf16[1,32,128]{2,1,0:T(8,128)(2,1)S(1)}, bf16[1,32,128]{2,1,0:T(8,128)(2,1)S(1)}, u32[]{:S(2)}, u32[]{:S(2)}) collective-permute-start(bf16[1,32,128]{2,1,0:T(8,128)(2,1)S(1)} %copy-done.5), channel_id=1, source_target_pairs={{0,8},{1,9},{2,10},{3,11},{4,12},{5,13},{6,14},{7,15},{8,0},{9,1},... | collective-permute-start | bytes 24584 | tf_op jit(solution)/shard_map/ppermute | solution.py:25
  6.6 0.0 copy-done
  6.6 0.5 %collective-permute-start.3 = (bf16[1024,128]{1,0:T(8,128)(2,1)S(1)}, bf16[1024,128]{1,0:T(8,128)(2,1)S(1)}, u32[]{:S(2)}, u32[]{:S(2)}) collective-permute-start(bf16[1024,128]{1,0:T(8,128)(2,1)S(1)} %bitcast.6), channel_id=1, source_target_pairs={{0,2},{1,5},{2,0},{3,7},{4,6},{5,1},{6,4},{7,3},{8,10},{9,13},{10,... | collective-permute-start | bytes 786440 | tf_op jit(solution)/shard_map/ppermute | solution.py:25
  7.2 1.5 %collective-permute-done = bf16[1,32,128]{2,1,0:T(8,128)(2,1)S(1)} collective-permute-done((bf16[1,32,128]{2,1,0:T(8,128)(2,1)S(1)}, bf16[1,32,128]{2,1,0:T(8,128)(2,1)S(1)}, u32[]{:S(2)}, u32[]{:S(2)}) %collective-permute-start) | collective-permute-done | bytes 8224 | tf_op jit(solution)/shard_map/ppermute | solution.py:25
  8.7 1.6 %collective-permute-start.1 = (bf16[2,32,128]{2,1,0:T(8,128)(2,1)S(1)}, bf16[2,32,128]{2,1,0:T(8,128)(2,1)S(1)}, u32[]{:S(2)}, u32[]{:S(2)}) collective-permute-start(bf16[2,32,128]{2,1,0:T(8,128)(2,1)S(1)} %constant_dynamic-update-slice_fusion.first_ref), channel_id=1, source_target_pairs={{0,4},{1,3},{2,6},{3,1},{4,0},{5,7},{6,2},{7,5},{8,12},{9,11},{10,... | collective-permute-start | bytes 49160 | tf_op jit(solution)/shard_map/ppermute | solution.py:25
  10.3 0.0 copy-start.2
  10.3 0.0 copy-start.1
  10.3 0.0 copy-start.3
  10.3 0.0 copy-start.4
  10.3 0.1 pad_add_fusion.place_ref
  10.4 0.6 %copy-done.2 = s32[3,8]{1,0:T(4,128)S(1)} copy-done((s32[3,8]{1,0:T(4,128)S(1)}, s32[3,8]{1,0:T(4,128)}, u32[]{:S(2)}) %copy-start.2) | copy-done | bytes 120
  11.0 0.0 copy-done.1
  11.0 0.0 copy-done.3
  11.0 0.0 copy-done.4
  11.0 0.7 %shard_map.83 = (f32[4,192]{1,0:T(4,128)S(1)}, f32[4,192]{1,0:T(4,128)S(1)}) custom-call(s32[3]{0:T(128)S(1)} %pad_add_fusion.place_ref, s32[3,8]{1,0:T(4,128)S(1)} %copy-done.1, s32[3,8]{1,0:T(4,128)S(1)} %copy-done.2, s32[3]{0:T(128)S(1)} %copy-done.3, s32[8]{0:T(128)S(1)} %copy-done.4), custom_call_target="tpu_custom_call" | custom-call | tf_op jit(solution)/shard_map/pallas_call | solution.py:288
  11.8 0.7 %collective-permute-done.1.second_ref = bf16[2,32,128]{2,1,0:T(8,128)(2,1)S(1)} collective-permute-done((bf16[2,32,128]{2,1,0:T(8,128)(2,1)S(1)}, bf16[2,32,128]{2,1,0:T(8,128)(2,1)S(1)}, u32[]{:S(2)}, u32[]{:S(2)}) %collective-permute-start.1) | collective-permute-done | bytes 16416 | tf_op jit(solution)/shard_map/ppermute | solution.py:25
  12.5 0.0 collective-permute-done.2.far_ref
  12.5 0.8 %shard_map.84 = (bf16[1,128,1024]{2,1,0:T(8,128)(2,1)S(1)}, f32[1,128,128]{2,1,0:T(8,128)S(1)}, f32[1,128,128]{2,1,0:T(8,128)S(1)}, f32[1,128,128]{2,1,0:T(8,128)S(1)}) custom-call(bf16[2,32,128]{2,1,0:T(8,128)(2,1)S(1)} %constant_dynamic-update-slice_fusion.first_ref, bf16[2,32,128]{2,1,0:T(8,128)(2,1)S(1)} %collective-permute-done.1.second_ref, ...), custom_call_target="tpu_custom_call" | custom-call | tf_op jit(solution)/shard_map/pallas_call | solution.py:288
  13.3 0.0 collective-permute-done.3.far_value_ref
  13.3 0.2 %shard_map.85 = (bf16[2,48,128]{2,1,0:T(8,128)(2,1)S(1)}, bf16[2,48,128]{2,1,0:T(8,128)(2,1)S(1)}) custom-call(bf16[1,128,1024]{2,1,0:T(8,128)(2,1)S(1)} %get-tuple-element.17.late_ref, f32[1,128,128]{2,1,0:T(8,128)S(1)} %get-tuple-element.18.mixed_ref, f32[1,128,128]{2,1,0:T(8,128)S(1)} %get-tuple-element.19.point_ref, ...), custom_call_target="tpu_custom_call" | custom-call | tf_op jit(solution)/shard_map/pallas_call | solution.py:288
  13.5 1.8 %collective-permute-start.4 = (bf16[2,48,128]{2,1,0:T(8,128)(2,1)S(1)}, bf16[2,48,128]{2,1,0:T(8,128)(2,1)S(1)}, u32[]{:S(2)}, u32[]{:S(2)}) collective-permute-start(bf16[2,48,128]{2,1,0:T(8,128)(2,1)S(1)} %get-tuple-element.21), channel_id=1, source_target_pairs={{0,5},{1,2},{2,7},{3,0},{4,1},{5,6},{6,3},{7,4},{8,13},{9,10},{10,... | collective-permute-start | bytes 73736 | tf_op jit(solution)/shard_map/ppermute | solution.py:25
  15.3 0.0 collective-permute-start.5
  15.3 1.5 %collective-permute-done.4.parcel_ref = bf16[2,48,128]{2,1,0:T(8,128)(2,1)S(1)} collective-permute-done((bf16[2,48,128]{2,1,0:T(8,128)(2,1)S(1)}, bf16[2,48,128]{2,1,0:T(8,128)(2,1)S(1)}, u32[]{:S(2)}, u32[]{:S(2)}) %collective-permute-start.4) | collective-permute-done | bytes 24608 | tf_op jit(solution)/shard_map/ppermute | solution.py:25
  16.8 0.0 collective-permute-done.5.keep_in
  16.8 0.1 shard_map.86
  16.9 2.4 %collective-permute-start.6 = (bf16[1,48,128]{2,1,0:T(8,128)(2,1)S(1)}, bf16[1,48,128]{2,1,0:T(8,128)(2,1)S(1)}, u32[]{:S(2)}, u32[]{:S(2)}) collective-permute-start(bf16[1,48,128]{2,1,0:T(8,128)(2,1)S(1)} %get-tuple-element.23), channel_id=1, source_target_pairs={{0,9},{1,8},{2,11},{3,10},{4,13},{5,12},{6,15},{7,14},{8,1},{9,0},... | collective-permute-start | bytes 36872 | tf_op jit(solution)/shard_map/ppermute | solution.py:25
  19.3 0.4 %collective-permute-start.7 = (bf16[1,48,128]{2,1,0:T(8,128)(2,1)S(1)}, bf16[1,48,128]{2,1,0:T(8,128)(2,1)S(1)}, u32[]{:S(2)}, u32[]{:S(2)}) collective-permute-start(bf16[1,48,128]{2,1,0:T(8,128)(2,1)S(1)} %get-tuple-element.24), channel_id=1, source_target_pairs={{0,1},{1,0},{2,3},{3,2},{4,5},{5,4},{6,7},{7,6},{8,9},{9,8},{10,11... | collective-permute-start | bytes 36872 | tf_op jit(solution)/shard_map/ppermute | solution.py:25
  19.7 1.3 %collective-permute-done.6.parcel_ref = bf16[1,48,128]{2,1,0:T(8,128)(2,1)S(1)} collective-permute-done((bf16[1,48,128]{2,1,0:T(8,128)(2,1)S(1)}, bf16[1,48,128]{2,1,0:T(8,128)(2,1)S(1)}, u32[]{:S(2)}, u32[]{:S(2)}) %collective-permute-start.6) | collective-permute-done | bytes 12320 | tf_op jit(solution)/shard_map/ppermute | solution.py:25
  20.9 0.0 collective-permute-done.7.keep_in
  20.9 0.7 %shard_map.87 = bf16[1,32,128]{2,1,0:T(8,128)(2,1)} custom-call(bf16[1,48,128]{2,1,0:T(8,128)(2,1)S(1)} %collective-permute-done.6.parcel_ref, bf16[1,48,128]{2,1,0:T(8,128)(2,1)S(1)} %collective-permute-done.7.keep_in), custom_call_target="tpu_custom_call" | custom-call | tf_op jit(solution)/shard_map/pallas_call | solution.py:288
  (2 shorter events, 0.0 us)
Async XLA Ops:
  0.0 4.0 %copy-start.5 = (bf16[1,32,128]{2,1,0:T(8,128)(2,1)S(1)}, bf16[1,32,128]{2,1,0:T(8,128)(2,1)}, u32[]{:S(2)}) copy-start(bf16[1,32,128]{2,1,0:T(8,128)(2,1)} %param.8) | copy-start | bytes 24580
  0.0 6.6 %copy-start = (bf16[256,4,128]{2,1,0:T(4,128)(2,1)S(1)}, bf16[256,4,128]{2,1,0:T(4,128)(2,1)}, u32[]{:S(2)}) copy-start(bf16[256,4,128]{2,1,0:T(4,128)(2,1)} %param.10) | copy-start | bytes 786436
  1.0 11.4 %collective-permute-start.2 = (bf16[1408,128]{1,0:T(8,128)(2,1)S(1)}, bf16[1408,128]{1,0:T(8,128)(2,1)S(1)}, u32[]{:S(2)}, u32[]{:S(2)}) collective-permute-start(bf16[1408,128]{1,0:T(8,128)(2,1)S(1)} %shard_map.82.near_ref), channel_id=1, source_target_pairs={{0,2},{1,5},{2,0},{3,7},{4,6},{5,1},{6,4},{7,3},{8,10},{9,13},{10,... | collective-permute-start | bytes 1081352 | tf_op jit(solution)/shard_map/ppermute | solution.py:25
  4.1 4.7 %collective-permute-start = (bf16[1,32,128]{2,1,0:T(8,128)(2,1)S(1)}, bf16[1,32,128]{2,1,0:T(8,128)(2,1)S(1)}, u32[]{:S(2)}, u32[]{:S(2)}) collective-permute-start(bf16[1,32,128]{2,1,0:T(8,128)(2,1)S(1)} %copy-done.5), channel_id=1, source_target_pairs={{0,8},{1,9},{2,10},{3,11},{4,12},{5,13},{6,14},{7,15},{8,0},{9,1},... | collective-permute-start | bytes 24584 | tf_op jit(solution)/shard_map/ppermute | solution.py:25
  6.6 6.6 %collective-permute-start.3 = (bf16[1024,128]{1,0:T(8,128)(2,1)S(1)}, bf16[1024,128]{1,0:T(8,128)(2,1)S(1)}, u32[]{:S(2)}, u32[]{:S(2)}) collective-permute-start(bf16[1024,128]{1,0:T(8,128)(2,1)S(1)} %bitcast.6), channel_id=1, source_target_pairs={{0,2},{1,5},{2,0},{3,7},{4,6},{5,1},{6,4},{7,3},{8,10},{9,13},{10,... | collective-permute-start | bytes 786440 | tf_op jit(solution)/shard_map/ppermute | solution.py:25
  8.7 3.7 %collective-permute-start.1 = (bf16[2,32,128]{2,1,0:T(8,128)(2,1)S(1)}, bf16[2,32,128]{2,1,0:T(8,128)(2,1)S(1)}, u32[]{:S(2)}, u32[]{:S(2)}) collective-permute-start(bf16[2,32,128]{2,1,0:T(8,128)(2,1)S(1)} %constant_dynamic-update-slice_fusion.first_ref), channel_id=1, source_target_pairs={{0,4},{1,3},{2,6},{3,1},{4,0},{5,7},{6,2},{7,5},{8,12},{9,11},{10,... | collective-permute-start | bytes 49160 | tf_op jit(solution)/shard_map/ppermute | solution.py:25
  10.3 0.7 %copy-start.2 = (s32[3,8]{1,0:T(4,128)S(1)}, s32[3,8]{1,0:T(4,128)}, u32[]{:S(2)}) copy-start(s32[3,8]{1,0:T(4,128)} %slot_ref.1) | copy-start | bytes 292
  10.3 0.7 %copy-start.1 = (s32[3,8]{1,0:T(4,128)S(1)}, s32[3,8]{1,0:T(4,128)}, u32[]{:S(2)}) copy-start(s32[3,8]{1,0:T(4,128)} %owner_ref.1) | copy-start | bytes 292
  10.3 0.7 %copy-start.3 = (s32[3]{0:T(128)S(1)}, s32[3]{0:T(128)}, u32[]{:S(2)}) copy-start(s32[3]{0:T(128)} %len_ref.1) | copy-start | bytes 40
  10.3 0.7 %copy-start.4 = (s32[8]{0:T(128)S(1)}, s32[8]{0:T(128)}, u32[]{:S(2)}) copy-start(s32[8]{0:T(128)} %request_ref.1) | copy-start | bytes 100
  13.5 3.3 %collective-permute-start.4 = (bf16[2,48,128]{2,1,0:T(8,128)(2,1)S(1)}, bf16[2,48,128]{2,1,0:T(8,128)(2,1)S(1)}, u32[]{:S(2)}, u32[]{:S(2)}) collective-permute-start(bf16[2,48,128]{2,1,0:T(8,128)(2,1)S(1)} %get-tuple-element.21), channel_id=1, source_target_pairs={{0,5},{1,2},{2,7},{3,0},{4,1},{5,6},{6,3},{7,4},{8,13},{9,10},{10,... | collective-permute-start | bytes 73736 | tf_op jit(solution)/shard_map/ppermute | solution.py:25
  15.3 1.5 %collective-permute-start.5 = (bf16[2,48,128]{2,1,0:T(8,128)(2,1)S(1)}, bf16[2,48,128]{2,1,0:T(8,128)(2,1)S(1)}, u32[]{:S(2)}, u32[]{:S(2)}) collective-permute-start(bf16[2,48,128]{2,1,0:T(8,128)(2,1)S(1)} %get-tuple-element.22), channel_id=1, source_target_pairs={{0,1},{1,0},{2,3},{3,2},{4,5},{5,4},{6,7},{7,6},{8,9},{9,8},{10,11... | collective-permute-start | bytes 73736 | tf_op jit(solution)/shard_map/ppermute | solution.py:25
  16.9 4.0 %collective-permute-start.6 = (bf16[1,48,128]{2,1,0:T(8,128)(2,1)S(1)}, bf16[1,48,128]{2,1,0:T(8,128)(2,1)S(1)}, u32[]{:S(2)}, u32[]{:S(2)}) collective-permute-start(bf16[1,48,128]{2,1,0:T(8,128)(2,1)S(1)} %get-tuple-element.23), channel_id=1, source_target_pairs={{0,9},{1,8},{2,11},{3,10},{4,13},{5,12},{6,15},{7,14},{8,1},{9,0},... | collective-permute-start | bytes 36872 | tf_op jit(solution)/shard_map/ppermute | solution.py:25
  19.3 1.7 %collective-permute-start.7 = (bf16[1,48,128]{2,1,0:T(8,128)(2,1)S(1)}, bf16[1,48,128]{2,1,0:T(8,128)(2,1)S(1)}, u32[]{:S(2)}, u32[]{:S(2)}) collective-permute-start(bf16[1,48,128]{2,1,0:T(8,128)(2,1)S(1)} %get-tuple-element.24), channel_id=1, source_target_pairs={{0,1},{1,0},{2,3},{3,2},{4,5},{5,4},{6,7},{7,6},{8,9},{9,8},{10,11... | collective-permute-start | bytes 36872 | tf_op jit(solution)/shard_map/ppermute | solution.py:25

commit v11 on v10

--- a/solution.py
+++ b/solution.py
@@ -10,8 +10,6 @@
 
 VMEM_BYTES = 32 * 1024 * 1024
 STAT_ROWS = 16
-CHUNK = 4
-PACK_BYTES = 4 * 1024 * 1024
 
 
 def exchange(value, even_bit, odd_bit, turn=0):
@@ -83,11 +81,10 @@
         return jnp.where(own_head(key.shape[0]), product, -jnp.inf)
 
     parts = []
-    for key_ref, bias, value_ref in sides:
-        prefix_rows = key_ref.shape[0] - 2 * slots * page_rows
-        page_key = suffix_rows(key_ref, prefix_rows, slots, page_rows)
-        page_value = suffix_rows(key_ref, prefix_rows + page_rows, slots, page_rows)
-        parts.append((scores(key_ref[0:prefix_rows]), value_ref))
+    for key_ref, pool_ref, bias, value_ref in sides:
+        page_key = suffix_rows(pool_ref, 0, slots, page_rows)
+        page_value = suffix_rows(pool_ref, page_rows, slots, page_rows)
+        parts.append((scores(key_ref[...]), value_ref))
         parts.append((scores(page_key) + bias, page_value))
     top = functools.reduce(jnp.maximum, [jnp.max(score, axis=1, keepdims=True) for score, _ in parts])
     high, low = split(top)
@@ -115,46 +112,35 @@
     )
 
 
-def pack_kernel(*refs):
-    *sources, rest_ref, sems = refs
-    start = 0
-    copies = []
-    for i, source in enumerate(sources):
-        rows = source.shape[0]
-        copies.append(pltpu.make_async_copy(source, rest_ref.at[start : start + rows], sems.at[i]))
-        start += rows
+def fetch_kernel(
+    queries_ref, owner_hbm, slot_hbm, len_hbm, request_hbm, *refs, rows_dev, page_len, kv_heads, sources
+):
+    del queries_ref
+    goals = refs[sources : 2 * sources]
+    near_ref, far_ref, owner_ref, slot_ref, len_ref, request_ref, sems = refs[2 * sources :]
+    pairs = [
+        (owner_hbm, owner_ref),
+        (slot_hbm, slot_ref),
+        (len_hbm, len_ref),
+        (request_hbm, request_ref),
+        *zip(refs[:sources], goals),
+    ]
+    copies = [pltpu.make_async_copy(*pair, sems.at[i]) for i, pair in enumerate(pairs)]
     for copy in copies:
         copy.start()
-    for copy in copies:
+    for copy in copies[:4]:
         copy.wait()
-
-
-def pack(*sources):
-    rows = sum(source.shape[0] for source in sources)
-    return pl.pallas_call(
-        pack_kernel,
-        out_shape=jax.ShapeDtypeStruct((rows, sources[0].shape[1]), sources[0].dtype),
-        in_specs=[pl.BlockSpec(memory_space=pltpu.HBM)] * len(sources),
-        out_specs=pl.BlockSpec(memory_space=pltpu.VMEM),
-        scratch_shapes=[pltpu.SemaphoreType.DMA((len(sources),))],
-        compiler_params=pltpu.CompilerParams(vmem_limit_bytes=VMEM_BYTES),
-        cost_estimate=pl.CostEstimate(flops=0, bytes_accessed=PACK_BYTES, transcendentals=0),
-    )(*(pltpu.with_memory_space_constraint(source, pltpu.HBM) for source in sources))
-
-
-def bias_kernel(
-    place_ref, owner_ref, slot_ref, len_ref, request_ref, near_ref, far_ref, *, rows_dev, page_len, kv_heads, blocks
-):
-    row_total = near_ref.shape[0]
+    blocks = lax.axis_size("blk")
+    me = lax.axis_index("blk")
+    odd_core = lax.axis_index("heads") % 2
+    query_bit, key_bit = 2 - odd_core, 1 + odd_core
     width = near_ref.shape[1]
-    me, query_bit, key_bit = place_ref[0], place_ref[1], place_ref[2]
     all_rows = request_ref.shape[0]
-    half = row_total // rows_dev // 2
     column = lax.broadcasted_iota(jnp.int32, (1, width), 1)
 
     def one(i):
         place = i // rows_dev
-        device = me ^ jnp.where(place >= half, query_bit, 0) ^ ((place % half) * 4)
+        device = me ^ jnp.where(place % 2 == 1, query_bit, 0) ^ ((place // 2) * 4)
         row = device * rows_dev + i % rows_dev
         request = request_ref[row]
 
@@ -176,15 +162,65 @@
                 (column >= first) & (column < first + shown), 0.0, -jnp.inf
             )
 
-    loop(row_total, one)
+    loop(near_ref.shape[0], one)
+    for copy in copies[4:]:
+        copy.wait()
+
+
+def attend(query, sides, sizes):
+    kv_heads, group, slots, page_rows, scale = sizes
+    rows = query.shape[0]
+    qheads = kv_heads * group
+
+    def own_head(width):
+        row = lax.broadcasted_iota(jnp.int32, (rows, width), 0)
+        column = lax.broadcasted_iota(jnp.int32, (rows, width), 1)
+        return (row % qheads) // group == column % kv_heads
+
+    def scores(key):
+        product = lax.dot_general(
+            query, key, (((1,), (1,)), ((), ())), preferred_element_type=jnp.float32
+        )
+        return jnp.where(own_head(key.shape[0]), product, -jnp.inf)
+
+    parts = []
+    for key_ref, pool_ref, bias, value_ref in sides:
+        page_key = suffix_rows(pool_ref, 0, slots, page_rows)
+        page_value = suffix_rows(pool_ref, page_rows, slots, page_rows)
+        parts.append((scores(key_ref[...]), value_ref))
+        parts.append((scores(page_key) + bias, page_value))
+    top = functools.reduce(jnp.maximum, [jnp.max(score, axis=1, keepdims=True) for score, _ in parts])
+    high, low = split(top)
+    point = high + low
+    total = mixed = 0.0
+    late = None
+    for score, value in parts:
+        weight = jnp.exp2((score - point) * scale)
+        total = total + jnp.sum(weight, axis=1, keepdims=True)
+        weight = weight.astype(jnp.bfloat16)
+        if value is None:
+            late = weight
+        else:
+            mixed = mixed + jnp.dot(weight, value[...], preferred_element_type=jnp.float32)
+    return point, total, mixed, late
+
+
+def chunk_bias(bias_ref, first, count, qheads):
+    return jnp.concatenate(
+        [
+            jnp.broadcast_to(bias_ref[pl.ds(first + j, 1), :], (qheads, bias_ref.shape[1]))
+            for j in range(count)
+        ],
+        axis=0,
+    )
 
 
 def weigh_kernel(
-    first_ref, second_ref, near_ref, near_value_ref, near_bias_ref, far_ref, far_bias_ref,
+    first_ref, second_ref, near_ref, near_pool_ref, near_value_ref, near_bias_ref, far_ref, far_pool_ref, far_bias_ref,
     late_ref, mixed_ref, point_ref, total_ref, *, sizes,
 ):
     half, qheads, head_dim = first_ref.shape
-    part = min(CHUNK // 2, half)
+    part = point_ref.shape[1] // qheads // 2
 
     def one(i):
         query = jnp.concatenate(
@@ -205,8 +241,8 @@
             )
 
         sides = (
-            (near_ref, bias(near_bias_ref), near_value_ref),
-            (far_ref, bias(far_bias_ref), None),
+            (near_ref, near_pool_ref, bias(near_bias_ref), near_value_ref),
+            (far_ref, far_pool_ref, bias(far_bias_ref), None),
         )
         point, total, mixed, late_ref[i] = attend(query, sides, sizes)
         mixed_ref[i] = mixed
@@ -216,7 +252,9 @@
     loop(half // part, one)
 
 
-def finish_kernel(late_ref, mixed_ref, point_ref, total_ref, far_value_ref, send_ref, keep_ref):
+def finish_kernel(
+    late_ref, mixed_ref, point_ref, total_ref, far_value_ref, send_ref, keep_ref, *, rows_dev
+):
     steps, rows, head_dim = mixed_ref.shape
     qheads = send_ref.shape[1] - STAT_ROWS
     part = rows // qheads // 2
@@ -229,8 +267,9 @@
         mixed = mixed / total_ref[i]
         for j in range(2 * part):
             rows = slice(j * qheads, (j + 1) * qheads)
-            out_ref = keep_ref if j < part else send_ref
-            out_ref[i * part + j % part] = write(
+            own, inner = divmod(j % part, rows_dev)
+            out_ref = send_ref if own else keep_ref
+            out_ref[j // part * (keep_ref.shape[0] // 2) + i * rows_dev + inner] = write(
                 mixed[rows],
                 to_row(point_ref[i, rows], diagonal),
                 to_row(total_ref[i, rows], diagonal),
@@ -309,38 +348,56 @@
     shared_bits = [1 << b for b in range(2, blocks.bit_length() - 1)]
 
     values = prefix_values.reshape(prefix_rows, head_dim)
-    near = pack(
-        prefix_keys.reshape(prefix_rows, head_dim),
-        suffix_pool.reshape(slots * 2 * page_rows, head_dim),
-    )
-    far = exchange(near, 1, 2)
+    keys = prefix_keys.reshape(prefix_rows, head_dim)
+    pool = suffix_pool.reshape(slots * 2 * page_rows, head_dim)
+    far = exchange(keys, 1, 2)
     far_values = exchange(values, 1, 2)
+    far_pool = exchange(pool, 1, 2)
     first = queries
+    second = exchange(first, 2, 1)
     for bit in shared_bits:
-        first = jnp.concatenate([first, exchange(first, bit, bit)], axis=0)
-    second = exchange(first, 2, 1)
+        first = jnp.concatenate([first, second], axis=0)
+        second = exchange(first, bit, bit)
     half = first.shape[0]
-    rows = 2 * half
-
-    place = jnp.stack([me, 2 - odd_core, 1 + odd_core]).astype(jnp.int32)
-    table = jax.ShapeDtypeStruct((rows, slots * page_rows), jnp.float32)
-    near_bias, far_bias = call(
-        bias_kernel, (table, table), (place, page_owner, page_slot, suffix_len, row_request), 5,
-        rows_dev=rows_dev, page_len=page_len, kv_heads=kv_heads, blocks=blocks,
-    )
+
+    tables = (page_owner, page_slot, suffix_len, row_request)
+    arrays = (keys, values, pool)
+    mask = jax.ShapeDtypeStruct((2 * half, slots * page_rows), jnp.float32)
+    near_keys, near_values, near_pool, near_mask, far_mask = pl.pallas_call(
+        functools.partial(
+            fetch_kernel,
+            rows_dev=rows_dev, page_len=page_len, kv_heads=kv_heads, sources=len(arrays),
+        ),
+        out_shape=[jax.ShapeDtypeStruct(array.shape, array.dtype) for array in arrays] + [mask] * 2,
+        in_specs=[pl.BlockSpec(memory_space=pltpu.VMEM)]
+        + [pl.BlockSpec(memory_space=pltpu.HBM)] * (len(tables) + len(arrays)),
+        out_specs=[pl.BlockSpec(memory_space=pltpu.VMEM)] * (len(arrays) + 2),
+        scratch_shapes=[pltpu.SMEM(table.shape, table.dtype) for table in tables]
+        + [pltpu.SemaphoreType.DMA((len(tables) + len(arrays),))],
+        compiler_params=pltpu.CompilerParams(vmem_limit_bytes=VMEM_BYTES),
+    )(
+        first,
+        *(pltpu.with_memory_space_constraint(operand, pltpu.HBM) for operand in tables + arrays),
+    )
+
     def parcels(count):
         shape = (count, qheads + STAT_ROWS, head_dim)
         return jax.ShapeDtypeStruct(shape, jnp.bfloat16), jax.ShapeDtypeStruct(shape, jnp.bfloat16)
 
-    part = min(CHUNK // 2, half)
+    part = 2 * rows_dev
     shape = (half // part, 2 * part * qheads)
     late = jax.ShapeDtypeStruct((*shape, prefix_rows), jnp.bfloat16)
     block = jax.ShapeDtypeStruct((*shape, head_dim), jnp.float32)
     weighed = call(
         weigh_kernel, (late, block, block, block),
-        (first, second, near, values, near_bias, far, far_bias), sizes=sizes,
-    )
-    send, keep = call(finish_kernel, parcels(half), (*weighed, far_values))
+        (
+            first, second, near_keys, near_pool, near_values, near_mask, far, far_pool, far_mask,
+        ),
+        sizes=sizes,
+    )
+    send, keep = call(
+        finish_kernel, parcels(half), (*weighed, far_values), rows_dev=rows_dev
+    )
     cross = 1 if shared_bits and lax.axis_size("heads") % 2 == 0 else 0
     arrived = exchange(send, 1, 2, 1) if cross else exchange(send, 2, 1)
     turn = cross

time: 21.8 us -> 21.3 us (0.977)
  starting transfers between devices: 12.3 us -> 14.2 us
  waiting for transfers between devices: 5.02 us -> 3.18 us
  Pallas kernels: 3.6 us -> 2.95 us
    ppermute x8 -> x9, starting transfers between devices: 12.3 us -> 14.2 us  [exchange(): return lax.ppermute(value, ('blk', 'heads'), pairs)]
    ppermute x8 -> x9, waiting for transfers between devices: 5.02 us -> 3.18 us  [exchange(): return lax.ppermute(value, ('blk', 'heads'), pairs)]
    pallas_call x5 -> x4, Pallas kernels: 2.56 us -> 1.84 us  [call(): pl.pallas_call(functools.partial(kernel, **static), out_shape=outs, in_sp...]
    unnamed x13 -> x1, local copies, waits for them, and re-layouts: 0.62 us -> 0.7 us
  transfers between devices with their start and end apart: 8 -> 9, of which waited for: 4 -> 3; matrix products, arithmetic and copies ran while one was open for 0% -> 3% of each run, Pallas kernels for 7% -> 9%
where the time goes in v11:
time: 21.3 us; the launch traced here: 21.1 us
  starting transfers between devices  14.2 us (67%)
  waiting for transfers between devices  3.18 us (15%)
  Pallas kernels  2.95 us (14%)
  local copies, waits for them, and re-layouts  0.7 us (3%)
    ppermute x9, starting transfers between devices, exchange(): return lax.ppermute(value, ('blk', 'heads'), pairs)  14.2 us
    ppermute x9, waiting for transfers between devices, exchange(): return lax.ppermute(value, ('blk', 'heads'), pairs)  3.18 us
    pallas_call x4, Pallas kernels, call(): pl.pallas_call(functools.partial(kernel, **static), out_shape=outs, in_sp...  1.84 us
    pallas_call x1, Pallas kernels, on_device(): pl.pallas_call(functools.partial(fetch_kernel, rows_dev=rows_dev, page_le...  1.11 us
    unnamed x1, local copies, waits for them, and re-layouts  0.7 us
  transfers between devices with their start and end apart: 9, of which 3 were waited for; matrix products, arithmetic and copies ran while one was open for 3% of the time, Pallas kernels for 9%

profile of v11, /device:TPU:0, one launch (start us, length us, event | category | flops | bytes accessed | tf_op | source)
XLA Modules:
  0.0 21.1 jit_solution(9204888712443849899)
XLA Ops:
  0.0 2.9 %collective-permute-start.2 = (bf16[1024,128]{1,0:T(8,128)(2,1)}, bf16[1024,128]{1,0:T(8,128)(2,1)S(1)}, u32[]{:S(2)}, u32[]{:S(2)}) collective-permute-start(bf16[1024,128]{1,0:T(8,128)(2,1)} %bitcast.3), channel_id=1, source_target_pairs={{0,2},{1,5},{2,0},{3,7},{4,6},{5,1},{6,4},{7,3},{8,10},{9,13},{10,... | collective-permute-start | bytes 786440 | tf_op jit(solution)/shard_map/ppermute | solution.py:23
  2.9 0.0 collective-permute-start.4
  3.0 2.1 %collective-permute-start = (bf16[1,32,128]{2,1,0:T(8,128)(2,1)}, bf16[1,32,128]{2,1,0:T(8,128)(2,1)S(1)}, u32[]{:S(2)}, u32[]{:S(2)}) collective-permute-start(bf16[1,32,128]{2,1,0:T(8,128)(2,1)} %param.8), channel_id=1, source_target_pairs={{0,4},{1,3},{2,6},{3,1},{4,0},{5,7},{6,2},{7,5},{8,12},{9,11},{10,... | collective-permute-start | bytes 24584 | tf_op jit(solution)/shard_map/ppermute | solution.py:23
  5.1 1.5 %collective-permute-start.3 = (bf16[384,128]{1,0:T(8,128)(2,1)}, bf16[384,128]{1,0:T(8,128)(2,1)S(1)}, u32[]{:S(2)}, u32[]{:S(2)}) collective-permute-start(bf16[384,128]{1,0:T(8,128)(2,1)} %bitcast.7), channel_id=1, source_target_pairs={{0,2},{1,5},{2,0},{3,7},{4,6},{5,1},{6,4},{7,3},{8,10},{9,13},{10,... | collective-permute-start | bytes 294920 | tf_op jit(solution)/shard_map/ppermute | solution.py:23
  6.5 0.7 %constant_dynamic-update-slice_fusion.1 = bf16[2,32,128]{2,1,0:T(8,128)(2,1)S(1)} fusion(bf16[1,32,128]{2,1,0:T(8,128)(2,1)} %param.8), kind=kLoop, calls=%fused_computation.1 | loop fusion | bytes 16384
  7.2 0.0 collective-permute-done
  7.3 2.8 %collective-permute-start.1 = (bf16[2,32,128]{2,1,0:T(8,128)(2,1)S(1)}, bf16[2,32,128]{2,1,0:T(8,128)(2,1)S(1)}, u32[]{:S(2)}, u32[]{:S(2)}) collective-permute-start(bf16[2,32,128]{2,1,0:T(8,128)(2,1)S(1)} %constant_dynamic-update-slice_fusion.queries_ref.first_ref), channel_id=1, source_target_pairs={{0,8},{1,9},{2,10},{3,11},{4,12},{5,13},{6,14},{7,15},{8,0},{9,1},... | collective-permute-start | bytes 49160 | tf_op jit(solution)/shard_map/ppermute | solution.py:23
  10.1 1.1 %shard_map.82 = (bf16[1024,128]{1,0:T(8,128)(2,1)S(1)}, bf16[1024,128]{1,0:T(8,128)(2,1)S(1)}, bf16[384,128]{1,0:T(8,128)(2,1)S(1)}, f32[4,192]{1,0:T(4,128)S(1)}, f32[4,192]{1,0:T(4,128)S(1)}) custom-call(bf16[2,32,128]{2,1,0:T(8,128)(2,1)S(1)} %constant_dynamic-update-slice_fusion.queries_ref.first_ref, s32[3,8]{1,0:T(4,128)} %owner_hbm.1, ...), custom_call_target="tpu_custom_call" | custom-call | tf_op jit(solution)/shard_map/pallas_call | solution.py:366
  11.2 0.7 %collective-permute-done.1.second_ref = bf16[2,32,128]{2,1,0:T(8,128)(2,1)S(1)} collective-permute-done((bf16[2,32,128]{2,1,0:T(8,128)(2,1)S(1)}, bf16[2,32,128]{2,1,0:T(8,128)(2,1)S(1)}, u32[]{:S(2)}, u32[]{:S(2)}) %collective-permute-start.1) | collective-permute-done | bytes 16416 | tf_op jit(solution)/shard_map/ppermute | solution.py:23
  11.9 0.0 collective-permute-done.3.far_pool_ref
  11.9 0.0 collective-permute-done.2.far_ref
  11.9 0.8 %shard_map.83 = (bf16[1,128,1024]{2,1,0:T(8,128)(2,1)S(1)}, f32[1,128,128]{2,1,0:T(8,128)S(1)}, f32[1,128,128]{2,1,0:T(8,128)S(1)}, f32[1,128,128]{2,1,0:T(8,128)S(1)}) custom-call(bf16[2,32,128]{2,1,0:T(8,128)(2,1)S(1)} %constant_dynamic-update-slice_fusion.queries_ref.first_ref, bf16[2,32,128]{2,1,0:T(8,128)(2,1)S(1)} %collective-permute-done.1.second_ref, ...), custom_call_target="tpu_custom_call" | custom-call | tf_op jit(solution)/shard_map/pallas_call | solution.py:327
  12.7 0.0 collective-permute-done.4.far_value_ref
  12.7 0.2 %shard_map.84 = (bf16[2,48,128]{2,1,0:T(8,128)(2,1)S(1)}, bf16[2,48,128]{2,1,0:T(8,128)(2,1)S(1)}) custom-call(bf16[1,128,1024]{2,1,0:T(8,128)(2,1)S(1)} %get-tuple-element.23.late_ref, f32[1,128,128]{2,1,0:T(8,128)S(1)} %get-tuple-element.24.mixed_ref, f32[1,128,128]{2,1,0:T(8,128)S(1)} %get-tuple-element.25.point_ref, ...), custom_call_target="tpu_custom_call" | custom-call | tf_op jit(solution)/shard_map/pallas_call | solution.py:327
  12.9 1.5 %collective-permute-start.5 = (bf16[2,48,128]{2,1,0:T(8,128)(2,1)S(1)}, bf16[2,48,128]{2,1,0:T(8,128)(2,1)S(1)}, u32[]{:S(2)}, u32[]{:S(2)}) collective-permute-start(bf16[2,48,128]{2,1,0:T(8,128)(2,1)S(1)} %get-tuple-element.27), channel_id=1, source_target_pairs={{0,5},{1,2},{2,7},{3,0},{4,1},{5,6},{6,3},{7,4},{8,13},{9,10},{10,... | collective-permute-start | bytes 73736 | tf_op jit(solution)/shard_map/ppermute | solution.py:23
  14.4 0.4 %collective-permute-start.6 = (bf16[2,48,128]{2,1,0:T(8,128)(2,1)S(1)}, bf16[2,48,128]{2,1,0:T(8,128)(2,1)S(1)}, u32[]{:S(2)}, u32[]{:S(2)}) collective-permute-start(bf16[2,48,128]{2,1,0:T(8,128)(2,1)S(1)} %get-tuple-element.28), channel_id=1, source_target_pairs={{0,1},{1,0},{2,3},{3,2},{4,5},{5,4},{6,7},{7,6},{8,9},{9,8},{10,11... | collective-permute-start | bytes 73736 | tf_op jit(solution)/shard_map/ppermute | solution.py:23
  14.8 1.4 %collective-permute-done.5.parcel_ref = bf16[2,48,128]{2,1,0:T(8,128)(2,1)S(1)} collective-permute-done((bf16[2,48,128]{2,1,0:T(8,128)(2,1)S(1)}, bf16[2,48,128]{2,1,0:T(8,128)(2,1)S(1)}, u32[]{:S(2)}, u32[]{:S(2)}) %collective-permute-start.5) | collective-permute-done | bytes 24608 | tf_op jit(solution)/shard_map/ppermute | solution.py:23
  16.3 0.0 collective-permute-done.6.keep_in
  16.3 0.1 shard_map.85
  16.4 2.6 %collective-permute-start.7 = (bf16[1,48,128]{2,1,0:T(8,128)(2,1)S(1)}, bf16[1,48,128]{2,1,0:T(8,128)(2,1)S(1)}, u32[]{:S(2)}, u32[]{:S(2)}) collective-permute-start(bf16[1,48,128]{2,1,0:T(8,128)(2,1)S(1)} %get-tuple-element.29), channel_id=1, source_target_pairs={{0,9},{1,8},{2,11},{3,10},{4,13},{5,12},{6,15},{7,14},{8,1},{9,0},... | collective-permute-start | bytes 36872 | tf_op jit(solution)/shard_map/ppermute | solution.py:23
  18.9 0.4 %collective-permute-start.8 = (bf16[1,48,128]{2,1,0:T(8,128)(2,1)S(1)}, bf16[1,48,128]{2,1,0:T(8,128)(2,1)S(1)}, u32[]{:S(2)}, u32[]{:S(2)}) collective-permute-start(bf16[1,48,128]{2,1,0:T(8,128)(2,1)S(1)} %get-tuple-element.30), channel_id=1, source_target_pairs={{0,1},{1,0},{2,3},{3,2},{4,5},{5,4},{6,7},{7,6},{8,9},{9,8},{10,11... | collective-permute-start | bytes 36872 | tf_op jit(solution)/shard_map/ppermute | solution.py:23
  19.3 1.1 %collective-permute-done.7.parcel_ref = bf16[1,48,128]{2,1,0:T(8,128)(2,1)S(1)} collective-permute-done((bf16[1,48,128]{2,1,0:T(8,128)(2,1)S(1)}, bf16[1,48,128]{2,1,0:T(8,128)(2,1)S(1)}, u32[]{:S(2)}, u32[]{:S(2)}) %collective-permute-start.7) | collective-permute-done | bytes 12320 | tf_op jit(solution)/shard_map/ppermute | solution.py:23
  20.4 0.0 collective-permute-done.8.keep_in
  20.4 0.7 %shard_map.86 = bf16[1,32,128]{2,1,0:T(8,128)(2,1)} custom-call(bf16[1,48,128]{2,1,0:T(8,128)(2,1)S(1)} %collective-permute-done.7.parcel_ref, bf16[1,48,128]{2,1,0:T(8,128)(2,1)S(1)} %collective-permute-done.8.keep_in), custom_call_target="tpu_custom_call" | custom-call | tf_op jit(solution)/shard_map/pallas_call | solution.py:327
  (1 shorter events, 0.0 us)
Async XLA Ops:
  0.0 11.9 %collective-permute-start.2 = (bf16[1024,128]{1,0:T(8,128)(2,1)}, bf16[1024,128]{1,0:T(8,128)(2,1)S(1)}, u32[]{:S(2)}, u32[]{:S(2)}) collective-permute-start(bf16[1024,128]{1,0:T(8,128)(2,1)} %bitcast.3), channel_id=1, source_target_pairs={{0,2},{1,5},{2,0},{3,7},{4,6},{5,1},{6,4},{7,3},{8,10},{9,13},{10,... | collective-permute-start | bytes 786440 | tf_op jit(solution)/shard_map/ppermute | solution.py:23
  2.9 9.8 %collective-permute-start.4 = (bf16[1024,128]{1,0:T(8,128)(2,1)}, bf16[1024,128]{1,0:T(8,128)(2,1)S(1)}, u32[]{:S(2)}, u32[]{:S(2)}) collective-permute-start(bf16[1024,128]{1,0:T(8,128)(2,1)} %bitcast.5), channel_id=1, source_target_pairs={{0,2},{1,5},{2,0},{3,7},{4,6},{5,1},{6,4},{7,3},{8,10},{9,13},{10,... | collective-permute-start | bytes 786440 | tf_op jit(solution)/shard_map/ppermute | solution.py:23
  3.0 4.3 %collective-permute-start = (bf16[1,32,128]{2,1,0:T(8,128)(2,1)}, bf16[1,32,128]{2,1,0:T(8,128)(2,1)S(1)}, u32[]{:S(2)}, u32[]{:S(2)}) collective-permute-start(bf16[1,32,128]{2,1,0:T(8,128)(2,1)} %param.8), channel_id=1, source_target_pairs={{0,4},{1,3},{2,6},{3,1},{4,0},{5,7},{6,2},{7,5},{8,12},{9,11},{10,... | collective-permute-start | bytes 24584 | tf_op jit(solution)/shard_map/ppermute | solution.py:23
  5.1 6.8 %collective-permute-start.3 = (bf16[384,128]{1,0:T(8,128)(2,1)}, bf16[384,128]{1,0:T(8,128)(2,1)S(1)}, u32[]{:S(2)}, u32[]{:S(2)}) collective-permute-start(bf16[384,128]{1,0:T(8,128)(2,1)} %bitcast.7), channel_id=1, source_target_pairs={{0,2},{1,5},{2,0},{3,7},{4,6},{5,1},{6,4},{7,3},{8,10},{9,13},{10,... | collective-permute-start | bytes 294920 | tf_op jit(solution)/shard_map/ppermute | solution.py:23
  7.3 4.6 %collective-permute-start.1 = (bf16[2,32,128]{2,1,0:T(8,128)(2,1)S(1)}, bf16[2,32,128]{2,1,0:T(8,128)(2,1)S(1)}, u32[]{:S(2)}, u32[]{:S(2)}) collective-permute-start(bf16[2,32,128]{2,1,0:T(8,128)(2,1)S(1)} %constant_dynamic-update-slice_fusion.queries_ref.first_ref), channel_id=1, source_target_pairs={{0,8},{1,9},{2,10},{3,11},{4,12},{5,13},{6,14},{7,15},{8,0},{9,1},... | collective-permute-start | bytes 49160 | tf_op jit(solution)/shard_map/ppermute | solution.py:23
  12.9 3.3 %collective-permute-start.5 = (bf16[2,48,128]{2,1,0:T(8,128)(2,1)S(1)}, bf16[2,48,128]{2,1,0:T(8,128)(2,1)S(1)}, u32[]{:S(2)}, u32[]{:S(2)}) collective-permute-start(bf16[2,48,128]{2,1,0:T(8,128)(2,1)S(1)} %get-tuple-element.27), channel_id=1, source_target_pairs={{0,5},{1,2},{2,7},{3,0},{4,1},{5,6},{6,3},{7,4},{8,13},{9,10},{10,... | collective-permute-start | bytes 73736 | tf_op jit(solution)/shard_map/ppermute | solution.py:23
  14.4 1.8 %collective-permute-start.6 = (bf16[2,48,128]{2,1,0:T(8,128)(2,1)S(1)}, bf16[2,48,128]{2,1,0:T(8,128)(2,1)S(1)}, u32[]{:S(2)}, u32[]{:S(2)}) collective-permute-start(bf16[2,48,128]{2,1,0:T(8,128)(2,1)S(1)} %get-tuple-element.28), channel_id=1, source_target_pairs={{0,1},{1,0},{2,3},{3,2},{4,5},{5,4},{6,7},{7,6},{8,9},{9,8},{10,11... | collective-permute-start | bytes 73736 | tf_op jit(solution)/shard_map/ppermute | solution.py:23
  16.4 4.0 %collective-permute-start.7 = (bf16[1,48,128]{2,1,0:T(8,128)(2,1)S(1)}, bf16[1,48,128]{2,1,0:T(8,128)(2,1)S(1)}, u32[]{:S(2)}, u32[]{:S(2)}) collective-permute-start(bf16[1,48,128]{2,1,0:T(8,128)(2,1)S(1)} %get-tuple-element.29), channel_id=1, source_target_pairs={{0,9},{1,8},{2,11},{3,10},{4,13},{5,12},{6,15},{7,14},{8,1},{9,0},... | collective-permute-start | bytes 36872 | tf_op jit(solution)/shard_map/ppermute | solution.py:23
  18.9 1.5 %collective-permute-start.8 = (bf16[1,48,128]{2,1,0:T(8,128)(2,1)S(1)}, bf16[1,48,128]{2,1,0:T(8,128)(2,1)S(1)}, u32[]{:S(2)}, u32[]{:S(2)}) collective-permute-start(bf16[1,48,128]{2,1,0:T(8,128)(2,1)S(1)} %get-tuple-element.30), channel_id=1, source_target_pairs={{0,1},{1,0},{2,3},{3,2},{4,5},{5,4},{6,7},{7,6},{8,9},{9,8},{10,11... | collective-permute-start | bytes 36872 | tf_op jit(solution)/shard_map/ppermute | solution.py:23

commit v12 on v11

--- a/solution.py
+++ b/solution.py
@@ -60,54 +60,6 @@
 def suffix_rows(rest_ref, start, slots, page_rows):
     return jnp.concatenate(
         [rest_ref[start + s * 2 * page_rows : start + s * 2 * page_rows + page_rows] for s in range(slots)],
-        axis=0,
-    )
-
-
-def attend(query, sides, sizes):
-    kv_heads, group, slots, page_rows, scale = sizes
-    rows = query.shape[0]
-    qheads = kv_heads * group
-
-    def own_head(width):
-        row = lax.broadcasted_iota(jnp.int32, (rows, width), 0)
-        column = lax.broadcasted_iota(jnp.int32, (rows, width), 1)
-        return (row % qheads) // group == column % kv_heads
-
-    def scores(key):
-        product = lax.dot_general(
-            query, key, (((1,), (1,)), ((), ())), preferred_element_type=jnp.float32
-        )
-        return jnp.where(own_head(key.shape[0]), product, -jnp.inf)
-
-    parts = []
-    for key_ref, pool_ref, bias, value_ref in sides:
-        page_key = suffix_rows(pool_ref, 0, slots, page_rows)
-        page_value = suffix_rows(pool_ref, page_rows, slots, page_rows)
-        parts.append((scores(key_ref[...]), value_ref))
-        parts.append((scores(page_key) + bias, page_value))
-    top = functools.reduce(jnp.maximum, [jnp.max(score, axis=1, keepdims=True) for score, _ in parts])
-    high, low = split(top)
-    point = high + low
-    total = mixed = 0.0
-    late = None
-    for score, value in parts:
-        weight = jnp.exp2((score - point) * scale)
-        total = total + jnp.sum(weight, axis=1, keepdims=True)
-        weight = weight.astype(jnp.bfloat16)
-        if value is None:
-            late = weight
-        else:
-            mixed = mixed + jnp.dot(weight, value[...], preferred_element_type=jnp.float32)
-    return point, total, mixed, late
-
-
-def chunk_bias(bias_ref, first, count, qheads):
-    return jnp.concatenate(
-        [
-            jnp.broadcast_to(bias_ref[pl.ds(first + j, 1), :], (qheads, bias_ref.shape[1]))
-            for j in range(count)
-        ],
         axis=0,
     )
 
@@ -184,25 +136,22 @@
         return jnp.where(own_head(key.shape[0]), product, -jnp.inf)
 
     parts = []
-    for key_ref, pool_ref, bias, value_ref in sides:
+    for key_ref, value_ref, pool_ref, mask in sides:
         page_key = suffix_rows(pool_ref, 0, slots, page_rows)
         page_value = suffix_rows(pool_ref, page_rows, slots, page_rows)
-        parts.append((scores(key_ref[...]), value_ref))
-        parts.append((scores(page_key) + bias, page_value))
+        parts.append((scores(key_ref[...]), value_ref[...]))
+        parts.append((scores(page_key) + mask, page_value))
     top = functools.reduce(jnp.maximum, [jnp.max(score, axis=1, keepdims=True) for score, _ in parts])
     high, low = split(top)
     point = high + low
     total = mixed = 0.0
-    late = None
     for score, value in parts:
         weight = jnp.exp2((score - point) * scale)
         total = total + jnp.sum(weight, axis=1, keepdims=True)
-        weight = weight.astype(jnp.bfloat16)
-        if value is None:
-            late = weight
-        else:
-            mixed = mixed + jnp.dot(weight, value[...], preferred_element_type=jnp.float32)
-    return point, total, mixed, late
+        mixed = mixed + jnp.dot(
+            weight.astype(jnp.bfloat16), value, preferred_element_type=jnp.float32
+        )
+    return point, total, mixed / total
 
 
 def chunk_bias(bias_ref, first, count, qheads):
@@ -215,12 +164,11 @@
     )
 
 
-def weigh_kernel(
-    first_ref, second_ref, near_ref, near_pool_ref, near_value_ref, near_bias_ref, far_ref, far_pool_ref, far_bias_ref,
-    late_ref, mixed_ref, point_ref, total_ref, *, sizes,
-):
+def attend_kernel(first_ref, second_ref, *refs, rows_dev, sizes):
+    *side_refs, send_ref, keep_ref = refs
     half, qheads, head_dim = first_ref.shape
-    part = point_ref.shape[1] // qheads // 2
+    part = 2 * rows_dev
+    diagonal = spread_rows(qheads, head_dim)
 
     def one(i):
         query = jnp.concatenate(
@@ -231,7 +179,7 @@
             axis=0,
         )
 
-        def bias(ref):
+        def mask(ref):
             return jnp.concatenate(
                 [
                     chunk_bias(ref, i * part, part, qheads),
@@ -240,43 +188,18 @@
                 axis=0,
             )
 
-        sides = (
-            (near_ref, near_pool_ref, bias(near_bias_ref), near_value_ref),
-            (far_ref, far_pool_ref, bias(far_bias_ref), None),
-        )
-        point, total, mixed, late_ref[i] = attend(query, sides, sizes)
-        mixed_ref[i] = mixed
-        point_ref[i] = jnp.broadcast_to(point, mixed.shape)
-        total_ref[i] = jnp.broadcast_to(total, mixed.shape)
-
-    loop(half // part, one)
-
-
-def finish_kernel(
-    late_ref, mixed_ref, point_ref, total_ref, far_value_ref, send_ref, keep_ref, *, rows_dev
-):
-    steps, rows, head_dim = mixed_ref.shape
-    qheads = send_ref.shape[1] - STAT_ROWS
-    part = rows // qheads // 2
-    diagonal = spread_rows(qheads, head_dim)
-
-    def one(i):
-        mixed = mixed_ref[i] + jnp.dot(
-            late_ref[i], far_value_ref[...], preferred_element_type=jnp.float32
-        )
-        mixed = mixed / total_ref[i]
+        sides = [(*side_refs[j : j + 3], mask(side_refs[j + 3])) for j in (0, 4)]
+        point, total, mixed = attend(query, sides, sizes)
         for j in range(2 * part):
             rows = slice(j * qheads, (j + 1) * qheads)
             own, inner = divmod(j % part, rows_dev)
             out_ref = send_ref if own else keep_ref
-            out_ref[j // part * (keep_ref.shape[0] // 2) + i * rows_dev + inner] = write(
-                mixed[rows],
-                to_row(point_ref[i, rows], diagonal),
-                to_row(total_ref[i, rows], diagonal),
+            out_ref[j // part * (half // 2) + i * rows_dev + inner] = write(
+                mixed[rows], to_row(point[rows], diagonal), to_row(total[rows], diagonal),
                 out_ref.dtype,
             )
 
-    loop(steps, one)
+    loop(half // part, one)
 
 
 def read(parcel):
@@ -323,12 +246,11 @@
     loop(count, one)
 
 
-def call(kernel, outs, operands, scalars=0, **static):
+def call(kernel, outs, operands, **static):
     return pl.pallas_call(
         functools.partial(kernel, **static),
         out_shape=outs,
-        in_specs=[pl.BlockSpec(memory_space=pltpu.SMEM)] * scalars
-        + [pl.BlockSpec(memory_space=pltpu.VMEM)] * (len(operands) - scalars),
+        in_specs=[pl.BlockSpec(memory_space=pltpu.VMEM)] * len(operands),
         compiler_params=pltpu.CompilerParams(vmem_limit_bytes=VMEM_BYTES),
     )(*operands)
 
@@ -350,7 +272,7 @@
     values = prefix_values.reshape(prefix_rows, head_dim)
     keys = prefix_keys.reshape(prefix_rows, head_dim)
     pool = suffix_pool.reshape(slots * 2 * page_rows, head_dim)
-    far = exchange(keys, 1, 2)
+    far_keys = exchange(keys, 1, 2)
     far_values = exchange(values, 1, 2)
     far_pool = exchange(pool, 1, 2)
     first = queries
@@ -384,19 +306,13 @@
         shape = (count, qheads + STAT_ROWS, head_dim)
         return jax.ShapeDtypeStruct(shape, jnp.bfloat16), jax.ShapeDtypeStruct(shape, jnp.bfloat16)
 
-    part = 2 * rows_dev
-    shape = (half // part, 2 * part * qheads)
-    late = jax.ShapeDtypeStruct((*shape, prefix_rows), jnp.bfloat16)
-    block = jax.ShapeDtypeStruct((*shape, head_dim), jnp.float32)
-    weighed = call(
-        weigh_kernel, (late, block, block, block),
+    send, keep = call(
+        attend_kernel, parcels(half),
         (
-            first, second, near_keys, near_pool, near_values, near_mask, far, far_pool, far_mask,
+            first, second, near_keys, near_values, near_pool, near_mask,
+            far_keys, far_values, far_pool, far_mask,
         ),
-        sizes=sizes,
-    )
-    send, keep = call(
-        finish_kernel, parcels(half), (*weighed, far_values), rows_dev=rows_dev
+        rows_dev=rows_dev, sizes=sizes,
     )
     cross = 1 if shared_bits and lax.axis_size("heads") % 2 == 0 else 0
     arrived = exchange(send, 1, 2, 1) if cross else exchange(send, 2, 1)

time: 21.3 us -> 21.1 us (level)
    pallas_call x4 -> x3, Pallas kernels: 1.84 us -> 1.68 us  [call(): pl.pallas_call(functools.partial(kernel, **static), out_shape=outs, in_sp...]
  transfers between devices with their start and end apart: 9 -> 9, of which waited for: 3 -> 3; matrix products, arithmetic and copies ran while one was open for 3% -> 3% of each run, Pallas kernels for 9% -> 5%
where the time goes in v12:
time: 21.1 us; the launch traced here: 20.9 us
  starting transfers between devices  14.3 us (68%)
  waiting for transfers between devices  3.15 us (15%)
  Pallas kernels  2.79 us (13%)
  local copies, waits for them, and re-layouts  0.7 us (3%)
    ppermute x9, starting transfers between devices, exchange(): return lax.ppermute(value, ('blk', 'heads'), pairs)  14.3 us
    ppermute x9, waiting for transfers between devices, exchange(): return lax.ppermute(value, ('blk', 'heads'), pairs)  3.15 us
    pallas_call x3, Pallas kernels, call(): pl.pallas_call(functools.partial(kernel, **static), out_shape=outs, in_sp...  1.68 us
    pallas_call x1, Pallas kernels, on_device(): pl.pallas_call(functools.partial(fetch_kernel, rows_dev=rows_dev, page_le...  1.11 us
    unnamed x1, local copies, waits for them, and re-layouts  0.7 us
  transfers between devices with their start and end apart: 9, of which 3 were waited for; matrix products, arithmetic and copies ran while one was open for 3% of the time, Pallas kernels for 5%

profile of v12, /device:TPU:0, one launch (start us, length us, event | category | flops | bytes accessed | tf_op | source)
XLA Modules:
  0.0 20.9 jit_solution(9360494968251597578)
XLA Ops:
  0.0 2.9 %collective-permute-start.2 = (bf16[1024,128]{1,0:T(8,128)(2,1)}, bf16[1024,128]{1,0:T(8,128)(2,1)S(1)}, u32[]{:S(2)}, u32[]{:S(2)}) collective-permute-start(bf16[1024,128]{1,0:T(8,128)(2,1)} %bitcast.3), channel_id=1, source_target_pairs={{0,2},{1,5},{2,0},{3,7},{4,6},{5,1},{6,4},{7,3},{8,10},{9,13},{10,... | collective-permute-start | bytes 786440 | tf_op jit(solution)/shard_map/ppermute | solution.py:23
  2.9 0.0 collective-permute-start.3
  3.0 2.1 %collective-permute-start = (bf16[1,32,128]{2,1,0:T(8,128)(2,1)}, bf16[1,32,128]{2,1,0:T(8,128)(2,1)S(1)}, u32[]{:S(2)}, u32[]{:S(2)}) collective-permute-start(bf16[1,32,128]{2,1,0:T(8,128)(2,1)} %param.8), channel_id=1, source_target_pairs={{0,4},{1,3},{2,6},{3,1},{4,0},{5,7},{6,2},{7,5},{8,12},{9,11},{10,... | collective-permute-start | bytes 24584 | tf_op jit(solution)/shard_map/ppermute | solution.py:23
  5.1 1.5 %collective-permute-start.4 = (bf16[384,128]{1,0:T(8,128)(2,1)}, bf16[384,128]{1,0:T(8,128)(2,1)S(1)}, u32[]{:S(2)}, u32[]{:S(2)}) collective-permute-start(bf16[384,128]{1,0:T(8,128)(2,1)} %bitcast.7), channel_id=1, source_target_pairs={{0,2},{1,5},{2,0},{3,7},{4,6},{5,1},{6,4},{7,3},{8,10},{9,13},{10,... | collective-permute-start | bytes 294920 | tf_op jit(solution)/shard_map/ppermute | solution.py:23
  6.5 0.7 %constant_dynamic-update-slice_fusion.1 = bf16[2,32,128]{2,1,0:T(8,128)(2,1)S(1)} fusion(bf16[1,32,128]{2,1,0:T(8,128)(2,1)} %param.8), kind=kLoop, calls=%fused_computation.1 | loop fusion | bytes 16384
  7.2 0.0 collective-permute-done
  7.3 2.8 %collective-permute-start.1 = (bf16[2,32,128]{2,1,0:T(8,128)(2,1)S(1)}, bf16[2,32,128]{2,1,0:T(8,128)(2,1)S(1)}, u32[]{:S(2)}, u32[]{:S(2)}) collective-permute-start(bf16[2,32,128]{2,1,0:T(8,128)(2,1)S(1)} %constant_dynamic-update-slice_fusion.queries_ref.first_ref), channel_id=1, source_target_pairs={{0,8},{1,9},{2,10},{3,11},{4,12},{5,13},{6,14},{7,15},{8,0},{9,1},... | collective-permute-start | bytes 49160 | tf_op jit(solution)/shard_map/ppermute | solution.py:23
  10.1 1.1 %shard_map.82 = (bf16[1024,128]{1,0:T(8,128)(2,1)S(1)}, bf16[1024,128]{1,0:T(8,128)(2,1)S(1)}, bf16[384,128]{1,0:T(8,128)(2,1)S(1)}, f32[4,192]{1,0:T(4,128)S(1)}, f32[4,192]{1,0:T(4,128)S(1)}) custom-call(bf16[2,32,128]{2,1,0:T(8,128)(2,1)S(1)} %constant_dynamic-update-slice_fusion.queries_ref.first_ref, s32[3,8]{1,0:T(4,128)} %owner_hbm.1, ...), custom_call_target="tpu_custom_call" | custom-call | tf_op jit(solution)/shard_map/pallas_call | solution.py:288
  11.2 0.7 %collective-permute-done.1.second_ref = bf16[2,32,128]{2,1,0:T(8,128)(2,1)S(1)} collective-permute-done((bf16[2,32,128]{2,1,0:T(8,128)(2,1)S(1)}, bf16[2,32,128]{2,1,0:T(8,128)(2,1)S(1)}, u32[]{:S(2)}, u32[]{:S(2)}) %collective-permute-start.1) | collective-permute-done | bytes 16416 | tf_op jit(solution)/shard_map/ppermute | solution.py:23
  11.9 0.0 collective-permute-done.4.refs_6_
  11.9 0.0 collective-permute-done.2.refs_4_
  11.9 0.0 collective-permute-done.3.refs_5_
  11.9 0.9 %shard_map.83 = (bf16[2,48,128]{2,1,0:T(8,128)(2,1)S(1)}, bf16[2,48,128]{2,1,0:T(8,128)(2,1)S(1)}) custom-call(bf16[2,32,128]{2,1,0:T(8,128)(2,1)S(1)} %constant_dynamic-update-slice_fusion.queries_ref.first_ref, bf16[2,32,128]{2,1,0:T(8,128)(2,1)S(1)} %collective-permute-done.1.second_ref, bf16[1024,128]{1,0:T(8,128)(2,1)S(1)} %get-tuple-element.14.refs_0_, ...), custom_call_target="tpu_custom_call" | custom-call | tf_op jit(solution)/shard_map/pallas_call | solution.py:250
  12.8 1.5 %collective-permute-start.5 = (bf16[2,48,128]{2,1,0:T(8,128)(2,1)S(1)}, bf16[2,48,128]{2,1,0:T(8,128)(2,1)S(1)}, u32[]{:S(2)}, u32[]{:S(2)}) collective-permute-start(bf16[2,48,128]{2,1,0:T(8,128)(2,1)S(1)} %get-tuple-element.19), channel_id=1, source_target_pairs={{0,5},{1,2},{2,7},{3,0},{4,1},{5,6},{6,3},{7,4},{8,13},{9,10},{10,... | collective-permute-start | bytes 73736 | tf_op jit(solution)/shard_map/ppermute | solution.py:23
  14.3 0.4 %collective-permute-start.6 = (bf16[2,48,128]{2,1,0:T(8,128)(2,1)S(1)}, bf16[2,48,128]{2,1,0:T(8,128)(2,1)S(1)}, u32[]{:S(2)}, u32[]{:S(2)}) collective-permute-start(bf16[2,48,128]{2,1,0:T(8,128)(2,1)S(1)} %get-tuple-element.20), channel_id=1, source_target_pairs={{0,1},{1,0},{2,3},{3,2},{4,5},{5,4},{6,7},{7,6},{8,9},{9,8},{10,11... | collective-permute-start | bytes 73736 | tf_op jit(solution)/shard_map/ppermute | solution.py:23
  14.7 1.4 %collective-permute-done.5.parcel_ref = bf16[2,48,128]{2,1,0:T(8,128)(2,1)S(1)} collective-permute-done((bf16[2,48,128]{2,1,0:T(8,128)(2,1)S(1)}, bf16[2,48,128]{2,1,0:T(8,128)(2,1)S(1)}, u32[]{:S(2)}, u32[]{:S(2)}) %collective-permute-start.5) | collective-permute-done | bytes 24608 | tf_op jit(solution)/shard_map/ppermute | solution.py:23
  16.1 0.0 collective-permute-done.6.keep_in
  16.1 0.1 shard_map.84
  16.2 2.6 %collective-permute-start.7 = (bf16[1,48,128]{2,1,0:T(8,128)(2,1)S(1)}, bf16[1,48,128]{2,1,0:T(8,128)(2,1)S(1)}, u32[]{:S(2)}, u32[]{:S(2)}) collective-permute-start(bf16[1,48,128]{2,1,0:T(8,128)(2,1)S(1)} %get-tuple-element.21), channel_id=1, source_target_pairs={{0,9},{1,8},{2,11},{3,10},{4,13},{5,12},{6,15},{7,14},{8,1},{9,0},... | collective-permute-start | bytes 36872 | tf_op jit(solution)/shard_map/ppermute | solution.py:23
  18.8 0.4 %collective-permute-start.8 = (bf16[1,48,128]{2,1,0:T(8,128)(2,1)S(1)}, bf16[1,48,128]{2,1,0:T(8,128)(2,1)S(1)}, u32[]{:S(2)}, u32[]{:S(2)}) collective-permute-start(bf16[1,48,128]{2,1,0:T(8,128)(2,1)S(1)} %get-tuple-element.22), channel_id=1, source_target_pairs={{0,1},{1,0},{2,3},{3,2},{4,5},{5,4},{6,7},{7,6},{8,9},{9,8},{10,11... | collective-permute-start | bytes 36872 | tf_op jit(solution)/shard_map/ppermute | solution.py:23
  19.2 1.0 %collective-permute-done.7.parcel_ref = bf16[1,48,128]{2,1,0:T(8,128)(2,1)S(1)} collective-permute-done((bf16[1,48,128]{2,1,0:T(8,128)(2,1)S(1)}, bf16[1,48,128]{2,1,0:T(8,128)(2,1)S(1)}, u32[]{:S(2)}, u32[]{:S(2)}) %collective-permute-start.7) | collective-permute-done | bytes 12320 | tf_op jit(solution)/shard_map/ppermute | solution.py:23
  20.2 0.0 collective-permute-done.8.keep_in
  20.2 0.7 %shard_map.85 = bf16[1,32,128]{2,1,0:T(8,128)(2,1)} custom-call(bf16[1,48,128]{2,1,0:T(8,128)(2,1)S(1)} %collective-permute-done.7.parcel_ref, bf16[1,48,128]{2,1,0:T(8,128)(2,1)S(1)} %collective-permute-done.8.keep_in), custom_call_target="tpu_custom_call" | custom-call | tf_op jit(solution)/shard_map/pallas_call | solution.py:250
  (1 shorter events, 0.0 us)
Async XLA Ops:
  0.0 11.9 %collective-permute-start.2 = (bf16[1024,128]{1,0:T(8,128)(2,1)}, bf16[1024,128]{1,0:T(8,128)(2,1)S(1)}, u32[]{:S(2)}, u32[]{:S(2)}) collective-permute-start(bf16[1024,128]{1,0:T(8,128)(2,1)} %bitcast.3), channel_id=1, source_target_pairs={{0,2},{1,5},{2,0},{3,7},{4,6},{5,1},{6,4},{7,3},{8,10},{9,13},{10,... | collective-permute-start | bytes 786440 | tf_op jit(solution)/shard_map/ppermute | solution.py:23
  2.9 9.0 %collective-permute-start.3 = (bf16[1024,128]{1,0:T(8,128)(2,1)}, bf16[1024,128]{1,0:T(8,128)(2,1)S(1)}, u32[]{:S(2)}, u32[]{:S(2)}) collective-permute-start(bf16[1024,128]{1,0:T(8,128)(2,1)} %bitcast.5), channel_id=1, source_target_pairs={{0,2},{1,5},{2,0},{3,7},{4,6},{5,1},{6,4},{7,3},{8,10},{9,13},{10,... | collective-permute-start | bytes 786440 | tf_op jit(solution)/shard_map/ppermute | solution.py:23
  3.0 4.3 %collective-permute-start = (bf16[1,32,128]{2,1,0:T(8,128)(2,1)}, bf16[1,32,128]{2,1,0:T(8,128)(2,1)S(1)}, u32[]{:S(2)}, u32[]{:S(2)}) collective-permute-start(bf16[1,32,128]{2,1,0:T(8,128)(2,1)} %param.8), channel_id=1, source_target_pairs={{0,4},{1,3},{2,6},{3,1},{4,0},{5,7},{6,2},{7,5},{8,12},{9,11},{10,... | collective-permute-start | bytes 24584 | tf_op jit(solution)/shard_map/ppermute | solution.py:23
  5.1 6.8 %collective-permute-start.4 = (bf16[384,128]{1,0:T(8,128)(2,1)}, bf16[384,128]{1,0:T(8,128)(2,1)S(1)}, u32[]{:S(2)}, u32[]{:S(2)}) collective-permute-start(bf16[384,128]{1,0:T(8,128)(2,1)} %bitcast.7), channel_id=1, source_target_pairs={{0,2},{1,5},{2,0},{3,7},{4,6},{5,1},{6,4},{7,3},{8,10},{9,13},{10,... | collective-permute-start | bytes 294920 | tf_op jit(solution)/shard_map/ppermute | solution.py:23
  7.3 4.6 %collective-permute-start.1 = (bf16[2,32,128]{2,1,0:T(8,128)(2,1)S(1)}, bf16[2,32,128]{2,1,0:T(8,128)(2,1)S(1)}, u32[]{:S(2)}, u32[]{:S(2)}) collective-permute-start(bf16[2,32,128]{2,1,0:T(8,128)(2,1)S(1)} %constant_dynamic-update-slice_fusion.queries_ref.first_ref), channel_id=1, source_target_pairs={{0,8},{1,9},{2,10},{3,11},{4,12},{5,13},{6,14},{7,15},{8,0},{9,1},... | collective-permute-start | bytes 49160 | tf_op jit(solution)/shard_map/ppermute | solution.py:23
  12.8 3.3 %collective-permute-start.5 = (bf16[2,48,128]{2,1,0:T(8,128)(2,1)S(1)}, bf16[2,48,128]{2,1,0:T(8,128)(2,1)S(1)}, u32[]{:S(2)}, u32[]{:S(2)}) collective-permute-start(bf16[2,48,128]{2,1,0:T(8,128)(2,1)S(1)} %get-tuple-element.19), channel_id=1, source_target_pairs={{0,5},{1,2},{2,7},{3,0},{4,1},{5,6},{6,3},{7,4},{8,13},{9,10},{10,... | collective-permute-start | bytes 73736 | tf_op jit(solution)/shard_map/ppermute | solution.py:23
  14.3 1.8 %collective-permute-start.6 = (bf16[2,48,128]{2,1,0:T(8,128)(2,1)S(1)}, bf16[2,48,128]{2,1,0:T(8,128)(2,1)S(1)}, u32[]{:S(2)}, u32[]{:S(2)}) collective-permute-start(bf16[2,48,128]{2,1,0:T(8,128)(2,1)S(1)} %get-tuple-element.20), channel_id=1, source_target_pairs={{0,1},{1,0},{2,3},{3,2},{4,5},{5,4},{6,7},{7,6},{8,9},{9,8},{10,11... | collective-permute-start | bytes 73736 | tf_op jit(solution)/shard_map/ppermute | solution.py:23
  16.2 4.0 %collective-permute-start.7 = (bf16[1,48,128]{2,1,0:T(8,128)(2,1)S(1)}, bf16[1,48,128]{2,1,0:T(8,128)(2,1)S(1)}, u32[]{:S(2)}, u32[]{:S(2)}) collective-permute-start(bf16[1,48,128]{2,1,0:T(8,128)(2,1)S(1)} %get-tuple-element.21), channel_id=1, source_target_pairs={{0,9},{1,8},{2,11},{3,10},{4,13},{5,12},{6,15},{7,14},{8,1},{9,0},... | collective-permute-start | bytes 36872 | tf_op jit(solution)/shard_map/ppermute | solution.py:23
  18.8 1.4 %collective-permute-start.8 = (bf16[1,48,128]{2,1,0:T(8,128)(2,1)S(1)}, bf16[1,48,128]{2,1,0:T(8,128)(2,1)S(1)}, u32[]{:S(2)}, u32[]{:S(2)}) collective-permute-start(bf16[1,48,128]{2,1,0:T(8,128)(2,1)S(1)} %get-tuple-element.22), channel_id=1, source_target_pairs={{0,1},{1,0},{2,3},{3,2},{4,5},{5,4},{6,7},{7,6},{8,9},{9,8},{10,11... | collective-permute-start | bytes 36872 | tf_op jit(solution)/shard_map/ppermute | solution.py:23

commit v13 on v12

--- a/solution.py
+++ b/solution.py
@@ -57,29 +57,52 @@
     return jnp.concatenate([top_high, top_low, total_high, total_low, blank], axis=0)
 
 
-def suffix_rows(rest_ref, start, slots, page_rows):
-    return jnp.concatenate(
-        [rest_ref[start + s * 2 * page_rows : start + s * 2 * page_rows + page_rows] for s in range(slots)],
-        axis=0,
-    )
+def suffix_rows(pool_ref, start, slots, page_rows, width):
+    rows = [
+        pool_ref[start + s * 2 * page_rows : start + s * 2 * page_rows + page_rows]
+        for s in range(slots)
+    ]
+    if width > slots * page_rows:
+        rows.append(jnp.zeros((width - slots * page_rows, pool_ref.shape[1]), pool_ref.dtype))
+    return jnp.concatenate(rows, axis=0)
+
+
+def fold(function, values, lanes):
+    tiles = [
+        value[:, at : at + lanes] for value in values for at in range(0, value.shape[1], lanes)
+    ]
+    return functools.reduce(function, tiles)
+
+
+def sort_heads(source, wide_ref, goal_ref):
+    heads, tokens, _ = goal_ref.shape
+    wide_ref[...] = source[...].astype(jnp.float32)
+    for g in range(heads):
+        goal_ref[g] = wide_ref[pl.ds(g, tokens, stride=heads), :].astype(goal_ref.dtype)
 
 
 def fetch_kernel(
-    queries_ref, owner_hbm, slot_hbm, len_hbm, request_hbm, *refs, rows_dev, page_len, kv_heads, sources
+    queries_ref, far_key_ref, far_value_ref,
+    owner_hbm, slot_hbm, len_hbm, request_hbm, key_hbm, value_hbm, pool_hbm,
+    far_key_out, far_value_out, key_out, value_out, pool_out, near_ref, far_ref,
+    owner_ref, slot_ref, len_ref, request_ref, key_ref, value_ref, wide_ref, sems,
+    *, rows_dev, page_len, kv_heads,
 ):
     del queries_ref
-    goals = refs[sources : 2 * sources]
-    near_ref, far_ref, owner_ref, slot_ref, len_ref, request_ref, sems = refs[2 * sources :]
     pairs = [
         (owner_hbm, owner_ref),
         (slot_hbm, slot_ref),
         (len_hbm, len_ref),
         (request_hbm, request_ref),
-        *zip(refs[:sources], goals),
+        (key_hbm, key_ref),
+        (value_hbm, value_ref),
+        (pool_hbm, pool_out),
     ]
     copies = [pltpu.make_async_copy(*pair, sems.at[i]) for i, pair in enumerate(pairs)]
     for copy in copies:
         copy.start()
+    sort_heads(far_key_ref, wide_ref.at[0], far_key_out)
+    sort_heads(far_value_ref, wide_ref.at[1], far_value_out)
     for copy in copies[:4]:
         copy.wait()
     blocks = lax.axis_size("blk")
@@ -117,51 +140,57 @@
     loop(near_ref.shape[0], one)
     for copy in copies[4:]:
         copy.wait()
+    sort_heads(key_ref, wide_ref.at[2], key_out)
+    sort_heads(value_ref, wide_ref.at[3], value_out)
 
 
 def attend(query, sides, sizes):
-    kv_heads, group, slots, page_rows, scale = sizes
-    rows = query.shape[0]
-    qheads = kv_heads * group
+    kv_heads, slots, page_rows, scale = sizes
+    rows, head_dim = query.shape
+    share = rows // kv_heads
+
+    def product(left, right):
+        return lax.dot_general(
+            left, right, (((1,), (1,)), ((), ())), preferred_element_type=jnp.float32
+        )
 
     def own_head(width):
         row = lax.broadcasted_iota(jnp.int32, (rows, width), 0)
         column = lax.broadcasted_iota(jnp.int32, (rows, width), 1)
-        return (row % qheads) // group == column % kv_heads
-
-    def scores(key):
-        product = lax.dot_general(
-            query, key, (((1,), (1,)), ((), ())), preferred_element_type=jnp.float32
+        return row // share == column % kv_heads
+
+    def by_head(function):
+        return jnp.concatenate(
+            [function(g, slice(g * share, (g + 1) * share)) for g in range(kv_heads)], axis=0
         )
-        return jnp.where(own_head(key.shape[0]), product, -jnp.inf)
 
     parts = []
     for key_ref, value_ref, pool_ref, mask in sides:
-        page_key = suffix_rows(pool_ref, 0, slots, page_rows)
-        page_value = suffix_rows(pool_ref, page_rows, slots, page_rows)
-        parts.append((scores(key_ref[...]), value_ref[...]))
-        parts.append((scores(page_key) + mask, page_value))
-    top = functools.reduce(jnp.maximum, [jnp.max(score, axis=1, keepdims=True) for score, _ in parts])
+        width = mask.shape[1]
+        page_key = suffix_rows(pool_ref, 0, slots, page_rows, width)
+        page_value = suffix_rows(pool_ref, page_rows, slots, page_rows, width)
+        parts.append((by_head(lambda g, at, ref=key_ref: product(query[at], ref[g])), value_ref, None))
+        page = jnp.where(own_head(width), product(query, page_key), -jnp.inf) + mask
+        parts.append((page, None, page_value))
+    top = jnp.max(
+        fold(jnp.maximum, [part[0] for part in parts], head_dim), axis=1, keepdims=True
+    )
     high, low = split(top)
     point = high + low
-    total = mixed = 0.0
-    for score, value in parts:
-        weight = jnp.exp2((score - point) * scale)
-        total = total + jnp.sum(weight, axis=1, keepdims=True)
-        mixed = mixed + jnp.dot(
-            weight.astype(jnp.bfloat16), value, preferred_element_type=jnp.float32
-        )
+    weights = [jnp.exp2((part[0] - point) * scale) for part in parts]
+    total = jnp.sum(fold(jnp.add, weights, head_dim), axis=1, keepdims=True)
+    mixed = 0.0
+    for weight, (_, value_ref, page_value) in zip(weights, parts):
+        weight = weight.astype(jnp.bfloat16)
+        if page_value is None:
+            mixed = mixed + by_head(
+                lambda g, at, left=weight, ref=value_ref: jnp.dot(
+                    left[at], ref[g], preferred_element_type=jnp.float32
+                )
+            )
+        else:
+            mixed = mixed + jnp.dot(weight, page_value, preferred_element_type=jnp.float32)
     return point, total, mixed / total
-
-
-def chunk_bias(bias_ref, first, count, qheads):
-    return jnp.concatenate(
-        [
-            jnp.broadcast_to(bias_ref[pl.ds(first + j, 1), :], (qheads, bias_ref.shape[1]))
-            for j in range(count)
-        ],
-        axis=0,
-    )
 
 
 def attend_kernel(first_ref, second_ref, *refs, rows_dev, sizes):
@@ -170,32 +199,43 @@
     part = 2 * rows_dev
     diagonal = spread_rows(qheads, head_dim)
 
+    kv_heads = sizes[0]
+    group = qheads // kv_heads
+
     def one(i):
+        taken = [(ref, i * part + j) for ref in (first_ref, second_ref) for j in range(part)]
+        wide = [ref[place].astype(jnp.float32) for ref, place in taken]
         query = jnp.concatenate(
-            [
-                ref[pl.ds(i * part, part)].reshape(part * qheads, head_dim)
-                for ref in (first_ref, second_ref)
-            ],
-            axis=0,
-        )
+            [row[g * group : (g + 1) * group] for g in range(kv_heads) for row in wide], axis=0
+        ).astype(first_ref.dtype)
 
         def mask(ref):
+            rows = [ref[pl.ds(i * part + j, 1), :] for j in range(part)]
+            rows += [ref[pl.ds(half + i * part + j, 1), :] for j in range(part)]
+            block = jnp.concatenate(
+                [jnp.broadcast_to(row, (group, row.shape[1])) for row in rows], axis=0
+            )
+            return jnp.concatenate([block] * kv_heads, axis=0)
+
+        sides = [(*side_refs[j : j + 3], mask(side_refs[j + 3])) for j in (0, 4)]
+        point, total, mixed = attend(query, sides, sizes)
+
+        def of_row(value, j):
+            share = 2 * part * group
             return jnp.concatenate(
                 [
-                    chunk_bias(ref, i * part, part, qheads),
-                    chunk_bias(ref, half + i * part, part, qheads),
+                    value[g * share + j * group : g * share + (j + 1) * group]
+                    for g in range(kv_heads)
                 ],
                 axis=0,
             )
 
-        sides = [(*side_refs[j : j + 3], mask(side_refs[j + 3])) for j in (0, 4)]
-        point, total, mixed = attend(query, sides, sizes)
         for j in range(2 * part):
-            rows = slice(j * qheads, (j + 1) * qheads)
             own, inner = divmod(j % part, rows_dev)
             out_ref = send_ref if own else keep_ref
             out_ref[j // part * (half // 2) + i * rows_dev + inner] = write(
-                mixed[rows], to_row(point[rows], diagonal), to_row(total[rows], diagonal),
+                of_row(mixed, j),
+                to_row(of_row(point, j), diagonal), to_row(of_row(total, j), diagonal),
                 out_ref.dtype,
             )
 
@@ -266,7 +306,7 @@
     prefix_rows = prefix_keys.shape[0] * kv_heads
     page_rows = page_len * kv_heads
     scale = math.log2(math.e) / math.sqrt(head_dim)
-    sizes = (kv_heads, qheads // kv_heads, slots, page_rows, scale)
+    sizes = (kv_heads, slots, page_rows, scale)
     shared_bits = [1 << b for b in range(2, blocks.bit_length() - 1)]
 
     values = prefix_values.reshape(prefix_rows, head_dim)
@@ -284,21 +324,27 @@
 
     tables = (page_owner, page_slot, suffix_len, row_request)
     arrays = (keys, values, pool)
-    mask = jax.ShapeDtypeStruct((2 * half, slots * page_rows), jnp.float32)
-    near_keys, near_values, near_pool, near_mask, far_mask = pl.pallas_call(
+    width = -(-slots * page_rows // head_dim) * head_dim
+    mask = jax.ShapeDtypeStruct((2 * half, width), jnp.float32)
+    sorted_shape = (kv_heads, prefix_rows // kv_heads, head_dim)
+    sorted_heads = jax.ShapeDtypeStruct(sorted_shape, keys.dtype)
+    far_keys, far_values, near_keys, near_values, near_pool, near_mask, far_mask = pl.pallas_call(
         functools.partial(
-            fetch_kernel,
-            rows_dev=rows_dev, page_len=page_len, kv_heads=kv_heads, sources=len(arrays),
+            fetch_kernel, rows_dev=rows_dev, page_len=page_len, kv_heads=kv_heads
         ),
-        out_shape=[jax.ShapeDtypeStruct(array.shape, array.dtype) for array in arrays] + [mask] * 2,
-        in_specs=[pl.BlockSpec(memory_space=pltpu.VMEM)]
+        out_shape=[sorted_heads] * 4 + [jax.ShapeDtypeStruct(pool.shape, pool.dtype)] + [mask] * 2,
+        in_specs=[pl.BlockSpec(memory_space=pltpu.VMEM)] * 3
         + [pl.BlockSpec(memory_space=pltpu.HBM)] * (len(tables) + len(arrays)),
-        out_specs=[pl.BlockSpec(memory_space=pltpu.VMEM)] * (len(arrays) + 2),
+        out_specs=[pl.BlockSpec(memory_space=pltpu.VMEM)] * 7,
         scratch_shapes=[pltpu.SMEM(table.shape, table.dtype) for table in tables]
-        + [pltpu.SemaphoreType.DMA((len(tables) + len(arrays),))],
+        + [pltpu.VMEM(keys.shape, keys.dtype)] * 2
+        + [
+            pltpu.VMEM((4, *keys.shape), jnp.float32),
+            pltpu.SemaphoreType.DMA((len(tables) + len(arrays),)),
+        ],
         compiler_params=pltpu.CompilerParams(vmem_limit_bytes=VMEM_BYTES),
     )(
-        first,
+        first, far_keys, far_values,
         *(pltpu.with_memory_space_constraint(operand, pltpu.HBM) for operand in tables + arrays),
     )
 

time: 21.1 us -> 21 us (level)
  waiting for transfers between devices: 3.15 us -> 2.91 us
    ppermute x9, waiting for transfers between devices: 3.15 us -> 2.91 us  [exchange(): return lax.ppermute(value, ('blk', 'heads'), pairs)]
  transfers between devices with their start and end apart: 9 -> 9, of which waited for: 3 -> 4; matrix products, arithmetic and copies ran while one was open for 3% -> 3% of each run, Pallas kernels for 5% -> 6%
where the time goes in v13:
time: 21 us; the launch traced here: 20.8 us
  starting transfers between devices  14.3 us (68%)
  waiting for transfers between devices  2.91 us (14%)
  Pallas kernels  2.78 us (13%)
  local copies, waits for them, and re-layouts  0.7 us (3%)
    ppermute x9, starting transfers between devices, exchange(): return lax.ppermute(value, ('blk', 'heads'), pairs)  14.3 us
    ppermute x9, waiting for transfers between devices, exchange(): return lax.ppermute(value, ('blk', 'heads'), pairs)  2.91 us
    pallas_call x3, Pallas kernels, call(): pl.pallas_call(functools.partial(kernel, **static), out_shape=outs, in_sp...  1.54 us
    pallas_call x1, Pallas kernels, on_device(): pl.pallas_call(functools.partial(fetch_kernel, rows_dev=rows_dev, page_le...  1.24 us
    unnamed x1, local copies, waits for them, and re-layouts  0.7 us
  transfers between devices with their start and end apart: 9, of which 4 were waited for; matrix products, arithmetic and copies ran while one was open for 3% of the time, Pallas kernels for 6%

profile of v13, /device:TPU:0, one launch (start us, length us, event | category | flops | bytes accessed | tf_op | source)
XLA Modules:
  0.0 20.8 jit_solution(14529869318000415057)
XLA Ops:
  0.0 2.9 %collective-permute-start.2 = (bf16[1024,128]{1,0:T(8,128)(2,1)}, bf16[1024,128]{1,0:T(8,128)(2,1)S(1)}, u32[]{:S(2)}, u32[]{:S(2)}) collective-permute-start(bf16[1024,128]{1,0:T(8,128)(2,1)} %bitcast.3), channel_id=1, source_target_pairs={{0,2},{1,5},{2,0},{3,7},{4,6},{5,1},{6,4},{7,3},{8,10},{9,13},{10,... | collective-permute-start | bytes 786440 | tf_op jit(solution)/shard_map/ppermute | solution.py:23
  2.9 0.0 collective-permute-start.3
  3.0 2.1 %collective-permute-start = (bf16[1,32,128]{2,1,0:T(8,128)(2,1)}, bf16[1,32,128]{2,1,0:T(8,128)(2,1)S(1)}, u32[]{:S(2)}, u32[]{:S(2)}) collective-permute-start(bf16[1,32,128]{2,1,0:T(8,128)(2,1)} %param.8), channel_id=1, source_target_pairs={{0,4},{1,3},{2,6},{3,1},{4,0},{5,7},{6,2},{7,5},{8,12},{9,11},{10,... | collective-permute-start | bytes 24584 | tf_op jit(solution)/shard_map/ppermute | solution.py:23
  5.1 1.5 %collective-permute-start.4 = (bf16[384,128]{1,0:T(8,128)(2,1)}, bf16[384,128]{1,0:T(8,128)(2,1)S(1)}, u32[]{:S(2)}, u32[]{:S(2)}) collective-permute-start(bf16[384,128]{1,0:T(8,128)(2,1)} %bitcast.7), channel_id=1, source_target_pairs={{0,2},{1,5},{2,0},{3,7},{4,6},{5,1},{6,4},{7,3},{8,10},{9,13},{10,... | collective-permute-start | bytes 294920 | tf_op jit(solution)/shard_map/ppermute | solution.py:23
  6.5 0.7 %constant_dynamic-update-slice_fusion.1 = bf16[2,32,128]{2,1,0:T(8,128)(2,1)S(1)} fusion(bf16[1,32,128]{2,1,0:T(8,128)(2,1)} %param.8), kind=kLoop, calls=%fused_computation.1 | loop fusion | bytes 16384
  7.2 0.0 collective-permute-done
  7.3 2.8 %collective-permute-start.1 = (bf16[2,32,128]{2,1,0:T(8,128)(2,1)S(1)}, bf16[2,32,128]{2,1,0:T(8,128)(2,1)S(1)}, u32[]{:S(2)}, u32[]{:S(2)}) collective-permute-start(bf16[2,32,128]{2,1,0:T(8,128)(2,1)S(1)} %constant_dynamic-update-slice_fusion.queries_ref.first_ref), channel_id=1, source_target_pairs={{0,8},{1,9},{2,10},{3,11},{4,12},{5,13},{6,14},{7,15},{8,0},{9,1},... | collective-permute-start | bytes 49160 | tf_op jit(solution)/shard_map/ppermute | solution.py:23
  10.1 0.0 collective-permute-done.2.far_key_ref
  10.1 0.3 %collective-permute-done.3.far_value_ref = bf16[1024,128]{1,0:T(8,128)(2,1)S(1)} collective-permute-done((bf16[1024,128]{1,0:T(8,128)(2,1)}, bf16[1024,128]{1,0:T(8,128)(2,1)S(1)}, u32[]{:S(2)}, u32[]{:S(2)}) %collective-permute-start.3) | collective-permute-done | bytes 262176 | tf_op jit(solution)/shard_map/ppermute | solution.py:23
  10.4 1.2 %shard_map.82 = (bf16[4,256,128]{2,1,0:T(8,128)(2,1)S(1)}, bf16[4,256,128]{2,1,0:T(8,128)(2,1)S(1)}, bf16[4,256,128]{2,1,0:T(8,128)(2,1)S(1)}, bf16[4,256,128]{2...) custom-call(bf16[2,32,128]{2,1,0:T(8,128)(2,1)S(1)} %constant_dynamic-update-slice_, ...), custom_call_target="tpu_custom_call" | custom-call | tf_op jit(solution)/shard_map/pallas_call | solution.py:331
  11.6 0.2 %collective-permute-done.1.second_ref = bf16[2,32,128]{2,1,0:T(8,128)(2,1)S(1)} collective-permute-done((bf16[2,32,128]{2,1,0:T(8,128)(2,1)S(1)}, bf16[2,32,128]{2,1,0:T(8,128)(2,1)S(1)}, u32[]{:S(2)}, u32[]{:S(2)}) %collective-permute-start.1) | collective-permute-done | bytes 16416 | tf_op jit(solution)/shard_map/ppermute | solution.py:23
  11.9 0.0 collective-permute-done.4.refs_6_
  11.9 0.7 %shard_map.83 = (bf16[2,48,128]{2,1,0:T(8,128)(2,1)S(1)}, bf16[2,48,128]{2,1,0:T(8,128)(2,1)S(1)}) custom-call(bf16[2,32,128]{2,1,0:T(8,128)(2,1)S(1)} %constant_dynamic-update-slice_fusion.queries_ref.first_ref, bf16[2,32,128]{2,1,0:T(8,128)(2,1)S(1)} %collective-permute-done.1.second_ref, bf16[4,256,128]{2,1,0:T(8,128)(2,1)S(1)} %get-tuple-element.16.refs_0_, ...), custom_call_target="tpu_custom_call" | custom-call | tf_op jit(solution)/shard_map/pallas_call | solution.py:290
  12.6 1.5 %collective-permute-start.5 = (bf16[2,48,128]{2,1,0:T(8,128)(2,1)S(1)}, bf16[2,48,128]{2,1,0:T(8,128)(2,1)S(1)}, u32[]{:S(2)}, u32[]{:S(2)}) collective-permute-start(bf16[2,48,128]{2,1,0:T(8,128)(2,1)S(1)} %get-tuple-element.23), channel_id=1, source_target_pairs={{0,5},{1,2},{2,7},{3,0},{4,1},{5,6},{6,3},{7,4},{8,13},{9,10},{10,... | collective-permute-start | bytes 73736 | tf_op jit(solution)/shard_map/ppermute | solution.py:23
  14.1 0.5 %collective-permute-start.6 = (bf16[2,48,128]{2,1,0:T(8,128)(2,1)S(1)}, bf16[2,48,128]{2,1,0:T(8,128)(2,1)S(1)}, u32[]{:S(2)}, u32[]{:S(2)}) collective-permute-start(bf16[2,48,128]{2,1,0:T(8,128)(2,1)S(1)} %get-tuple-element.24), channel_id=1, source_target_pairs={{0,1},{1,0},{2,3},{3,2},{4,5},{5,4},{6,7},{7,6},{8,9},{9,8},{10,11... | collective-permute-start | bytes 73736 | tf_op jit(solution)/shard_map/ppermute | solution.py:23
  14.6 1.3 %collective-permute-done.5.parcel_ref = bf16[2,48,128]{2,1,0:T(8,128)(2,1)S(1)} collective-permute-done((bf16[2,48,128]{2,1,0:T(8,128)(2,1)S(1)}, bf16[2,48,128]{2,1,0:T(8,128)(2,1)S(1)}, u32[]{:S(2)}, u32[]{:S(2)}) %collective-permute-start.5) | collective-permute-done | bytes 24608 | tf_op jit(solution)/shard_map/ppermute | solution.py:23
  15.9 0.0 collective-permute-done.6.keep_in
  15.9 0.1 shard_map.84
  16.0 2.6 %collective-permute-start.7 = (bf16[1,48,128]{2,1,0:T(8,128)(2,1)S(1)}, bf16[1,48,128]{2,1,0:T(8,128)(2,1)S(1)}, u32[]{:S(2)}, u32[]{:S(2)}) collective-permute-start(bf16[1,48,128]{2,1,0:T(8,128)(2,1)S(1)} %get-tuple-element.25), channel_id=1, source_target_pairs={{0,9},{1,8},{2,11},{3,10},{4,13},{5,12},{6,15},{7,14},{8,1},{9,0},... | collective-permute-start | bytes 36872 | tf_op jit(solution)/shard_map/ppermute | solution.py:23
  18.7 0.4 %collective-permute-start.8 = (bf16[1,48,128]{2,1,0:T(8,128)(2,1)S(1)}, bf16[1,48,128]{2,1,0:T(8,128)(2,1)S(1)}, u32[]{:S(2)}, u32[]{:S(2)}) collective-permute-start(bf16[1,48,128]{2,1,0:T(8,128)(2,1)S(1)} %get-tuple-element.26), channel_id=1, source_target_pairs={{0,1},{1,0},{2,3},{3,2},{4,5},{5,4},{6,7},{7,6},{8,9},{9,8},{10,11... | collective-permute-start | bytes 36872 | tf_op jit(solution)/shard_map/ppermute | solution.py:23
  19.0 1.0 %collective-permute-done.7.parcel_ref = bf16[1,48,128]{2,1,0:T(8,128)(2,1)S(1)} collective-permute-done((bf16[1,48,128]{2,1,0:T(8,128)(2,1)S(1)}, bf16[1,48,128]{2,1,0:T(8,128)(2,1)S(1)}, u32[]{:S(2)}, u32[]{:S(2)}) %collective-permute-start.7) | collective-permute-done | bytes 12320 | tf_op jit(solution)/shard_map/ppermute | solution.py:23
  20.1 0.0 collective-permute-done.8.keep_in
  20.1 0.7 %shard_map.85 = bf16[1,32,128]{2,1,0:T(8,128)(2,1)} custom-call(bf16[1,48,128]{2,1,0:T(8,128)(2,1)S(1)} %collective-permute-done.7.parcel_ref, bf16[1,48,128]{2,1,0:T(8,128)(2,1)S(1)} %collective-permute-done.8.keep_in), custom_call_target="tpu_custom_call" | custom-call | tf_op jit(solution)/shard_map/pallas_call | solution.py:290
  (1 shorter events, 0.0 us)
Async XLA Ops:
  0.0 10.1 %collective-permute-start.2 = (bf16[1024,128]{1,0:T(8,128)(2,1)}, bf16[1024,128]{1,0:T(8,128)(2,1)S(1)}, u32[]{:S(2)}, u32[]{:S(2)}) collective-permute-start(bf16[1024,128]{1,0:T(8,128)(2,1)} %bitcast.3), channel_id=1, source_target_pairs={{0,2},{1,5},{2,0},{3,7},{4,6},{5,1},{6,4},{7,3},{8,10},{9,13},{10,... | collective-permute-start | bytes 786440 | tf_op jit(solution)/shard_map/ppermute | solution.py:23
  2.9 7.5 %collective-permute-start.3 = (bf16[1024,128]{1,0:T(8,128)(2,1)}, bf16[1024,128]{1,0:T(8,128)(2,1)S(1)}, u32[]{:S(2)}, u32[]{:S(2)}) collective-permute-start(bf16[1024,128]{1,0:T(8,128)(2,1)} %bitcast.5), channel_id=1, source_target_pairs={{0,2},{1,5},{2,0},{3,7},{4,6},{5,1},{6,4},{7,3},{8,10},{9,13},{10,... | collective-permute-start | bytes 786440 | tf_op jit(solution)/shard_map/ppermute | solution.py:23
  3.0 4.3 %collective-permute-start = (bf16[1,32,128]{2,1,0:T(8,128)(2,1)}, bf16[1,32,128]{2,1,0:T(8,128)(2,1)S(1)}, u32[]{:S(2)}, u32[]{:S(2)}) collective-permute-start(bf16[1,32,128]{2,1,0:T(8,128)(2,1)} %param.8), channel_id=1, source_target_pairs={{0,4},{1,3},{2,6},{3,1},{4,0},{5,7},{6,2},{7,5},{8,12},{9,11},{10,... | collective-permute-start | bytes 24584 | tf_op jit(solution)/shard_map/ppermute | solution.py:23
  5.1 6.8 %collective-permute-start.4 = (bf16[384,128]{1,0:T(8,128)(2,1)}, bf16[384,128]{1,0:T(8,128)(2,1)S(1)}, u32[]{:S(2)}, u32[]{:S(2)}) collective-permute-start(bf16[384,128]{1,0:T(8,128)(2,1)} %bitcast.7), channel_id=1, source_target_pairs={{0,2},{1,5},{2,0},{3,7},{4,6},{5,1},{6,4},{7,3},{8,10},{9,13},{10,... | collective-permute-start | bytes 294920 | tf_op jit(solution)/shard_map/ppermute | solution.py:23
  7.3 4.6 %collective-permute-start.1 = (bf16[2,32,128]{2,1,0:T(8,128)(2,1)S(1)}, bf16[2,32,128]{2,1,0:T(8,128)(2,1)S(1)}, u32[]{:S(2)}, u32[]{:S(2)}) collective-permute-start(bf16[2,32,128]{2,1,0:T(8,128)(2,1)S(1)} %constant_dynamic-update-slice_fusion.queries_ref.first_ref), channel_id=1, source_target_pairs={{0,8},{1,9},{2,10},{3,11},{4,12},{5,13},{6,14},{7,15},{8,0},{9,1},... | collective-permute-start | bytes 49160 | tf_op jit(solution)/shard_map/ppermute | solution.py:23
  12.6 3.3 %collective-permute-start.5 = (bf16[2,48,128]{2,1,0:T(8,128)(2,1)S(1)}, bf16[2,48,128]{2,1,0:T(8,128)(2,1)S(1)}, u32[]{:S(2)}, u32[]{:S(2)}) collective-permute-start(bf16[2,48,128]{2,1,0:T(8,128)(2,1)S(1)} %get-tuple-element.23), channel_id=1, source_target_pairs={{0,5},{1,2},{2,7},{3,0},{4,1},{5,6},{6,3},{7,4},{8,13},{9,10},{10,... | collective-permute-start | bytes 73736 | tf_op jit(solution)/shard_map/ppermute | solution.py:23
  14.1 1.8 %collective-permute-start.6 = (bf16[2,48,128]{2,1,0:T(8,128)(2,1)S(1)}, bf16[2,48,128]{2,1,0:T(8,128)(2,1)S(1)}, u32[]{:S(2)}, u32[]{:S(2)}) collective-permute-start(bf16[2,48,128]{2,1,0:T(8,128)(2,1)S(1)} %get-tuple-element.24), channel_id=1, source_target_pairs={{0,1},{1,0},{2,3},{3,2},{4,5},{5,4},{6,7},{7,6},{8,9},{9,8},{10,11... | collective-permute-start | bytes 73736 | tf_op jit(solution)/shard_map/ppermute | solution.py:23
  16.0 4.0 %collective-permute-start.7 = (bf16[1,48,128]{2,1,0:T(8,128)(2,1)S(1)}, bf16[1,48,128]{2,1,0:T(8,128)(2,1)S(1)}, u32[]{:S(2)}, u32[]{:S(2)}) collective-permute-start(bf16[1,48,128]{2,1,0:T(8,128)(2,1)S(1)} %get-tuple-element.25), channel_id=1, source_target_pairs={{0,9},{1,8},{2,11},{3,10},{4,13},{5,12},{6,15},{7,14},{8,1},{9,0},... | collective-permute-start | bytes 36872 | tf_op jit(solution)/shard_map/ppermute | solution.py:23
  18.7 1.4 %collective-permute-start.8 = (bf16[1,48,128]{2,1,0:T(8,128)(2,1)S(1)}, bf16[1,48,128]{2,1,0:T(8,128)(2,1)S(1)}, u32[]{:S(2)}, u32[]{:S(2)}) collective-permute-start(bf16[1,48,128]{2,1,0:T(8,128)(2,1)S(1)} %get-tuple-element.26), channel_id=1, source_target_pairs={{0,1},{1,0},{2,3},{3,2},{4,5},{5,4},{6,7},{7,6},{8,9},{9,8},{10,11... | collective-permute-start | bytes 36872 | tf_op jit(solution)/shard_map/ppermute | solution.py:23

commit v14 on v13

--- a/solution.py
+++ b/solution.py
@@ -45,26 +45,29 @@
     return jnp.sum(jnp.where(diagonal, row, 0.0), axis=1, keepdims=True)
 
 
-def split(value):
-    high = value.astype(jnp.bfloat16).astype(jnp.float32)
-    return high, (value - high).astype(jnp.bfloat16).astype(jnp.float32)
+def split(value, pieces):
+    found = []
+    for _ in range(pieces):
+        found.append(value.astype(jnp.bfloat16).astype(jnp.float32))
+        value = value - found[-1]
+    return found
 
 
 def stat_block(top_row, total_row):
-    top_high, top_low = split(top_row)
-    total_high, total_low = split(total_row)
-    blank = jnp.zeros((STAT_ROWS - 4, top_row.shape[1]), jnp.float32)
-    return jnp.concatenate([top_high, top_low, total_high, total_low, blank], axis=0)
-
-
-def suffix_rows(pool_ref, start, slots, page_rows, width):
-    rows = [
-        pool_ref[start + s * 2 * page_rows : start + s * 2 * page_rows + page_rows]
-        for s in range(slots)
-    ]
-    if width > slots * page_rows:
-        rows.append(jnp.zeros((width - slots * page_rows, pool_ref.shape[1]), pool_ref.dtype))
-    return jnp.concatenate(rows, axis=0)
+    rows = split(top_row, 3) + split(total_row, 2)
+    blank = jnp.zeros((STAT_ROWS - len(rows), top_row.shape[1]), jnp.float32)
+    return jnp.concatenate([*rows, blank], axis=0)
+
+
+def suffix_rows(pool_refs, start, page_rows):
+    return jnp.concatenate(
+        [
+            pool_ref[at + start : at + start + page_rows]
+            for pool_ref in pool_refs
+            for at in range(0, pool_ref.shape[0], 2 * page_rows)
+        ],
+        axis=0,
+    )
 
 
 def fold(function, values, lanes):
@@ -84,7 +87,7 @@
 def fetch_kernel(
     queries_ref, far_key_ref, far_value_ref,
     owner_hbm, slot_hbm, len_hbm, request_hbm, key_hbm, value_hbm, pool_hbm,
-    far_key_out, far_value_out, key_out, value_out, pool_out, near_ref, far_ref,
+    far_key_out, far_value_out, key_out, value_out, pool_out, mask_ref,
     owner_ref, slot_ref, len_ref, request_ref, key_ref, value_ref, wide_ref, sems,
     *, rows_dev, page_len, kv_heads,
 ):
@@ -109,7 +112,7 @@
     me = lax.axis_index("blk")
     odd_core = lax.axis_index("heads") % 2
     query_bit, key_bit = 2 - odd_core, 1 + odd_core
-    width = near_ref.shape[1]
+    width = mask_ref.shape[1]
     all_rows = request_ref.shape[0]
     column = lax.broadcasted_iota(jnp.int32, (1, width), 1)
 
@@ -129,23 +132,23 @@
         else:
             later = lax.fori_loop(0, all_rows, count, jnp.int32(0))
         limit = len_ref[request] - later
-        for holder, out_ref in ((me, near_ref), (me ^ key_bit, far_ref)):
+        visible = column < 0
+        for holder, start in ((me, 0), (me ^ key_bit, width // 2)):
             page = lax.rem(holder - owner_ref[request, 0] + blocks, blocks)
             shown = jnp.clip(limit - page * page_len, 0, page_len) * kv_heads
-            first = slot_ref[request, page] * (page_len * kv_heads)
-            out_ref[pl.ds(i, 1), :] = jnp.where(
-                (column >= first) & (column < first + shown), 0.0, -jnp.inf
-            )
-
-    loop(near_ref.shape[0], one)
+            first = start + slot_ref[request, page] * (page_len * kv_heads)
+            visible = visible | ((column >= first) & (column < first + shown))
+        mask_ref[pl.ds(i, 1), :] = jnp.where(visible, 0.0, -jnp.inf)
+
+    loop(mask_ref.shape[0], one)
     for copy in copies[4:]:
         copy.wait()
     sort_heads(key_ref, wide_ref.at[2], key_out)
     sort_heads(value_ref, wide_ref.at[3], value_out)
 
 
-def attend(query, sides, sizes):
-    kv_heads, slots, page_rows, scale = sizes
+def attend(query, sides, pool_refs, mask, sizes):
+    kv_heads, page_rows, scale = sizes
     rows, head_dim = query.shape
     share = rows // kv_heads
 
@@ -164,20 +167,17 @@
             [function(g, slice(g * share, (g + 1) * share)) for g in range(kv_heads)], axis=0
         )
 
-    parts = []
-    for key_ref, value_ref, pool_ref, mask in sides:
-        width = mask.shape[1]
-        page_key = suffix_rows(pool_ref, 0, slots, page_rows, width)
-        page_value = suffix_rows(pool_ref, page_rows, slots, page_rows, width)
-        parts.append((by_head(lambda g, at, ref=key_ref: product(query[at], ref[g])), value_ref, None))
-        page = jnp.where(own_head(width), product(query, page_key), -jnp.inf) + mask
-        parts.append((page, None, page_value))
+    parts = [
+        (by_head(lambda g, at, ref=key_ref: product(query[at], ref[g])), value_ref, None)
+        for key_ref, value_ref in sides
+    ]
+    page = product(query, suffix_rows(pool_refs, 0, page_rows))
+    page = jnp.where(own_head(page.shape[1]), page, -jnp.inf) + mask
+    parts.append((page, None, suffix_rows(pool_refs, page_rows, page_rows)))
     top = jnp.max(
         fold(jnp.maximum, [part[0] for part in parts], head_dim), axis=1, keepdims=True
     )
-    high, low = split(top)
-    point = high + low
-    weights = [jnp.exp2((part[0] - point) * scale) for part in parts]
+    weights = [jnp.exp2((part[0] - top) * scale) for part in parts]
     total = jnp.sum(fold(jnp.add, weights, head_dim), axis=1, keepdims=True)
     mixed = 0.0
     for weight, (_, value_ref, page_value) in zip(weights, parts):
@@ -190,11 +190,13 @@
             )
         else:
             mixed = mixed + jnp.dot(weight, page_value, preferred_element_type=jnp.float32)
-    return point, total, mixed / total
-
-
-def attend_kernel(first_ref, second_ref, *refs, rows_dev, sizes):
-    *side_refs, send_ref, keep_ref = refs
+    return top, total, mixed * (1.0 / total)
+
+
+def attend_kernel(
+    first_ref, second_ref, near_key_ref, near_value_ref, near_pool_ref,
+    far_key_ref, far_value_ref, far_pool_ref, mask_ref, send_ref, keep_ref, *, rows_dev, sizes
+):
     half, qheads, head_dim = first_ref.shape
     part = 2 * rows_dev
     diagonal = spread_rows(qheads, head_dim)
@@ -209,16 +211,15 @@
             [row[g * group : (g + 1) * group] for g in range(kv_heads) for row in wide], axis=0
         ).astype(first_ref.dtype)
 
-        def mask(ref):
-            rows = [ref[pl.ds(i * part + j, 1), :] for j in range(part)]
-            rows += [ref[pl.ds(half + i * part + j, 1), :] for j in range(part)]
-            block = jnp.concatenate(
-                [jnp.broadcast_to(row, (group, row.shape[1])) for row in rows], axis=0
-            )
-            return jnp.concatenate([block] * kv_heads, axis=0)
-
-        sides = [(*side_refs[j : j + 3], mask(side_refs[j + 3])) for j in (0, 4)]
-        point, total, mixed = attend(query, sides, sizes)
+        places = [i * part + j for j in range(part)] + [half + i * part + j for j in range(part)]
+        masks = [mask_ref[pl.ds(place, 1), :] for place in places]
+        block = jnp.concatenate(
+            [jnp.broadcast_to(row, (group, row.shape[1])) for row in masks], axis=0
+        )
+        point, total, mixed = attend(
+            query, ((near_key_ref, near_value_ref), (far_key_ref, far_value_ref)),
+            (near_pool_ref, far_pool_ref), jnp.concatenate([block] * kv_heads, axis=0), sizes,
+        )
 
         def of_row(value, j):
             share = 2 * part * group
@@ -246,7 +247,7 @@
     parcel = parcel.astype(jnp.float32)
     qheads = parcel.shape[0] - STAT_ROWS
     stats = parcel[qheads:]
-    return parcel[:qheads], stats[0:1] + stats[1:2], stats[2:3] + stats[3:4]
+    return parcel[:qheads], stats[0:1] + stats[1:2] + stats[2:3], stats[3:4] + stats[4:5]
 
 
 def write(mixed, top, total, dtype):
@@ -306,7 +307,7 @@
     prefix_rows = prefix_keys.shape[0] * kv_heads
     page_rows = page_len * kv_heads
     scale = math.log2(math.e) / math.sqrt(head_dim)
-    sizes = (kv_heads, slots, page_rows, scale)
+    sizes = (kv_heads, page_rows, scale)
     shared_bits = [1 << b for b in range(2, blocks.bit_length() - 1)]
 
     values = prefix_values.reshape(prefix_rows, head_dim)
@@ -324,18 +325,17 @@
 
     tables = (page_owner, page_slot, suffix_len, row_request)
     arrays = (keys, values, pool)
-    width = -(-slots * page_rows // head_dim) * head_dim
-    mask = jax.ShapeDtypeStruct((2 * half, width), jnp.float32)
+    mask = jax.ShapeDtypeStruct((2 * half, pool.shape[0]), jnp.float32)
     sorted_shape = (kv_heads, prefix_rows // kv_heads, head_dim)
     sorted_heads = jax.ShapeDtypeStruct(sorted_shape, keys.dtype)
-    far_keys, far_values, near_keys, near_values, near_pool, near_mask, far_mask = pl.pallas_call(
+    far_keys, far_values, near_keys, near_values, near_pool, near_and_far = pl.pallas_call(
         functools.partial(
             fetch_kernel, rows_dev=rows_dev, page_len=page_len, kv_heads=kv_heads
         ),
-        out_shape=[sorted_heads] * 4 + [jax.ShapeDtypeStruct(pool.shape, pool.dtype)] + [mask] * 2,
+        out_shape=[sorted_heads] * 4 + [jax.ShapeDtypeStruct(pool.shape, pool.dtype), mask],
         in_specs=[pl.BlockSpec(memory_space=pltpu.VMEM)] * 3
         + [pl.BlockSpec(memory_space=pltpu.HBM)] * (len(tables) + len(arrays)),
-        out_specs=[pl.BlockSpec(memory_space=pltpu.VMEM)] * 7,
+        out_specs=[pl.BlockSpec(memory_space=pltpu.VMEM)] * 6,
         scratch_shapes=[pltpu.SMEM(table.shape, table.dtype) for table in tables]
         + [pltpu.VMEM(keys.shape, keys.dtype)] * 2
         + [
@@ -355,8 +355,8 @@
     send, keep = call(
         attend_kernel, parcels(half),
         (
-            first, second, near_keys, near_values, near_pool, near_mask,
-            far_keys, far_values, far_pool, far_mask,
+            first, second, near_keys, near_values, near_pool,
+            far_keys, far_values, far_pool, near_and_far,
         ),
         rows_dev=rows_dev, sizes=sizes,
     )

time: 21 us -> 21 us (level)
  no operation moved by 1% of the time
where the time goes in v14:
time: 21 us; the launch traced here: 20.7 us
  starting transfers between devices  14.3 us (68%)
  waiting for transfers between devices  2.91 us (14%)
  Pallas kernels  2.77 us (13%)
  local copies, waits for them, and re-layouts  0.7 us (3%)
    ppermute x9, starting transfers between devices, exchange(): return lax.ppermute(value, ('blk', 'heads'), pairs)  14.3 us
    ppermute x9, waiting for transfers between devices, exchange(): return lax.ppermute(value, ('blk', 'heads'), pairs)  2.91 us
    pallas_call x3, Pallas kernels, call(): pl.pallas_call(functools.partial(kernel, **static), out_shape=outs, in_sp...  1.52 us
    pallas_call x1, Pallas kernels, on_device(): pl.pallas_call(functools.partial(fetch_kernel, rows_dev=rows_dev, page_le...  1.24 us
    unnamed x1, local copies, waits for them, and re-layouts  0.7 us
  transfers between devices with their start and end apart: 9, of which 4 were waited for; matrix products, arithmetic and copies ran while one was open for 3% of the time, Pallas kernels for 6%

profile of v14, /device:TPU:0, one launch (start us, length us, event | category | flops | bytes accessed | tf_op | source)
XLA Modules:
  0.0 20.7 jit_solution(3278153404976453273)
XLA Ops:
  0.0 2.9 %collective-permute-start.2 = (bf16[1024,128]{1,0:T(8,128)(2,1)}, bf16[1024,128]{1,0:T(8,128)(2,1)S(1)}, u32[]{:S(2)}, u32[]{:S(2)}) collective-permute-start(bf16[1024,128]{1,0:T(8,128)(2,1)} %bitcast.3), channel_id=1, source_target_pairs={{0,2},{1,5},{2,0},{3,7},{4,6},{5,1},{6,4},{7,3},{8,10},{9,13},{10,... | collective-permute-start | bytes 786440 | tf_op jit(solution)/shard_map/ppermute | solution.py:23
  2.9 0.0 collective-permute-start.3
  3.0 2.1 %collective-permute-start = (bf16[1,32,128]{2,1,0:T(8,128)(2,1)}, bf16[1,32,128]{2,1,0:T(8,128)(2,1)S(1)}, u32[]{:S(2)}, u32[]{:S(2)}) collective-permute-start(bf16[1,32,128]{2,1,0:T(8,128)(2,1)} %param.8), channel_id=1, source_target_pairs={{0,4},{1,3},{2,6},{3,1},{4,0},{5,7},{6,2},{7,5},{8,12},{9,11},{10,... | collective-permute-start | bytes 24584 | tf_op jit(solution)/shard_map/ppermute | solution.py:23
  5.1 1.5 %collective-permute-start.4 = (bf16[384,128]{1,0:T(8,128)(2,1)}, bf16[384,128]{1,0:T(8,128)(2,1)S(1)}, u32[]{:S(2)}, u32[]{:S(2)}) collective-permute-start(bf16[384,128]{1,0:T(8,128)(2,1)} %bitcast.7), channel_id=1, source_target_pairs={{0,2},{1,5},{2,0},{3,7},{4,6},{5,1},{6,4},{7,3},{8,10},{9,13},{10,... | collective-permute-start | bytes 294920 | tf_op jit(solution)/shard_map/ppermute | solution.py:23
  6.5 0.7 %constant_dynamic-update-slice_fusion.1 = bf16[2,32,128]{2,1,0:T(8,128)(2,1)S(1)} fusion(bf16[1,32,128]{2,1,0:T(8,128)(2,1)} %param.8), kind=kLoop, calls=%fused_computation.1 | loop fusion | bytes 16384
  7.2 0.0 collective-permute-done
  7.3 2.8 %collective-permute-start.1 = (bf16[2,32,128]{2,1,0:T(8,128)(2,1)S(1)}, bf16[2,32,128]{2,1,0:T(8,128)(2,1)S(1)}, u32[]{:S(2)}, u32[]{:S(2)}) collective-permute-start(bf16[2,32,128]{2,1,0:T(8,128)(2,1)S(1)} %constant_dynamic-update-slice_fusion.queries_ref.first_ref), channel_id=1, source_target_pairs={{0,8},{1,9},{2,10},{3,11},{4,12},{5,13},{6,14},{7,15},{8,0},{9,1},... | collective-permute-start | bytes 49160 | tf_op jit(solution)/shard_map/ppermute | solution.py:23
  10.1 0.0 collective-permute-done.2.far_key_ref
  10.1 0.3 %collective-permute-done.3.far_value_ref = bf16[1024,128]{1,0:T(8,128)(2,1)S(1)} collective-permute-done((bf16[1024,128]{1,0:T(8,128)(2,1)}, bf16[1024,128]{1,0:T(8,128)(2,1)S(1)}, u32[]{:S(2)}, u32[]{:S(2)}) %collective-permute-start.3) | collective-permute-done | bytes 262176 | tf_op jit(solution)/shard_map/ppermute | solution.py:23
  10.4 1.2 %shard_map.82 = (bf16[4,256,128]{2,1,0:T(8,128)(2,1)S(1)}, bf16[4,256,128]{2,1,0:T(8,128)(2,1)S(1)}, bf16[4,256,128]{2,1,0:T(8,128)(2,1)S(1)}, bf16[4,256,128]{2...) custom-call(bf16[2,32,128]{2,1,0:T(8,128)(2,1)S(1)} %constant_dynamic-update-slice_fusion.queries_ref.first_ref, ...), custom_call_target="tpu_custom_call" | custom-call | tf_op jit(solution)/shard_map/pallas_call | solution.py:331
  11.6 0.2 %collective-permute-done.1.second_ref = bf16[2,32,128]{2,1,0:T(8,128)(2,1)S(1)} collective-permute-done((bf16[2,32,128]{2,1,0:T(8,128)(2,1)S(1)}, bf16[2,32,128]{2,1,0:T(8,128)(2,1)S(1)}, u32[]{:S(2)}, u32[]{:S(2)}) %collective-permute-start.1) | collective-permute-done | bytes 16416 | tf_op jit(solution)/shard_map/ppermute | solution.py:23
  11.9 0.0 collective-permute-done.4.far_pool_ref
  11.9 0.7 %shard_map.83 = (bf16[2,48,128]{2,1,0:T(8,128)(2,1)S(1)}, bf16[2,48,128]{2,1,0:T(8,128)(2,1)S(1)}) custom-call(bf16[2,32,128]{2,1,0:T(8,128)(2,1)S(1)} %constant_dynamic-update-slice_fusion.queries_ref.first_ref, bf16[2,32,128]{2,1,0:T(8,128)(2,1)S(1)} %collective-permute-done.1.second_ref, bf16[4,256,128]{2,1,0:T(8,128)(2,1)S(1)} %get-tuple-element.15.near_key_ref, ...), custom_call_target="tpu_custom_call" | custom-call | tf_op jit(solution)/shard_map/pallas_call | solution.py:291
  12.6 1.5 %collective-permute-start.5 = (bf16[2,48,128]{2,1,0:T(8,128)(2,1)S(1)}, bf16[2,48,128]{2,1,0:T(8,128)(2,1)S(1)}, u32[]{:S(2)}, u32[]{:S(2)}) collective-permute-start(bf16[2,48,128]{2,1,0:T(8,128)(2,1)S(1)} %get-tuple-element.21), channel_id=1, source_target_pairs={{0,5},{1,2},{2,7},{3,0},{4,1},{5,6},{6,3},{7,4},{8,13},{9,10},{10,... | collective-permute-start | bytes 73736 | tf_op jit(solution)/shard_map/ppermute | solution.py:23
  14.1 0.5 %collective-permute-start.6 = (bf16[2,48,128]{2,1,0:T(8,128)(2,1)S(1)}, bf16[2,48,128]{2,1,0:T(8,128)(2,1)S(1)}, u32[]{:S(2)}, u32[]{:S(2)}) collective-permute-start(bf16[2,48,128]{2,1,0:T(8,128)(2,1)S(1)} %get-tuple-element.22), channel_id=1, source_target_pairs={{0,1},{1,0},{2,3},{3,2},{4,5},{5,4},{6,7},{7,6},{8,9},{9,8},{10,11... | collective-permute-start | bytes 73736 | tf_op jit(solution)/shard_map/ppermute | solution.py:23
  14.6 1.3 %collective-permute-done.5.parcel_ref = bf16[2,48,128]{2,1,0:T(8,128)(2,1)S(1)} collective-permute-done((bf16[2,48,128]{2,1,0:T(8,128)(2,1)S(1)}, bf16[2,48,128]{2,1,0:T(8,128)(2,1)S(1)}, u32[]{:S(2)}, u32[]{:S(2)}) %collective-permute-start.5) | collective-permute-done | bytes 24608 | tf_op jit(solution)/shard_map/ppermute | solution.py:23
  15.9 0.0 collective-permute-done.6.keep_in
  15.9 0.1 shard_map.84
  16.0 2.6 %collective-permute-start.7 = (bf16[1,48,128]{2,1,0:T(8,128)(2,1)S(1)}, bf16[1,48,128]{2,1,0:T(8,128)(2,1)S(1)}, u32[]{:S(2)}, u32[]{:S(2)}) collective-permute-start(bf16[1,48,128]{2,1,0:T(8,128)(2,1)S(1)} %get-tuple-element.23), channel_id=1, source_target_pairs={{0,9},{1,8},{2,11},{3,10},{4,13},{5,12},{6,15},{7,14},{8,1},{9,0},... | collective-permute-start | bytes 36872 | tf_op jit(solution)/shard_map/ppermute | solution.py:23
  18.6 0.4 %collective-permute-start.8 = (bf16[1,48,128]{2,1,0:T(8,128)(2,1)S(1)}, bf16[1,48,128]{2,1,0:T(8,128)(2,1)S(1)}, u32[]{:S(2)}, u32[]{:S(2)}) collective-permute-start(bf16[1,48,128]{2,1,0:T(8,128)(2,1)S(1)} %get-tuple-element.24), channel_id=1, source_target_pairs={{0,1},{1,0},{2,3},{3,2},{4,5},{5,4},{6,7},{7,6},{8,9},{9,8},{10,11... | collective-permute-start | bytes 36872 | tf_op jit(solution)/shard_map/ppermute | solution.py:23
  19.0 1.0 %collective-permute-done.7.parcel_ref = bf16[1,48,128]{2,1,0:T(8,128)(2,1)S(1)} collective-permute-done((bf16[1,48,128]{2,1,0:T(8,128)(2,1)S(1)}, bf16[1,48,128]{2,1,0:T(8,128)(2,1)S(1)}, u32[]{:S(2)}, u32[]{:S(2)}) %collective-permute-start.7) | collective-permute-done | bytes 12320 | tf_op jit(solution)/shard_map/ppermute | solution.py:23
  20.0 0.0 collective-permute-done.8.keep_in
  20.0 0.7 %shard_map.85 = bf16[1,32,128]{2,1,0:T(8,128)(2,1)} custom-call(bf16[1,48,128]{2,1,0:T(8,128)(2,1)S(1)} %collective-permute-done.7.parcel_ref, bf16[1,48,128]{2,1,0:T(8,128)(2,1)S(1)} %collective-permute-done.8.keep_in), custom_call_target="tpu_custom_call" | custom-call | tf_op jit(solution)/shard_map/pallas_call | solution.py:291
  (1 shorter events, 0.0 us)
Async XLA Ops:
  0.0 10.1 %collective-permute-start.2 = (bf16[1024,128]{1,0:T(8,128)(2,1)}, bf16[1024,128]{1,0:T(8,128)(2,1)S(1)}, u32[]{:S(2)}, u32[]{:S(2)}) collective-permute-start(bf16[1024,128]{1,0:T(8,128)(2,1)} %bitcast.3), channel_id=1, source_target_pairs={{0,2},{1,5},{2,0},{3,7},{4,6},{5,1},{6,4},{7,3},{8,10},{9,13},{10,... | collective-permute-start | bytes 786440 | tf_op jit(solution)/shard_map/ppermute | solution.py:23
  2.9 7.5 %collective-permute-start.3 = (bf16[1024,128]{1,0:T(8,128)(2,1)}, bf16[1024,128]{1,0:T(8,128)(2,1)S(1)}, u32[]{:S(2)}, u32[]{:S(2)}) collective-permute-start(bf16[1024,128]{1,0:T(8,128)(2,1)} %bitcast.5), channel_id=1, source_target_pairs={{0,2},{1,5},{2,0},{3,7},{4,6},{5,1},{6,4},{7,3},{8,10},{9,13},{10,... | collective-permute-start | bytes 786440 | tf_op jit(solution)/shard_map/ppermute | solution.py:23
  3.0 4.3 %collective-permute-start = (bf16[1,32,128]{2,1,0:T(8,128)(2,1)}, bf16[1,32,128]{2,1,0:T(8,128)(2,1)S(1)}, u32[]{:S(2)}, u32[]{:S(2)}) collective-permute-start(bf16[1,32,128]{2,1,0:T(8,128)(2,1)} %param.8), channel_id=1, source_target_pairs={{0,4},{1,3},{2,6},{3,1},{4,0},{5,7},{6,2},{7,5},{8,12},{9,11},{10,... | collective-permute-start | bytes 24584 | tf_op jit(solution)/shard_map/ppermute | solution.py:23
  5.1 6.8 %collective-permute-start.4 = (bf16[384,128]{1,0:T(8,128)(2,1)}, bf16[384,128]{1,0:T(8,128)(2,1)S(1)}, u32[]{:S(2)}, u32[]{:S(2)}) collective-permute-start(bf16[384,128]{1,0:T(8,128)(2,1)} %bitcast.7), channel_id=1, source_target_pairs={{0,2},{1,5},{2,0},{3,7},{4,6},{5,1},{6,4},{7,3},{8,10},{9,13},{10,... | collective-permute-start | bytes 294920 | tf_op jit(solution)/shard_map/ppermute | solution.py:23
  7.3 4.6 %collective-permute-start.1 = (bf16[2,32,128]{2,1,0:T(8,128)(2,1)S(1)}, bf16[2,32,128]{2,1,0:T(8,128)(2,1)S(1)}, u32[]{:S(2)}, u32[]{:S(2)}) collective-permute-start(bf16[2,32,128]{2,1,0:T(8,128)(2,1)S(1)} %constant_dynamic-update-slice_fusion.queries_ref.first_ref), channel_id=1, source_target_pairs={{0,8},{1,9},{2,10},{3,11},{4,12},{5,13},{6,14},{7,15},{8,0},{9,1},... | collective-permute-start | bytes 49160 | tf_op jit(solution)/shard_map/ppermute | solution.py:23
  12.6 3.3 %collective-permute-start.5 = (bf16[2,48,128]{2,1,0:T(8,128)(2,1)S(1)}, bf16[2,48,128]{2,1,0:T(8,128)(2,1)S(1)}, u32[]{:S(2)}, u32[]{:S(2)}) collective-permute-start(bf16[2,48,128]{2,1,0:T(8,128)(2,1)S(1)} %get-tuple-element.21), channel_id=1, source_target_pairs={{0,5},{1,2},{2,7},{3,0},{4,1},{5,6},{6,3},{7,4},{8,13},{9,10},{10,... | collective-permute-start | bytes 73736 | tf_op jit(solution)/shard_map/ppermute | solution.py:23
  14.1 1.8 %collective-permute-start.6 = (bf16[2,48,128]{2,1,0:T(8,128)(2,1)S(1)}, bf16[2,48,128]{2,1,0:T(8,128)(2,1)S(1)}, u32[]{:S(2)}, u32[]{:S(2)}) collective-permute-start(bf16[2,48,128]{2,1,0:T(8,128)(2,1)S(1)} %get-tuple-element.22), channel_id=1, source_target_pairs={{0,1},{1,0},{2,3},{3,2},{4,5},{5,4},{6,7},{7,6},{8,9},{9,8},{10,11... | collective-permute-start | bytes 73736 | tf_op jit(solution)/shard_map/ppermute | solution.py:23
  16.0 4.0 %collective-permute-start.7 = (bf16[1,48,128]{2,1,0:T(8,128)(2,1)S(1)}, bf16[1,48,128]{2,1,0:T(8,128)(2,1)S(1)}, u32[]{:S(2)}, u32[]{:S(2)}) collective-permute-start(bf16[1,48,128]{2,1,0:T(8,128)(2,1)S(1)} %get-tuple-element.23), channel_id=1, source_target_pairs={{0,9},{1,8},{2,11},{3,10},{4,13},{5,12},{6,15},{7,14},{8,1},{9,0},... | collective-permute-start | bytes 36872 | tf_op jit(solution)/shard_map/ppermute | solution.py:23
  18.6 1.4 %collective-permute-start.8 = (bf16[1,48,128]{2,1,0:T(8,128)(2,1)S(1)}, bf16[1,48,128]{2,1,0:T(8,128)(2,1)S(1)}, u32[]{:S(2)}, u32[]{:S(2)}) collective-permute-start(bf16[1,48,128]{2,1,0:T(8,128)(2,1)S(1)} %get-tuple-element.24), channel_id=1, source_target_pairs={{0,1},{1,0},{2,3},{3,2},{4,5},{5,4},{6,7},{7,6},{8,9},{9,8},{10,11... | collective-permute-start | bytes 36872 | tf_op jit(solution)/shard_map/ppermute | solution.py:23

commit v15 on v14

--- a/solution.py
+++ b/solution.py
@@ -84,10 +84,16 @@
         goal_ref[g] = wide_ref[pl.ds(g, tokens, stride=heads), :].astype(goal_ref.dtype)
 
 
+def sort_kernel(key_ref, value_ref, mask_ref, key_out, value_out, wide_ref):
+    del mask_ref
+    sort_heads(key_ref, wide_ref.at[0], key_out)
+    sort_heads(value_ref, wide_ref.at[1], value_out)
+
+
 def fetch_kernel(
-    queries_ref, far_key_ref, far_value_ref,
+    queries_ref,
     owner_hbm, slot_hbm, len_hbm, request_hbm, key_hbm, value_hbm, pool_hbm,
-    far_key_out, far_value_out, key_out, value_out, pool_out, mask_ref,
+    key_out, value_out, pool_out, mask_ref,
     owner_ref, slot_ref, len_ref, request_ref, key_ref, value_ref, wide_ref, sems,
     *, rows_dev, page_len, kv_heads,
 ):
@@ -104,8 +110,6 @@
     copies = [pltpu.make_async_copy(*pair, sems.at[i]) for i, pair in enumerate(pairs)]
     for copy in copies:
         copy.start()
-    sort_heads(far_key_ref, wide_ref.at[0], far_key_out)
-    sort_heads(far_value_ref, wide_ref.at[1], far_value_out)
     for copy in copies[:4]:
         copy.wait()
     blocks = lax.axis_size("blk")
@@ -143,8 +147,8 @@
     loop(mask_ref.shape[0], one)
     for copy in copies[4:]:
         copy.wait()
-    sort_heads(key_ref, wide_ref.at[2], key_out)
-    sort_heads(value_ref, wide_ref.at[3], value_out)
+    sort_heads(key_ref, wide_ref.at[0], key_out)
+    sort_heads(value_ref, wide_ref.at[1], value_out)
 
 
 def attend(query, sides, pool_refs, mask, sizes):
@@ -287,11 +291,12 @@
     loop(count, one)
 
 
-def call(kernel, outs, operands, **static):
+def call(kernel, outs, operands, scratch=(), **static):
     return pl.pallas_call(
         functools.partial(kernel, **static),
         out_shape=outs,
         in_specs=[pl.BlockSpec(memory_space=pltpu.VMEM)] * len(operands),
+        scratch_shapes=scratch,
         compiler_params=pltpu.CompilerParams(vmem_limit_bytes=VMEM_BYTES),
     )(*operands)
 
@@ -328,24 +333,29 @@
     mask = jax.ShapeDtypeStruct((2 * half, pool.shape[0]), jnp.float32)
     sorted_shape = (kv_heads, prefix_rows // kv_heads, head_dim)
     sorted_heads = jax.ShapeDtypeStruct(sorted_shape, keys.dtype)
-    far_keys, far_values, near_keys, near_values, near_pool, near_and_far = pl.pallas_call(
+    near_keys, near_values, near_pool, near_and_far = pl.pallas_call(
         functools.partial(
             fetch_kernel, rows_dev=rows_dev, page_len=page_len, kv_heads=kv_heads
         ),
-        out_shape=[sorted_heads] * 4 + [jax.ShapeDtypeStruct(pool.shape, pool.dtype), mask],
-        in_specs=[pl.BlockSpec(memory_space=pltpu.VMEM)] * 3
+        out_shape=[sorted_heads] * 2 + [jax.ShapeDtypeStruct(pool.shape, pool.dtype), mask],
+        in_specs=[pl.BlockSpec(memory_space=pltpu.VMEM)]
         + [pl.BlockSpec(memory_space=pltpu.HBM)] * (len(tables) + len(arrays)),
-        out_specs=[pl.BlockSpec(memory_space=pltpu.VMEM)] * 6,
+        out_specs=[pl.BlockSpec(memory_space=pltpu.VMEM)] * 4,
         scratch_shapes=[pltpu.SMEM(table.shape, table.dtype) for table in tables]
         + [pltpu.VMEM(keys.shape, keys.dtype)] * 2
         + [
-            pltpu.VMEM((4, *keys.shape), jnp.float32),
+            pltpu.VMEM((2, *keys.shape), jnp.float32),
             pltpu.SemaphoreType.DMA((len(tables) + len(arrays),)),
         ],
         compiler_params=pltpu.CompilerParams(vmem_limit_bytes=VMEM_BYTES),
     )(
-        first, far_keys, far_values,
+        first,
         *(pltpu.with_memory_space_constraint(operand, pltpu.HBM) for operand in tables + arrays),
+    )
+
+    far_keys, far_values = call(
+        sort_kernel, (sorted_heads, sorted_heads), (far_keys, far_values, near_and_far),
+        scratch=[pltpu.VMEM((2, *keys.shape), jnp.float32)],
     )
 
     def parcels(count):

time: 21 us -> 21 us (level)
    pallas_call x3 -> x4, Pallas kernels: 1.52 us -> 1.65 us  [call(): pl.pallas_call(functools.partial(kernel, **static), out_shape=outs, in_sp...]
  transfers between devices with their start and end apart: 9 -> 9, of which waited for: 4 -> 3; matrix products, arithmetic and copies ran while one was open for 3% -> 3% of each run, Pallas kernels for 6% -> 7%
where the time goes in v15:
time: 21 us; the launch traced here: 20.7 us
  starting transfers between devices  14.2 us (68%)
  waiting for transfers between devices  2.89 us (14%)
  Pallas kernels  2.89 us (14%)
  local copies, waits for them, and re-layouts  0.7 us (3%)
    ppermute x9, starting transfers between devices, exchange(): return lax.ppermute(value, ('blk', 'heads'), pairs)  14.2 us
    ppermute x9, waiting for transfers between devices, exchange(): return lax.ppermute(value, ('blk', 'heads'), pairs)  2.89 us
    pallas_call x4, Pallas kernels, call(): pl.pallas_call(functools.partial(kernel, **static), out_shape=outs, in_sp...  1.65 us
    pallas_call x1, Pallas kernels, on_device(): pl.pallas_call(functools.partial(fetch_kernel, rows_dev=rows_dev, page_le...  1.24 us
    unnamed x1, local copies, waits for them, and re-layouts  0.7 us
  transfers between devices with their start and end apart: 9, of which 3 were waited for; matrix products, arithmetic and copies ran while one was open for 3% of the time, Pallas kernels for 7%

profile of v15, /device:TPU:0, one launch (start us, length us, event | category | flops | bytes accessed | tf_op | source)
XLA Modules:
  0.0 20.7 jit_solution(13434652298726831730)
XLA Ops:
  0.0 2.9 %collective-permute-start.2 = (bf16[1024,128]{1,0:T(8,128)(2,1)}, bf16[1024,128]{1,0:T(8,128)(2,1)S(1)}, u32[]{:S(2)}, u32[]{:S(2)}) collective-permute-start(bf16[1024,128]{1,0:T(8,128)(2,1)} %bitcast.3), channel_id=1, source_target_pairs={{0,2},{1,5},{2,0},{3,7},{4,6},{5,1},{6,4},{7,3},{8,10},{9,13},{10,... | collective-permute-start | bytes 786440 | tf_op jit(solution)/shard_map/ppermute | solution.py:23
  2.9 0.0 collective-permute-start.3
  3.0 2.1 %collective-permute-start = (bf16[1,32,128]{2,1,0:T(8,128)(2,1)}, bf16[1,32,128]{2,1,0:T(8,128)(2,1)S(1)}, u32[]{:S(2)}, u32[]{:S(2)}) collective-permute-start(bf16[1,32,128]{2,1,0:T(8,128)(2,1)} %param.8), channel_id=1, source_target_pairs={{0,4},{1,3},{2,6},{3,1},{4,0},{5,7},{6,2},{7,5},{8,12},{9,11},{10,... | collective-permute-start | bytes 24584 | tf_op jit(solution)/shard_map/ppermute | solution.py:23
  5.1 1.5 %collective-permute-start.4 = (bf16[384,128]{1,0:T(8,128)(2,1)}, bf16[384,128]{1,0:T(8,128)(2,1)S(1)}, u32[]{:S(2)}, u32[]{:S(2)}) collective-permute-start(bf16[384,128]{1,0:T(8,128)(2,1)} %bitcast.7), channel_id=1, source_target_pairs={{0,2},{1,5},{2,0},{3,7},{4,6},{5,1},{6,4},{7,3},{8,10},{9,13},{10,... | collective-permute-start | bytes 294920 | tf_op jit(solution)/shard_map/ppermute | solution.py:23
  6.5 0.7 %constant_dynamic-update-slice_fusion.1 = bf16[2,32,128]{2,1,0:T(8,128)(2,1)S(1)} fusion(bf16[1,32,128]{2,1,0:T(8,128)(2,1)} %param.8), kind=kLoop, calls=%fused_computation.1 | loop fusion | bytes 16384
  7.2 0.0 collective-permute-done
  7.3 2.8 %collective-permute-start.1 = (bf16[2,32,128]{2,1,0:T(8,128)(2,1)S(1)}, bf16[2,32,128]{2,1,0:T(8,128)(2,1)S(1)}, u32[]{:S(2)}, u32[]{:S(2)}) collective-permute-start(bf16[2,32,128]{2,1,0:T(8,128)(2,1)S(1)} %constant_dynamic-update-slice_fusion.queries_ref.first_ref), channel_id=1, source_target_pairs={{0,8},{1,9},{2,10},{3,11},{4,12},{5,13},{6,14},{7,15},{8,0},{9,1},... | collective-permute-start | bytes 49160 | tf_op jit(solution)/shard_map/ppermute | solution.py:23
  10.1 1.2 %shard_map.82 = (bf16[4,256,128]{2,1,0:T(8,128)(2,1)S(1)}, bf16[4,256,128]{2,1,0:T(8,128)(2,1)S(1)}, bf16[384,128]{1,0:T(8,128)(2,1)S(1)}, f32[4,384]{1,0:T(4,128)S(1)}) custom-call(bf16[2,32,128]{2,1,0:T(8,128)(2,1)S(1)} %constant_dynamic-update-slice_fusion.queries_ref.first_ref, s32[3,8]{1,0:T(4,128)} %owner_hbm.1, s32[3,8]{1,0:T(4,128)} %slot_hbm.1, ...), custom_call_target="tpu_custom_call" | custom-call | tf_op jit(solution)/shard_map/pallas_call | solution.py:336
  11.3 0.0 collective-permute-done.2.key_ref
  11.3 0.0 collective-permute-done.3.value_ref
  11.4 0.1 shard_map.83
  11.5 0.4 %collective-permute-done.1.second_ref = bf16[2,32,128]{2,1,0:T(8,128)(2,1)S(1)} collective-permute-done((bf16[2,32,128]{2,1,0:T(8,128)(2,1)S(1)}, bf16[2,32,128]{2,1,0:T(8,128)(2,1)S(1)}, u32[]{:S(2)}, u32[]{:S(2)}) %collective-permute-start.1) | collective-permute-done | bytes 16416 | tf_op jit(solution)/shard_map/ppermute | solution.py:23
  11.9 0.0 collective-permute-done.4.far_pool_ref
  11.9 0.7 %shard_map.84 = (bf16[2,48,128]{2,1,0:T(8,128)(2,1)S(1)}, bf16[2,48,128]{2,1,0:T(8,128)(2,1)S(1)}) custom-call(bf16[2,32,128]{2,1,0:T(8,128)(2,1)S(1)} %constant_dynamic-update-slice_fusion.queries_ref.first_ref, bf16[2,32,128]{2,1,0:T(8,128)(2,1)S(1)} %collective-permute-done.1.second_ref, bf16[4,256,128]{2,1,0:T(8,128)(2,1)S(1)} %get-tuple-element.15.near_key_ref, ...), custom_call_target="tpu_custom_call" | custom-call | tf_op jit(solution)/shard_map/pallas_call | solution.py:295
  12.6 1.5 %collective-permute-start.5 = (bf16[2,48,128]{2,1,0:T(8,128)(2,1)S(1)}, bf16[2,48,128]{2,1,0:T(8,128)(2,1)S(1)}, u32[]{:S(2)}, u32[]{:S(2)}) collective-permute-start(bf16[2,48,128]{2,1,0:T(8,128)(2,1)S(1)} %get-tuple-element.21), channel_id=1, source_target_pairs={{0,5},{1,2},{2,7},{3,0},{4,1},{5,6},{6,3},{7,4},{8,13},{9,10},{10,... | collective-permute-start | bytes 73736 | tf_op jit(solution)/shard_map/ppermute | solution.py:23
  14.1 0.4 %collective-permute-start.6 = (bf16[2,48,128]{2,1,0:T(8,128)(2,1)S(1)}, bf16[2,48,128]{2,1,0:T(8,128)(2,1)S(1)}, u32[]{:S(2)}, u32[]{:S(2)}) collective-permute-start(bf16[2,48,128]{2,1,0:T(8,128)(2,1)S(1)} %get-tuple-element.22), channel_id=1, source_target_pairs={{0,1},{1,0},{2,3},{3,2},{4,5},{5,4},{6,7},{7,6},{8,9},{9,8},{10,11... | collective-permute-start | bytes 73736 | tf_op jit(solution)/shard_map/ppermute | solution.py:23
  14.5 1.4 %collective-permute-done.5.parcel_ref = bf16[2,48,128]{2,1,0:T(8,128)(2,1)S(1)} collective-permute-done((bf16[2,48,128]{2,1,0:T(8,128)(2,1)S(1)}, bf16[2,48,128]{2,1,0:T(8,128)(2,1)S(1)}, u32[]{:S(2)}, u32[]{:S(2)}) %collective-permute-start.5) | collective-permute-done | bytes 24608 | tf_op jit(solution)/shard_map/ppermute | solution.py:23
  15.9 0.0 collective-permute-done.6.keep_in
  15.9 0.1 shard_map.85
  16.0 2.6 %collective-permute-start.7 = (bf16[1,48,128]{2,1,0:T(8,128)(2,1)S(1)}, bf16[1,48,128]{2,1,0:T(8,128)(2,1)S(1)}, u32[]{:S(2)}, u32[]{:S(2)}) collective-permute-start(bf16[1,48,128]{2,1,0:T(8,128)(2,1)S(1)} %get-tuple-element.23), channel_id=1, source_target_pairs={{0,9},{1,8},{2,11},{3,10},{4,13},{5,12},{6,15},{7,14},{8,1},{9,0},... | collective-permute-start | bytes 36872 | tf_op jit(solution)/shard_map/ppermute | solution.py:23
  18.6 0.4 %collective-permute-start.8 = (bf16[1,48,128]{2,1,0:T(8,128)(2,1)S(1)}, bf16[1,48,128]{2,1,0:T(8,128)(2,1)S(1)}, u32[]{:S(2)}, u32[]{:S(2)}) collective-permute-start(bf16[1,48,128]{2,1,0:T(8,128)(2,1)S(1)} %get-tuple-element.24), channel_id=1, source_target_pairs={{0,1},{1,0},{2,3},{3,2},{4,5},{5,4},{6,7},{7,6},{8,9},{9,8},{10,11... | collective-permute-start | bytes 36872 | tf_op jit(solution)/shard_map/ppermute | solution.py:23
  19.0 1.1 %collective-permute-done.7.parcel_ref = bf16[1,48,128]{2,1,0:T(8,128)(2,1)S(1)} collective-permute-done((bf16[1,48,128]{2,1,0:T(8,128)(2,1)S(1)}, bf16[1,48,128]{2,1,0:T(8,128)(2,1)S(1)}, u32[]{:S(2)}, u32[]{:S(2)}) %collective-permute-start.7) | collective-permute-done | bytes 12320 | tf_op jit(solution)/shard_map/ppermute | solution.py:23
  20.0 0.0 collective-permute-done.8.keep_in
  20.0 0.7 %shard_map.86 = bf16[1,32,128]{2,1,0:T(8,128)(2,1)} custom-call(bf16[1,48,128]{2,1,0:T(8,128)(2,1)S(1)} %collective-permute-done.7.parcel_ref, bf16[1,48,128]{2,1,0:T(8,128)(2,1)S(1)} %collective-permute-done.8.keep_in), custom_call_target="tpu_custom_call" | custom-call | tf_op jit(solution)/shard_map/pallas_call | solution.py:295
  (1 shorter events, 0.0 us)
Async XLA Ops:
  0.0 11.3 %collective-permute-start.2 = (bf16[1024,128]{1,0:T(8,128)(2,1)}, bf16[1024,128]{1,0:T(8,128)(2,1)S(1)}, u32[]{:S(2)}, u32[]{:S(2)}) collective-permute-start(bf16[1024,128]{1,0:T(8,128)(2,1)} %bitcast.3), channel_id=1, source_target_pairs={{0,2},{1,5},{2,0},{3,7},{4,6},{5,1},{6,4},{7,3},{8,10},{9,13},{10,... | collective-permute-start | bytes 786440 | tf_op jit(solution)/shard_map/ppermute | solution.py:23
  2.9 8.4 %collective-permute-start.3 = (bf16[1024,128]{1,0:T(8,128)(2,1)}, bf16[1024,128]{1,0:T(8,128)(2,1)S(1)}, u32[]{:S(2)}, u32[]{:S(2)}) collective-permute-start(bf16[1024,128]{1,0:T(8,128)(2,1)} %bitcast.5), channel_id=1, source_target_pairs={{0,2},{1,5},{2,0},{3,7},{4,6},{5,1},{6,4},{7,3},{8,10},{9,13},{10,... | collective-permute-start | bytes 786440 | tf_op jit(solution)/shard_map/ppermute | solution.py:23
  3.0 4.3 %collective-permute-start = (bf16[1,32,128]{2,1,0:T(8,128)(2,1)}, bf16[1,32,128]{2,1,0:T(8,128)(2,1)S(1)}, u32[]{:S(2)}, u32[]{:S(2)}) collective-permute-start(bf16[1,32,128]{2,1,0:T(8,128)(2,1)} %param.8), channel_id=1, source_target_pairs={{0,4},{1,3},{2,6},{3,1},{4,0},{5,7},{6,2},{7,5},{8,12},{9,11},{10,... | collective-permute-start | bytes 24584 | tf_op jit(solution)/shard_map/ppermute | solution.py:23
  5.1 6.8 %collective-permute-start.4 = (bf16[384,128]{1,0:T(8,128)(2,1)}, bf16[384,128]{1,0:T(8,128)(2,1)S(1)}, u32[]{:S(2)}, u32[]{:S(2)}) collective-permute-start(bf16[384,128]{1,0:T(8,128)(2,1)} %bitcast.7), channel_id=1, source_target_pairs={{0,2},{1,5},{2,0},{3,7},{4,6},{5,1},{6,4},{7,3},{8,10},{9,13},{10,... | collective-permute-start | bytes 294920 | tf_op jit(solution)/shard_map/ppermute | solution.py:23
  7.3 4.6 %collective-permute-start.1 = (bf16[2,32,128]{2,1,0:T(8,128)(2,1)S(1)}, bf16[2,32,128]{2,1,0:T(8,128)(2,1)S(1)}, u32[]{:S(2)}, u32[]{:S(2)}) collective-permute-start(bf16[2,32,128]{2,1,0:T(8,128)(2,1)S(1)} %constant_dynamic-update-slice_fusion.queries_ref.first_ref), channel_id=1, source_target_pairs={{0,8},{1,9},{2,10},{3,11},{4,12},{5,13},{6,14},{7,15},{8,0},{9,1},... | collective-permute-start | bytes 49160 | tf_op jit(solution)/shard_map/ppermute | solution.py:23
  12.6 3.3 %collective-permute-start.5 = (bf16[2,48,128]{2,1,0:T(8,128)(2,1)S(1)}, bf16[2,48,128]{2,1,0:T(8,128)(2,1)S(1)}, u32[]{:S(2)}, u32[]{:S(2)}) collective-permute-start(bf16[2,48,128]{2,1,0:T(8,128)(2,1)S(1)} %get-tuple-element.21), channel_id=1, source_target_pairs={{0,5},{1,2},{2,7},{3,0},{4,1},{5,6},{6,3},{7,4},{8,13},{9,10},{10,... | collective-permute-start | bytes 73736 | tf_op jit(solution)/shard_map/ppermute | solution.py:23
  14.1 1.8 %collective-permute-start.6 = (bf16[2,48,128]{2,1,0:T(8,128)(2,1)S(1)}, bf16[2,48,128]{2,1,0:T(8,128)(2,1)S(1)}, u32[]{:S(2)}, u32[]{:S(2)}) collective-permute-start(bf16[2,48,128]{2,1,0:T(8,128)(2,1)S(1)} %get-tuple-element.22), channel_id=1, source_target_pairs={{0,1},{1,0},{2,3},{3,2},{4,5},{5,4},{6,7},{7,6},{8,9},{9,8},{10,11... | collective-permute-start | bytes 73736 | tf_op jit(solution)/shard_map/ppermute | solution.py:23
  16.0 4.0 %collective-permute-start.7 = (bf16[1,48,128]{2,1,0:T(8,128)(2,1)S(1)}, bf16[1,48,128]{2,1,0:T(8,128)(2,1)S(1)}, u32[]{:S(2)}, u32[]{:S(2)}) collective-permute-start(bf16[1,48,128]{2,1,0:T(8,128)(2,1)S(1)} %get-tuple-element.23), channel_id=1, source_target_pairs={{0,9},{1,8},{2,11},{3,10},{4,13},{5,12},{6,15},{7,14},{8,1},{9,0},... | collective-permute-start | bytes 36872 | tf_op jit(solution)/shard_map/ppermute | solution.py:23
  18.6 1.5 %collective-permute-start.8 = (bf16[1,48,128]{2,1,0:T(8,128)(2,1)S(1)}, bf16[1,48,128]{2,1,0:T(8,128)(2,1)S(1)}, u32[]{:S(2)}, u32[]{:S(2)}) collective-permute-start(bf16[1,48,128]{2,1,0:T(8,128)(2,1)S(1)} %get-tuple-element.24), channel_id=1, source_target_pairs={{0,1},{1,0},{2,3},{3,2},{4,5},{5,4},{6,7},{7,6},{8,9},{9,8},{10,11... | collective-permute-start | bytes 36872 | tf_op jit(solution)/shard_map/ppermute | solution.py:23

commit v16 on v14

--- a/solution.py
+++ b/solution.py
@@ -45,18 +45,16 @@
     return jnp.sum(jnp.where(diagonal, row, 0.0), axis=1, keepdims=True)
 
 
-def split(value, pieces):
-    found = []
-    for _ in range(pieces):
-        found.append(value.astype(jnp.bfloat16).astype(jnp.float32))
-        value = value - found[-1]
-    return found
+def split(value):
+    high = value.astype(jnp.bfloat16).astype(jnp.float32)
+    return high, (value - high).astype(jnp.bfloat16).astype(jnp.float32)
 
 
 def stat_block(top_row, total_row):
-    rows = split(top_row, 3) + split(total_row, 2)
-    blank = jnp.zeros((STAT_ROWS - len(rows), top_row.shape[1]), jnp.float32)
-    return jnp.concatenate([*rows, blank], axis=0)
+    top_high, top_low = split(top_row)
+    total_high, total_low = split(total_row)
+    blank = jnp.zeros((STAT_ROWS - 4, top_row.shape[1]), jnp.float32)
+    return jnp.concatenate([top_high, top_low, total_high, total_low, blank], axis=0)
 
 
 def suffix_rows(pool_refs, start, page_rows):
@@ -177,7 +175,9 @@
     top = jnp.max(
         fold(jnp.maximum, [part[0] for part in parts], head_dim), axis=1, keepdims=True
     )
-    weights = [jnp.exp2((part[0] - top) * scale) for part in parts]
+    high, low = split(top)
+    point = high + low
+    weights = [jnp.exp2((part[0] - point) * scale) for part in parts]
     total = jnp.sum(fold(jnp.add, weights, head_dim), axis=1, keepdims=True)
     mixed = 0.0
     for weight, (_, value_ref, page_value) in zip(weights, parts):
@@ -190,7 +190,7 @@
             )
         else:
             mixed = mixed + jnp.dot(weight, page_value, preferred_element_type=jnp.float32)
-    return top, total, mixed * (1.0 / total)
+    return point, total, mixed / total
 
 
 def attend_kernel(
@@ -247,7 +247,7 @@
     parcel = parcel.astype(jnp.float32)
     qheads = parcel.shape[0] - STAT_ROWS
     stats = parcel[qheads:]
-    return parcel[:qheads], stats[0:1] + stats[1:2] + stats[2:3], stats[3:4] + stats[4:5]
+    return parcel[:qheads], stats[0:1] + stats[1:2], stats[2:3] + stats[3:4]
 
 
 def write(mixed, top, total, dtype):

time: 21 us -> 21 us (level)
  no operation moved by 1% of the time
where the time goes in v16:
time: 21 us; the launch traced here: 20.8 us
  starting transfers between devices  14.3 us (68%)
  waiting for transfers between devices  2.91 us (14%)
  Pallas kernels  2.79 us (13%)
  local copies, waits for them, and re-layouts  0.7 us (3%)
    ppermute x9, starting transfers between devices, exchange(): return lax.ppermute(value, ('blk', 'heads'), pairs)  14.3 us
    ppermute x9, waiting for transfers between devices, exchange(): return lax.ppermute(value, ('blk', 'heads'), pairs)  2.91 us
    pallas_call x3, Pallas kernels, call(): pl.pallas_call(functools.partial(kernel, **static), out_shape=outs, in_sp...  1.55 us
    pallas_call x1, Pallas kernels, on_device(): pl.pallas_call(functools.partial(fetch_kernel, rows_dev=rows_dev, page_le...  1.24 us
    unnamed x1, local copies, waits for them, and re-layouts  0.7 us
  transfers between devices with their start and end apart: 9, of which 4 were waited for; matrix products, arithmetic and copies ran while one was open for 3% of the time, Pallas kernels for 6%

profile of v16, /device:TPU:0, one launch (start us, length us, event | category | flops | bytes accessed | tf_op | source)
XLA Modules:
  0.0 20.8 jit_solution(8168625918510175320)
XLA Ops:
  0.0 2.9 %collective-permute-start.2 = (bf16[1024,128]{1,0:T(8,128)(2,1)}, bf16[1024,128]{1,0:T(8,128)(2,1)S(1)}, u32[]{:S(2)}, u32[]{:S(2)}) collective-permute-start(bf16[1024,128]{1,0:T(8,128)(2,1)} %bitcast.3), channel_id=1, source_target_pairs={{0,2},{1,5},{2,0},{3,7},{4,6},{5,1},{6,4},{7,3},{8,10},{9,13},{10,... | collective-permute-start | bytes 786440 | tf_op jit(solution)/shard_map/ppermute | solution.py:23
  2.9 0.0 collective-permute-start.3
  3.0 2.1 %collective-permute-start = (bf16[1,32,128]{2,1,0:T(8,128)(2,1)}, bf16[1,32,128]{2,1,0:T(8,128)(2,1)S(1)}, u32[]{:S(2)}, u32[]{:S(2)}) collective-permute-start(bf16[1,32,128]{2,1,0:T(8,128)(2,1)} %param.8), channel_id=1, source_target_pairs={{0,4},{1,3},{2,6},{3,1},{4,0},{5,7},{6,2},{7,5},{8,12},{9,11},{10,... | collective-permute-start | bytes 24584 | tf_op jit(solution)/shard_map/ppermute | solution.py:23
  5.1 1.5 %collective-permute-start.4 = (bf16[384,128]{1,0:T(8,128)(2,1)}, bf16[384,128]{1,0:T(8,128)(2,1)S(1)}, u32[]{:S(2)}, u32[]{:S(2)}) collective-permute-start(bf16[384,128]{1,0:T(8,128)(2,1)} %bitcast.7), channel_id=1, source_target_pairs={{0,2},{1,5},{2,0},{3,7},{4,6},{5,1},{6,4},{7,3},{8,10},{9,13},{10,... | collective-permute-start | bytes 294920 | tf_op jit(solution)/shard_map/ppermute | solution.py:23
  6.5 0.7 %constant_dynamic-update-slice_fusion.1 = bf16[2,32,128]{2,1,0:T(8,128)(2,1)S(1)} fusion(bf16[1,32,128]{2,1,0:T(8,128)(2,1)} %param.8), kind=kLoop, calls=%fused_computation.1 | loop fusion | bytes 16384
  7.2 0.0 collective-permute-done
  7.3 2.8 %collective-permute-start.1 = (bf16[2,32,128]{2,1,0:T(8,128)(2,1)S(1)}, bf16[2,32,128]{2,1,0:T(8,128)(2,1)S(1)}, u32[]{:S(2)}, u32[]{:S(2)}) collective-permute-start(bf16[2,32,128]{2,1,0:T(8,128)(2,1)S(1)} %constant_dynamic-update-slice_fusion.queries_ref.first_ref), channel_id=1, source_target_pairs={{0,8},{1,9},{2,10},{3,11},{4,12},{5,13},{6,14},{7,15},{8,0},{9,1},... | collective-permute-start | bytes 49160 | tf_op jit(solution)/shard_map/ppermute | solution.py:23
  10.1 0.0 collective-permute-done.2.far_key_ref
  10.1 0.3 %collective-permute-done.3.far_value_ref = bf16[1024,128]{1,0:T(8,128)(2,1)S(1)} collective-permute-done((bf16[1024,128]{1,0:T(8,128)(2,1)}, bf16[1024,128]{1,0:T(8,128)(2,1)S(1)}, u32[]{:S(2)}, u32[]{:S(2)}) %collective-permute-start.3) | collective-permute-done | bytes 262176 | tf_op jit(solution)/shard_map/ppermute | solution.py:23
  10.4 1.2 %shard_map.82 = (bf16[4,256,128]{2,1,0:T(8,128)(2,1)S(1)}, bf16[4,256,128]{2,1,0:T(8,128)(2,1)S(1)}, bf16[4,256,128]{2,1,0:T(8,128)(2,1)S(1)}, bf16[4,256,128]{2...) custom-call(bf16[2,32,128]{2,1,0:T(8,128)(2,1)S(1)} %constant_dynamic-update-slice_fusion.queries_ref.first_ref, ...), custom_call_target="tpu_custom_call" | custom-call | tf_op jit(solution)/shard_map/pallas_call | solution.py:331
  11.6 0.2 %collective-permute-done.1.second_ref = bf16[2,32,128]{2,1,0:T(8,128)(2,1)S(1)} collective-permute-done((bf16[2,32,128]{2,1,0:T(8,128)(2,1)S(1)}, bf16[2,32,128]{2,1,0:T(8,128)(2,1)S(1)}, u32[]{:S(2)}, u32[]{:S(2)}) %collective-permute-start.1) | collective-permute-done | bytes 16416 | tf_op jit(solution)/shard_map/ppermute | solution.py:23
  11.9 0.0 collective-permute-done.4.far_pool_ref
  11.9 0.7 %shard_map.83 = (bf16[2,48,128]{2,1,0:T(8,128)(2,1)S(1)}, bf16[2,48,128]{2,1,0:T(8,128)(2,1)S(1)}) custom-call(bf16[2,32,128]{2,1,0:T(8,128)(2,1)S(1)} %constant_dynamic-update-slice_fusion.queries_ref.first_ref, bf16[2,32,128]{2,1,0:T(8,128)(2,1)S(1)} %collective-permute-done.1.second_ref, bf16[4,256,128]{2,1,0:T(8,128)(2,1)S(1)} %get-tuple-element.15.near_key_ref, ...), custom_call_target="tpu_custom_call" | custom-call | tf_op jit(solution)/shard_map/pallas_call | solution.py:291
  12.6 1.5 %collective-permute-start.5 = (bf16[2,48,128]{2,1,0:T(8,128)(2,1)S(1)}, bf16[2,48,128]{2,1,0:T(8,128)(2,1)S(1)}, u32[]{:S(2)}, u32[]{:S(2)}) collective-permute-start(bf16[2,48,128]{2,1,0:T(8,128)(2,1)S(1)} %get-tuple-element.21), channel_id=1, source_target_pairs={{0,5},{1,2},{2,7},{3,0},{4,1},{5,6},{6,3},{7,4},{8,13},{9,10},{10,... | collective-permute-start | bytes 73736 | tf_op jit(solution)/shard_map/ppermute | solution.py:23
  14.1 0.5 %collective-permute-start.6 = (bf16[2,48,128]{2,1,0:T(8,128)(2,1)S(1)}, bf16[2,48,128]{2,1,0:T(8,128)(2,1)S(1)}, u32[]{:S(2)}, u32[]{:S(2)}) collective-permute-start(bf16[2,48,128]{2,1,0:T(8,128)(2,1)S(1)} %get-tuple-element.22), channel_id=1, source_target_pairs={{0,1},{1,0},{2,3},{3,2},{4,5},{5,4},{6,7},{7,6},{8,9},{9,8},{10,11... | collective-permute-start | bytes 73736 | tf_op jit(solution)/shard_map/ppermute | solution.py:23
  14.6 1.3 %collective-permute-done.5.parcel_ref = bf16[2,48,128]{2,1,0:T(8,128)(2,1)S(1)} collective-permute-done((bf16[2,48,128]{2,1,0:T(8,128)(2,1)S(1)}, bf16[2,48,128]{2,1,0:T(8,128)(2,1)S(1)}, u32[]{:S(2)}, u32[]{:S(2)}) %collective-permute-start.5) | collective-permute-done | bytes 24608 | tf_op jit(solution)/shard_map/ppermute | solution.py:23
  15.9 0.0 collective-permute-done.6.keep_in
  15.9 0.1 shard_map.84
  16.0 2.6 %collective-permute-start.7 = (bf16[1,48,128]{2,1,0:T(8,128)(2,1)S(1)}, bf16[1,48,128]{2,1,0:T(8,128)(2,1)S(1)}, u32[]{:S(2)}, u32[]{:S(2)}) collective-permute-start(bf16[1,48,128]{2,1,0:T(8,128)(2,1)S(1)} %get-tuple-element.23), channel_id=1, source_target_pairs={{0,9},{1,8},{2,11},{3,10},{4,13},{5,12},{6,15},{7,14},{8,1},{9,0},... | collective-permute-start | bytes 36872 | tf_op jit(solution)/shard_map/ppermute | solution.py:23
  18.7 0.4 %collective-permute-start.8 = (bf16[1,48,128]{2,1,0:T(8,128)(2,1)S(1)}, bf16[1,48,128]{2,1,0:T(8,128)(2,1)S(1)}, u32[]{:S(2)}, u32[]{:S(2)}) collective-permute-start(bf16[1,48,128]{2,1,0:T(8,128)(2,1)S(1)} %get-tuple-element.24), channel_id=1, source_target_pairs={{0,1},{1,0},{2,3},{3,2},{4,5},{5,4},{6,7},{7,6},{8,9},{9,8},{10,11... | collective-permute-start | bytes 36872 | tf_op jit(solution)/shard_map/ppermute | solution.py:23
  19.1 1.0 %collective-permute-done.7.parcel_ref = bf16[1,48,128]{2,1,0:T(8,128)(2,1)S(1)} collective-permute-done((bf16[1,48,128]{2,1,0:T(8,128)(2,1)S(1)}, bf16[1,48,128]{2,1,0:T(8,128)(2,1)S(1)}, u32[]{:S(2)}, u32[]{:S(2)}) %collective-permute-start.7) | collective-permute-done | bytes 12320 | tf_op jit(solution)/shard_map/ppermute | solution.py:23
  20.1 0.0 collective-permute-done.8.keep_in
  20.1 0.7 %shard_map.85 = bf16[1,32,128]{2,1,0:T(8,128)(2,1)} custom-call(bf16[1,48,128]{2,1,0:T(8,128)(2,1)S(1)} %collective-permute-done.7.parcel_ref, bf16[1,48,128]{2,1,0:T(8,128)(2,1)S(1)} %collective-permute-done.8.keep_in), custom_call_target="tpu_custom_call" | custom-call | tf_op jit(solution)/shard_map/pallas_call | solution.py:291
  (1 shorter events, 0.0 us)
Async XLA Ops:
  0.0 10.1 %collective-permute-start.2 = (bf16[1024,128]{1,0:T(8,128)(2,1)}, bf16[1024,128]{1,0:T(8,128)(2,1)S(1)}, u32[]{:S(2)}, u32[]{:S(2)}) collective-permute-start(bf16[1024,128]{1,0:T(8,128)(2,1)} %bitcast.3), channel_id=1, source_target_pairs={{0,2},{1,5},{2,0},{3,7},{4,6},{5,1},{6,4},{7,3},{8,10},{9,13},{10,... | collective-permute-start | bytes 786440 | tf_op jit(solution)/shard_map/ppermute | solution.py:23
  2.9 7.5 %collective-permute-start.3 = (bf16[1024,128]{1,0:T(8,128)(2,1)}, bf16[1024,128]{1,0:T(8,128)(2,1)S(1)}, u32[]{:S(2)}, u32[]{:S(2)}) collective-permute-start(bf16[1024,128]{1,0:T(8,128)(2,1)} %bitcast.5), channel_id=1, source_target_pairs={{0,2},{1,5},{2,0},{3,7},{4,6},{5,1},{6,4},{7,3},{8,10},{9,13},{10,... | collective-permute-start | bytes 786440 | tf_op jit(solution)/shard_map/ppermute | solution.py:23
  3.0 4.3 %collective-permute-start = (bf16[1,32,128]{2,1,0:T(8,128)(2,1)}, bf16[1,32,128]{2,1,0:T(8,128)(2,1)S(1)}, u32[]{:S(2)}, u32[]{:S(2)}) collective-permute-start(bf16[1,32,128]{2,1,0:T(8,128)(2,1)} %param.8), channel_id=1, source_target_pairs={{0,4},{1,3},{2,6},{3,1},{4,0},{5,7},{6,2},{7,5},{8,12},{9,11},{10,... | collective-permute-start | bytes 24584 | tf_op jit(solution)/shard_map/ppermute | solution.py:23
  5.1 6.8 %collective-permute-start.4 = (bf16[384,128]{1,0:T(8,128)(2,1)}, bf16[384,128]{1,0:T(8,128)(2,1)S(1)}, u32[]{:S(2)}, u32[]{:S(2)}) collective-permute-start(bf16[384,128]{1,0:T(8,128)(2,1)} %bitcast.7), channel_id=1, source_target_pairs={{0,2},{1,5},{2,0},{3,7},{4,6},{5,1},{6,4},{7,3},{8,10},{9,13},{10,... | collective-permute-start | bytes 294920 | tf_op jit(solution)/shard_map/ppermute | solution.py:23
  7.3 4.6 %collective-permute-start.1 = (bf16[2,32,128]{2,1,0:T(8,128)(2,1)S(1)}, bf16[2,32,128]{2,1,0:T(8,128)(2,1)S(1)}, u32[]{:S(2)}, u32[]{:S(2)}) collective-permute-start(bf16[2,32,128]{2,1,0:T(8,128)(2,1)S(1)} %constant_dynamic-update-slice_fusion.queries_ref.first_ref), channel_id=1, source_target_pairs={{0,8},{1,9},{2,10},{3,11},{4,12},{5,13},{6,14},{7,15},{8,0},{9,1},... | collective-permute-start | bytes 49160 | tf_op jit(solution)/shard_map/ppermute | solution.py:23
  12.6 3.3 %collective-permute-start.5 = (bf16[2,48,128]{2,1,0:T(8,128)(2,1)S(1)}, bf16[2,48,128]{2,1,0:T(8,128)(2,1)S(1)}, u32[]{:S(2)}, u32[]{:S(2)}) collective-permute-start(bf16[2,48,128]{2,1,0:T(8,128)(2,1)S(1)} %get-tuple-element.21), channel_id=1, source_target_pairs={{0,5},{1,2},{2,7},{3,0},{4,1},{5,6},{6,3},{7,4},{8,13},{9,10},{10,... | collective-permute-start | bytes 73736 | tf_op jit(solution)/shard_map/ppermute | solution.py:23
  14.1 1.8 %collective-permute-start.6 = (bf16[2,48,128]{2,1,0:T(8,128)(2,1)S(1)}, bf16[2,48,128]{2,1,0:T(8,128)(2,1)S(1)}, u32[]{:S(2)}, u32[]{:S(2)}) collective-permute-start(bf16[2,48,128]{2,1,0:T(8,128)(2,1)S(1)} %get-tuple-element.22), channel_id=1, source_target_pairs={{0,1},{1,0},{2,3},{3,2},{4,5},{5,4},{6,7},{7,6},{8,9},{9,8},{10,11... | collective-permute-start | bytes 73736 | tf_op jit(solution)/shard_map/ppermute | solution.py:23
  16.0 4.0 %collective-permute-start.7 = (bf16[1,48,128]{2,1,0:T(8,128)(2,1)S(1)}, bf16[1,48,128]{2,1,0:T(8,128)(2,1)S(1)}, u32[]{:S(2)}, u32[]{:S(2)}) collective-permute-start(bf16[1,48,128]{2,1,0:T(8,128)(2,1)S(1)} %get-tuple-element.23), channel_id=1, source_target_pairs={{0,9},{1,8},{2,11},{3,10},{4,13},{5,12},{6,15},{7,14},{8,1},{9,0},... | collective-permute-start | bytes 36872 | tf_op jit(solution)/shard_map/ppermute | solution.py:23
  18.7 1.4 %collective-permute-start.8 = (bf16[1,48,128]{2,1,0:T(8,128)(2,1)S(1)}, bf16[1,48,128]{2,1,0:T(8,128)(2,1)S(1)}, u32[]{:S(2)}, u32[]{:S(2)}) collective-permute-start(bf16[1,48,128]{2,1,0:T(8,128)(2,1)S(1)} %get-tuple-element.24), channel_id=1, source_target_pairs={{0,1},{1,0},{2,3},{3,2},{4,5},{5,4},{6,7},{7,6},{8,9},{9,8},{10,11... | collective-permute-start | bytes 36872 | tf_op jit(solution)/shard_map/ppermute | solution.py:23

commit v17 on v13

--- a/solution.py
+++ b/solution.py
@@ -231,9 +231,8 @@
             )
 
         for j in range(2 * part):
-            own, inner = divmod(j % part, rows_dev)
-            out_ref = send_ref if own else keep_ref
-            out_ref[j // part * (half // 2) + i * rows_dev + inner] = write(
+            out_ref = keep_ref if j < part else send_ref
+            out_ref[i * part + j % part] = write(
                 of_row(mixed, j),
                 to_row(of_row(point, j), diagonal), to_row(of_row(total, j), diagonal),
                 out_ref.dtype,
@@ -361,15 +360,15 @@
         rows_dev=rows_dev, sizes=sizes,
     )
     cross = 1 if shared_bits and lax.axis_size("heads") % 2 == 0 else 0
-    arrived = exchange(send, 1, 2, 1) if cross else exchange(send, 2, 1)
     turn = cross
     for bit in reversed(shared_bits):
+        arrived = exchange(send, bit, bit, turn)
         if turn:
             keep = exchange(keep, 0, 0, turn)
         half //= 2
         send, keep = call(merge_kernel, parcels(half), (arrived, keep), scale=scale)
-        turn = cross if bit == shared_bits[0] else 0
-        arrived = exchange(send, bit, bit, turn)
+        turn = 0
+    arrived = exchange(send, 2, 1, cross)
     if cross:
         keep = exchange(keep, 0, 0, cross)
     return call(

time: 21 us -> 21 us (level)
  no operation moved by 1% of the time
where the time goes in v17:
time: 21 us; the launch traced here: 20.8 us
  starting transfers between devices  14.5 us (69%)
  waiting for transfers between devices  2.79 us (13%)
  Pallas kernels  2.78 us (13%)
  local copies, waits for them, and re-layouts  0.7 us (3%)
    ppermute x9, starting transfers between devices, exchange(): return lax.ppermute(value, ('blk', 'heads'), pairs)  14.5 us
    ppermute x9, waiting for transfers between devices, exchange(): return lax.ppermute(value, ('blk', 'heads'), pairs)  2.79 us
    pallas_call x3, Pallas kernels, call(): pl.pallas_call(functools.partial(kernel, **static), out_shape=outs, in_sp...  1.54 us
    pallas_call x1, Pallas kernels, on_device(): pl.pallas_call(functools.partial(fetch_kernel, rows_dev=rows_dev, page_le...  1.24 us
    unnamed x1, local copies, waits for them, and re-layouts  0.7 us
  transfers between devices with their start and end apart: 9, of which 4 were waited for; matrix products, arithmetic and copies ran while one was open for 3% of the time, Pallas kernels for 6%

profile of v17, /device:TPU:0, one launch (start us, length us, event | category | flops | bytes accessed | tf_op | source)
XLA Modules:
  0.0 20.8 jit_solution(3485712096184685493)
XLA Ops:
  0.0 2.9 %collective-permute-start.2 = (bf16[1024,128]{1,0:T(8,128)(2,1)}, bf16[1024,128]{1,0:T(8,128)(2,1)S(1)}, u32[]{:S(2)}, u32[]{:S(2)}) collective-permute-start(bf16[1024,128]{1,0:T(8,128)(2,1)} %bitcast.3), channel_id=1, source_target_pairs={{0,2},{1,5},{2,0},{3,7},{4,6},{5,1},{6,4},{7,3},{8,10},{9,13},{10,... | collective-permute-start | bytes 786440 | tf_op jit(solution)/shard_map/ppermute | solution.py:23
  2.9 0.0 collective-permute-start.3
  3.0 2.1 %collective-permute-start = (bf16[1,32,128]{2,1,0:T(8,128)(2,1)}, bf16[1,32,128]{2,1,0:T(8,128)(2,1)S(1)}, u32[]{:S(2)}, u32[]{:S(2)}) collective-permute-start(bf16[1,32,128]{2,1,0:T(8,128)(2,1)} %param.8), channel_id=1, source_target_pairs={{0,4},{1,3},{2,6},{3,1},{4,0},{5,7},{6,2},{7,5},{8,12},{9,11},{10,... | collective-permute-start | bytes 24584 | tf_op jit(solution)/shard_map/ppermute | solution.py:23
  5.1 1.5 %collective-permute-start.4 = (bf16[384,128]{1,0:T(8,128)(2,1)}, bf16[384,128]{1,0:T(8,128)(2,1)S(1)}, u32[]{:S(2)}, u32[]{:S(2)}) collective-permute-start(bf16[384,128]{1,0:T(8,128)(2,1)} %bitcast.7), channel_id=1, source_target_pairs={{0,2},{1,5},{2,0},{3,7},{4,6},{5,1},{6,4},{7,3},{8,10},{9,13},{10,... | collective-permute-start | bytes 294920 | tf_op jit(solution)/shard_map/ppermute | solution.py:23
  6.5 0.7 %constant_dynamic-update-slice_fusion.1 = bf16[2,32,128]{2,1,0:T(8,128)(2,1)S(1)} fusion(bf16[1,32,128]{2,1,0:T(8,128)(2,1)} %param.8), kind=kLoop, calls=%fused_computation.1 | loop fusion | bytes 16384
  7.2 0.0 collective-permute-done
  7.3 2.8 %collective-permute-start.1 = (bf16[2,32,128]{2,1,0:T(8,128)(2,1)S(1)}, bf16[2,32,128]{2,1,0:T(8,128)(2,1)S(1)}, u32[]{:S(2)}, u32[]{:S(2)}) collective-permute-start(bf16[2,32,128]{2,1,0:T(8,128)(2,1)S(1)} %constant_dynamic-update-slice_fusion.queries_ref.first_ref), channel_id=1, source_target_pairs={{0,8},{1,9},{2,10},{3,11},{4,12},{5,13},{6,14},{7,15},{8,0},{9,1},... | collective-permute-start | bytes 49160 | tf_op jit(solution)/shard_map/ppermute | solution.py:23
  10.1 0.0 collective-permute-done.2.far_key_ref
  10.1 0.3 %collective-permute-done.3.far_value_ref = bf16[1024,128]{1,0:T(8,128)(2,1)S(1)} collective-permute-done((bf16[1024,128]{1,0:T(8,128)(2,1)}, bf16[1024,128]{1,0:T(8,128)(2,1)S(1)}, u32[]{:S(2)}, u32[]{:S(2)}) %collective-permute-start.3) | collective-permute-done | bytes 262176 | tf_op jit(solution)/shard_map/ppermute | solution.py:23
  10.4 1.2 %shard_map.82 = (bf16[4,256,128]{2,1,0:T(8,128)(2,1)S(1)}, bf16[4,256,128]{2,1,0:T(8,128)(2,1)S(1)}, bf16[4,256,128]{2,1,0:T(8,128)(2,1)S(1)}, bf16[4,256,128]{2...) custom-call(bf16[2,32,128]{2,1,0:T(8,128)(2,1)S(1)} %constant_dynamic-update-slice_, ...), custom_call_target="tpu_custom_call" | custom-call | tf_op jit(solution)/shard_map/pallas_call | solution.py:330
  11.6 0.2 %collective-permute-done.1.second_ref = bf16[2,32,128]{2,1,0:T(8,128)(2,1)S(1)} collective-permute-done((bf16[2,32,128]{2,1,0:T(8,128)(2,1)S(1)}, bf16[2,32,128]{2,1,0:T(8,128)(2,1)S(1)}, u32[]{:S(2)}, u32[]{:S(2)}) %collective-permute-start.1) | collective-permute-done | bytes 16416 | tf_op jit(solution)/shard_map/ppermute | solution.py:23
  11.9 0.0 collective-permute-done.4.refs_6_
  11.9 0.7 %shard_map.83 = (bf16[2,48,128]{2,1,0:T(8,128)(2,1)S(1)}, bf16[2,48,128]{2,1,0:T(8,128)(2,1)S(1)}) custom-call(bf16[2,32,128]{2,1,0:T(8,128)(2,1)S(1)} %constant_dynamic-update-slice_fusion.queries_ref.first_ref, bf16[2,32,128]{2,1,0:T(8,128)(2,1)S(1)} %collective-permute-done.1.second_ref, bf16[4,256,128]{2,1,0:T(8,128)(2,1)S(1)} %get-tuple-element.16.refs_0_, ...), custom_call_target="tpu_custom_call" | custom-call | tf_op jit(solution)/shard_map/pallas_call | solution.py:289
  12.6 1.5 %collective-permute-start.5 = (bf16[2,48,128]{2,1,0:T(8,128)(2,1)S(1)}, bf16[2,48,128]{2,1,0:T(8,128)(2,1)S(1)}, u32[]{:S(2)}, u32[]{:S(2)}) collective-permute-start(bf16[2,48,128]{2,1,0:T(8,128)(2,1)S(1)} %get-tuple-element.23), channel_id=1, source_target_pairs={{0,9},{1,8},{2,11},{3,10},{4,13},{5,12},{6,15},{7,14},{8,1},{9,0},... | collective-permute-start | bytes 73736 | tf_op jit(solution)/shard_map/ppermute | solution.py:23
  14.2 1.5 %collective-permute-start.6 = (bf16[2,48,128]{2,1,0:T(8,128)(2,1)S(1)}, bf16[2,48,128]{2,1,0:T(8,128)(2,1)S(1)}, u32[]{:S(2)}, u32[]{:S(2)}) collective-permute-start(bf16[2,48,128]{2,1,0:T(8,128)(2,1)S(1)} %get-tuple-element.24), channel_id=1, source_target_pairs={{0,1},{1,0},{2,3},{3,2},{4,5},{5,4},{6,7},{7,6},{8,9},{9,8},{10,11... | collective-permute-start | bytes 73736 | tf_op jit(solution)/shard_map/ppermute | solution.py:23
  15.7 1.1 %collective-permute-done.5.parcel_ref = bf16[2,48,128]{2,1,0:T(8,128)(2,1)S(1)} collective-permute-done((bf16[2,48,128]{2,1,0:T(8,128)(2,1)S(1)}, bf16[2,48,128]{2,1,0:T(8,128)(2,1)S(1)}, u32[]{:S(2)}, u32[]{:S(2)}) %collective-permute-start.5) | collective-permute-done | bytes 24608 | tf_op jit(solution)/shard_map/ppermute | solution.py:23
  16.8 0.0 collective-permute-done.6.keep_in
  16.8 0.1 shard_map.84
  16.9 1.5 %collective-permute-start.7 = (bf16[1,48,128]{2,1,0:T(8,128)(2,1)S(1)}, bf16[1,48,128]{2,1,0:T(8,128)(2,1)S(1)}, u32[]{:S(2)}, u32[]{:S(2)}) collective-permute-start(bf16[1,48,128]{2,1,0:T(8,128)(2,1)S(1)} %get-tuple-element.25), channel_id=1, source_target_pairs={{0,3},{1,4},{2,1},{3,6},{4,7},{5,0},{6,5},{7,2},{8,11},{9,12},{10,... | collective-permute-start | bytes 36872 | tf_op jit(solution)/shard_map/ppermute | solution.py:23
  18.5 0.5 %collective-permute-start.8 = (bf16[1,48,128]{2,1,0:T(8,128)(2,1)S(1)}, bf16[1,48,128]{2,1,0:T(8,128)(2,1)S(1)}, u32[]{:S(2)}, u32[]{:S(2)}) collective-permute-start(bf16[1,48,128]{2,1,0:T(8,128)(2,1)S(1)} %get-tuple-element.26), channel_id=1, source_target_pairs={{0,1},{1,0},{2,3},{3,2},{4,5},{5,4},{6,7},{7,6},{8,9},{9,8},{10,11... | collective-permute-start | bytes 36872 | tf_op jit(solution)/shard_map/ppermute | solution.py:23
  19.0 1.1 %collective-permute-done.7.parcel_ref = bf16[1,48,128]{2,1,0:T(8,128)(2,1)S(1)} collective-permute-done((bf16[1,48,128]{2,1,0:T(8,128)(2,1)S(1)}, bf16[1,48,128]{2,1,0:T(8,128)(2,1)S(1)}, u32[]{:S(2)}, u32[]{:S(2)}) %collective-permute-start.7) | collective-permute-done | bytes 12320 | tf_op jit(solution)/shard_map/ppermute | solution.py:23
  20.1 0.0 collective-permute-done.8.keep_in
  20.1 0.7 %shard_map.85 = bf16[1,32,128]{2,1,0:T(8,128)(2,1)} custom-call(bf16[1,48,128]{2,1,0:T(8,128)(2,1)S(1)} %collective-permute-done.7.parcel_ref, bf16[1,48,128]{2,1,0:T(8,128)(2,1)S(1)} %collective-permute-done.8.keep_in), custom_call_target="tpu_custom_call" | custom-call | tf_op jit(solution)/shard_map/pallas_call | solution.py:289
  (1 shorter events, 0.0 us)
Async XLA Ops:
  0.0 10.1 %collective-permute-start.2 = (bf16[1024,128]{1,0:T(8,128)(2,1)}, bf16[1024,128]{1,0:T(8,128)(2,1)S(1)}, u32[]{:S(2)}, u32[]{:S(2)}) collective-permute-start(bf16[1024,128]{1,0:T(8,128)(2,1)} %bitcast.3), channel_id=1, source_target_pairs={{0,2},{1,5},{2,0},{3,7},{4,6},{5,1},{6,4},{7,3},{8,10},{9,13},{10,... | collective-permute-start | bytes 786440 | tf_op jit(solution)/shard_map/ppermute | solution.py:23
  2.9 7.5 %collective-permute-start.3 = (bf16[1024,128]{1,0:T(8,128)(2,1)}, bf16[1024,128]{1,0:T(8,128)(2,1)S(1)}, u32[]{:S(2)}, u32[]{:S(2)}) collective-permute-start(bf16[1024,128]{1,0:T(8,128)(2,1)} %bitcast.5), channel_id=1, source_target_pairs={{0,2},{1,5},{2,0},{3,7},{4,6},{5,1},{6,4},{7,3},{8,10},{9,13},{10,... | collective-permute-start | bytes 786440 | tf_op jit(solution)/shard_map/ppermute | solution.py:23
  3.0 4.3 %collective-permute-start = (bf16[1,32,128]{2,1,0:T(8,128)(2,1)}, bf16[1,32,128]{2,1,0:T(8,128)(2,1)S(1)}, u32[]{:S(2)}, u32[]{:S(2)}) collective-permute-start(bf16[1,32,128]{2,1,0:T(8,128)(2,1)} %param.8), channel_id=1, source_target_pairs={{0,4},{1,3},{2,6},{3,1},{4,0},{5,7},{6,2},{7,5},{8,12},{9,11},{10,... | collective-permute-start | bytes 24584 | tf_op jit(solution)/shard_map/ppermute | solution.py:23
  5.1 6.8 %collective-permute-start.4 = (bf16[384,128]{1,0:T(8,128)(2,1)}, bf16[384,128]{1,0:T(8,128)(2,1)S(1)}, u32[]{:S(2)}, u32[]{:S(2)}) collective-permute-start(bf16[384,128]{1,0:T(8,128)(2,1)} %bitcast.7), channel_id=1, source_target_pairs={{0,2},{1,5},{2,0},{3,7},{4,6},{5,1},{6,4},{7,3},{8,10},{9,13},{10,... | collective-permute-start | bytes 294920 | tf_op jit(solution)/shard_map/ppermute | solution.py:23
  7.3 4.6 %collective-permute-start.1 = (bf16[2,32,128]{2,1,0:T(8,128)(2,1)S(1)}, bf16[2,32,128]{2,1,0:T(8,128)(2,1)S(1)}, u32[]{:S(2)}, u32[]{:S(2)}) collective-permute-start(bf16[2,32,128]{2,1,0:T(8,128)(2,1)S(1)} %constant_dynamic-update-slice_fusion.queries_ref.first_ref), channel_id=1, source_target_pairs={{0,8},{1,9},{2,10},{3,11},{4,12},{5,13},{6,14},{7,15},{8,0},{9,1},... | collective-permute-start | bytes 49160 | tf_op jit(solution)/shard_map/ppermute | solution.py:23
  12.6 4.2 %collective-permute-start.5 = (bf16[2,48,128]{2,1,0:T(8,128)(2,1)S(1)}, bf16[2,48,128]{2,1,0:T(8,128)(2,1)S(1)}, u32[]{:S(2)}, u32[]{:S(2)}) collective-permute-start(bf16[2,48,128]{2,1,0:T(8,128)(2,1)S(1)} %get-tuple-element.23), channel_id=1, source_target_pairs={{0,9},{1,8},{2,11},{3,10},{4,13},{5,12},{6,15},{7,14},{8,1},{9,0},... | collective-permute-start | bytes 73736 | tf_op jit(solution)/shard_map/ppermute | solution.py:23
  14.2 2.7 %collective-permute-start.6 = (bf16[2,48,128]{2,1,0:T(8,128)(2,1)S(1)}, bf16[2,48,128]{2,1,0:T(8,128)(2,1)S(1)}, u32[]{:S(2)}, u32[]{:S(2)}) collective-permute-start(bf16[2,48,128]{2,1,0:T(8,128)(2,1)S(1)} %get-tuple-element.24), channel_id=1, source_target_pairs={{0,1},{1,0},{2,3},{3,2},{4,5},{5,4},{6,7},{7,6},{8,9},{9,8},{10,11... | collective-permute-start | bytes 73736 | tf_op jit(solution)/shard_map/ppermute | solution.py:23
  16.9 3.1 %collective-permute-start.7 = (bf16[1,48,128]{2,1,0:T(8,128)(2,1)S(1)}, bf16[1,48,128]{2,1,0:T(8,128)(2,1)S(1)}, u32[]{:S(2)}, u32[]{:S(2)}) collective-permute-start(bf16[1,48,128]{2,1,0:T(8,128)(2,1)S(1)} %get-tuple-element.25), channel_id=1, source_target_pairs={{0,3},{1,4},{2,1},{3,6},{4,7},{5,0},{6,5},{7,2},{8,11},{9,12},{10,... | collective-permute-start | bytes 36872 | tf_op jit(solution)/shard_map/ppermute | solution.py:23
  18.5 1.6 %collective-permute-start.8 = (bf16[1,48,128]{2,1,0:T(8,128)(2,1)S(1)}, bf16[1,48,128]{2,1,0:T(8,128)(2,1)S(1)}, u32[]{:S(2)}, u32[]{:S(2)}) collective-permute-start(bf16[1,48,128]{2,1,0:T(8,128)(2,1)S(1)} %get-tuple-element.26), channel_id=1, source_target_pairs={{0,1},{1,0},{2,3},{3,2},{4,5},{5,4},{6,7},{7,6},{8,9},{9,8},{10,11... | collective-permute-start | bytes 36872 | tf_op jit(solution)/shard_map/ppermute | solution.py:23
